TPU v7x, 128 devices: a whole 4x4x4 slice. The times are simulated.
128 devices in a mesh: tensor: 8 (over z, x_hi), tokens: 16 (over y, x_lo, core).
Axes of the slice: x: 4 (x_hi: 2, x_lo: 2; x = x_hi * 2 + x_lo), y: 4, z: 4, core: 2. Of those that a mesh axis runs over, the one named last changes fastest.
Arguments:
- hidden: bfloat16 [4096, 8192], P('tokens', 'tensor'), may hold values from -24 to 24
- w_query: bfloat16 [8192, 8192], P(None, 'tensor'), may hold values from -0.0625 to 0.0625
- w_key: bfloat16 [8192, 1024], P(None, 'tensor'), may hold values from -0.0625 to 0.0625
- w_value: bfloat16 [8192, 1024], P(None, 'tensor'), may hold values from -0.0625 to 0.0625
- key_codes: int32 [4096, 1024], P('tokens', 'tensor'), may hold values from 0 to 15
- codebook: float32 [1024, 16], P('tensor'), may hold values from -24 to 24
- positions: int32 [4096], P('tokens'), may hold values from 0 to 3071, as said below
- cotangent: bfloat16 [4096, 8192], P('tokens', 'tensor'), may hold values from -6 to 6
Outputs:
- attention_out: bfloat16 [4096, 8192], P('tokens', 'tensor')
- codebook_grad: float32 [1024, 16], P('tensor')
Inputs may be any that keep to these rules, and one draw needn't show every extreme that they name: positions are 0 at the first token of each packed document and rise by one within it; exactly one document has 3072 tokens and every other is shorter.
All inputs are finite; a program needn't handle non-finite values.
Results may differ from a plain program's by a relative error of at most 0.0095.
The roundings to bfloat16 on the way count: a program that leaves them out, or rounds other values in their place, can miss the bound.
Values may be sent and summed in bfloat16 or wider, within the bound.
No kernel may reach another device: no remote copies, remote signals or barrier semaphores. Data moves between devices by JAX's collectives and lax.ppermute only.
A program may use at most 128 MiB of HBM per device.

v0:
```python
import functools
import math

import jax
import jax.numpy as jnp
from jax import lax
from jax.experimental import pallas as pl
from jax.experimental.pallas import tpu as pltpu
from jax.sharding import PartitionSpec as P

HD = 128
ROPE_BASE = 500000.0
NEG_BIG = -1e30
LOG2E = math.log2(math.e)
SCALE = 1.0 / math.sqrt(HD)
BLOCK = 512
NN = (((1,), (0,)), ((), ()))
TN = (((0,), (0,)), ((), ()))
TAIL = 16


def sincos(angle):
    turns = jnp.floor(angle * (2.0 / math.pi) + 0.5)
    r = angle - turns * 1.5703125
    r = r - turns * 4.837512969970703125e-4
    r = r - turns * 7.54978995489188216e-8
    z = r * r
    s = ((-1.9515295891e-4 * z + 8.3321608736e-3) * z - 1.6666654611e-1) * z * r + r
    c = ((2.443315711809948e-5 * z - 1.388731625493765e-3) * z + 4.166664568298827e-2) * z * z
    c = c - 0.5 * z + 1.0
    quadrant = turns.astype(jnp.int32)
    odd = (quadrant & 1) == 1
    sine = jnp.where(odd, c, s)
    cosine = jnp.where(odd, s, c)
    sine = jnp.where((quadrant & 2) == 0, sine, -sine)
    cosine = jnp.where(((quadrant + 1) & 2) == 0, cosine, -cosine)
    return sine, cosine


def slots(pieces):
    own, x, y1, y2, y3, core = pieces
    found = [(0, own, 0), (2, x, 0)]
    for y, ref in ((1, y1), (2, y2), (3, y3)):
        found += [(4 * y, ref, 0), (4 * y + 2, ref, 1)]
    return found + [(2 * j + 1, core, j) for j in range(8)]


def prep_kernel(
    rows, ranks, levels, heads,
    info, inverse, book, cot, p_own, p_x, p_y1, p_y2, p_y3, p_core,
    keys, cos_k, sin_k, codes, cot_t, packed_s,
):
    me = info[3]
    tall = rows + TAIL
    for bits, ref, at in slots((p_own, p_x, p_y1, p_y2, p_y3, p_core)):
        start = pl.multiple_of((me ^ bits) * tall, TAIL)
        packed_s[pl.ds(start, tall), :] = ref[at * tall : (at + 1) * tall, :]
    for h in range(heads):
        cot_t[h] = cot[:, h * HD : (h + 1) * HD].T
    eye = lax.broadcasted_iota(jnp.int32, (HD, HD), 0) == lax.broadcasted_iota(
        jnp.int32, (HD, HD), 1
    )
    lane = lax.broadcasted_iota(jnp.int32, (HD, HD), 1)
    ones = jnp.ones((2 * HD, HD), jnp.bfloat16)

    @pl.loop(0, ranks)
    def _(i):
        source = pl.multiple_of(i * tall, TAIL)
        tail = packed_s[pl.ds(source + rows, TAIL), :].astype(jnp.float32)
        for part in range(rows // HD):
            target = pl.multiple_of(i * rows + part * HD, HD)
            high = jnp.where(eye, tail[part : part + 1, :], 0.0)
            low = jnp.where(eye, tail[rows // HD + part : rows // HD + part + 1, :], 0.0)
            digits = jnp.concatenate([high, low], axis=1).astype(jnp.bfloat16)
            place = lax.dot_general(digits, ones, NN, preferred_element_type=jnp.float32)
            sine, cosine = sincos(place * inverse[...])
            sine = jnp.where(lane < HD // 2, -sine, sine)
            cos_k[pl.ds(target, HD), :] = cosine
            sin_k[pl.ds(target, HD), :] = sine
            raw = packed_s[pl.ds(source + part * HD, HD), :]
            codes[pl.ds(target, HD), :] = raw
            code = raw.astype(jnp.float32).astype(jnp.int32)
            layer = [book[e : e + 1, :] for e in range(levels)]
            bit = 1
            while len(layer) > 1:
                on = (code & bit) != 0
                layer = [jnp.where(on, layer[j + 1], layer[j]) for j in range(0, len(layer), 2)]
                bit *= 2
            deq = layer[0]
            turned = deq * cosine + pltpu.roll(deq, HD // 2, 1) * sine
            keys[pl.ds(target, HD), :] = turned.astype(jnp.bfloat16)


def project_kernel(count, names, started, place, *refs):
    pieces, refs = refs[:count], refs[count:]
    weights, refs = refs[: len(names)], refs[len(names) :]
    before, after = (refs[: len(names)], refs[len(names) :]) if started else ((), refs)
    step = pl.program_id(0)
    chunk = weights[0].shape[0]
    per = pieces[0].shape[1] // chunk

    @pl.when(step == 0)
    def _():
        for j, ref in enumerate(after):
            ref[...] = before[j][...] if started else jnp.zeros_like(ref)

    for n in range(count):
        @pl.when(step // per == n)
        def _():
            at = pl.multiple_of((step % per) * chunk, chunk)
            x = pieces[n][:, pl.ds(at, chunk)]
            for w, ref in zip(weights, after):
                ref[...] += jnp.dot(x, w[...], preferred_element_type=jnp.float32)


def visible_block(base, block, own, earliest, rows):
    key = base + lax.broadcasted_iota(jnp.int32, (block, rows), 0)
    query = own + lax.broadcasted_iota(jnp.int32, (block, rows), 1)
    return (key <= query) & (key >= earliest)


def over_blocks(info, rows, body):
    own, first, edge = info[0], info[1], info[2]
    last = (own + rows + BLOCK - 1) // BLOCK

    @pl.loop(first, last)
    def _(b):
        masked = (b * BLOCK < edge) | (b * BLOCK + BLOCK > own)

        @pl.when(masked)
        def _():
            body(b, True)

        @pl.when(jnp.logical_not(masked))
        def _():
            body(b, False)


def stats_kernel(
    heads, rows, levels, weight,
    info, q_pre, cos_k, sin_k, keys, early, true, codes, book,
    q_rot, q_t, log_total, bins, peak_s, mass_s,
):
    own = info[0]
    mine = pl.ds(pl.multiple_of(own, rows), rows)
    cos_q, sin_q = cos_k[mine, :], sin_k[mine, :]
    for h in range(heads):
        x = q_pre[:, h * HD : (h + 1) * HD]
        turned = (x * cos_q + pltpu.roll(x, HD // 2, 1) * sin_q).astype(jnp.bfloat16)
        q_rot[h] = turned
        q_t[h] = turned.T
    code = codes[...]
    for level in range(levels):
        entry = weight * (book[level : level + 1, :] - true[...])
        bins[level : level + 1, :] = jnp.sum(
            jnp.where(code == level, entry, 0.0), axis=0, keepdims=True
        )
    peak_s[...] = jnp.full_like(peak_s, NEG_BIG)
    mass_s[...] = jnp.zeros_like(mass_s)

    def body(b, masked):
        base = pl.multiple_of(b * BLOCK, BLOCK)
        k = keys[pl.ds(base, BLOCK), :]
        if masked:
            seen = visible_block(base, BLOCK, own, early[...], rows)
        for h in range(heads):
            t = lax.dot_general(k, q_t[h], NN, preferred_element_type=jnp.float32)
            t = t * (SCALE * LOG2E)
            if masked:
                t = jnp.where(seen, t, NEG_BIG)
            old = peak_s[h : h + 1, :]
            new = jnp.maximum(old, jnp.max(t, axis=0, keepdims=True))
            fresh = jnp.sum(jnp.exp2(t - new), axis=0, keepdims=True)
            mass_s[h : h + 1, :] = mass_s[h : h + 1, :] * jnp.exp2(old - new) + fresh
            peak_s[h : h + 1, :] = new

    over_blocks(info, rows, body)
    log_total[...] = peak_s[...] + jnp.log(mass_s[...]) * LOG2E


def grad_kernel(
    heads, rows, levels,
    info, q_rot, q_t, log_total, keys, early, cot, cot_t, cos_k, sin_k, codes, init,
    v_own, v_x, v_y1, v_y2, v_y3, v_core,
    out, bins, probs_s, out_s, delta_s, acc_s, values,
):
    own, first, me = info[0], info[1], info[3]

    for bits, ref, at in slots((v_own, v_x, v_y1, v_y2, v_y3, v_core)):
        start = pl.multiple_of((me ^ bits) * rows, rows)
        values[pl.ds(start, rows), :] = ref[at * rows : (at + 1) * rows, :]
    out_s[...] = jnp.zeros_like(out_s)

    def forward(b, masked):
        base = pl.multiple_of(b * BLOCK, BLOCK)
        k = keys[pl.ds(base, BLOCK), :]
        v = values[pl.ds(base, BLOCK), :]
        if masked:
            seen = visible_block(base, BLOCK, own, early[...], rows)
        for h in range(heads):
            s = lax.dot_general(k, q_t[h], NN, preferred_element_type=jnp.float32)
            p = jnp.exp2(s * (SCALE * LOG2E) - log_total[h : h + 1, :])
            if masked:
                p = jnp.where(seen, p, 0.0)
            probs_s[b - first, h] = p
            out_s[h] += lax.dot_general(
                p.astype(jnp.bfloat16), v, TN, preferred_element_type=jnp.float32
            )

    over_blocks(info, rows, forward)
    for h in range(heads):
        o = out_s[h].astype(jnp.bfloat16)
        out[:, h * HD : (h + 1) * HD] = o
        prod = cot[:, h * HD : (h + 1) * HD].astype(jnp.float32) * o.astype(jnp.float32)
        delta_s[h : h + 1, :] = jnp.sum(prod.T, axis=0, keepdims=True)
    acc_s[...] = jnp.zeros_like(acc_s)
    last = (own + rows + BLOCK - 1) // BLOCK

    @pl.loop(first, last)
    def _(b):
        base = pl.multiple_of(b * BLOCK, BLOCK)
        v = values[pl.ds(base, BLOCK), :]
        dk = jnp.zeros((BLOCK, HD), jnp.float32)
        for h in range(heads):
            dp = lax.dot_general(v, cot_t[h], NN, preferred_element_type=jnp.float32)
            ds = (probs_s[b - first, h] * (dp - delta_s[h : h + 1, :])).astype(jnp.bfloat16)
            dk = dk + lax.dot_general(ds, q_rot[h], NN, preferred_element_type=jnp.float32)
        dk = dk * SCALE
        g = dk * cos_k[pl.ds(base, BLOCK), :] - pltpu.roll(dk, HD // 2, 1) * sin_k[pl.ds(base, BLOCK), :]
        code = codes[pl.ds(base, BLOCK), :].astype(jnp.float32)
        for level in range(levels):
            chosen = jnp.where(code == level, g, 0.0)
            acc_s[level] += jnp.sum(chosen.reshape(BLOCK // 8, 8, HD), axis=0)

    bins[...] = init[...] + jnp.sum(acc_s[...], axis=1)


def vmem():
    return pl.BlockSpec(memory_space=pltpu.VMEM)


def smem():
    return pl.BlockSpec(memory_space=pltpu.SMEM)


def cost(flops, size):
    return pl.CostEstimate(flops=flops, bytes_accessed=size, transcendentals=0)


def shards(hidden, w_query, w_key, w_value, key_codes, codebook, positions, cotangent):
    rows, part = hidden.shape
    width = w_query.shape[1]
    heads = width // HD
    levels = codebook.shape[1]
    ranks = lax.axis_size("tokens")
    total = rows * ranks
    group = lax.axis_size("tensor")
    rank = lax.axis_index("tensor")
    me = lax.axis_index("tokens")
    own = me * rows
    bf16, f32 = jnp.bfloat16, jnp.float32

    cross = lambda x, d: lax.ppermute(x, "tokens", [(i, i ^ d) for i in range(ranks)])

    def everyone(x):
        x_side = cross(x, 2)
        pair = jnp.concatenate([x, x_side], axis=0)
        y_side = [cross(pair, 4 * y) for y in (1, 2, 3)]
        core = cross(jnp.concatenate([pair] + y_side, axis=0), 1)
        return (x, x_side, *y_side, core)

    flip = [(i, i ^ 1) for i in range(group)]
    up = [(i, (i + 2) % group) for i in range(group)]
    down = [(i, (i - 2) % group) for i in range(group)]
    send = functools.partial(lax.ppermute, axis_name="tensor")
    n = rows // 2
    other = send(hidden, perm=flip)
    low = send(hidden, perm=up)
    high = send(hidden, perm=down)
    far = jnp.concatenate([send(low[:n], perm=up), send(high[n:], perm=down)], axis=0)
    other_low = send(other, perm=up)
    other_high = send(other, perm=down)
    other_far = send(far, perm=flip)

    digits = jnp.stack([positions // 64 * 64, positions % 64]).reshape(2 * rows // HD, HD)
    digits = jnp.pad(digits, ((0, TAIL - digits.shape[0]), (0, 0)))
    packed = everyone(jnp.concatenate([key_codes, digits], axis=0).astype(bf16))
    index = own + jnp.arange(rows)
    early = (index - positions).astype(jnp.int32)
    info = jnp.stack([own, jnp.min(early) // BLOCK, jnp.max(early), me]).astype(jnp.int32)
    early = early[None, :]
    book = codebook.T
    inverse = jnp.exp((jnp.arange(HD) % (HD // 2)).astype(f32) * (-2.0 * math.log(ROPE_BASE) / HD))

    keys, cos_k, sin_k, codes, cot_t = pl.pallas_call(
        functools.partial(prep_kernel, rows, ranks, levels, heads),
        out_shape=(
            jax.ShapeDtypeStruct((total, HD), bf16),
            jax.ShapeDtypeStruct((total, HD), f32),
            jax.ShapeDtypeStruct((total, HD), f32),
            jax.ShapeDtypeStruct((total, HD), bf16),
            jax.ShapeDtypeStruct((heads, HD, rows), bf16),
        ),
        in_specs=[smem()] + [vmem()] * 9,
        out_specs=(vmem(),) * 5,
        scratch_shapes=[pltpu.VMEM((ranks * (rows + TAIL), HD), bf16)],
        compiler_params=pltpu.CompilerParams(vmem_limit_bytes=16 << 20),
        cost_estimate=cost(1 << 32, 16 << 20),
        name="prep",
    )(info, inverse[None, :], book, cotangent, *packed)

    def project(pieces, weights, sums, chunk):
        count, names = len(pieces), range(len(weights))
        per = part // chunk
        place = jnp.stack([shard for _, shard in pieces]).astype(jnp.int32)
        whole = lambda shape: pl.BlockSpec(shape, lambda i, place: (0, 0))
        sizes = [(rows, w.shape[1]) for w in weights]
        return pl.pallas_call(
            functools.partial(project_kernel, count, names, sums is not None),
            out_shape=[jax.ShapeDtypeStruct(size, f32) for size in sizes],
            grid_spec=pltpu.PrefetchScalarGridSpec(
                num_scalar_prefetch=1,
                grid=(count * per,),
                in_specs=[whole((rows, part))] * count
                + [
                    pl.BlockSpec((chunk, w.shape[1]), lambda i, place: (place[i // per] * per + i % per, 0))
                    for w in weights
                ]
                + ([whole(size) for size in sizes] if sums is not None else []),
                out_specs=[whole(size) for size in sizes],
            ),
            compiler_params=pltpu.CompilerParams(vmem_limit_bytes=20 << 20),
            cost_estimate=cost(
                2 * rows * part * count * sum(w.shape[1] for w in weights),
                part * count * sum(w.shape[1] for w in weights) * 2,
            ),
            name="project",
        )(place, *[piece for piece, _ in pieces], *weights, *(sums if sums is not None else ()))

    everything = (w_query, w_key, w_value)
    mate = rank ^ 1
    sums = project([(hidden, rank)], everything, None, part // 2)
    sums = project([(low, (rank - 2) % group), (high, (rank + 2) % group), (other, mate)], everything, sums, part // 2)
    rest = [
        (far, (rank + 4) % group),
        (other_low, (mate - 2) % group),
        (other_high, (mate + 2) % group),
        (other_far, (mate + 4) % group),
    ]
    (value_sum,) = project(rest, (w_value,), sums[2:], part)
    query_pre, key_true = project(rest, (w_query, w_key), sums[:2], part // 2)
    values = everyone(value_sum.astype(bf16))

    def log_totals(first, count):
        return pl.pallas_call(
            functools.partial(stats_kernel, count, rows, levels, levels / total),
            out_shape=(
                jax.ShapeDtypeStruct((count, rows, HD), bf16),
                jax.ShapeDtypeStruct((count, HD, rows), bf16),
                jax.ShapeDtypeStruct((count, rows), f32),
                jax.ShapeDtypeStruct((levels, HD), f32),
            ),
            in_specs=[smem()] + [vmem()] * 8,
            out_specs=(vmem(),) * 4,
            scratch_shapes=[pltpu.VMEM((count, rows), f32)] * 2,
            compiler_params=pltpu.CompilerParams(vmem_limit_bytes=16 << 20),
            cost_estimate=cost(2 * rows * width * total, 4 << 20),
            name="stats",
        )(info, query_pre, cos_k, sin_k, keys, early, key_true, key_codes, book)

    q_rot, q_t, log_total, init = log_totals(0, heads)

    most = total // BLOCK
    attention_out, local = pl.pallas_call(
        functools.partial(grad_kernel, heads, rows, levels),
        out_shape=(
            jax.ShapeDtypeStruct((rows, width), bf16),
            jax.ShapeDtypeStruct((levels, HD), f32),
        ),
        in_specs=[smem()] + [vmem()] * 17,
        out_specs=(vmem(),) * 2,
        scratch_shapes=[
            pltpu.VMEM((min(most, 7), heads, BLOCK, rows), f32),
            pltpu.VMEM((heads, rows, HD), f32),
            pltpu.VMEM((heads, rows), f32),
            pltpu.VMEM((levels, 8, HD), f32),
            pltpu.VMEM((total, HD), bf16),
        ],
        compiler_params=pltpu.CompilerParams(vmem_limit_bytes=42 << 20),
        cost_estimate=cost(8 * rows * width * total, 8 << 20),
        name="grad",
    )(info, q_rot, q_t, log_total, keys, early, cotangent, cot_t, cos_k, sin_k, codes, init, *values)
    for d in (1, 2, 4, 8):
        local = local + cross(local, d)
    return (attention_out, local.T)


def solution(mesh):
    placed = (
        P("tokens", "tensor"),
        P(None, "tensor"),
        P(None, "tensor"),
        P(None, "tensor"),
        P("tokens", "tensor"),
        P("tensor", None),
        P("tokens"),
        P("tokens", "tensor"),
    )
    return jax.shard_map(
        shards,
        mesh=mesh,
        in_specs=placed,
        out_specs=(P("tokens", "tensor"), P("tensor", None)),
        check_vma=False,
    )
```

profile of v0, /device:TPU:0, one launch (start us, length us, event | category | flops | bytes accessed | tf_op | source)
XLA Modules:
  0.0 148.6 jit_solution(11471966534218185502)
XLA Ops:
  0.6 4.2 %collective-permute-start.2 = (bf16[256,1024]{1,0:T(8,128)(2,1)}, bf16[256,1024]{1,0:T(8,128)(2,1)S(1)}, u32[]{:S(2)}, u32[]{:S(2)}) collective-permute-start(bf16[256,1024]{1,0:T(8,128)(2,1)} %refs_0_.1), channel_id=1, source_target_pairs={{0,96},{16,112},{32,0},{48,16},{64,32},{80,48},{96,64},{112,80},{1... | collective-permute-start | bytes 1572872 | tf_op jit(solution)/shard_map/ppermute | solution.py:279
  4.8 3.0 %collective-permute-start.4 = (bf16[256,1024]{1,0:T(8,128)(2,1)}, bf16[256,1024]{1,0:T(8,128)(2,1)}, u32[]{:S(2)}, u32[]{:S(2)}) collective-permute-start(bf16[256,1024]{1,0:T(8,128)(2,1)} %refs_0_.1), channel_id=1, source_target_pairs={{0,16},{16,0},{32,48},{48,32},{64,80},{80,64},{96,112},{112,96},{1... | collective-permute-start | bytes 1572872 | tf_op jit(solution)/shard_map/ppermute | solution.py:277
  7.8 1.9 %fusion.4 = (s32[]{:T(128)}, s32[]{:T(128)}, s32[256]{0:T(256)}, bf16[256]{0:T(256)(128)(2,1)S(1)}, bf16[256]{0:T(256)(128)(2,1)S(1)}) fusion(s32[256]{0:T(256)} %param.14, s32[]{:T(128)} %mul.20), kind=kLoop, calls=%fused_computation.35 | loop fusion | flops 6654 | bytes 3084 | tf_op jit(solution)/shard_map/reduce_min | solution.py:290
  13.8 5.9 %collective-permute-done.refs_0_ = bf16[256,1024]{1,0:T(8,128)(2,1)S(1)} collective-permute-done((bf16[256,1024]{1,0:T(8,128)(2,1)}, bf16[256,1024]{1,0:T(8,128)(2,1)S(1)}, u32[]{:S(2)}, u32[]{:S(2)}) %collective-permute-start) | collective-permute-done | bytes 524320 | tf_op jit(solution)/shard_map/ppermute | solution.py:278
  21.2 3.2 %collective-permute-start.3 = (bf16[128,1024]{1,0:T(8,128)(2,1)}, bf16[128,1024]{1,0:T(8,128)(2,1)}, u32[]{:S(2)}, u32[]{:S(2)}) collective-permute-start(bf16[128,1024]{1,0:T(8,128)(2,1)} %slice.9), channel_id=1, source_target_pairs={{0,96},{16,112},{32,0},{48,16},{64,32},{80,48},{96,64},{112,80},{1... | collective-permute-start | bytes 786440 | tf_op jit(solution)/shard_map/ppermute | solution.py:280
  24.4 5.8 %copy-done = bf16[8192,1024]{1,0:T(8,128)(2,1)S(1)} copy-done((bf16[8192,1024]{1,0:T(8,128)(2,1)S(1)}, bf16[8192,1024]{1,0:T(8,128)(2,1)}, u32[]{:S(2)}) %copy-start) | copy-done | bytes 16777240
  40.2 3.3 %collective-permute-start.10 = (bf16[544,128]{1,0:T(8,128)(2,1)S(1)}, bf16[544,128]{1,0:T(8,128)(2,1)S(1)}, u32[]{:S(2)}, u32[]{:S(2)}) collective-permute-start(bf16[544,128]{1,0:T(8,128)(2,1)S(1)} %pad_maximum_fusion), channel_id=1, source_target_pairs={{0,8},{1,9},{2,10},{3,11},{4,12},{5,13},{6,14},{7,15},{8,0},{9,1},... | collective-permute-start | bytes 417800 | tf_op jit(solution)/shard_map/ppermute | solution.py:263
  44.2 2.0 %collective-permute-start.5 = (bf16[256,1024]{1,0:T(8,128)(2,1)}, bf16[256,1024]{1,0:T(8,128)(2,1)S(1)}, u32[]{:S(2)}, u32[]{:S(2)}) collective-permute-start(bf16[256,1024]{1,0:T(8,128)(2,1)} %collective-permute-done.4.refs_2_), channel_id=1, source_target_pairs={{0,32},{16,48},{32,64},{48,80},{64,96},{80,112},{96,0},{112,16},{1... | collective-permute-start | bytes 1572872 | tf_op jit(solution)/shard_map/ppermute | solution.py:281
  48.2 3.1 %collective-permute-start.7 = (bf16[256,1024]{1,0:T(8,128)(2,1)S(1)}, bf16[256,1024]{1,0:T(8,128)(2,1)S(1)}, u32[]{:S(2)}, u32[]{:S(2)}) collective-permute-start(bf16[256,1024]{1,0:T(8,128)(2,1)S(1)} %constant_dynamic-update-slice_fusion.refs_0_), channel_id=1, source_target_pairs={{0,16},{16,0},{32,48},{48,32},{64,80},{80,64},{96,112},{112,96},{1... | collective-permute-start | bytes 1572872 | tf_op jit(solution)/shard_map/ppermute | solution.py:283
  53.6 5.8 %copy-done.1 = bf16[8192,1024]{1,0:T(8,128)(2,1)S(1)} copy-done((bf16[8192,1024]{1,0:T(8,128)(2,1)S(1)}, bf16[8192,1024]{1,0:T(8,128)(2,1)}, u32[]{:S(2)}) %copy-start.1) | copy-done | bytes 16777240
  61.0 5.7 %project.5 = (f32[256,1024]{1,0:T(8,128)S(1)}, f32[256,128]{1,0:T(8,128)S(1)}, f32[256,128]{1,0:T(8,128)S(1)}) custom-call(s32[3]{0:T(128)S(1)} %pad_add_fusion.2.place, bf16[256,1024]{1,0:T(8,128)(2,1)S(1)} %collective-permute-done.refs_0_, bf16[256,1024]{1,0:T(8,128)(2,1)S(1)} %collective-permute-done.2.refs_1_, ...), custom_call_target="tpu_custom_call" | custom-call | flops 2013265920 | bytes 7864320 | tf_op jit(solution)/shard_map/project/pallas_call | solution.py:318
  66.7 1.8 %project.7 = f32[256,128]{1,0:T(8,128)S(1)} custom-call(s32[4]{0:T(128)S(1)} %pad_add_fusion.1.place, bf16[256,1024]{1,0:T(8,128)(2,1)S(1)} %constant_dynamic-update-slice_fusion.refs_0_, bf16[256,1024]{1,0:T(8,128)(2,1)S(1)} %collective-permute-done.5.refs_1_, bf16[256,1024]{1,0:T(8,128)(2,1)S(1)} %collective-permute-done.6.refs_2_, ...), custom_call_target="tpu_custom_call" | custom-call | flops 268435456 | bytes 1048576 | tf_op jit(solution)/shard_map/project/pallas_call | solution.py:318
  69.4 3.5 %collective-permute-done.13.v_x = bf16[256,128]{1,0:T(8,128)(2,1)S(1)} collective-permute-done((bf16[256,128]{1,0:T(8,128)(2,1)S(1)}, bf16[256,128]{1,0:T(8,128)(2,1)S(1)}, u32[]{:S(2)}, u32[]{:S(2)}) %collective-permute-start.13) | collective-permute-done | bytes 65568 | tf_op jit(solution)/shard_map/ppermute | solution.py:263
  75.2 2.2 %collective-permute-start.16 = (bf16[512,128]{1,0:T(8,128)(2,1)S(1)}, bf16[512,128]{1,0:T(8,128)(2,1)S(1)}, u32[]{:S(2)}, u32[]{:S(2)}) collective-permute-start(bf16[512,128]{1,0:T(8,128)(2,1)S(1)} %pad_maximum_fusion.1), channel_id=1, source_target_pairs={{0,12},{1,13},{2,14},{3,15},{4,8},{5,9},{6,10},{7,11},{8,4},{9,5},... | collective-permute-start | bytes 393224 | tf_op jit(solution)/shard_map/ppermute | solution.py:263
  79.1 4.8 %collective-permute-done.15.v_y2 = bf16[512,128]{1,0:T(8,128)(2,1)S(1)} collective-permute-done((bf16[512,128]{1,0:T(8,128)(2,1)S(1)}, bf16[512,128]{1,0:T(8,128)(2,1)S(1)}, u32[]{:S(2)}, u32[]{:S(2)}) %collective-permute-start.15) | collective-permute-done | bytes 131104 | tf_op jit(solution)/shard_map/ppermute | solution.py:263
  84.2 6.5 %prep.1 = (bf16[4096,128]{1,0:T(8,128)(2,1)S(1)}, f32[4096,128]{1,0:T(8,128)S(1)}, f32[4096,128]{1,0:T(8,128)S(1)}, bf16[4096,128]{1,0:T(8,128)(2,1)S(1)}, bf16[8,128,256]{2,1,0:T(8,128)(2,1)S(1)}) custom-call(s32[4]{0:T(128)S(1)} %pad_add_fusion.info, f32[1,128]{1,0:T(1,128)S(1)} %copy-done.13, f32[16,128]{1,0:T(8,128)S(1)} %bitcast.20, ...), custom_call_target="tpu_custom_call" | custom-call | flops 4294967296 | bytes 16777216 | tf_op jit(solution)/shard_map/prep/pallas_call | solution.py:295
  92.6 5.0 %project.6 = (f32[256,1024]{1,0:T(8,128)S(1)}, f32[256,128]{1,0:T(8,128)S(1)}) custom-call(s32[4]{0:T(128)S(1)} %pad_add_fusion.1.place, bf16[256,1024]{1,0:T(8,128)(2,1)S(1)} %constant_dynamic-update-slice_fusion.refs_0_, bf16[256,1024]{1,0:T(8,128)(2,1)S(1)} %collective-permute-done.5.refs_1_, bf16[256,1024]{1,0:T(8,128)(2,1)S(1)} %collective-permute-done.6.refs_2_, ...), custom_call_target="tpu_custom_call" | custom-call | flops 2415919104 | bytes 9437184 | tf_op jit(solution)/shard_map/project/pallas_call | solution.py:318
  97.7 3.1 %stats.1 = (bf16[8,256,128]{2,1,0:T(8,128)(2,1)S(1)}, bf16[8,128,256]{2,1,0:T(8,128)(2,1)S(1)}, f32[8,256]{1,0:T(8,128)S(1)}, f32[16,128]{1,0:T(8,128)S(1)}) custom-call(s32[4]{0:T(128)S(1)} %pad_add_fusion.info, f32[256,1024]{1,0:T(8,128)S(1)} %get-tuple-element.26.q_pre, f32[4096,128]{1,0:T(8,128)S(1)} %get-tuple-element.27.cos_k, ...), custom_call_target="tpu_custom_call" | custom-call | flops 2147483648 | bytes 4194304 | tf_op jit(solution)/shard_map/stats/pallas_call | solution.py:355
  105.3 5.1 %grad.1 = (bf16[256,1024]{1,0:T(8,128)(2,1)}, f32[16,128]{1,0:T(8,128)S(1)}) custom-call(s32[4]{0:T(128)S(1)} %pad_add_fusion.info, bf16[8,256,128]{2,1,0:T(8,128)(2,1)S(1)} %get-tuple-element.31.q_rot, bf16[8,128,256]{2,1,0:T(8,128)(2,1)S(1)} %get-tuple-element.32.q_t, f32[8,256]{1,0:T(8,128)S(1)} %get-tuple-element.33.log_total, ...), custom_call_target="tpu_custom_call" | custom-call | flops 8589934592 | bytes 8388608 | tf_op jit(solution)/shard_map/grad/pallas_call | solution.py:374
  111.7 5.2 %collective-permute-start.19 = (f32[16,128]{1,0:T(8,128)S(1)}, f32[16,128]{1,0:T(8,128)S(1)}, u32[]{:S(2)}, u32[]{:S(2)}) collective-permute-start(f32[16,128]{1,0:T(8,128)S(1)} %add.88), channel_id=1, source_target_pairs={{0,2},{1,3},{2,0},{3,1},{4,6},{5,7},{6,4},{7,5},{8,10},{9,11},{10,... | collective-permute-start | bytes 24584 | tf_op jit(solution)/shard_map/ppermute | solution.py:263
  116.9 1.6 %collective-permute-done.19 = f32[16,128]{1,0:T(8,128)S(1)} collective-permute-done((f32[16,128]{1,0:T(8,128)S(1)}, f32[16,128]{1,0:T(8,128)S(1)}, u32[]{:S(2)}, u32[]{:S(2)}) %collective-permute-start.19) | collective-permute-done | bytes 8224 | tf_op jit(solution)/shard_map/ppermute | solution.py:263
  118.5 5.3 %collective-permute-start.20 = (f32[16,128]{1,0:T(8,128)S(1)}, f32[16,128]{1,0:T(8,128)S(1)}, u32[]{:S(2)}, u32[]{:S(2)}) collective-permute-start(f32[16,128]{1,0:T(8,128)S(1)} %add.89), channel_id=1, source_target_pairs={{0,4},{1,5},{2,6},{3,7},{4,0},{5,1},{6,2},{7,3},{8,12},{9,13},{10,... | collective-permute-start | bytes 24584 | tf_op jit(solution)/shard_map/ppermute | solution.py:263
  123.9 1.6 %collective-permute-done.20 = f32[16,128]{1,0:T(8,128)S(1)} collective-permute-done((f32[16,128]{1,0:T(8,128)S(1)}, f32[16,128]{1,0:T(8,128)S(1)}, u32[]{:S(2)}, u32[]{:S(2)}) %collective-permute-start.20) | collective-permute-done | bytes 8224 | tf_op jit(solution)/shard_map/ppermute | solution.py:263
  125.5 20.9 %collective-permute-start.21 = (f32[16,128]{1,0:T(8,128)S(1)}, f32[16,128]{1,0:T(8,128)S(1)}, u32[]{:S(2)}, u32[]{:S(2)}) collective-permute-start(f32[16,128]{1,0:T(8,128)S(1)} %add.90), channel_id=1, source_target_pairs={{0,8},{1,9},{2,10},{3,11},{4,12},{5,13},{6,14},{7,15},{8,0},{9,1},... | collective-permute-start | bytes 24584 | tf_op jit(solution)/shard_map/ppermute | solution.py:263
  (121 shorter events, 34.5 us)
Async XLA Ops:
  0.6 19.8 %collective-permute-start.2 = (bf16[256,1024]{1,0:T(8,128)(2,1)}, bf16[256,1024]{1,0:T(8,128)(2,1)S(1)}, u32[]{:S(2)}, u32[]{:S(2)}) collective-permute-start(bf16[256,1024]{1,0:T(8,128)(2,1)} %refs_0_.1), channel_id=1, source_target_pairs={{0,96},{16,112},{32,0},{48,16},{64,32},{80,48},{96,64},{112,80},{1... | collective-permute-start | bytes 1572872 | tf_op jit(solution)/shard_map/ppermute | solution.py:279
  4.8 14.8 %collective-permute-start = (bf16[256,1024]{1,0:T(8,128)(2,1)}, bf16[256,1024]{1,0:T(8,128)(2,1)S(1)}, u32[]{:S(2)}, u32[]{:S(2)}) collective-permute-start(bf16[256,1024]{1,0:T(8,128)(2,1)} %refs_0_.1), channel_id=1, source_target_pairs={{0,32},{16,48},{32,64},{48,80},{64,96},{80,112},{96,0},{112,16},{1... | collective-permute-start | bytes 1572872 | tf_op jit(solution)/shard_map/ppermute | solution.py:278
  4.8 39.4 %collective-permute-start.4 = (bf16[256,1024]{1,0:T(8,128)(2,1)}, bf16[256,1024]{1,0:T(8,128)(2,1)}, u32[]{:S(2)}, u32[]{:S(2)}) collective-permute-start(bf16[256,1024]{1,0:T(8,128)(2,1)} %refs_0_.1), channel_id=1, source_target_pairs={{0,16},{16,0},{32,48},{48,32},{64,80},{80,64},{96,112},{112,96},{1... | collective-permute-start | bytes 1572872 | tf_op jit(solution)/shard_map/ppermute | solution.py:277
  12.5 26.7 %collective-permute-start.8 = (bf16[272,128]{1,0:T(8,128)(2,1)S(1)}, bf16[272,128]{1,0:T(8,128)(2,1)S(1)}, u32[]{:S(2)}, u32[]{:S(2)}) collective-permute-start(bf16[272,128]{1,0:T(8,128)(2,1)S(1)} %pad_maximum_fusion.2.p_own), channel_id=1, source_target_pairs={{0,2},{1,3},{2,0},{3,1},{4,6},{5,7},{6,4},{7,5},{8,10},{9,11},{10,... | collective-permute-start | bytes 208904 | tf_op jit(solution)/shard_map/ppermute | solution.py:263
  20.3 23.9 %collective-permute-start.1 = (bf16[128,1024]{1,0:T(8,128)(2,1)}, bf16[128,1024]{1,0:T(8,128)(2,1)}, u32[]{:S(2)}, u32[]{:S(2)}) collective-permute-start(bf16[128,1024]{1,0:T(8,128)(2,1)} %slice.8), channel_id=1, source_target_pairs={{0,32},{16,48},{32,64},{48,80},{64,96},{80,112},{96,0},{112,16},{1... | collective-permute-start | bytes 786440 | tf_op jit(solution)/shard_map/ppermute | solution.py:280
  21.2 26.0 %collective-permute-start.3 = (bf16[128,1024]{1,0:T(8,128)(2,1)}, bf16[128,1024]{1,0:T(8,128)(2,1)}, u32[]{:S(2)}, u32[]{:S(2)}) collective-permute-start(bf16[128,1024]{1,0:T(8,128)(2,1)} %slice.9), channel_id=1, source_target_pairs={{0,96},{16,112},{32,0},{48,16},{64,32},{80,48},{96,64},{112,80},{1... | collective-permute-start | bytes 786440 | tf_op jit(solution)/shard_map/ppermute | solution.py:280
  40.2 12.7 %collective-permute-start.10 = (bf16[544,128]{1,0:T(8,128)(2,1)S(1)}, bf16[544,128]{1,0:T(8,128)(2,1)S(1)}, u32[]{:S(2)}, u32[]{:S(2)}) collective-permute-start(bf16[544,128]{1,0:T(8,128)(2,1)S(1)} %pad_maximum_fusion), channel_id=1, source_target_pairs={{0,8},{1,9},{2,10},{3,11},{4,12},{5,13},{6,14},{7,15},{8,0},{9,1},... | collective-permute-start | bytes 417800 | tf_op jit(solution)/shard_map/ppermute | solution.py:263
  43.5 8.4 %collective-permute-start.9 = (bf16[544,128]{1,0:T(8,128)(2,1)S(1)}, bf16[544,128]{1,0:T(8,128)(2,1)S(1)}, u32[]{:S(2)}, u32[]{:S(2)}) collective-permute-start(bf16[544,128]{1,0:T(8,128)(2,1)S(1)} %pad_maximum_fusion), channel_id=1, source_target_pairs={{0,4},{1,5},{2,6},{3,7},{4,0},{5,1},{6,2},{7,3},{8,12},{9,13},{10,... | collective-permute-start | bytes 417800 | tf_op jit(solution)/shard_map/ppermute | solution.py:263
  44.2 22.5 %collective-permute-start.6 = (bf16[256,1024]{1,0:T(8,128)(2,1)}, bf16[256,1024]{1,0:T(8,128)(2,1)S(1)}, u32[]{:S(2)}, u32[]{:S(2)}) collective-permute-start(bf16[256,1024]{1,0:T(8,128)(2,1)} %collective-permute-done.4.refs_2_), channel_id=1, source_target_pairs={{0,96},{16,112},{32,0},{48,16},{64,32},{80,48},{96,64},{112,80},{1... | collective-permute-start | bytes 1572872 | tf_op jit(solution)/shard_map/ppermute | solution.py:282
  44.2 22.5 %collective-permute-start.5 = (bf16[256,1024]{1,0:T(8,128)(2,1)}, bf16[256,1024]{1,0:T(8,128)(2,1)S(1)}, u32[]{:S(2)}, u32[]{:S(2)}) collective-permute-start(bf16[256,1024]{1,0:T(8,128)(2,1)} %collective-permute-done.4.refs_2_), channel_id=1, source_target_pairs={{0,32},{16,48},{32,64},{48,80},{64,96},{80,112},{96,0},{112,16},{1... | collective-permute-start | bytes 1572872 | tf_op jit(solution)/shard_map/ppermute | solution.py:281
  48.2 18.5 %collective-permute-start.7 = (bf16[256,1024]{1,0:T(8,128)(2,1)S(1)}, bf16[256,1024]{1,0:T(8,128)(2,1)S(1)}, u32[]{:S(2)}, u32[]{:S(2)}) collective-permute-start(bf16[256,1024]{1,0:T(8,128)(2,1)S(1)} %constant_dynamic-update-slice_fusion.refs_0_), channel_id=1, source_target_pairs={{0,16},{16,0},{32,48},{48,32},{64,80},{80,64},{96,112},{112,96},{1... | collective-permute-start | bytes 1572872 | tf_op jit(solution)/shard_map/ppermute | solution.py:283
  51.9 17.4 %collective-permute-start.11 = (bf16[544,128]{1,0:T(8,128)(2,1)S(1)}, bf16[544,128]{1,0:T(8,128)(2,1)S(1)}, u32[]{:S(2)}, u32[]{:S(2)}) collective-permute-start(bf16[544,128]{1,0:T(8,128)(2,1)S(1)} %pad_maximum_fusion), channel_id=1, source_target_pairs={{0,12},{1,13},{2,14},{3,15},{4,8},{5,9},{6,10},{7,11},{8,4},{9,5},... | collective-permute-start | bytes 417800 | tf_op jit(solution)/shard_map/ppermute | solution.py:263
  61.0 31.6 %slice-start.1 = ((s8[16777216]{0:T(1024)(128)(4,1)}), s8[4194304]{0:T(1024)(128)(4,1)S(1)}, s32[]{:S(2)}) async-start(s8[16777216]{0:T(1024)(128)(4,1)} %bitcast.16), calls=%async_computation.1 | async-start | bytes 8388608
  61.0 31.6 %slice-start.2 = ((s8[16777216]{0:T(1024)(128)(4,1)}), s8[4194304]{0:T(1024)(128)(4,1)S(1)}, s32[]{:S(2)}) async-start(s8[16777216]{0:T(1024)(128)(4,1)} %bitcast.16), calls=%async_computation.2 | async-start | bytes 8388608
  68.6 4.3 %collective-permute-start.13 = (bf16[256,128]{1,0:T(8,128)(2,1)S(1)}, bf16[256,128]{1,0:T(8,128)(2,1)S(1)}, u32[]{:S(2)}, u32[]{:S(2)}) collective-permute-start(bf16[256,128]{1,0:T(8,128)(2,1)S(1)} %get-tuple-element.43.v_own), channel_id=1, source_target_pairs={{0,2},{1,3},{2,0},{3,1},{4,6},{5,7},{6,4},{7,5},{8,10},{9,11},{10,... | collective-permute-start | bytes 196616 | tf_op jit(solution)/shard_map/ppermute | solution.py:263
  69.3 14.9 %collective-permute-start.12 = (bf16[2176,128]{1,0:T(8,128)(2,1)S(1)}, bf16[2176,128]{1,0:T(8,128)(2,1)S(1)}, u32[]{:S(2)}, u32[]{:S(2)}) collective-permute-start(bf16[2176,128]{1,0:T(8,128)(2,1)S(1)} %constant_dynamic-update-slice_fusion.2), channel_id=1, source_target_pairs={{0,1},{1,0},{2,3},{3,2},{4,5},{5,4},{6,7},{7,6},{8,9},{9,8},{10,11... | collective-permute-start | bytes 1671176 | tf_op jit(solution)/shard_map/ppermute | solution.py:263
  72.9 6.1 %collective-permute-start.14 = (bf16[512,128]{1,0:T(8,128)(2,1)S(1)}, bf16[512,128]{1,0:T(8,128)(2,1)S(1)}, u32[]{:S(2)}, u32[]{:S(2)}) collective-permute-start(bf16[512,128]{1,0:T(8,128)(2,1)S(1)} %pad_maximum_fusion.1), channel_id=1, source_target_pairs={{0,4},{1,5},{2,6},{3,7},{4,0},{5,1},{6,2},{7,3},{8,12},{9,13},{10,... | collective-permute-start | bytes 393224 | tf_op jit(solution)/shard_map/ppermute | solution.py:263
  75.2 8.7 %collective-permute-start.16 = (bf16[512,128]{1,0:T(8,128)(2,1)S(1)}, bf16[512,128]{1,0:T(8,128)(2,1)S(1)}, u32[]{:S(2)}, u32[]{:S(2)}) collective-permute-start(bf16[512,128]{1,0:T(8,128)(2,1)S(1)} %pad_maximum_fusion.1), channel_id=1, source_target_pairs={{0,12},{1,13},{2,14},{3,15},{4,8},{5,9},{6,10},{7,11},{8,4},{9,5},... | collective-permute-start | bytes 393224 | tf_op jit(solution)/shard_map/ppermute | solution.py:263
  77.4 6.5 %collective-permute-start.15 = (bf16[512,128]{1,0:T(8,128)(2,1)S(1)}, bf16[512,128]{1,0:T(8,128)(2,1)S(1)}, u32[]{:S(2)}, u32[]{:S(2)}) collective-permute-start(bf16[512,128]{1,0:T(8,128)(2,1)S(1)} %pad_maximum_fusion.1), channel_id=1, source_target_pairs={{0,8},{1,9},{2,10},{3,11},{4,12},{5,13},{6,14},{7,15},{8,0},{9,1},... | collective-permute-start | bytes 393224 | tf_op jit(solution)/shard_map/ppermute | solution.py:263
  83.9 16.9 %collective-permute-start.17 = (bf16[2048,128]{1,0:T(8,128)(2,1)S(1)}, bf16[2048,128]{1,0:T(8,128)(2,1)S(1)}, u32[]{:S(2)}, u32[]{:S(2)}) collective-permute-start(bf16[2048,128]{1,0:T(8,128)(2,1)S(1)} %constant_dynamic-update-slice_fusion.8), channel_id=1, source_target_pairs={{0,1},{1,0},{2,3},{3,2},{4,5},{5,4},{6,7},{7,6},{8,9},{9,8},{10,11... | collective-permute-start | bytes 1572872 | tf_op jit(solution)/shard_map/ppermute | solution.py:263
  110.4 1.3 collective-permute-start.18
  111.7 6.8 %collective-permute-start.19 = (f32[16,128]{1,0:T(8,128)S(1)}, f32[16,128]{1,0:T(8,128)S(1)}, u32[]{:S(2)}, u32[]{:S(2)}) collective-permute-start(f32[16,128]{1,0:T(8,128)S(1)} %add.88), channel_id=1, source_target_pairs={{0,2},{1,3},{2,0},{3,1},{4,6},{5,7},{6,4},{7,5},{8,10},{9,11},{10,... | collective-permute-start | bytes 24584 | tf_op jit(solution)/shard_map/ppermute | solution.py:263
  118.5 6.9 %collective-permute-start.20 = (f32[16,128]{1,0:T(8,128)S(1)}, f32[16,128]{1,0:T(8,128)S(1)}, u32[]{:S(2)}, u32[]{:S(2)}) collective-permute-start(f32[16,128]{1,0:T(8,128)S(1)} %add.89), channel_id=1, source_target_pairs={{0,4},{1,5},{2,6},{3,7},{4,0},{5,1},{6,2},{7,3},{8,12},{9,13},{10,... | collective-permute-start | bytes 24584 | tf_op jit(solution)/shard_map/ppermute | solution.py:263
  125.5 22.5 %collective-permute-start.21 = (f32[16,128]{1,0:T(8,128)S(1)}, f32[16,128]{1,0:T(8,128)S(1)}, u32[]{:S(2)}, u32[]{:S(2)}) collective-permute-start(f32[16,128]{1,0:T(8,128)S(1)} %add.90), channel_id=1, source_target_pairs={{0,8},{1,9},{2,10},{3,11},{4,12},{5,13},{6,14},{7,15},{8,0},{9,1},... | collective-permute-start | bytes 24584 | tf_op jit(solution)/shard_map/ppermute | solution.py:263
  (29 other events, 186.1 us)
where the time goes:
time: 151 us; the launch traced here: 149 us
  starting transfers between devices  57.9 us (38%)
  local copies, waits for them, and re-layouts  31.3 us (21%)
  Pallas kernels  28.5 us (19%)
  waiting for transfers between devices  20.7 us (14%)
  other arithmetic  6.53 us (4%)
  between operations  3.6 us (2%)
    ppermute x14, starting transfers between devices, shards(): lax.ppermute(x, 'tokens', [(i, i ^ d) for i in range(ranks)])  42.3 us
    unnamed x70, local copies, waits for them, and re-layouts  28.8 us
    ppermute x14, waiting for transfers between devices, shards(): lax.ppermute(x, 'tokens', [(i, i ^ d) for i in range(ranks)])  14.9 us
    pallas_call x4, Pallas kernels, project(): pl.pallas_call(functools.partial(project_kernel, count, names, sums is no...  13.8 us
    pallas_call x1, Pallas kernels, shards(): pl.pallas_call(functools.partial(prep_kernel, rows, ranks, levels, heads)...  6.51 us
    ppermute x1, waiting for transfers between devices, shards(): low = send(hidden, perm=up)  5.85 us
    pallas_call x1, Pallas kernels, shards(): pl.pallas_call(functools.partial(grad_kernel, heads, rows, levels), out_s...  5.14 us
    ppermute x1, starting transfers between devices, shards(): high = send(hidden, perm=down)  4.19 us
  transfers between devices with their start and end apart: 22, of which 8 were waited for; matrix products, arithmetic and copies ran while one was open for 8% of the time, Pallas kernels for 16%

commit v1 on v0

v1 whole, which is shorter than its diff:
```python
import functools
import math

import jax
import jax.numpy as jnp
from jax import lax
from jax.experimental import pallas as pl
from jax.experimental.pallas import tpu as pltpu
from jax.sharding import PartitionSpec as P

HD = 128
ROPE_BASE = 500000.0
NEG_BIG = -1e30
LOG2E = math.log2(math.e)
SCALE = 1.0 / math.sqrt(HD)
BLOCK = 512
NN = (((1,), (0,)), ((), ()))
TN = (((0,), (0,)), ((), ()))
TAIL = 16


def sincos(angle):
    turns = jnp.floor(angle * (2.0 / math.pi) + 0.5)
    r = angle - turns * 1.5703125
    r = r - turns * 4.837512969970703125e-4
    r = r - turns * 7.54978995489188216e-8
    z = r * r
    s = ((-1.9515295891e-4 * z + 8.3321608736e-3) * z - 1.6666654611e-1) * z * r + r
    c = ((2.443315711809948e-5 * z - 1.388731625493765e-3) * z + 4.166664568298827e-2) * z * z
    c = c - 0.5 * z + 1.0
    quadrant = turns.astype(jnp.int32)
    odd = (quadrant & 1) == 1
    sine = jnp.where(odd, c, s)
    cosine = jnp.where(odd, s, c)
    sine = jnp.where((quadrant & 2) == 0, sine, -sine)
    cosine = jnp.where(((quadrant + 1) & 2) == 0, cosine, -cosine)
    return sine, cosine


def slots(pieces):
    own, x, y1, y2, y3, core = pieces
    found = [(0, own, 0), (2, x, 0)]
    for y, ref in ((1, y1), (2, y2), (3, y3)):
        found += [(4 * y, ref, 0), (4 * y + 2, ref, 1)]
    return found + [(2 * j + 1, core, j) for j in range(8)]


def token_rank():
    return lax.axis_index("tokens")


def pack_kernel(rows, key_codes, positions, packed, early, info):
    packed[:rows, :] = key_codes[...].astype(jnp.float32).astype(jnp.bfloat16)
    place = positions[...]
    high, low = place & ~63, place & 63
    wide = [x[:, j * HD : (j + 1) * HD] for x in (high, low) for j in range(rows // HD)]
    blank = jnp.zeros((TAIL - len(wide), HD), jnp.int32)
    tail = jnp.concatenate(wide + [blank], axis=0)
    packed[rows:, :] = tail.astype(jnp.float32).astype(jnp.bfloat16)
    index = token_rank() * rows + lax.broadcasted_iota(jnp.int32, (1, rows), 1)
    first = index - place
    early[...] = first
    first = first.astype(jnp.float32)
    info[0] = jnp.min(first).astype(jnp.int32) // BLOCK
    info[1] = jnp.max(first).astype(jnp.int32)


def prep_kernel(
    rows, ranks, levels, heads,
    inverse, book, cot, p_own, p_x, p_y1, p_y2, p_y3, p_core,
    keys, cos_k, sin_k, codes, cot_t, packed_s, sems,
):
    me = token_rank()
    tall = rows + TAIL
    copies = []
    for j, (bits, ref, at) in enumerate(slots((p_own, p_x, p_y1, p_y2, p_y3, p_core))):
        start = pl.multiple_of((me ^ bits) * tall, TAIL)
        copies.append(
            pltpu.make_async_copy(
                ref.at[at * tall : (at + 1) * tall, :], packed_s.at[pl.ds(start, tall), :], sems.at[j]
            )
        )
    for copy in copies:
        copy.start()
    for h in range(heads):
        cot_t[h] = cot[:, h * HD : (h + 1) * HD].T
    for copy in copies:
        copy.wait()
    eye = lax.broadcasted_iota(jnp.int32, (HD, HD), 0) == lax.broadcasted_iota(
        jnp.int32, (HD, HD), 1
    )
    lane = lax.broadcasted_iota(jnp.int32, (HD, HD), 1)
    ones = jnp.ones((2 * HD, HD), jnp.bfloat16)

    @pl.loop(0, ranks)
    def _(i):
        source = pl.multiple_of(i * tall, TAIL)
        tail = packed_s[pl.ds(source + rows, TAIL), :].astype(jnp.float32)
        for part in range(rows // HD):
            target = pl.multiple_of(i * rows + part * HD, HD)
            high = jnp.where(eye, tail[part : part + 1, :], 0.0)
            low = jnp.where(eye, tail[rows // HD + part : rows // HD + part + 1, :], 0.0)
            digits = jnp.concatenate([high, low], axis=1).astype(jnp.bfloat16)
            place = lax.dot_general(digits, ones, NN, preferred_element_type=jnp.float32)
            sine, cosine = sincos(place * inverse[...])
            sine = jnp.where(lane < HD // 2, -sine, sine)
            cos_k[pl.ds(target, HD), :] = cosine
            sin_k[pl.ds(target, HD), :] = sine
            raw = packed_s[pl.ds(source + part * HD, HD), :]
            codes[pl.ds(target, HD), :] = raw
            code = raw.astype(jnp.float32).astype(jnp.int32)
            layer = [book[e : e + 1, :] for e in range(levels)]
            bit = 1
            while len(layer) > 1:
                on = (code & bit) != 0
                layer = [jnp.where(on, layer[j + 1], layer[j]) for j in range(0, len(layer), 2)]
                bit *= 2
            deq = layer[0]
            turned = deq * cosine + pltpu.roll(deq, HD // 2, 1) * sine
            keys[pl.ds(target, HD), :] = turned.astype(jnp.bfloat16)


def project_kernel(pieces_at, chunk, count, started, place, *refs):
    pieces, refs = refs[: len(pieces_at)], refs[len(pieces_at) :]
    weights, refs = refs[:count], refs[count:]
    before, after = (refs[:count], refs[count:]) if started else ((), refs)
    step = pl.program_id(0)

    @pl.when(step == 0)
    def _():
        for j, ref in enumerate(after):
            ref[...] = before[j][...] if started else jnp.zeros_like(ref)

    for piece, (start, stop) in zip(pieces, pieces_at):
        @pl.when((step >= start) & (step < stop))
        def _():
            at = pl.multiple_of((step - start) * chunk, chunk)
            x = piece[:, pl.ds(at, chunk)]
            for w, ref in zip(weights, after):
                ref[...] += jnp.dot(x, w[...], preferred_element_type=jnp.float32)


def value_kernel(first, chunk, place, w, before, *refs):
    pieces, value = refs[:-1], refs[-1]
    total = before[...]
    step = first
    for piece in pieces:
        for at in range(0, piece.shape[1], chunk):
            start = pl.multiple_of(place[step] * chunk, chunk)
            total += jnp.dot(
                piece[:, at : at + chunk], w[pl.ds(start, chunk), :], preferred_element_type=jnp.float32
            )
            step += 1
    value[...] = total.astype(jnp.bfloat16)


def visible_block(base, block, own, earliest, rows):
    key = base + lax.broadcasted_iota(jnp.int32, (block, rows), 0)
    query = own + lax.broadcasted_iota(jnp.int32, (block, rows), 1)
    return (key <= query) & (key >= earliest)


def over_blocks(own, info, rows, body):
    first, edge = info[0], info[1]
    last = (own + rows + BLOCK - 1) // BLOCK

    @pl.loop(first, last)
    def _(b):
        masked = (b * BLOCK < edge) | (b * BLOCK + BLOCK > own)

        @pl.when(masked)
        def _():
            body(b, True)

        @pl.when(jnp.logical_not(masked))
        def _():
            body(b, False)


def stats_kernel(
    begin, heads, rows, levels, weight,
    info, q_pre, early, true, codes, book, cos_k, sin_k, keys_k,
    q_rot, q_t, log_total, bins, peak_s, mass_s, cos_q, sin_q, keys, sems,
):
    own = token_rank() * rows
    mine = pl.ds(pl.multiple_of(own, rows), rows)
    copies = [
        pltpu.make_async_copy(cos_k.at[mine, :], cos_q, sems.at[0]),
        pltpu.make_async_copy(sin_k.at[mine, :], sin_q, sems.at[1]),
        pltpu.make_async_copy(keys_k, keys, sems.at[2]),
    ]
    for copy in copies:
        copy.start()
    if begin == 0:
        code = codes[...]
        for level in range(levels):
            entry = weight * (book[level : level + 1, :] - true[...])
            bins[level : level + 1, :] = jnp.sum(
                jnp.where(code == level, entry, 0.0), axis=0, keepdims=True
            )
    else:
        bins[...] = jnp.zeros_like(bins)
    peak_s[...] = jnp.full_like(peak_s, NEG_BIG)
    mass_s[...] = jnp.zeros_like(mass_s)
    copies[0].wait()
    copies[1].wait()
    for h in range(heads):
        x = q_pre[:, (begin + h) * HD : (begin + h + 1) * HD]
        turned = (x * cos_q[...] + pltpu.roll(x, HD // 2, 1) * sin_q[...]).astype(jnp.bfloat16)
        q_rot[h] = turned
        q_t[h] = turned.T
    copies[2].wait()

    def body(b, masked):
        base = pl.multiple_of(b * BLOCK, BLOCK)
        k = keys[pl.ds(base, BLOCK), :]
        if masked:
            seen = visible_block(base, BLOCK, own, early[...], rows)
        for h in range(heads):
            t = lax.dot_general(k, q_t[h], NN, preferred_element_type=jnp.float32)
            t = t * (SCALE * LOG2E)
            if masked:
                t = jnp.where(seen, t, NEG_BIG)
            old = peak_s[h : h + 1, :]
            new = jnp.maximum(old, jnp.max(t, axis=0, keepdims=True))
            fresh = jnp.sum(jnp.exp2(t - new), axis=0, keepdims=True)
            mass_s[h : h + 1, :] = mass_s[h : h + 1, :] * jnp.exp2(old - new) + fresh
            peak_s[h : h + 1, :] = new

    over_blocks(own, info, rows, body)
    log_total[...] = peak_s[...] + jnp.log(mass_s[...]) * LOG2E


def grad_kernel(
    heads, rows, levels,
    info, q_rot_0, q_t_0, log_total_0, q_rot_1, q_t_1, log_total_1, early, cot, cot_t, init,
    keys_k, cos_f, sin_f, codes_f, v_own, v_x, v_y1, v_y2, v_y3, v_core,
    out, bins, probs_s, out_s, delta_s, acc_s, values, keys, cos_k, sin_k, codes, sems,
):
    me = token_rank()
    own, first = me * rows, info[0]
    part = heads // 2
    q_rot = [q_rot_0.at[h] for h in range(part)] + [q_rot_1.at[h] for h in range(part)]
    q_t = [q_t_0.at[h] for h in range(part)] + [q_t_1.at[h] for h in range(part)]
    log_total = [ref.at[h : h + 1, :] for ref in (log_total_0, log_total_1) for h in range(part)]
    copies = [pltpu.make_async_copy(keys_k, keys, sems.at[0])]
    for j, (bits, ref, at) in enumerate(slots((v_own, v_x, v_y1, v_y2, v_y3, v_core))):
        start = pl.multiple_of((me ^ bits) * rows, rows)
        copies.append(
            pltpu.make_async_copy(
                ref.at[at * rows : (at + 1) * rows, :], values.at[pl.ds(start, rows), :], sems.at[1 + j]
            )
        )
    late = [
        pltpu.make_async_copy(cos_f, cos_k, sems.at[17]),
        pltpu.make_async_copy(sin_f, sin_k, sems.at[18]),
        pltpu.make_async_copy(codes_f, codes, sems.at[19]),
    ]
    for copy in copies + late:
        copy.start()
    out_s[...] = jnp.zeros_like(out_s)
    for copy in copies:
        copy.wait()

    def forward(b, masked):
        base = pl.multiple_of(b * BLOCK, BLOCK)
        k = keys[pl.ds(base, BLOCK), :]
        v = values[pl.ds(base, BLOCK), :]
        if masked:
            seen = visible_block(base, BLOCK, own, early[...], rows)
        for h in range(heads):
            s = lax.dot_general(k, q_t[h][...], NN, preferred_element_type=jnp.float32)
            p = jnp.exp2(s * (SCALE * LOG2E) - log_total[h][...])
            if masked:
                p = jnp.where(seen, p, 0.0)
            probs_s[b - first, h] = p
            out_s[h] += lax.dot_general(
                p.astype(jnp.bfloat16), v, TN, preferred_element_type=jnp.float32
            )

    over_blocks(own, info, rows, forward)
    for h in range(heads):
        o = out_s[h].astype(jnp.bfloat16)
        out[:, h * HD : (h + 1) * HD] = o
        prod = cot[:, h * HD : (h + 1) * HD].astype(jnp.float32) * o.astype(jnp.float32)
        delta_s[h : h + 1, :] = jnp.sum(prod.T, axis=0, keepdims=True)
    acc_s[...] = jnp.zeros_like(acc_s)
    last = (own + rows + BLOCK - 1) // BLOCK
    for copy in late:
        copy.wait()

    @pl.loop(first, last)
    def _(b):
        base = pl.multiple_of(b * BLOCK, BLOCK)
        v = values[pl.ds(base, BLOCK), :]
        dk = jnp.zeros((BLOCK, HD), jnp.float32)
        for h in range(heads):
            dp = lax.dot_general(v, cot_t[h], NN, preferred_element_type=jnp.float32)
            ds = (probs_s[b - first, h] * (dp - delta_s[h : h + 1, :])).astype(jnp.bfloat16)
            dk = dk + lax.dot_general(ds, q_rot[h][...], NN, preferred_element_type=jnp.float32)
        dk = dk * SCALE
        g = dk * cos_k[pl.ds(base, BLOCK), :] - pltpu.roll(dk, HD // 2, 1) * sin_k[pl.ds(base, BLOCK), :]
        code = codes[pl.ds(base, BLOCK), :].astype(jnp.float32)
        for level in range(levels):
            chosen = jnp.where(code == level, g, 0.0)
            acc_s[level] += jnp.sum(chosen.reshape(BLOCK // 8, 8, HD), axis=0)

    bins[...] = init[...] + jnp.sum(acc_s[...], axis=1)


def anywhere():
    return pl.BlockSpec(memory_space=pl.ANY)


def vmem():
    return pl.BlockSpec(memory_space=pltpu.VMEM)


def smem():
    return pl.BlockSpec(memory_space=pltpu.SMEM)


def cost(flops, size):
    return pl.CostEstimate(flops=flops, bytes_accessed=size, transcendentals=0)


def shards(hidden, w_query, w_key, w_value, key_codes, codebook, positions, cotangent):
    rows, part = hidden.shape
    width = w_query.shape[1]
    heads = width // HD
    levels = codebook.shape[1]
    ranks = lax.axis_size("tokens")
    total = rows * ranks
    group = lax.axis_size("tensor")
    rank = lax.axis_index("tensor")
    me = lax.axis_index("tokens")
    own = me * rows
    bf16, f32 = jnp.bfloat16, jnp.float32

    cross = lambda x, d: lax.ppermute(x, "tokens", [(i, i ^ d) for i in range(ranks)])

    def everyone(x, second=lambda v: v, third=lambda v: v):
        x_side = cross(x, 2)
        pair = second(jnp.concatenate([x, x_side], axis=0))
        y_side = [cross(pair, 4 * y) for y in (1, 2, 3)]
        core = cross(third(jnp.concatenate([pair] + y_side, axis=0)), 1)
        return (x, x_side, *y_side, core)

    def after(*others):
        return lambda v: lax.optimization_barrier((v, others))[0]

    flip = [(i, i ^ 1) for i in range(group)]
    up = [(i, (i + 2) % group) for i in range(group)]
    down = [(i, (i - 2) % group) for i in range(group)]
    send = functools.partial(lax.ppermute, axis_name="tensor")
    n = part // 2
    low = send(hidden, perm=up)
    high = send(hidden, perm=down)
    other = send(hidden, perm=flip)
    places = positions[None, :]
    packed, early, info = pl.pallas_call(
        functools.partial(pack_kernel, rows),
        out_shape=(
            jax.ShapeDtypeStruct((rows + TAIL, HD), bf16),
            jax.ShapeDtypeStruct((1, rows), jnp.int32),
            jax.ShapeDtypeStruct((2,), jnp.int32),
        ),
        in_specs=[vmem()] * 2,
        out_specs=(vmem(), vmem(), smem()),
        name="pack",
    )(key_codes, places)
    book = codebook.T
    inverse = jnp.exp((jnp.arange(HD) % (HD // 2)).astype(f32) * (-2.0 * math.log(ROPE_BASE) / HD))

    mate = rank ^ 1
    turn = lambda x, by: (x + by) % group
    shard = [rank, turn(rank, -2), turn(rank, 2), mate, turn(rank, 4)]
    shard += [turn(mate, -2), turn(mate, 2), turn(mate, 4)]
    place = jnp.stack([2 * x + j for x in shard for j in (0, 1)]).astype(jnp.int32)

    def project(pieces, first, weights, sums, share=1.0):
        steps, at = [], 0
        for piece in pieces:
            steps.append((at, at + piece.shape[1] // n))
            at = steps[-1][1]
        count = len(weights)
        whole = lambda shape: pl.BlockSpec(shape, lambda i, place: (0, 0))
        sizes = [(rows, w.shape[1]) for w in weights]
        flops = 2 * rows * n * at * sum(w.shape[1] for w in weights)
        return pl.pallas_call(
            functools.partial(project_kernel, steps, n, count, sums is not None),
            out_shape=[jax.ShapeDtypeStruct(size, f32) for size in sizes],
            grid_spec=pltpu.PrefetchScalarGridSpec(
                num_scalar_prefetch=1,
                grid=(at,),
                in_specs=[whole(piece.shape) for piece in pieces]
                + [pl.BlockSpec((n, w.shape[1]), lambda i, place: (place[first + i], 0)) for w in weights]
                + ([whole(size) for size in sizes] if sums is not None else []),
                out_specs=[whole(size) for size in sizes],
            ),
            compiler_params=pltpu.CompilerParams(vmem_limit_bytes=50 << 20),
            cost_estimate=cost(int(flops * share), int(flops * share) // rows),
            name="project",
        )(place, *pieces, *weights, *(sums if sums is not None else ()))

    everything = (w_query, w_key, w_value)
    sums = project([hidden], 0, everything, None)
    x_side = after(sums[0])(cross(packed, 2))
    pair = jnp.concatenate([packed, x_side], axis=0)
    y_side = [cross(pair, 4 * y) for y in (1, 2, 3)]
    low, high, other = after(*y_side)((low, high, other))
    far_a = send(low[:, :n], perm=up)
    far_b = send(high[:, n:], perm=down)
    other_low = send(other, perm=up)
    other_high = send(other, perm=down)
    other_far_a = send(far_a, perm=flip)
    other_far_b = send(far_b, perm=flip)
    sums = project([low, high, other], 2, everything, sums, 16.0)
    core = cross(jnp.concatenate([pair] + y_side, axis=0), 1)
    packed = (packed, x_side, *y_side, core)

    keys, cos_k, sin_k, codes, cot_t = pl.pallas_call(
        functools.partial(prep_kernel, rows, ranks, levels, heads),
        out_shape=(
            jax.ShapeDtypeStruct((total, HD), bf16),
            jax.ShapeDtypeStruct((total, HD), f32),
            jax.ShapeDtypeStruct((total, HD), f32),
            jax.ShapeDtypeStruct((total, HD), bf16),
            jax.ShapeDtypeStruct((heads, HD, rows), bf16),
        ),
        in_specs=[vmem()] * 3 + [anywhere()] * 6,
        out_specs=(vmem(),) * 5,
        scratch_shapes=[
            pltpu.VMEM((ranks * (rows + TAIL), HD), bf16),
            pltpu.SemaphoreType.DMA((ranks,)),
        ],
        compiler_params=pltpu.CompilerParams(vmem_limit_bytes=16 << 20),
        cost_estimate=cost(0, 0),
        name="prep",
    )(inverse[None, :], book, cotangent, *packed)

    sums, keys = lax.optimization_barrier((sums, keys))
    sums = project([far_a, far_b], 8, everything, sums, 0.0)
    rest = [other_low, other_high, other_far_a, other_far_b]
    value = pl.pallas_call(
        functools.partial(value_kernel, 10, n),
        out_shape=jax.ShapeDtypeStruct((rows, HD), bf16),
        in_specs=[smem()] + [vmem()] * (2 + len(rest)),
        out_specs=vmem(),
        compiler_params=pltpu.CompilerParams(vmem_limit_bytes=16 << 20),
        cost_estimate=cost(0, 0),
        name="value",
    )(place, w_value, sums[2], *rest)
    query_pre, key_true = project(rest, 10, (w_query, w_key), sums[:2])

    def log_totals(begin, count, query_pre):
        return pl.pallas_call(
            functools.partial(stats_kernel, begin, count, rows, levels, levels / total),
            out_shape=(
                jax.ShapeDtypeStruct((count, rows, HD), bf16),
                jax.ShapeDtypeStruct((count, HD, rows), bf16),
                jax.ShapeDtypeStruct((count, rows), f32),
                jax.ShapeDtypeStruct((levels, HD), f32),
            ),
            in_specs=[smem()] + [vmem()] * 5 + [anywhere()] * 3,
            out_specs=(vmem(),) * 4,
            scratch_shapes=[pltpu.VMEM((count, rows), f32)] * 2
            + [pltpu.VMEM((rows, HD), f32)] * 2
            + [pltpu.VMEM((total, HD), bf16), pltpu.SemaphoreType.DMA((3,))],
            compiler_params=pltpu.CompilerParams(vmem_limit_bytes=24 << 20),
            cost_estimate=cost(2 * rows * count * HD * total, 4 << 20),
            name="stats",
        )(info, query_pre, early, key_true, key_codes, book, cos_k, sin_k, keys)

    totals = []

    def second(pair):
        pair, ready = lax.optimization_barrier((pair, query_pre))
        totals.extend(log_totals(0, heads // 2, ready))
        return pair

    values = everyone(value, second, lambda v: after(totals[2])(v))
    q_rot_0, q_t_0, log_total_0, init = totals
    query_late, _ = lax.optimization_barrier((query_pre, values[2:5]))
    q_rot_1, q_t_1, log_total_1, _ = log_totals(heads // 2, heads // 2, query_late)

    most = total // BLOCK
    attention_out, local = pl.pallas_call(
        functools.partial(grad_kernel, heads, rows, levels),
        out_shape=(
            jax.ShapeDtypeStruct((rows, width), bf16),
            jax.ShapeDtypeStruct((levels, HD), f32),
        ),
        in_specs=[smem()] + [vmem()] * 10 + [anywhere()] * 10,
        out_specs=(vmem(),) * 2,
        scratch_shapes=[
            pltpu.VMEM((min(most, 7), heads, BLOCK, rows), f32),
            pltpu.VMEM((heads, rows, HD), f32),
            pltpu.VMEM((heads, rows), f32),
            pltpu.VMEM((levels, 8, HD), f32),
            pltpu.VMEM((total, HD), bf16),
            pltpu.VMEM((total, HD), bf16),
            pltpu.VMEM((total, HD), f32),
            pltpu.VMEM((total, HD), f32),
            pltpu.VMEM((total, HD), bf16),
            pltpu.SemaphoreType.DMA((20,)),
        ],
        compiler_params=pltpu.CompilerParams(vmem_limit_bytes=52 << 20),
        cost_estimate=cost(8 * rows * width * total, 8 << 20),
        name="grad",
    )(
        info, q_rot_0, q_t_0, log_total_0, q_rot_1, q_t_1, log_total_1, early, cotangent, cot_t, init,
        keys, cos_k, sin_k, codes, *values,
    )
    for d in (1, 2, 4, 8):
        local = local + cross(local, d)
    return (attention_out, local.T)


def solution(mesh):
    placed = (
        P("tokens", "tensor"),
        P(None, "tensor"),
        P(None, "tensor"),
        P(None, "tensor"),
        P("tokens", "tensor"),
        P("tensor", None),
        P("tokens"),
        P("tokens", "tensor"),
    )
    return jax.shard_map(
        shards,
        mesh=mesh,
        in_specs=placed,
        out_specs=(P("tokens", "tensor"), P("tensor", None)),
        check_vma=False,
    )
```

time: 151 us -> 140 us (0.927)
  local copies, waits for them, and re-layouts: 31.3 us -> 6.63 us
  Pallas kernels: 28.5 us -> 46.1 us
  starting transfers between devices: 57.9 us -> 64.6 us
  other arithmetic: 6.53 us -> 0.67 us
  between operations: 3.6 us -> 1.1 us
    unnamed x70 -> x40, local copies, waits for them, and re-layouts: 28.8 us -> 6.48 us
    pallas_call x5 -> x8, Pallas kernels: 16.9 us -> 30.9 us  [the longest x4 22.8 us: project(): pl.pallas_call(functools.partial(project_kernel, steps, n, count, sums is...]
    ppermute x1, waiting for transfers between devices: 5.85 us -> 0.01 us  [shards(): low = send(hidden, perm=up)]
    ppermute x14, starting transfers between devices: 42.3 us -> 47.1 us  [shards(): lax.ppermute(x, 'tokens', [(i, i ^ d) for i in range(ranks)])]
    ppermute x14, waiting for transfers between devices: 14.9 us -> 18.8 us  [shards(): lax.ppermute(x, 'tokens', [(i, i ^ d) for i in range(ranks)])]
    ppermute x1, starting transfers between devices: 0.01 us -> 3.22 us  [shards(): other_high = send(other, perm=down)]
    pallas_call x1, Pallas kernels: 5.14 us -> 7.61 us  [shards(): pl.pallas_call(functools.partial(grad_kernel, heads, rows, levels), out_s...]
    ppermute x1, starting transfers between devices: 0.01 us -> 2.07 us  [shards(): low = send(hidden, perm=up)]
  transfers between devices with their start and end apart: 22 -> 23, of which waited for: 8 -> 11; matrix products, arithmetic and copies ran while one was open for 8% -> 1% of each run, Pallas kernels for 16% -> 27%
where the time goes in v1:
time: 140 us; the launch traced here: 139 us
  starting transfers between devices  64.6 us (46%)
  Pallas kernels  46.1 us (33%)
  waiting for transfers between devices  19.6 us (14%)
  local copies, waits for them, and re-layouts  6.63 us (5%)
    ppermute x14, starting transfers between devices, shards(): lax.ppermute(x, 'tokens', [(i, i ^ d) for i in range(ranks)])  47.1 us
    pallas_call x4, Pallas kernels, project(): pl.pallas_call(functools.partial(project_kernel, steps, n, count, sums is...  22.8 us
    ppermute x14, waiting for transfers between devices, shards(): lax.ppermute(x, 'tokens', [(i, i ^ d) for i in range(ranks)])  18.8 us
    pallas_call x1, Pallas kernels, shards(): pl.pallas_call(functools.partial(prep_kernel, rows, ranks, levels, heads)...  7.62 us
    pallas_call x1, Pallas kernels, shards(): pl.pallas_call(functools.partial(grad_kernel, heads, rows, levels), out_s...  7.61 us
    unnamed x40, local copies, waits for them, and re-layouts  6.48 us
    pallas_call x2, Pallas kernels, log_totals(): pl.pallas_call(functools.partial(stats_kernel, begin, count, rows, levels...  5.42 us
    ppermute x1, starting transfers between devices, shards(): far_b = send(high[:, n:], perm=down)  3.29 us
  transfers between devices with their start and end apart: 23, of which 11 were waited for; matrix products, arithmetic and copies ran while one was open for 1% of the time, Pallas kernels for 27%

profile of v1, /device:TPU:0, one launch (start us, length us, event | category | flops | bytes accessed | tf_op | source)
XLA Modules:
  0.0 138.7 jit_solution(5694079886722770401)
XLA Ops:
  0.6 2.1 %collective-permute-start = (bf16[256,1024]{1,0:T(8,128)(2,1)}, bf16[256,1024]{1,0:T(8,128)(2,1)S(1)}, u32[]{:S(2)}, u32[]{:S(2)}) collective-permute-start(bf16[256,1024]{1,0:T(8,128)(2,1)} %refs_0_.1), channel_id=1, source_target_pairs={{0,32},{16,48},{32,64},{48,80},{64,96},{80,112},{96,0},{112,16},{1... | collective-permute-start | bytes 1572872 | tf_op jit(solution)/shard_map/ppermute | solution.py:357
  2.7 2.2 %collective-permute-start.1 = (bf16[256,1024]{1,0:T(8,128)(2,1)}, bf16[256,1024]{1,0:T(8,128)(2,1)S(1)}, u32[]{:S(2)}, u32[]{:S(2)}) collective-permute-start(bf16[256,1024]{1,0:T(8,128)(2,1)} %refs_0_.1), channel_id=1, source_target_pairs={{0,96},{16,112},{32,0},{48,16},{64,32},{80,48},{96,64},{112,80},{1... | collective-permute-start | bytes 1572872 | tf_op jit(solution)/shard_map/ppermute | solution.py:358
  4.9 3.0 %collective-permute-start.2 = (bf16[256,1024]{1,0:T(8,128)(2,1)}, bf16[256,1024]{1,0:T(8,128)(2,1)}, u32[]{:S(2)}, u32[]{:S(2)}) collective-permute-start(bf16[256,1024]{1,0:T(8,128)(2,1)} %refs_0_.1), channel_id=1, source_target_pairs={{0,16},{16,0},{32,48},{48,32},{64,80},{80,64},{96,112},{112,96},{1... | collective-permute-start | bytes 1572872 | tf_op jit(solution)/shard_map/ppermute | solution.py:359
  13.9 3.1 %project.4 = (f32[256,1024]{1,0:T(8,128)S(1)}, f32[256,128]{1,0:T(8,128)S(1)}, f32[256,128]{1,0:T(8,128)S(1)}) custom-call(s32[16]{0:T(128)S(1)} %stack.67.place, bf16[256,1024]{1,0:T(8,128)(2,1)S(1)} %copy-done.6, bf16[8192,1024]{1,0:T(8,128)(2,1)} %refs_4_.5, bf16[8192,128]{1,0:T(8,128)(2,1)S(1)} %copy-done, bf16[8192,128]{1,0:T(8,128)(2,1)} %w.1), custom_call_target="tpu_custom_call" | custom-call | flops 671088640 | bytes 2621440 | tf_op jit(solution)/shard_map/project/pallas_call | solution.py:390
  17.1 4.5 %collective-permute-done.3.p_x = bf16[272,128]{1,0:T(8,128)(2,1)S(1)} collective-permute-done((bf16[272,128]{1,0:T(8,128)(2,1)}, bf16[272,128]{1,0:T(8,128)(2,1)S(1)}, u32[]{:S(2)}, u32[]{:S(2)}) %collective-permute-start.3) | collective-permute-done | bytes 69664 | tf_op jit(solution)/shard_map/ppermute | solution.py:340
  23.3 2.9 %collective-permute-start.5 = (bf16[544,128]{1,0:T(8,128)(2,1)S(1)}, bf16[544,128]{1,0:T(8,128)(2,1)S(1)}, u32[]{:S(2)}, u32[]{:S(2)}) collective-permute-start(bf16[544,128]{1,0:T(8,128)(2,1)S(1)} %get-tuple-element.83), channel_id=1, source_target_pairs={{0,8},{1,9},{2,10},{3,11},{4,12},{5,13},{6,14},{7,15},{8,0},{9,1},... | collective-permute-start | bytes 417800 | tf_op jit(solution)/shard_map/ppermute | solution.py:340
  26.2 2.0 %collective-permute-done.4.p_y1 = bf16[544,128]{1,0:T(8,128)(2,1)S(1)} collective-permute-done((bf16[544,128]{1,0:T(8,128)(2,1)S(1)}, bf16[544,128]{1,0:T(8,128)(2,1)S(1)}, u32[]{:S(2)}, u32[]{:S(2)}) %collective-permute-start.4) | collective-permute-done | bytes 139296 | tf_op jit(solution)/shard_map/ppermute | solution.py:340
  28.1 2.4 %collective-permute-start.6 = (bf16[544,128]{1,0:T(8,128)(2,1)S(1)}, bf16[544,128]{1,0:T(8,128)(2,1)S(1)}, u32[]{:S(2)}, u32[]{:S(2)}) collective-permute-start(bf16[544,128]{1,0:T(8,128)(2,1)S(1)} %get-tuple-element.83), channel_id=1, source_target_pairs={{0,12},{1,13},{2,14},{3,15},{4,8},{5,9},{6,10},{7,11},{8,4},{9,5},... | collective-permute-start | bytes 417800 | tf_op jit(solution)/shard_map/ppermute | solution.py:340
  31.6 2.9 %collective-permute-done.6.p_y3 = bf16[544,128]{1,0:T(8,128)(2,1)S(1)} collective-permute-done((bf16[544,128]{1,0:T(8,128)(2,1)S(1)}, bf16[544,128]{1,0:T(8,128)(2,1)S(1)}, u32[]{:S(2)}, u32[]{:S(2)}) %collective-permute-start.6) | collective-permute-done | bytes 139296 | tf_op jit(solution)/shard_map/ppermute | solution.py:340
  34.6 3.3 %collective-permute-start.8 = (bf16[256,512]{1,0:T(8,128)(2,1)S(1)}, bf16[256,512]{1,0:T(8,128)(2,1)S(1)}, u32[]{:S(2)}, u32[]{:S(2)}) collective-permute-start(bf16[256,512]{1,0:T(8,128)(2,1)S(1)} %slice.7), channel_id=1, source_target_pairs={{0,96},{16,112},{32,0},{48,16},{64,32},{80,48},{96,64},{112,80},{1... | collective-permute-start | bytes 786440 | tf_op jit(solution)/shard_map/ppermute | solution.py:413
  38.1 3.2 %collective-permute-start.11 = (bf16[256,1024]{1,0:T(8,128)(2,1)}, bf16[256,1024]{1,0:T(8,128)(2,1)S(1)}, u32[]{:S(2)}, u32[]{:S(2)}) collective-permute-start(bf16[256,1024]{1,0:T(8,128)(2,1)} %collective-permute-done.2.refs_2_), channel_id=1, source_target_pairs={{0,96},{16,112},{32,0},{48,16},{64,32},{80,48},{96,64},{112,80},{1... | collective-permute-start | bytes 1572872 | tf_op jit(solution)/shard_map/ppermute | solution.py:415
  42.1 2.0 %collective-permute-start.12 = (bf16[256,512]{1,0:T(8,128)(2,1)S(1)}, bf16[256,512]{1,0:T(8,128)(2,1)S(1)}, u32[]{:S(2)}, u32[]{:S(2)}) collective-permute-start(bf16[256,512]{1,0:T(8,128)(2,1)S(1)} %collective-permute-done.7.refs_0_), channel_id=1, source_target_pairs={{0,16},{16,0},{32,48},{48,32},{64,80},{80,64},{96,112},{112,96},{1... | collective-permute-start | bytes 786440 | tf_op jit(solution)/shard_map/ppermute | solution.py:416
  46.7 7.7 %project.5 = (f32[256,1024]{1,0:T(8,128)S(1)}, f32[256,128]{1,0:T(8,128)S(1)}, f32[256,128]{1,0:T(8,128)S(1)}) custom-call(s32[16]{0:T(128)S(1)} %stack.67.place, bf16[256,1024]{1,0:T(8,128)(2,1)S(1)} %collective-permute-done.refs_0_, bf16[256,1024]{1,0:T(8,128)(2,1)S(1)} %copy-done.10, bf16[256,1024]{1,0:T(8,128)(2,1)} %collective-permute-done.2.refs_2_, ...), custom_call_target="tpu_custom_call" | custom-call | flops 32212254720 | bytes 125829120 | tf_op jit(solution)/shard_map/project/pallas_call | solution.py:390
  54.5 7.6 %prep.1 = (bf16[4096,128]{1,0:T(8,128)(2,1)S(1)}, f32[4096,128]{1,0:T(8,128)S(1)}, f32[4096,128]{1,0:T(8,128)S(1)}, bf16[4096,128]{1,0:T(8,128)(2,1)S(1)}, bf16[8,128,256]{2,1,0:T(8,128)(2,1)S(1)}) custom-call(f32[1,128]{1,0:T(1,128)S(1)} %fusion.2.inverse, f32[16,128]{1,0:T(8,128)S(1)} %bitcast.20, bf16[256,1024]{1,0:T(8,128)(2,1)S(1)} %copy-done.7, ...), custom_call_target="tpu_custom_call" | custom-call | tf_op jit(solution)/shard_map/prep/pallas_call | solution.py:422
  63.1 5.3 %project.6 = (f32[256,1024]{1,0:T(8,128)S(1)}, f32[256,128]{1,0:T(8,128)S(1)}, f32[256,128]{1,0:T(8,128)S(1)}) custom-call(s32[16]{0:T(128)S(1)} %stack.67.place, bf16[256,512]{1,0:T(8,128)(2,1)S(1)} %collective-permute-done.7.refs_0_, bf16[256,512]{1,0:T(8,128)(2,1)S(1)} %collective-permute-done.8.refs_1_, bf16[8192,1024]{1,0:T(8,128)(2,1)} %refs_4_.5, ...), custom_call_target="tpu_custom_call" | custom-call | tf_op jit(solution)/shard_map/project/pallas_call | solution.py:390
  71.1 6.7 %project.7 = (f32[256,1024]{1,0:T(8,128)S(1)}, f32[256,128]{1,0:T(8,128)S(1)}) custom-call(s32[16]{0:T(128)S(1)} %stack.67.place, bf16[256,1024]{1,0:T(8,128)(2,1)S(1)} %collective-permute-done.10.refs_0_, bf16[256,1024]{1,0:T(8,128)(2,1)S(1)} %collective-permute-done.11.refs_1_, bf16[256,512]{1,0:T(8,128)(2,1)S(1)} %collective-permute-done.12.refs_2_, ...), custom_call_target="tpu_custom_call" | custom-call | flops 1811939328 | bytes 7077888 | tf_op jit(solution)/shard_map/project/pallas_call | solution.py:390
  78.0 3.7 %collective-permute-start.16 = (bf16[512,128]{1,0:T(8,128)(2,1)S(1)}, bf16[512,128]{1,0:T(8,128)(2,1)S(1)}, u32[]{:S(2)}, u32[]{:S(2)}) collective-permute-start(bf16[512,128]{1,0:T(8,128)(2,1)S(1)} %pad_maximum_fusion.1), channel_id=1, source_target_pairs={{0,8},{1,9},{2,10},{3,11},{4,12},{5,13},{6,14},{7,15},{8,0},{9,1},... | collective-permute-start | bytes 393224 | tf_op jit(solution)/shard_map/ppermute | solution.py:340
  82.6 2.6 %stats.2 = (bf16[4,256,128]{2,1,0:T(8,128)(2,1)S(1)}, bf16[4,128,256]{2,1,0:T(8,128)(2,1)S(1)}, f32[4,256]{1,0:T(4,128)S(1)}, f32[16,128]{1,0:T(8,128)S(1)}) custom-call(s32[2]{0:T(128)S(1)} %copy-done.13, f32[256,1024]{1,0:T(8,128)S(1)} %get-tuple-element.72.q_pre, s32[1,256]{1,0:T(1,128)S(1)} %copy-done.12, f32[256,128]{1,0:T(8,128)S(1)} %get-tuple-element.64.true, ...), custom_call_target="tpu_custom_call" | custom-call | flops 1073741824 | bytes 4194304 | tf_op jit(solution)/shard_map/stats/pallas_call | solution.py:457
  86.2 1.7 %collective-permute-done.17.v_y3 = bf16[512,128]{1,0:T(8,128)(2,1)S(1)} collective-permute-done((bf16[512,128]{1,0:T(8,128)(2,1)S(1)}, bf16[512,128]{1,0:T(8,128)(2,1)S(1)}, u32[]{:S(2)}, u32[]{:S(2)}) %collective-permute-start.17) | collective-permute-done | bytes 131104 | tf_op jit(solution)/shard_map/ppermute | solution.py:340
  88.1 2.8 %stats.3 = (bf16[4,256,128]{2,1,0:T(8,128)(2,1)S(1)}, bf16[4,128,256]{2,1,0:T(8,128)(2,1)S(1)}, f32[4,256]{1,0:T(4,128)S(1)}, f32[16,128]{1,0:T(8,128)}) custom-call(s32[2]{0:T(128)S(1)} %copy-done.13, f32[256,1024]{1,0:T(8,128)S(1)} %get-tuple-element.72.q_pre, s32[1,256]{1,0:T(1,128)S(1)} %copy-done.12, f32[256,128]{1,0:T(8,128)S(1)} %get-tuple-element.64.true, ...), custom_call_target="tpu_custom_call" | custom-call | flops 1073741824 | bytes 4194304 | tf_op jit(solution)/shard_map/stats/pallas_call | solution.py:457
  91.7 7.6 %grad.1 = (bf16[256,1024]{1,0:T(8,128)(2,1)}, f32[16,128]{1,0:T(8,128)S(1)}) custom-call(s32[2]{0:T(128)S(1)} %copy-done.13, bf16[4,256,128]{2,1,0:T(8,128)(2,1)S(1)} %get-tuple-element.68.q_rot_0, bf16[4,128,256]{2,1,0:T(8,128)(2,1)S(1)} %get-tuple-element.69.q_t_0, f32[4,256]{1,0:T(4,128)S(1)} %get-tuple-element.70.log_total_0, ...), custom_call_target="tpu_custom_call" | custom-call | flops 8589934592 | bytes 8388608 | tf_op jit(solution)/shard_map/grad/pallas_call | solution.py:488
  100.7 4.7 %collective-permute-start.20 = (f32[16,128]{1,0:T(8,128)S(1)}, f32[16,128]{1,0:T(8,128)S(1)}, u32[]{:S(2)}, u32[]{:S(2)}) collective-permute-start(f32[16,128]{1,0:T(8,128)S(1)} %add.107), channel_id=1, source_target_pairs={{0,2},{1,3},{2,0},{3,1},{4,6},{5,7},{6,4},{7,5},{8,10},{9,11},{10,... | collective-permute-start | bytes 24584 | tf_op jit(solution)/shard_map/ppermute | solution.py:340
  107.1 7.7 %collective-permute-start.21 = (f32[16,128]{1,0:T(8,128)S(1)}, f32[16,128]{1,0:T(8,128)S(1)}, u32[]{:S(2)}, u32[]{:S(2)}) collective-permute-start(f32[16,128]{1,0:T(8,128)S(1)} %add.108), channel_id=1, source_target_pairs={{0,4},{1,5},{2,6},{3,7},{4,0},{5,1},{6,2},{7,3},{8,12},{9,13},{10,... | collective-permute-start | bytes 24584 | tf_op jit(solution)/shard_map/ppermute | solution.py:340
  116.4 20.1 %collective-permute-start.22 = (f32[16,128]{1,0:T(8,128)S(1)}, f32[16,128]{1,0:T(8,128)S(1)}, u32[]{:S(2)}, u32[]{:S(2)}) collective-permute-start(f32[16,128]{1,0:T(8,128)S(1)} %add.109), channel_id=1, source_target_pairs={{0,8},{1,9},{2,10},{3,11},{4,12},{5,13},{6,14},{7,15},{8,0},{9,1},... | collective-permute-start | bytes 24584 | tf_op jit(solution)/shard_map/ppermute | solution.py:340
  (83 shorter events, 25.8 us)
Async XLA Ops:
  0.6 33.8 %collective-permute-start = (bf16[256,1024]{1,0:T(8,128)(2,1)}, bf16[256,1024]{1,0:T(8,128)(2,1)S(1)}, u32[]{:S(2)}, u32[]{:S(2)}) collective-permute-start(bf16[256,1024]{1,0:T(8,128)(2,1)} %refs_0_.1), channel_id=1, source_target_pairs={{0,32},{16,48},{32,64},{48,80},{64,96},{80,112},{96,0},{112,16},{1... | collective-permute-start | bytes 1572872 | tf_op jit(solution)/shard_map/ppermute | solution.py:357
  2.7 31.7 %collective-permute-start.1 = (bf16[256,1024]{1,0:T(8,128)(2,1)}, bf16[256,1024]{1,0:T(8,128)(2,1)S(1)}, u32[]{:S(2)}, u32[]{:S(2)}) collective-permute-start(bf16[256,1024]{1,0:T(8,128)(2,1)} %refs_0_.1), channel_id=1, source_target_pairs={{0,96},{16,112},{32,0},{48,16},{64,32},{80,48},{96,64},{112,80},{1... | collective-permute-start | bytes 1572872 | tf_op jit(solution)/shard_map/ppermute | solution.py:358
  4.9 29.5 %collective-permute-start.2 = (bf16[256,1024]{1,0:T(8,128)(2,1)}, bf16[256,1024]{1,0:T(8,128)(2,1)}, u32[]{:S(2)}, u32[]{:S(2)}) collective-permute-start(bf16[256,1024]{1,0:T(8,128)(2,1)} %refs_0_.1), channel_id=1, source_target_pairs={{0,16},{16,0},{32,48},{48,32},{64,80},{80,64},{96,112},{112,96},{1... | collective-permute-start | bytes 1572872 | tf_op jit(solution)/shard_map/ppermute | solution.py:359
  9.5 12.1 %collective-permute-start.3 = (bf16[272,128]{1,0:T(8,128)(2,1)}, bf16[272,128]{1,0:T(8,128)(2,1)S(1)}, u32[]{:S(2)}, u32[]{:S(2)}) collective-permute-start(bf16[272,128]{1,0:T(8,128)(2,1)} %get-tuple-element.43.p_own), channel_id=1, source_target_pairs={{0,2},{1,3},{2,0},{3,1},{4,6},{5,7},{6,4},{7,5},{8,10},{9,11},{10,... | collective-permute-start | bytes 208904 | tf_op jit(solution)/shard_map/ppermute | solution.py:340
  21.6 6.5 %collective-permute-start.4 = (bf16[544,128]{1,0:T(8,128)(2,1)S(1)}, bf16[544,128]{1,0:T(8,128)(2,1)S(1)}, u32[]{:S(2)}, u32[]{:S(2)}) collective-permute-start(bf16[544,128]{1,0:T(8,128)(2,1)S(1)} %get-tuple-element.83), channel_id=1, source_target_pairs={{0,4},{1,5},{2,6},{3,7},{4,0},{5,1},{6,2},{7,3},{8,12},{9,13},{10,... | collective-permute-start | bytes 417800 | tf_op jit(solution)/shard_map/ppermute | solution.py:340
  23.3 8.3 %collective-permute-start.5 = (bf16[544,128]{1,0:T(8,128)(2,1)S(1)}, bf16[544,128]{1,0:T(8,128)(2,1)S(1)}, u32[]{:S(2)}, u32[]{:S(2)}) collective-permute-start(bf16[544,128]{1,0:T(8,128)(2,1)S(1)} %get-tuple-element.83), channel_id=1, source_target_pairs={{0,8},{1,9},{2,10},{3,11},{4,12},{5,13},{6,14},{7,15},{8,0},{9,1},... | collective-permute-start | bytes 417800 | tf_op jit(solution)/shard_map/ppermute | solution.py:340
  28.1 6.3 %collective-permute-start.6 = (bf16[544,128]{1,0:T(8,128)(2,1)S(1)}, bf16[544,128]{1,0:T(8,128)(2,1)S(1)}, u32[]{:S(2)}, u32[]{:S(2)}) collective-permute-start(bf16[544,128]{1,0:T(8,128)(2,1)S(1)} %get-tuple-element.83), channel_id=1, source_target_pairs={{0,12},{1,13},{2,14},{3,15},{4,8},{5,9},{6,10},{7,11},{8,4},{9,5},... | collective-permute-start | bytes 417800 | tf_op jit(solution)/shard_map/ppermute | solution.py:340
  34.5 7.7 %collective-permute-start.7 = (bf16[256,512]{1,0:T(8,128)(2,1)S(1)}, bf16[256,512]{1,0:T(8,128)(2,1)S(1)}, u32[]{:S(2)}, u32[]{:S(2)}) collective-permute-start(bf16[256,512]{1,0:T(8,128)(2,1)S(1)} %slice.6), channel_id=1, source_target_pairs={{0,32},{16,48},{32,64},{48,80},{64,96},{80,112},{96,0},{112,16},{1... | collective-permute-start | bytes 786440 | tf_op jit(solution)/shard_map/ppermute | solution.py:412
  34.6 9.6 %collective-permute-start.8 = (bf16[256,512]{1,0:T(8,128)(2,1)S(1)}, bf16[256,512]{1,0:T(8,128)(2,1)S(1)}, u32[]{:S(2)}, u32[]{:S(2)}) collective-permute-start(bf16[256,512]{1,0:T(8,128)(2,1)S(1)} %slice.7), channel_id=1, source_target_pairs={{0,96},{16,112},{32,0},{48,16},{64,32},{80,48},{96,64},{112,80},{1... | collective-permute-start | bytes 786440 | tf_op jit(solution)/shard_map/ppermute | solution.py:413
  37.9 16.5 %collective-permute-start.9 = (bf16[2176,128]{1,0:T(8,128)(2,1)S(1)}, bf16[2176,128]{1,0:T(8,128)(2,1)S(1)}, u32[]{:S(2)}, u32[]{:S(2)}) collective-permute-start(bf16[2176,128]{1,0:T(8,128)(2,1)S(1)} %constant_dynamic-update-slice_fusion.2), channel_id=1, source_target_pairs={{0,1},{1,0},{2,3},{3,2},{4,5},{5,4},{6,7},{7,6},{8,9},{9,8},{10,11... | collective-permute-start | bytes 1671176 | tf_op jit(solution)/shard_map/ppermute | solution.py:340
  38.0 30.4 %collective-permute-start.10 = (bf16[256,1024]{1,0:T(8,128)(2,1)}, bf16[256,1024]{1,0:T(8,128)(2,1)S(1)}, u32[]{:S(2)}, u32[]{:S(2)}) collective-permute-start(bf16[256,1024]{1,0:T(8,128)(2,1)} %collective-permute-done.2.refs_2_), channel_id=1, source_target_pairs={{0,32},{16,48},{32,64},{48,80},{64,96},{80,112},{96,0},{112,16},{1... | collective-permute-start | bytes 1572872 | tf_op jit(solution)/shard_map/ppermute | solution.py:414
  38.1 30.3 %collective-permute-start.11 = (bf16[256,1024]{1,0:T(8,128)(2,1)}, bf16[256,1024]{1,0:T(8,128)(2,1)S(1)}, u32[]{:S(2)}, u32[]{:S(2)}) collective-permute-start(bf16[256,1024]{1,0:T(8,128)(2,1)} %collective-permute-done.2.refs_2_), channel_id=1, source_target_pairs={{0,96},{16,112},{32,0},{48,16},{64,32},{80,48},{96,64},{112,80},{1... | collective-permute-start | bytes 1572872 | tf_op jit(solution)/shard_map/ppermute | solution.py:415
  42.1 26.3 %collective-permute-start.12 = (bf16[256,512]{1,0:T(8,128)(2,1)S(1)}, bf16[256,512]{1,0:T(8,128)(2,1)S(1)}, u32[]{:S(2)}, u32[]{:S(2)}) collective-permute-start(bf16[256,512]{1,0:T(8,128)(2,1)S(1)} %collective-permute-done.7.refs_0_), channel_id=1, source_target_pairs={{0,16},{16,0},{32,48},{48,32},{64,80},{80,64},{96,112},{112,96},{1... | collective-permute-start | bytes 786440 | tf_op jit(solution)/shard_map/ppermute | solution.py:416
  44.1 24.3 %collective-permute-start.13 = (bf16[256,512]{1,0:T(8,128)(2,1)S(1)}, bf16[256,512]{1,0:T(8,128)(2,1)S(1)}, u32[]{:S(2)}, u32[]{:S(2)}) collective-permute-start(bf16[256,512]{1,0:T(8,128)(2,1)S(1)} %collective-permute-done.8.refs_1_), channel_id=1, source_target_pairs={{0,16},{16,0},{32,48},{48,32},{64,80},{80,64},{96,112},{112,96},{1... | collective-permute-start | bytes 786440 | tf_op jit(solution)/shard_map/ppermute | solution.py:417
  63.1 25.0 %copy-start.4 = (bf16[4096,128]{1,0:T(8,128)(2,1)}, bf16[4096,128]{1,0:T(8,128)(2,1)S(1)}, u32[]{:S(2)}) copy-start(bf16[4096,128]{1,0:T(8,128)(2,1)S(1)} %get-tuple-element.67.keys_k) | copy-start | bytes 3145732
  69.6 8.2 %collective-permute-start.14 = (bf16[256,128]{1,0:T(8,128)(2,1)S(1)}, bf16[256,128]{1,0:T(8,128)(2,1)S(1)}, u32[]{:S(2)}, u32[]{:S(2)}) collective-permute-start(bf16[256,128]{1,0:T(8,128)(2,1)S(1)} %value.1.v_own), channel_id=1, source_target_pairs={{0,2},{1,3},{2,0},{3,1},{4,6},{5,7},{6,4},{7,5},{8,10},{9,11},{10,... | collective-permute-start | bytes 196616 | tf_op jit(solution)/shard_map/ppermute | solution.py:340
  77.8 7.4 %collective-permute-start.15 = (bf16[512,128]{1,0:T(8,128)(2,1)S(1)}, bf16[512,128]{1,0:T(8,128)(2,1)S(1)}, u32[]{:S(2)}, u32[]{:S(2)}) collective-permute-start(bf16[512,128]{1,0:T(8,128)(2,1)S(1)} %pad_maximum_fusion.1), channel_id=1, source_target_pairs={{0,4},{1,5},{2,6},{3,7},{4,0},{5,1},{6,2},{7,3},{8,12},{9,13},{10,... | collective-permute-start | bytes 393224 | tf_op jit(solution)/shard_map/ppermute | solution.py:340
  78.0 8.2 %collective-permute-start.16 = (bf16[512,128]{1,0:T(8,128)(2,1)S(1)}, bf16[512,128]{1,0:T(8,128)(2,1)S(1)}, u32[]{:S(2)}, u32[]{:S(2)}) collective-permute-start(bf16[512,128]{1,0:T(8,128)(2,1)S(1)} %pad_maximum_fusion.1), channel_id=1, source_target_pairs={{0,8},{1,9},{2,10},{3,11},{4,12},{5,13},{6,14},{7,15},{8,0},{9,1},... | collective-permute-start | bytes 393224 | tf_op jit(solution)/shard_map/ppermute | solution.py:340
  81.7 6.2 %collective-permute-start.17 = (bf16[512,128]{1,0:T(8,128)(2,1)S(1)}, bf16[512,128]{1,0:T(8,128)(2,1)S(1)}, u32[]{:S(2)}, u32[]{:S(2)}) collective-permute-start(bf16[512,128]{1,0:T(8,128)(2,1)S(1)} %pad_maximum_fusion.1), channel_id=1, source_target_pairs={{0,12},{1,13},{2,14},{3,15},{4,8},{5,9},{6,10},{7,11},{8,4},{9,5},... | collective-permute-start | bytes 393224 | tf_op jit(solution)/shard_map/ppermute | solution.py:340
  88.0 3.0 %collective-permute-start.18 = (bf16[2048,128]{1,0:T(8,128)(2,1)S(1)}, bf16[2048,128]{1,0:T(8,128)(2,1)S(1)}, u32[]{:S(2)}, u32[]{:S(2)}) collective-permute-start(bf16[2048,128]{1,0:T(8,128)(2,1)S(1)} %pad_maximum_fusion), channel_id=1, source_target_pairs={{0,1},{1,0},{2,3},{3,2},{4,5},{5,4},{6,7},{7,6},{8,9},{9,8},{10,11... | collective-permute-start | bytes 1572872 | tf_op jit(solution)/shard_map/ppermute | solution.py:340
  99.3 1.4 collective-permute-start.19
  100.7 6.4 %collective-permute-start.20 = (f32[16,128]{1,0:T(8,128)S(1)}, f32[16,128]{1,0:T(8,128)S(1)}, u32[]{:S(2)}, u32[]{:S(2)}) collective-permute-start(f32[16,128]{1,0:T(8,128)S(1)} %add.107), channel_id=1, source_target_pairs={{0,2},{1,3},{2,0},{3,1},{4,6},{5,7},{6,4},{7,5},{8,10},{9,11},{10,... | collective-permute-start | bytes 24584 | tf_op jit(solution)/shard_map/ppermute | solution.py:340
  107.1 9.3 %collective-permute-start.21 = (f32[16,128]{1,0:T(8,128)S(1)}, f32[16,128]{1,0:T(8,128)S(1)}, u32[]{:S(2)}, u32[]{:S(2)}) collective-permute-start(f32[16,128]{1,0:T(8,128)S(1)} %add.108), channel_id=1, source_target_pairs={{0,4},{1,5},{2,6},{3,7},{4,0},{5,1},{6,2},{7,3},{8,12},{9,13},{10,... | collective-permute-start | bytes 24584 | tf_op jit(solution)/shard_map/ppermute | solution.py:340
  116.4 21.7 %collective-permute-start.22 = (f32[16,128]{1,0:T(8,128)S(1)}, f32[16,128]{1,0:T(8,128)S(1)}, u32[]{:S(2)}, u32[]{:S(2)}) collective-permute-start(f32[16,128]{1,0:T(8,128)S(1)} %add.109), channel_id=1, source_target_pairs={{0,8},{1,9},{2,10},{3,11},{4,12},{5,13},{6,14},{7,15},{8,0},{9,1},... | collective-permute-start | bytes 24584 | tf_op jit(solution)/shard_map/ppermute | solution.py:340
  (17 other events, 155.9 us)

commit v2 on v1

--- a/solution.py
+++ b/solution.py
@@ -37,6 +37,13 @@
     return sine, cosine
 
 
+def slots_y_first(pieces):
+    own, y1, y2, y3, x, core = pieces
+    found = [(0, own, 0), (4, y1, 0), (8, y2, 0), (12, y3, 0)]
+    found += [(2 | 4 * j, x, j) for j in range(4)]
+    return found + [(1 | (4 * j if j < 4 else 2 | 4 * (j - 4)), core, j) for j in range(8)]
+
+
 def slots(pieces):
     own, x, y1, y2, y3, core = pieces
     found = [(0, own, 0), (2, x, 0)]
@@ -67,13 +74,13 @@
 
 def prep_kernel(
     rows, ranks, levels, heads,
-    inverse, book, cot, p_own, p_x, p_y1, p_y2, p_y3, p_core,
+    inverse, book, cot, p_own, p_y1, p_y2, p_y3, p_x, p_core,
     keys, cos_k, sin_k, codes, cot_t, packed_s, sems,
 ):
     me = token_rank()
     tall = rows + TAIL
     copies = []
-    for j, (bits, ref, at) in enumerate(slots((p_own, p_x, p_y1, p_y2, p_y3, p_core))):
+    for j, (bits, ref, at) in enumerate(slots_y_first((p_own, p_y1, p_y2, p_y3, p_x, p_core))):
         start = pl.multiple_of((me ^ bits) * tall, TAIL)
         copies.append(
             pltpu.make_async_copy(
@@ -120,37 +127,59 @@
             keys[pl.ds(target, HD), :] = turned.astype(jnp.bfloat16)
 
 
-def project_kernel(pieces_at, chunk, count, started, place, *refs):
-    pieces, refs = refs[: len(pieces_at)], refs[len(pieces_at) :]
-    weights, refs = refs[:count], refs[count:]
-    before, after = (refs[:count], refs[count:]) if started else ((), refs)
-    step = pl.program_id(0)
-
-    @pl.when(step == 0)
-    def _():
-        for j, ref in enumerate(after):
-            ref[...] = before[j][...] if started else jnp.zeros_like(ref)
-
-    for piece, (start, stop) in zip(pieces, pieces_at):
-        @pl.when((step >= start) & (step < stop))
-        def _():
-            at = pl.multiple_of((step - start) * chunk, chunk)
-            x = piece[:, pl.ds(at, chunk)]
-            for w, ref in zip(weights, after):
-                ref[...] += jnp.dot(x, w[...], preferred_element_type=jnp.float32)
-
-
-def value_kernel(first, chunk, place, w, before, *refs):
-    pieces, value = refs[:-1], refs[-1]
-    total = before[...]
-    step = first
+def shard_rows(place, n, part):
+    return pl.ds(pl.multiple_of(place[n] * part, part), part)
+
+
+def fetch(pieces, x_s, sem):
+    copies, at = [], 0
     for piece in pieces:
-        for at in range(0, piece.shape[1], chunk):
-            start = pl.multiple_of(place[step] * chunk, chunk)
-            total += jnp.dot(
-                piece[:, at : at + chunk], w[pl.ds(start, chunk), :], preferred_element_type=jnp.float32
-            )
-            step += 1
+        width = piece.shape[1]
+        copies.append(pltpu.make_async_copy(piece, x_s.at[:, at : at + width], sem(len(copies))))
+        at += width
+    return copies
+
+
+def project_kernel(
+    count, part, place, wq, wk, wv, *refs,
+):
+    pieces, (q_out, kv_out, x_s, wq_s, wkv_s, sems) = refs[:count], refs[count:]
+    copies = []
+    for n, piece in enumerate(pieces):
+        rows = shard_rows(place, n, part)
+        copies.append([
+            pltpu.make_async_copy(piece, x_s.at[n], sems.at[4 * n]),
+            pltpu.make_async_copy(wq.at[rows, :], wq_s.at[n], sems.at[4 * n + 1]),
+            pltpu.make_async_copy(wk.at[rows, :], wkv_s.at[n, :, :HD], sems.at[4 * n + 2]),
+            pltpu.make_async_copy(wv.at[rows, :], wkv_s.at[n, :, HD:], sems.at[4 * n + 3]),
+        ])
+        for copy in copies[-1]:
+            copy.start()
+    for n in range(count):
+        for copy in copies[n]:
+            copy.wait()
+        x = x_s[n]
+        q = jnp.dot(x, wq_s[n], preferred_element_type=jnp.float32)
+        kv = jnp.dot(x, wkv_s[n], preferred_element_type=jnp.float32)
+        q_out[...] = q if n == 0 else q_out[...] + q
+        kv_out[...] = kv if n == 0 else kv_out[...] + kv
+
+
+def value_kernel(first, count, part, place, w, before, *refs):
+    pieces, (value, x_s, w_s, before_s, sems) = refs[:-5], refs[-5:]
+    copies = fetch(pieces, x_s, lambda j: sems.at[j])
+    copies.append(pltpu.make_async_copy(before.at[:, HD:], before_s, sems.at[len(copies)]))
+    for n in range(count):
+        copies.append(
+            pltpu.make_async_copy(w.at[shard_rows(place, first + n, part), :], w_s.at[n], sems.at[len(copies)])
+        )
+    for copy in copies:
+        copy.start()
+    for copy in copies:
+        copy.wait()
+    total = before_s[...]
+    for n in range(count):
+        total += jnp.dot(x_s[:, n * part : (n + 1) * part], w_s[n], preferred_element_type=jnp.float32)
     value[...] = total.astype(jnp.bfloat16)
 
 
@@ -178,38 +207,62 @@
 
 
 def stats_kernel(
-    begin, heads, rows, levels, weight,
-    info, q_pre, early, true, codes, book, cos_k, sin_k, keys_k,
-    q_rot, q_t, log_total, bins, peak_s, mass_s, cos_q, sin_q, keys, sems,
+    begin, heads, rows, levels, weight, first, count, part,
+    place, info, early, codes, book, cos_k, sin_k, keys_k, q_before, kv_before, wq, wk, *refs,
 ):
+    pieces = refs[:-17]
+    (
+        q_rot, q_t, log_total, bins,
+        peak_s, mass_s, cos_q, sin_q, keys, x_s, wq_s, wk_s, q_s, true_s, x_sems, w_sems, sems,
+    ) = refs[-17:]
     own = token_rank() * rows
     mine = pl.ds(pl.multiple_of(own, rows), rows)
-    copies = [
-        pltpu.make_async_copy(cos_k.at[mine, :], cos_q, sems.at[0]),
-        pltpu.make_async_copy(sin_k.at[mine, :], sin_q, sems.at[1]),
-        pltpu.make_async_copy(keys_k, keys, sems.at[2]),
+    columns = pl.ds(begin * HD, heads * HD)
+    loads = fetch(pieces, x_s, lambda j: x_sems.at[j])
+    weights = []
+    for n in range(count):
+        at = shard_rows(place, first + n, part)
+        row = [pltpu.make_async_copy(wq.at[at, columns], wq_s.at[n], w_sems.at[2 * n])]
+        if begin == 0:
+            row.append(pltpu.make_async_copy(wk.at[at, :], wk_s.at[n], w_sems.at[2 * n + 1]))
+        weights.append(row)
+    before = [pltpu.make_async_copy(q_before.at[:, columns], q_s, sems.at[0])]
+    if begin == 0:
+        before.append(pltpu.make_async_copy(kv_before.at[:, :HD], true_s, sems.at[1]))
+    tables = [
+        pltpu.make_async_copy(cos_k.at[mine, :], cos_q, sems.at[2]),
+        pltpu.make_async_copy(sin_k.at[mine, :], sin_q, sems.at[3]),
+        pltpu.make_async_copy(keys_k, keys, sems.at[4]),
     ]
-    for copy in copies:
+    for copy in before + loads + sum(weights, []) + tables:
         copy.start()
+    peak_s[...] = jnp.full_like(peak_s, NEG_BIG)
+    mass_s[...] = jnp.zeros_like(mass_s)
+    for copy in before + loads:
+        copy.wait()
+    for n in range(count):
+        for copy in weights[n]:
+            copy.wait()
+        x = x_s[:, n * part : (n + 1) * part]
+        q_s[...] += jnp.dot(x, wq_s[n], preferred_element_type=jnp.float32)
+        if begin == 0:
+            true_s[...] += jnp.dot(x, wk_s[n], preferred_element_type=jnp.float32)
     if begin == 0:
         code = codes[...]
         for level in range(levels):
-            entry = weight * (book[level : level + 1, :] - true[...])
+            entry = weight * (book[level : level + 1, :] - true_s[...])
             bins[level : level + 1, :] = jnp.sum(
                 jnp.where(code == level, entry, 0.0), axis=0, keepdims=True
             )
     else:
         bins[...] = jnp.zeros_like(bins)
-    peak_s[...] = jnp.full_like(peak_s, NEG_BIG)
-    mass_s[...] = jnp.zeros_like(mass_s)
-    copies[0].wait()
-    copies[1].wait()
+    for copy in tables:
+        copy.wait()
     for h in range(heads):
-        x = q_pre[:, (begin + h) * HD : (begin + h + 1) * HD]
+        x = q_s[:, h * HD : (h + 1) * HD]
         turned = (x * cos_q[...] + pltpu.roll(x, HD // 2, 1) * sin_q[...]).astype(jnp.bfloat16)
         q_rot[h] = turned
         q_t[h] = turned.T
-    copies[2].wait()
 
     def body(b, masked):
         base = pl.multiple_of(b * BLOCK, BLOCK)
@@ -339,8 +392,8 @@
 
     cross = lambda x, d: lax.ppermute(x, "tokens", [(i, i ^ d) for i in range(ranks)])
 
-    def everyone(x, second=lambda v: v, third=lambda v: v):
-        x_side = cross(x, 2)
+    def everyone(x, first, second, third):
+        x_side = first(cross(x, 2))
         pair = second(jnp.concatenate([x, x_side], axis=0))
         y_side = [cross(pair, 4 * y) for y in (1, 2, 3)]
         core = cross(third(jnp.concatenate([pair] + y_side, axis=0)), 1)
@@ -374,50 +427,57 @@
 
     mate = rank ^ 1
     turn = lambda x, by: (x + by) % group
-    shard = [rank, turn(rank, -2), turn(rank, 2), mate, turn(rank, 4)]
-    shard += [turn(mate, -2), turn(mate, 2), turn(mate, 4)]
-    place = jnp.stack([2 * x + j for x in shard for j in (0, 1)]).astype(jnp.int32)
-
-    def project(pieces, first, weights, sums, share=1.0):
-        steps, at = [], 0
-        for piece in pieces:
-            steps.append((at, at + piece.shape[1] // n))
-            at = steps[-1][1]
-        count = len(weights)
-        whole = lambda shape: pl.BlockSpec(shape, lambda i, place: (0, 0))
-        sizes = [(rows, w.shape[1]) for w in weights]
-        flops = 2 * rows * n * at * sum(w.shape[1] for w in weights)
-        return pl.pallas_call(
-            functools.partial(project_kernel, steps, n, count, sums is not None),
-            out_shape=[jax.ShapeDtypeStruct(size, f32) for size in sizes],
-            grid_spec=pltpu.PrefetchScalarGridSpec(
-                num_scalar_prefetch=1,
-                grid=(at,),
-                in_specs=[whole(piece.shape) for piece in pieces]
-                + [pl.BlockSpec((n, w.shape[1]), lambda i, place: (place[first + i], 0)) for w in weights]
-                + ([whole(size) for size in sizes] if sums is not None else []),
-                out_specs=[whole(size) for size in sizes],
-            ),
-            compiler_params=pltpu.CompilerParams(vmem_limit_bytes=50 << 20),
-            cost_estimate=cost(int(flops * share), int(flops * share) // rows),
-            name="project",
-        )(place, *pieces, *weights, *(sums if sums is not None else ()))
-
-    everything = (w_query, w_key, w_value)
-    sums = project([hidden], 0, everything, None)
-    x_side = after(sums[0])(cross(packed, 2))
-    pair = jnp.concatenate([packed, x_side], axis=0)
-    y_side = [cross(pair, 4 * y) for y in (1, 2, 3)]
-    low, high, other = after(*y_side)((low, high, other))
+    shard = [rank, turn(rank, -2), turn(rank, 2), mate]
+    shard += [turn(rank, 4), turn(mate, -2), turn(mate, 2), turn(mate, 4)]
+    place = jnp.stack(shard).astype(jnp.int32)
+
+    y_side = [cross(packed, 4 * y) for y in (1, 2, 3)]
+    column = jnp.concatenate([packed] + y_side, axis=0)
+    x_side = cross(column, 2)
+    low, high, other = after(column)((low, high, other))
     far_a = send(low[:, :n], perm=up)
     far_b = send(high[:, n:], perm=down)
     other_low = send(other, perm=up)
     other_high = send(other, perm=down)
     other_far_a = send(far_a, perm=flip)
     other_far_b = send(far_b, perm=flip)
-    sums = project([low, high, other], 2, everything, sums, 16.0)
-    core = cross(jnp.concatenate([pair] + y_side, axis=0), 1)
-    packed = (packed, x_side, *y_side, core)
+
+    half = group // 2
+    low, high, other = after(far_a, far_b)((low, high, other))
+    q_sum, kv_sum = pl.pallas_call(
+        functools.partial(project_kernel, half, part),
+        out_shape=(jax.ShapeDtypeStruct((rows, width), f32), jax.ShapeDtypeStruct((rows, 2 * HD), f32)),
+        in_specs=[smem()] + [anywhere()] * (3 + half),
+        out_specs=(vmem(),) * 2,
+        scratch_shapes=[
+            pltpu.VMEM((half, rows, part), bf16),
+            pltpu.VMEM((half, part, width), bf16),
+            pltpu.VMEM((half, part, 2 * HD), bf16),
+            pltpu.SemaphoreType.DMA((4 * half,)),
+        ],
+        compiler_params=pltpu.CompilerParams(vmem_limit_bytes=50 << 20),
+        cost_estimate=cost(1 << 34, 0),
+        name="project",
+    )(place, w_query, w_key, w_value, hidden, low, high, other)
+    core = cross(jnp.concatenate([column, x_side], axis=0), 1)
+    packed = (packed, *y_side, x_side, core)
+
+    rest = [far_a, far_b, other_low, other_high, other_far_a, other_far_b]
+    value = pl.pallas_call(
+        functools.partial(value_kernel, half, half, part),
+        out_shape=jax.ShapeDtypeStruct((rows, HD), bf16),
+        in_specs=[smem()] + [anywhere()] * (2 + len(rest)),
+        out_specs=vmem(),
+        scratch_shapes=[
+            pltpu.VMEM((rows, half * part), bf16),
+            pltpu.VMEM((half, part, HD), bf16),
+            pltpu.VMEM((rows, HD), f32),
+            pltpu.SemaphoreType.DMA((half + len(rest) + 1,)),
+        ],
+        compiler_params=pltpu.CompilerParams(vmem_limit_bytes=50 << 20),
+        cost_estimate=cost(0, 0),
+        name="value",
+    )(place, w_value, kv_sum, *rest)
 
     keys, cos_k, sin_k, codes, cot_t = pl.pallas_call(
         functools.partial(prep_kernel, rows, ranks, levels, heads),
@@ -435,54 +495,55 @@
             pltpu.SemaphoreType.DMA((ranks,)),
         ],
         compiler_params=pltpu.CompilerParams(vmem_limit_bytes=16 << 20),
-        cost_estimate=cost(0, 0),
+        cost_estimate=cost(1 << 32, 0),
         name="prep",
-    )(inverse[None, :], book, cotangent, *packed)
-
-    sums, keys = lax.optimization_barrier((sums, keys))
-    sums = project([far_a, far_b], 8, everything, sums, 0.0)
-    rest = [other_low, other_high, other_far_a, other_far_b]
-    value = pl.pallas_call(
-        functools.partial(value_kernel, 10, n),
-        out_shape=jax.ShapeDtypeStruct((rows, HD), bf16),
-        in_specs=[smem()] + [vmem()] * (2 + len(rest)),
-        out_specs=vmem(),
-        compiler_params=pltpu.CompilerParams(vmem_limit_bytes=16 << 20),
-        cost_estimate=cost(0, 0),
-        name="value",
-    )(place, w_value, sums[2], *rest)
-    query_pre, key_true = project(rest, 10, (w_query, w_key), sums[:2])
-
-    def log_totals(begin, count, query_pre):
+    )(after(value)(inverse[None, :]), book, cotangent, *packed)
+
+    def log_totals(begin, count, place):
         return pl.pallas_call(
-            functools.partial(stats_kernel, begin, count, rows, levels, levels / total),
+            functools.partial(
+                stats_kernel, begin, count, rows, levels, levels / total, half, half, part
+            ),
             out_shape=(
                 jax.ShapeDtypeStruct((count, rows, HD), bf16),
                 jax.ShapeDtypeStruct((count, HD, rows), bf16),
                 jax.ShapeDtypeStruct((count, rows), f32),
                 jax.ShapeDtypeStruct((levels, HD), f32),
             ),
-            in_specs=[smem()] + [vmem()] * 5 + [anywhere()] * 3,
+            in_specs=[smem()] * 2 + [vmem()] * 3 + [anywhere()] * (7 + len(rest)),
             out_specs=(vmem(),) * 4,
             scratch_shapes=[pltpu.VMEM((count, rows), f32)] * 2
             + [pltpu.VMEM((rows, HD), f32)] * 2
-            + [pltpu.VMEM((total, HD), bf16), pltpu.SemaphoreType.DMA((3,))],
-            compiler_params=pltpu.CompilerParams(vmem_limit_bytes=24 << 20),
-            cost_estimate=cost(2 * rows * count * HD * total, 4 << 20),
+            + [
+                pltpu.VMEM((total, HD), bf16),
+                pltpu.VMEM((rows, half * part), bf16),
+                pltpu.VMEM((half, part, count * HD), bf16),
+                pltpu.VMEM((half, part, HD), bf16),
+                pltpu.VMEM((rows, count * HD), f32),
+                pltpu.VMEM((rows, HD), f32),
+                pltpu.SemaphoreType.DMA((len(rest),)),
+                pltpu.SemaphoreType.DMA((2 * half,)),
+                pltpu.SemaphoreType.DMA((5,)),
+            ],
+            compiler_params=pltpu.CompilerParams(vmem_limit_bytes=50 << 20),
+            cost_estimate=cost(1 << 34, 0),
             name="stats",
-        )(info, query_pre, early, key_true, key_codes, book, cos_k, sin_k, keys)
+        )(
+            place, info, early, key_codes, book, cos_k, sin_k, keys,
+            q_sum, kv_sum, w_query, w_key, *rest,
+        )
 
     totals = []
 
     def second(pair):
-        pair, ready = lax.optimization_barrier((pair, query_pre))
+        pair, ready = lax.optimization_barrier((pair, place))
         totals.extend(log_totals(0, heads // 2, ready))
         return pair
 
-    values = everyone(value, second, lambda v: after(totals[2])(v))
+    values = everyone(value, after(keys), second, lambda v: after(totals[2])(v))
     q_rot_0, q_t_0, log_total_0, init = totals
-    query_late, _ = lax.optimization_barrier((query_pre, values[2:5]))
-    q_rot_1, q_t_1, log_total_1, _ = log_totals(heads // 2, heads // 2, query_late)
+    late, _ = lax.optimization_barrier((place, values[2:5]))
+    q_rot_1, q_t_1, log_total_1, _ = log_totals(heads // 2, heads // 2, late)
 
     most = total // BLOCK
     attention_out, local = pl.pallas_call(

time: 140 us -> 130 us (0.929)
  Pallas kernels: 46.1 us -> 37.2 us
  waiting for transfers between devices: 19.6 us -> 16.2 us
  local copies, waits for them, and re-layouts: 6.63 us -> 9.56 us
    pallas_call x5 -> x2, Pallas kernels: 23.9 us -> 8.91 us  [the longest x1 6.21 us: shards(): pl.pallas_call(functools.partial(project_kernel, half, part), out_shape=(...]
    ppermute x14, waiting for transfers between devices: 18.8 us -> 10.7 us  [shards(): lax.ppermute(x, 'tokens', [(i, i ^ d) for i in range(ranks)])]
    pallas_call x2, Pallas kernels: 5.42 us -> 11.5 us  [log_totals(): pl.pallas_call(functools.partial(stats_kernel, begin, count, rows, levels...]
    ppermute x1, waiting for transfers between devices: 0.01 us -> 2.97 us  [shards(): other_far_b = send(far_b, perm=flip)]
    ppermute x1, waiting for transfers between devices: 0.01 us -> 2.54 us  [shards(): other_low = send(other, perm=up)]
    unnamed x40 -> x34, local copies, waits for them, and re-layouts: 6.48 us -> 7.98 us
  transfers between devices with their start and end apart: 23 -> 23, of which waited for: 11 -> 8; matrix products, arithmetic and copies ran while one was open for 1% -> 4% of each run, Pallas kernels for 27% -> 23%
where the time goes in v2:
time: 130 us; the launch traced here: 129 us
  starting transfers between devices  64.3 us (49%)
  Pallas kernels  37.2 us (29%)
  waiting for transfers between devices  16.2 us (12%)
  local copies, waits for them, and re-layouts  9.56 us (7%)
    ppermute x14, starting transfers between devices, shards(): lax.ppermute(x, 'tokens', [(i, i ^ d) for i in range(ranks)])  46.9 us
    pallas_call x2, Pallas kernels, log_totals(): pl.pallas_call(functools.partial(stats_kernel, begin, count, rows, levels...  11.5 us
    ppermute x14, waiting for transfers between devices, shards(): lax.ppermute(x, 'tokens', [(i, i ^ d) for i in range(ranks)])  10.7 us
    unnamed x34, local copies, waits for them, and re-layouts  7.98 us
    pallas_call x1, Pallas kernels, shards(): pl.pallas_call(functools.partial(prep_kernel, rows, ranks, levels, heads)...  7.61 us
    pallas_call x1, Pallas kernels, shards(): pl.pallas_call(functools.partial(grad_kernel, heads, rows, levels), out_s...  7.59 us
    pallas_call x1, Pallas kernels, shards(): pl.pallas_call(functools.partial(project_kernel, half, part), out_shape=(...  6.21 us
    ppermute x1, starting transfers between devices, shards(): other_high = send(other, perm=down)  3.23 us
  transfers between devices with their start and end apart: 23, of which 8 were waited for; matrix products, arithmetic and copies ran while one was open for 4% of the time, Pallas kernels for 23%

profile of v2, /device:TPU:0, one launch (start us, length us, event | category | flops | bytes accessed | tf_op | source)
XLA Modules:
  0.0 128.8 jit_solution(11295197810062573430)
XLA Ops:
  0.6 2.1 %collective-permute-start = (bf16[256,1024]{1,0:T(8,128)(2,1)}, bf16[256,1024]{1,0:T(8,128)(2,1)S(1)}, u32[]{:S(2)}, u32[]{:S(2)}) collective-permute-start(bf16[256,1024]{1,0:T(8,128)(2,1)} %refs_0_.1), channel_id=1, source_target_pairs={{0,32},{16,48},{32,64},{48,80},{64,96},{80,112},{96,0},{112,16},{1... | collective-permute-start | bytes 1572872 | tf_op jit(solution)/shard_map/ppermute | solution.py:410
  2.7 2.2 %collective-permute-start.1 = (bf16[256,1024]{1,0:T(8,128)(2,1)}, bf16[256,1024]{1,0:T(8,128)(2,1)S(1)}, u32[]{:S(2)}, u32[]{:S(2)}) collective-permute-start(bf16[256,1024]{1,0:T(8,128)(2,1)} %refs_0_.1), channel_id=1, source_target_pairs={{0,96},{16,112},{32,0},{48,16},{64,32},{80,48},{96,64},{112,80},{1... | collective-permute-start | bytes 1572872 | tf_op jit(solution)/shard_map/ppermute | solution.py:411
  4.9 3.0 %collective-permute-start.2 = (bf16[256,1024]{1,0:T(8,128)(2,1)}, bf16[256,1024]{1,0:T(8,128)(2,1)S(1)}, u32[]{:S(2)}, u32[]{:S(2)}) collective-permute-start(bf16[256,1024]{1,0:T(8,128)(2,1)} %refs_0_.1), channel_id=1, source_target_pairs={{0,16},{16,0},{32,48},{48,32},{64,80},{80,64},{96,112},{112,96},{1... | collective-permute-start | bytes 1572872 | tf_op jit(solution)/shard_map/ppermute | solution.py:412
  9.5 1.7 %collective-permute-start.3 = (bf16[272,128]{1,0:T(8,128)(2,1)}, bf16[272,128]{1,0:T(8,128)(2,1)S(1)}, u32[]{:S(2)}, u32[]{:S(2)}) collective-permute-start(bf16[272,128]{1,0:T(8,128)(2,1)} %get-tuple-element.34.p_own), channel_id=1, source_target_pairs={{0,4},{1,5},{2,6},{3,7},{4,0},{5,1},{6,2},{7,3},{8,12},{9,13},{10,... | collective-permute-start | bytes 208904 | tf_op jit(solution)/shard_map/ppermute | solution.py:393
  11.2 2.9 %collective-permute-start.4 = (bf16[272,128]{1,0:T(8,128)(2,1)}, bf16[272,128]{1,0:T(8,128)(2,1)S(1)}, u32[]{:S(2)}, u32[]{:S(2)}) collective-permute-start(bf16[272,128]{1,0:T(8,128)(2,1)} %get-tuple-element.34.p_own), channel_id=1, source_target_pairs={{0,8},{1,9},{2,10},{3,11},{4,12},{5,13},{6,14},{7,15},{8,0},{9,1},... | collective-permute-start | bytes 208904 | tf_op jit(solution)/shard_map/ppermute | solution.py:393
  18.4 2.9 %collective-permute-done.5.p_y3 = bf16[272,128]{1,0:T(8,128)(2,1)S(1)} collective-permute-done((bf16[272,128]{1,0:T(8,128)(2,1)}, bf16[272,128]{1,0:T(8,128)(2,1)S(1)}, u32[]{:S(2)}, u32[]{:S(2)}) %collective-permute-start.5) | collective-permute-done | bytes 69664 | tf_op jit(solution)/shard_map/ppermute | solution.py:393
  23.5 3.2 %collective-permute-start.7 = (bf16[256,512]{1,0:T(8,128)(2,1)}, bf16[256,512]{1,0:T(8,128)(2,1)S(1)}, u32[]{:S(2)}, u32[]{:S(2)}) collective-permute-start(bf16[256,512]{1,0:T(8,128)(2,1)} %slice.7), channel_id=1, source_target_pairs={{0,96},{16,112},{32,0},{48,16},{64,32},{80,48},{96,64},{112,80},{1... | collective-permute-start | bytes 786440 | tf_op jit(solution)/shard_map/ppermute | solution.py:439
  26.8 2.0 %collective-permute-done.13.p_x = bf16[1088,128]{1,0:T(8,128)(2,1)S(1)} collective-permute-done((bf16[1088,128]{1,0:T(8,128)(2,1)}, bf16[1088,128]{1,0:T(8,128)(2,1)S(1)}, u32[]{:S(2)}, u32[]{:S(2)}) %collective-permute-start.13) | collective-permute-done | bytes 278560 | tf_op jit(solution)/shard_map/ppermute | solution.py:393
  29.5 3.2 %collective-permute-start.9 = (bf16[256,1024]{1,0:T(8,128)(2,1)S(1)}, bf16[256,1024]{1,0:T(8,128)(2,1)S(1)}, u32[]{:S(2)}, u32[]{:S(2)}) collective-permute-start(bf16[256,1024]{1,0:T(8,128)(2,1)S(1)} %collective-permute-done.2.refs_3_), channel_id=1, source_target_pairs={{0,96},{16,112},{32,0},{48,16},{64,32},{80,48},{96,64},{112,80},{1... | collective-permute-start | bytes 1572872 | tf_op jit(solution)/shard_map/ppermute | solution.py:441
  33.5 2.8 %collective-permute-start.11 = (bf16[256,512]{1,0:T(8,128)(2,1)S(1)}, bf16[256,512]{1,0:T(8,128)(2,1)S(1)}, u32[]{:S(2)}, u32[]{:S(2)}) collective-permute-start(bf16[256,512]{1,0:T(8,128)(2,1)S(1)} %collective-permute-done.7.refs_1_), channel_id=1, source_target_pairs={{0,16},{16,0},{32,48},{48,32},{64,80},{80,64},{96,112},{112,96},{1... | collective-permute-start | bytes 786440 | tf_op jit(solution)/shard_map/ppermute | solution.py:443
  36.3 6.2 %project.1 = (f32[256,1024]{1,0:T(8,128)S(1)}, f32[256,256]{1,0:T(8,128)S(1)}) custom-call(s32[8]{0:T(128)S(1)} %stack.35.place, bf16[8192,1024]{1,0:T(8,128)(2,1)} %wq.5, bf16[8192,128]{1,0:T(8,128)(2,1)} %wk.5, bf16[8192,128]{1,0:T(8,128)(2,1)} %w.1, bf16[256,1024]{1,0:T(8,128)(2,1)S(1)} %copy-done.2, bf16[256,1024]{1,0:T(8,128)(2,1)S(1)} %collective-permute-done.refs_1_, ...), custom_call_target="tpu_custom_call" | custom-call | flops 17179869184 | tf_op jit(solution)/shard_map/project/pallas_call | solution.py:447
  42.5 2.5 %collective-permute-done.8.refs_2_ = bf16[256,1024]{1,0:T(8,128)(2,1)S(1)} collective-permute-done((bf16[256,1024]{1,0:T(8,128)(2,1)S(1)}, bf16[256,1024]{1,0:T(8,128)(2,1)S(1)}, u32[]{:S(2)}, u32[]{:S(2)}) %collective-permute-start.8) | collective-permute-done | bytes 524320 | tf_op jit(solution)/shard_map/ppermute | solution.py:440
  45.1 3.0 %collective-permute-done.11.refs_5_ = bf16[256,512]{1,0:T(8,128)(2,1)S(1)} collective-permute-done((bf16[256,512]{1,0:T(8,128)(2,1)S(1)}, bf16[256,512]{1,0:T(8,128)(2,1)S(1)}, u32[]{:S(2)}, u32[]{:S(2)}) %collective-permute-start.11) | collective-permute-done | bytes 262176 | tf_op jit(solution)/shard_map/ppermute | solution.py:443
  48.0 2.7 %value.1.v_own = bf16[256,128]{1,0:T(8,128)(2,1)S(1)} custom-call(s32[8]{0:T(128)S(1)} %stack.35.place, bf16[8192,128]{1,0:T(8,128)(2,1)} %w.1, f32[256,256]{1,0:T(8,128)S(1)} %get-tuple-element.41.before.kv_before, bf16[256,512]{1,0:T(8,128)(2,1)S(1)} %collective-permute-done.6.refs_0_, bf16[256,512]{1,0:T(8,128)(2,1)S(1)} %collective-permute-done.7.refs_1_, ...), custom_call_target="tpu_custom_call" | custom-call | tf_op jit(solution)/shard_map/value/pallas_call | solution.py:466
  51.5 7.6 %prep.1 = (bf16[4096,128]{1,0:T(8,128)(2,1)S(1)}, f32[4096,128]{1,0:T(8,128)S(1)}, f32[4096,128]{1,0:T(8,128)S(1)}, bf16[4096,128]{1,0:T(8,128)(2,1)S(1)}, bf16[8,128,256]{2,1,0:T(8,128)(2,1)S(1)}) custom-call(f32[1,128]{1,0:T(1,128)S(1)} %fusion.2.inverse, f32[16,128]{1,0:T(8,128)S(1)} %bitcast.12, bf16[256,1024]{1,0:T(8,128)(2,1)S(1)} %copy-done.3, ...), custom_call_target="tpu_custom_call" | custom-call | flops 4294967296 | tf_op jit(solution)/shard_map/prep/pallas_call | solution.py:482
  62.9 2.9 %collective-permute-start.16 = (bf16[512,128]{1,0:T(8,128)(2,1)S(1)}, bf16[512,128]{1,0:T(8,128)(2,1)S(1)}, u32[]{:S(2)}, u32[]{:S(2)}) collective-permute-start(bf16[512,128]{1,0:T(8,128)(2,1)S(1)} %pad_maximum_fusion.1), channel_id=1, source_target_pairs={{0,8},{1,9},{2,10},{3,11},{4,12},{5,13},{6,14},{7,15},{8,0},{9,1},... | collective-permute-start | bytes 393224 | tf_op jit(solution)/shard_map/ppermute | solution.py:393
  65.8 1.7 %collective-permute-start.17 = (bf16[512,128]{1,0:T(8,128)(2,1)S(1)}, bf16[512,128]{1,0:T(8,128)(2,1)S(1)}, u32[]{:S(2)}, u32[]{:S(2)}) collective-permute-start(bf16[512,128]{1,0:T(8,128)(2,1)S(1)} %pad_maximum_fusion.1), channel_id=1, source_target_pairs={{0,12},{1,13},{2,14},{3,15},{4,8},{5,9},{6,10},{7,11},{8,4},{9,5},... | collective-permute-start | bytes 393224 | tf_op jit(solution)/shard_map/ppermute | solution.py:393
  67.6 6.1 %stats.2 = (bf16[4,256,128]{2,1,0:T(8,128)(2,1)S(1)}, bf16[4,128,256]{2,1,0:T(8,128)(2,1)S(1)}, f32[4,256]{1,0:T(4,128)S(1)}, f32[16,128]{1,0:T(8,128)S(1)}) custom-call(s32[8]{0:T(128)S(1)} %stack.35.place, s32[2]{0:T(128)S(1)} %copy-done.6, s32[1,256]{1,0:T(1,128)S(1)} %copy-done.5, s32[256,128]{1,0:T(8,128)S(1)} %copy-done, f32[16,128]{1,0:T(8,128)S(1)} %bitcast.13, ...), custom_call_target="tpu_custom_call" | custom-call | flops 17179869184 | tf_op jit(solution)/shard_map/stats/pallas_call | solution.py:503
  73.8 5.5 %stats.3 = (bf16[4,256,128]{2,1,0:T(8,128)(2,1)S(1)}, bf16[4,128,256]{2,1,0:T(8,128)(2,1)S(1)}, f32[4,256]{1,0:T(4,128)S(1)}, f32[16,128]{1,0:T(8,128)}) custom-call(s32[8]{0:T(128)S(1)} %stack.35.place, s32[2]{0:T(128)S(1)} %copy-done.6, s32[1,256]{1,0:T(1,128)S(1)} %copy-done.5, s32[256,128]{1,0:T(8,128)S(1)} %copy-done, f32[16,128]{1,0:T(8,128)S(1)} %bitcast.14, ...), custom_call_target="tpu_custom_call" | custom-call | flops 17179869184 | tf_op jit(solution)/shard_map/stats/pallas_call | solution.py:503
  80.1 7.6 %grad.1 = (bf16[256,1024]{1,0:T(8,128)(2,1)}, f32[16,128]{1,0:T(8,128)S(1)}) custom-call(s32[2]{0:T(128)S(1)} %copy-done.6, bf16[4,256,128]{2,1,0:T(8,128)(2,1)S(1)} %get-tuple-element.50.q_rot_0, bf16[4,128,256]{2,1,0:T(8,128)(2,1)S(1)} %get-tuple-element.51.q_t_0, f32[4,256]{1,0:T(4,128)S(1)} %get-tuple-element.52.log_total_0, ...), custom_call_target="tpu_custom_call" | custom-call | flops 8589934592 | bytes 8388608 | tf_op jit(solution)/shard_map/grad/pallas_call | solution.py:549
  89.1 6.4 %collective-permute-start.20 = (f32[16,128]{1,0:T(8,128)S(1)}, f32[16,128]{1,0:T(8,128)S(1)}, u32[]{:S(2)}, u32[]{:S(2)}) collective-permute-start(f32[16,128]{1,0:T(8,128)S(1)} %add.75), channel_id=1, source_target_pairs={{0,2},{1,3},{2,0},{3,1},{4,6},{5,7},{6,4},{7,5},{8,10},{9,11},{10,... | collective-permute-start | bytes 24584 | tf_op jit(solution)/shard_map/ppermute | solution.py:393
  97.1 8.3 %collective-permute-start.21 = (f32[16,128]{1,0:T(8,128)S(1)}, f32[16,128]{1,0:T(8,128)S(1)}, u32[]{:S(2)}, u32[]{:S(2)}) collective-permute-start(f32[16,128]{1,0:T(8,128)S(1)} %add.76), channel_id=1, source_target_pairs={{0,4},{1,5},{2,6},{3,7},{4,0},{5,1},{6,2},{7,3},{8,12},{9,13},{10,... | collective-permute-start | bytes 24584 | tf_op jit(solution)/shard_map/ppermute | solution.py:393
  105.4 1.6 %collective-permute-done.21 = f32[16,128]{1,0:T(8,128)S(1)} collective-permute-done((f32[16,128]{1,0:T(8,128)S(1)}, f32[16,128]{1,0:T(8,128)S(1)}, u32[]{:S(2)}, u32[]{:S(2)}) %collective-permute-start.21) | collective-permute-done | bytes 8224 | tf_op jit(solution)/shard_map/ppermute | solution.py:393
  107.0 19.5 %collective-permute-start.22 = (f32[16,128]{1,0:T(8,128)S(1)}, f32[16,128]{1,0:T(8,128)S(1)}, u32[]{:S(2)}, u32[]{:S(2)}) collective-permute-start(f32[16,128]{1,0:T(8,128)S(1)} %add.77), channel_id=1, source_target_pairs={{0,8},{1,9},{2,10},{3,11},{4,12},{5,13},{6,14},{7,15},{8,0},{9,1},... | collective-permute-start | bytes 24584 | tf_op jit(solution)/shard_map/ppermute | solution.py:393
  (74 shorter events, 20.2 us)
Async XLA Ops:
  0.6 35.7 %copy-start.2 = (bf16[256,1024]{1,0:T(8,128)(2,1)S(1)}, bf16[256,1024]{1,0:T(8,128)(2,1)}, u32[]{:S(2)}) copy-start(bf16[256,1024]{1,0:T(8,128)(2,1)} %refs_0_.1) | copy-start | bytes 1572868
  0.6 22.0 %collective-permute-start = (bf16[256,1024]{1,0:T(8,128)(2,1)}, bf16[256,1024]{1,0:T(8,128)(2,1)S(1)}, u32[]{:S(2)}, u32[]{:S(2)}) collective-permute-start(bf16[256,1024]{1,0:T(8,128)(2,1)} %refs_0_.1), channel_id=1, source_target_pairs={{0,32},{16,48},{32,64},{48,80},{64,96},{80,112},{96,0},{112,16},{1... | collective-permute-start | bytes 1572872 | tf_op jit(solution)/shard_map/ppermute | solution.py:410
  2.7 19.9 %collective-permute-start.1 = (bf16[256,1024]{1,0:T(8,128)(2,1)}, bf16[256,1024]{1,0:T(8,128)(2,1)S(1)}, u32[]{:S(2)}, u32[]{:S(2)}) collective-permute-start(bf16[256,1024]{1,0:T(8,128)(2,1)} %refs_0_.1), channel_id=1, source_target_pairs={{0,96},{16,112},{32,0},{48,16},{64,32},{80,48},{96,64},{112,80},{1... | collective-permute-start | bytes 1572872 | tf_op jit(solution)/shard_map/ppermute | solution.py:411
  4.9 17.7 %collective-permute-start.2 = (bf16[256,1024]{1,0:T(8,128)(2,1)}, bf16[256,1024]{1,0:T(8,128)(2,1)S(1)}, u32[]{:S(2)}, u32[]{:S(2)}) collective-permute-start(bf16[256,1024]{1,0:T(8,128)(2,1)} %refs_0_.1), channel_id=1, source_target_pairs={{0,16},{16,0},{32,48},{48,32},{64,80},{80,64},{96,112},{112,96},{1... | collective-permute-start | bytes 1572872 | tf_op jit(solution)/shard_map/ppermute | solution.py:412
  9.5 6.1 %collective-permute-start.3 = (bf16[272,128]{1,0:T(8,128)(2,1)}, bf16[272,128]{1,0:T(8,128)(2,1)S(1)}, u32[]{:S(2)}, u32[]{:S(2)}) collective-permute-start(bf16[272,128]{1,0:T(8,128)(2,1)} %get-tuple-element.34.p_own), channel_id=1, source_target_pairs={{0,4},{1,5},{2,6},{3,7},{4,0},{5,1},{6,2},{7,3},{8,12},{9,13},{10,... | collective-permute-start | bytes 208904 | tf_op jit(solution)/shard_map/ppermute | solution.py:393
  11.2 6.6 %collective-permute-start.4 = (bf16[272,128]{1,0:T(8,128)(2,1)}, bf16[272,128]{1,0:T(8,128)(2,1)S(1)}, u32[]{:S(2)}, u32[]{:S(2)}) collective-permute-start(bf16[272,128]{1,0:T(8,128)(2,1)} %get-tuple-element.34.p_own), channel_id=1, source_target_pairs={{0,8},{1,9},{2,10},{3,11},{4,12},{5,13},{6,14},{7,15},{8,0},{9,1},... | collective-permute-start | bytes 208904 | tf_op jit(solution)/shard_map/ppermute | solution.py:393
  15.6 5.7 %collective-permute-start.5 = (bf16[272,128]{1,0:T(8,128)(2,1)}, bf16[272,128]{1,0:T(8,128)(2,1)S(1)}, u32[]{:S(2)}, u32[]{:S(2)}) collective-permute-start(bf16[272,128]{1,0:T(8,128)(2,1)} %get-tuple-element.34.p_own), channel_id=1, source_target_pairs={{0,12},{1,13},{2,14},{3,15},{4,8},{5,9},{6,10},{7,11},{8,4},{9,5},... | collective-permute-start | bytes 208904 | tf_op jit(solution)/shard_map/ppermute | solution.py:393
  22.0 6.8 %collective-permute-start.13 = (bf16[1088,128]{1,0:T(8,128)(2,1)}, bf16[1088,128]{1,0:T(8,128)(2,1)S(1)}, u32[]{:S(2)}, u32[]{:S(2)}) collective-permute-start(bf16[1088,128]{1,0:T(8,128)(2,1)} %get-tuple-element.65), channel_id=1, source_target_pairs={{0,2},{1,3},{2,0},{3,1},{4,6},{5,7},{6,4},{7,5},{8,10},{9,11},{10,... | collective-permute-start | bytes 835592 | tf_op jit(solution)/shard_map/ppermute | solution.py:393
  22.6 10.1 %collective-permute-start.6 = (bf16[256,512]{1,0:T(8,128)(2,1)S(1)}, bf16[256,512]{1,0:T(8,128)(2,1)S(1)}, u32[]{:S(2)}, u32[]{:S(2)}) collective-permute-start(bf16[256,512]{1,0:T(8,128)(2,1)S(1)} %slice.6), channel_id=1, source_target_pairs={{0,32},{16,48},{32,64},{48,80},{64,96},{80,112},{96,0},{112,16},{1... | collective-permute-start | bytes 786440 | tf_op jit(solution)/shard_map/ppermute | solution.py:438
  23.5 9.3 %collective-permute-start.7 = (bf16[256,512]{1,0:T(8,128)(2,1)}, bf16[256,512]{1,0:T(8,128)(2,1)S(1)}, u32[]{:S(2)}, u32[]{:S(2)}) collective-permute-start(bf16[256,512]{1,0:T(8,128)(2,1)} %slice.7), channel_id=1, source_target_pairs={{0,96},{16,112},{32,0},{48,16},{64,32},{80,48},{96,64},{112,80},{1... | collective-permute-start | bytes 786440 | tf_op jit(solution)/shard_map/ppermute | solution.py:439
  29.5 21.9 %collective-permute-start.14 = (bf16[2176,128]{1,0:T(8,128)(2,1)}, bf16[2176,128]{1,0:T(8,128)(2,1)S(1)}, u32[]{:S(2)}, u32[]{:S(2)}) collective-permute-start(bf16[2176,128]{1,0:T(8,128)(2,1)} %constant_dynamic-update-slice_fusion.4), channel_id=1, source_target_pairs={{0,1},{1,0},{2,3},{3,2},{4,5},{5,4},{6,7},{7,6},{8,9},{9,8},{10,11... | collective-permute-start | bytes 1671176 | tf_op jit(solution)/shard_map/ppermute | solution.py:393
  29.5 15.5 %collective-permute-start.8 = (bf16[256,1024]{1,0:T(8,128)(2,1)S(1)}, bf16[256,1024]{1,0:T(8,128)(2,1)S(1)}, u32[]{:S(2)}, u32[]{:S(2)}) collective-permute-start(bf16[256,1024]{1,0:T(8,128)(2,1)S(1)} %collective-permute-done.2.refs_3_), channel_id=1, source_target_pairs={{0,32},{16,48},{32,64},{48,80},{64,96},{80,112},{96,0},{112,16},{1... | collective-permute-start | bytes 1572872 | tf_op jit(solution)/shard_map/ppermute | solution.py:440
  29.5 15.5 %collective-permute-start.9 = (bf16[256,1024]{1,0:T(8,128)(2,1)S(1)}, bf16[256,1024]{1,0:T(8,128)(2,1)S(1)}, u32[]{:S(2)}, u32[]{:S(2)}) collective-permute-start(bf16[256,1024]{1,0:T(8,128)(2,1)S(1)} %collective-permute-done.2.refs_3_), channel_id=1, source_target_pairs={{0,96},{16,112},{32,0},{48,16},{64,32},{80,48},{96,64},{112,80},{1... | collective-permute-start | bytes 1572872 | tf_op jit(solution)/shard_map/ppermute | solution.py:441
  32.8 12.3 %collective-permute-start.10 = (bf16[256,512]{1,0:T(8,128)(2,1)S(1)}, bf16[256,512]{1,0:T(8,128)(2,1)S(1)}, u32[]{:S(2)}, u32[]{:S(2)}) collective-permute-start(bf16[256,512]{1,0:T(8,128)(2,1)S(1)} %collective-permute-done.6.refs_0_), channel_id=1, source_target_pairs={{0,16},{16,0},{32,48},{48,32},{64,80},{80,64},{96,112},{112,96},{1... | collective-permute-start | bytes 786440 | tf_op jit(solution)/shard_map/ppermute | solution.py:442
  33.5 14.5 %collective-permute-start.11 = (bf16[256,512]{1,0:T(8,128)(2,1)S(1)}, bf16[256,512]{1,0:T(8,128)(2,1)S(1)}, u32[]{:S(2)}, u32[]{:S(2)}) collective-permute-start(bf16[256,512]{1,0:T(8,128)(2,1)S(1)} %collective-permute-done.7.refs_1_), channel_id=1, source_target_pairs={{0,16},{16,0},{32,48},{48,32},{64,80},{80,64},{96,112},{112,96},{1... | collective-permute-start | bytes 786440 | tf_op jit(solution)/shard_map/ppermute | solution.py:443
  50.8 12.0 %collective-permute-start.12 = (bf16[256,128]{1,0:T(8,128)(2,1)S(1)}, bf16[256,128]{1,0:T(8,128)(2,1)S(1)}, u32[]{:S(2)}, u32[]{:S(2)}) collective-permute-start(bf16[256,128]{1,0:T(8,128)(2,1)S(1)} %value.1.v_own), channel_id=1, source_target_pairs={{0,2},{1,3},{2,0},{3,1},{4,6},{5,7},{6,4},{7,5},{8,10},{9,11},{10,... | collective-permute-start | bytes 196616 | tf_op jit(solution)/shard_map/ppermute | solution.py:393
  62.8 10.9 %collective-permute-start.15 = (bf16[512,128]{1,0:T(8,128)(2,1)S(1)}, bf16[512,128]{1,0:T(8,128)(2,1)S(1)}, u32[]{:S(2)}, u32[]{:S(2)}) collective-permute-start(bf16[512,128]{1,0:T(8,128)(2,1)S(1)} %pad_maximum_fusion.1), channel_id=1, source_target_pairs={{0,4},{1,5},{2,6},{3,7},{4,0},{5,1},{6,2},{7,3},{8,12},{9,13},{10,... | collective-permute-start | bytes 393224 | tf_op jit(solution)/shard_map/ppermute | solution.py:393
  62.9 10.8 %collective-permute-start.16 = (bf16[512,128]{1,0:T(8,128)(2,1)S(1)}, bf16[512,128]{1,0:T(8,128)(2,1)S(1)}, u32[]{:S(2)}, u32[]{:S(2)}) collective-permute-start(bf16[512,128]{1,0:T(8,128)(2,1)S(1)} %pad_maximum_fusion.1), channel_id=1, source_target_pairs={{0,8},{1,9},{2,10},{3,11},{4,12},{5,13},{6,14},{7,15},{8,0},{9,1},... | collective-permute-start | bytes 393224 | tf_op jit(solution)/shard_map/ppermute | solution.py:393
  65.8 7.9 %collective-permute-start.17 = (bf16[512,128]{1,0:T(8,128)(2,1)S(1)}, bf16[512,128]{1,0:T(8,128)(2,1)S(1)}, u32[]{:S(2)}, u32[]{:S(2)}) collective-permute-start(bf16[512,128]{1,0:T(8,128)(2,1)S(1)} %pad_maximum_fusion.1), channel_id=1, source_target_pairs={{0,12},{1,13},{2,14},{3,15},{4,8},{5,9},{6,10},{7,11},{8,4},{9,5},... | collective-permute-start | bytes 393224 | tf_op jit(solution)/shard_map/ppermute | solution.py:393
  73.7 5.6 %collective-permute-start.18 = (bf16[2048,128]{1,0:T(8,128)(2,1)S(1)}, bf16[2048,128]{1,0:T(8,128)(2,1)S(1)}, u32[]{:S(2)}, u32[]{:S(2)}) collective-permute-start(bf16[2048,128]{1,0:T(8,128)(2,1)S(1)} %pad_maximum_fusion), channel_id=1, source_target_pairs={{0,1},{1,0},{2,3},{3,2},{4,5},{5,4},{6,7},{7,6},{8,9},{9,8},{10,11... | collective-permute-start | bytes 1572872 | tf_op jit(solution)/shard_map/ppermute | solution.py:393
  87.7 1.4 %collective-permute-start.19 = (f32[16,128]{1,0:T(8,128)S(1)}, f32[16,128]{1,0:T(8,128)S(1)}, u32[]{:S(2)}, u32[]{:S(2)}) collective-permute-start(f32[16,128]{1,0:T(8,128)S(1)} %get-tuple-element.63), channel_id=1, source_target_pairs={{0,1},{1,0},{2,3},{3,2},{4,5},{5,4},{6,7},{7,6},{8,9},{9,8},{10,11... | collective-permute-start | bytes 24584 | tf_op jit(solution)/shard_map/ppermute | solution.py:393
  89.1 8.0 %collective-permute-start.20 = (f32[16,128]{1,0:T(8,128)S(1)}, f32[16,128]{1,0:T(8,128)S(1)}, u32[]{:S(2)}, u32[]{:S(2)}) collective-permute-start(f32[16,128]{1,0:T(8,128)S(1)} %add.75), channel_id=1, source_target_pairs={{0,2},{1,3},{2,0},{3,1},{4,6},{5,7},{6,4},{7,5},{8,10},{9,11},{10,... | collective-permute-start | bytes 24584 | tf_op jit(solution)/shard_map/ppermute | solution.py:393
  97.1 9.9 %collective-permute-start.21 = (f32[16,128]{1,0:T(8,128)S(1)}, f32[16,128]{1,0:T(8,128)S(1)}, u32[]{:S(2)}, u32[]{:S(2)}) collective-permute-start(f32[16,128]{1,0:T(8,128)S(1)} %add.76), channel_id=1, source_target_pairs={{0,4},{1,5},{2,6},{3,7},{4,0},{5,1},{6,2},{7,3},{8,12},{9,13},{10,... | collective-permute-start | bytes 24584 | tf_op jit(solution)/shard_map/ppermute | solution.py:393
  107.0 21.2 %collective-permute-start.22 = (f32[16,128]{1,0:T(8,128)S(1)}, f32[16,128]{1,0:T(8,128)S(1)}, u32[]{:S(2)}, u32[]{:S(2)}) collective-permute-start(f32[16,128]{1,0:T(8,128)S(1)} %add.77), channel_id=1, source_target_pairs={{0,8},{1,9},{2,10},{3,11},{4,12},{5,13},{6,14},{7,15},{8,0},{9,1},... | collective-permute-start | bytes 24584 | tf_op jit(solution)/shard_map/ppermute | solution.py:393
  (14 other events, 94.6 us)

commit v3 on v2

--- a/solution.py
+++ b/solution.py
@@ -75,7 +75,7 @@
 def prep_kernel(
     rows, ranks, levels, heads,
     inverse, book, cot, p_own, p_y1, p_y2, p_y3, p_x, p_core,
-    keys, cos_k, sin_k, codes, cot_t, packed_s, sems,
+    keys_f, cos_f, sin_f, codes_f, cot_t, packed_s, keys, cos_k, sin_k, codes, sems, out_sems,
 ):
     me = token_rank()
     tall = rows + TAIL
@@ -96,35 +96,51 @@
     eye = lax.broadcasted_iota(jnp.int32, (HD, HD), 0) == lax.broadcasted_iota(
         jnp.int32, (HD, HD), 1
     )
-    lane = lax.broadcasted_iota(jnp.int32, (HD, HD), 1)
+    left = lax.broadcasted_iota(jnp.int32, (HD, HD), 1) < HD // 2
     ones = jnp.ones((2 * HD, HD), jnp.bfloat16)
+    sides = rows // HD
+    outs = [(keys, keys_f), (cos_k, cos_f), (sin_k, sin_f), (codes, codes_f)]
 
     @pl.loop(0, ranks)
     def _(i):
         source = pl.multiple_of(i * tall, TAIL)
         tail = packed_s[pl.ds(source + rows, TAIL), :].astype(jnp.float32)
-        for part in range(rows // HD):
-            target = pl.multiple_of(i * rows + part * HD, HD)
+        places = []
+        for part in range(sides):
             high = jnp.where(eye, tail[part : part + 1, :], 0.0)
-            low = jnp.where(eye, tail[rows // HD + part : rows // HD + part + 1, :], 0.0)
+            low = jnp.where(eye, tail[sides + part : sides + part + 1, :], 0.0)
             digits = jnp.concatenate([high, low], axis=1).astype(jnp.bfloat16)
-            place = lax.dot_general(digits, ones, NN, preferred_element_type=jnp.float32)
-            sine, cosine = sincos(place * inverse[...])
-            sine = jnp.where(lane < HD // 2, -sine, sine)
-            cos_k[pl.ds(target, HD), :] = cosine
-            sin_k[pl.ds(target, HD), :] = sine
-            raw = packed_s[pl.ds(source + part * HD, HD), :]
-            codes[pl.ds(target, HD), :] = raw
-            code = raw.astype(jnp.float32).astype(jnp.int32)
-            layer = [book[e : e + 1, :] for e in range(levels)]
-            bit = 1
-            while len(layer) > 1:
-                on = (code & bit) != 0
-                layer = [jnp.where(on, layer[j + 1], layer[j]) for j in range(0, len(layer), 2)]
-                bit *= 2
-            deq = layer[0]
-            turned = deq * cosine + pltpu.roll(deq, HD // 2, 1) * sine
-            keys[pl.ds(target, HD), :] = turned.astype(jnp.bfloat16)
+            places.append(lax.dot_general(digits, ones, NN, preferred_element_type=jnp.float32))
+        for part in range(0, sides, 2):
+            sine, cosine = sincos(jnp.where(left, places[part], places[part + 1]) * inverse[...])
+            sine_r, cosine_r = pltpu.roll(sine, HD // 2, 1), pltpu.roll(cosine, HD // 2, 1)
+            tables = (
+                (jnp.where(left, cosine, cosine_r), jnp.where(left, -sine, sine_r)),
+                (jnp.where(left, cosine_r, cosine), jnp.where(left, -sine_r, sine)),
+            )
+            for side, (cosine, sine) in enumerate(tables):
+                at = part + side
+                target = pl.multiple_of(i * rows + at * HD, HD)
+                cos_k[pl.ds(target, HD), :] = cosine
+                sin_k[pl.ds(target, HD), :] = sine
+                raw = packed_s[pl.ds(source + at * HD, HD), :]
+                codes[pl.ds(target, HD), :] = raw
+                code = raw.astype(jnp.float32).astype(jnp.int32)
+                layer = [book[e : e + 1, :] for e in range(levels)]
+                bit = 1
+                while len(layer) > 1:
+                    on = (code & bit) != 0
+                    layer = [jnp.where(on, layer[j + 1], layer[j]) for j in range(0, len(layer), 2)]
+                    bit *= 2
+                deq = layer[0]
+                turned = deq * cosine + pltpu.roll(deq, HD // 2, 1) * sine
+                keys[pl.ds(target, HD), :] = turned.astype(jnp.bfloat16)
+        block = pl.ds(pl.multiple_of(i * rows, rows), rows)
+        for j, (ref, full) in enumerate(outs):
+            pltpu.make_async_copy(ref.at[block, :], full.at[block, :], out_sems.at[j]).start()
+
+    for j, (ref, full) in enumerate(outs):
+        pltpu.make_async_copy(ref, full, out_sems.at[j]).wait()
 
 
 def shard_rows(place, n, part):
@@ -489,12 +505,17 @@
             jax.ShapeDtypeStruct((heads, HD, rows), bf16),
         ),
         in_specs=[vmem()] * 3 + [anywhere()] * 6,
-        out_specs=(vmem(),) * 5,
+        out_specs=(anywhere(),) * 4 + (vmem(),),
         scratch_shapes=[
             pltpu.VMEM((ranks * (rows + TAIL), HD), bf16),
+            pltpu.VMEM((total, HD), bf16),
+            pltpu.VMEM((total, HD), f32),
+            pltpu.VMEM((total, HD), f32),
+            pltpu.VMEM((total, HD), bf16),
             pltpu.SemaphoreType.DMA((ranks,)),
+            pltpu.SemaphoreType.DMA((4,)),
         ],
-        compiler_params=pltpu.CompilerParams(vmem_limit_bytes=16 << 20),
+        compiler_params=pltpu.CompilerParams(vmem_limit_bytes=14 << 20),
         cost_estimate=cost(1 << 32, 0),
         name="prep",
     )(after(value)(inverse[None, :]), book, cotangent, *packed)
@@ -566,7 +587,7 @@
             pltpu.VMEM((total, HD), bf16),
             pltpu.SemaphoreType.DMA((20,)),
         ],
-        compiler_params=pltpu.CompilerParams(vmem_limit_bytes=52 << 20),
+        compiler_params=pltpu.CompilerParams(vmem_limit_bytes=44 << 20),
         cost_estimate=cost(8 * rows * width * total, 8 << 20),
         name="grad",
     )(

time: 130 us -> 137 us (1.054)
  Pallas kernels: 37.2 us -> 44.9 us
    pallas_call x1, Pallas kernels: 7.61 us -> 15.3 us  [shards(): pl.pallas_call(functools.partial(prep_kernel, rows, ranks, levels, heads)...]
  transfers between devices with their start and end apart: 23 -> 23, of which waited for: 8 -> 8; matrix products, arithmetic and copies ran while one was open for 4% -> 4% of each run, Pallas kernels for 23% -> 28%
where the time goes in v3:
time: 137 us; the launch traced here: 135 us
  starting transfers between devices  63.7 us (46%)
  Pallas kernels  44.9 us (33%)
  waiting for transfers between devices  15.4 us (11%)
  local copies, waits for them, and re-layouts  9.76 us (7%)
    ppermute x14, starting transfers between devices, shards(): lax.ppermute(x, 'tokens', [(i, i ^ d) for i in range(ranks)])  46.4 us
    pallas_call x1, Pallas kernels, shards(): pl.pallas_call(functools.partial(prep_kernel, rows, ranks, levels, heads)...  15.3 us
    pallas_call x2, Pallas kernels, log_totals(): pl.pallas_call(functools.partial(stats_kernel, begin, count, rows, levels...  11.8 us
    ppermute x14, waiting for transfers between devices, shards(): lax.ppermute(x, 'tokens', [(i, i ^ d) for i in range(ranks)])  10.9 us
    unnamed x34, local copies, waits for them, and re-layouts  8.18 us
    pallas_call x1, Pallas kernels, shards(): pl.pallas_call(functools.partial(grad_kernel, heads, rows, levels), out_s...  7.33 us
    pallas_call x1, Pallas kernels, shards(): pl.pallas_call(functools.partial(project_kernel, half, part), out_shape=(...  6.21 us
    ppermute x1, starting transfers between devices, shards(): other_high = send(other, perm=down)  3.23 us
  transfers between devices with their start and end apart: 23, of which 8 were waited for; matrix products, arithmetic and copies ran while one was open for 4% of the time, Pallas kernels for 28%

profile of v3, /device:TPU:0, one launch (start us, length us, event | category | flops | bytes accessed | tf_op | source)
XLA Modules:
  0.0 135.4 jit_solution(15030031614346155167)
XLA Ops:
  0.6 2.1 %collective-permute-start = (bf16[256,1024]{1,0:T(8,128)(2,1)}, bf16[256,1024]{1,0:T(8,128)(2,1)S(1)}, u32[]{:S(2)}, u32[]{:S(2)}) collective-permute-start(bf16[256,1024]{1,0:T(8,128)(2,1)} %refs_0_.1), channel_id=1, source_target_pairs={{0,32},{16,48},{32,64},{48,80},{64,96},{80,112},{96,0},{112,16},{1... | collective-permute-start | bytes 1572872 | tf_op jit(solution)/shard_map/ppermute | solution.py:426
  2.7 2.2 %collective-permute-start.1 = (bf16[256,1024]{1,0:T(8,128)(2,1)}, bf16[256,1024]{1,0:T(8,128)(2,1)S(1)}, u32[]{:S(2)}, u32[]{:S(2)}) collective-permute-start(bf16[256,1024]{1,0:T(8,128)(2,1)} %refs_0_.1), channel_id=1, source_target_pairs={{0,96},{16,112},{32,0},{48,16},{64,32},{80,48},{96,64},{112,80},{1... | collective-permute-start | bytes 1572872 | tf_op jit(solution)/shard_map/ppermute | solution.py:427
  4.9 3.0 %collective-permute-start.2 = (bf16[256,1024]{1,0:T(8,128)(2,1)}, bf16[256,1024]{1,0:T(8,128)(2,1)S(1)}, u32[]{:S(2)}, u32[]{:S(2)}) collective-permute-start(bf16[256,1024]{1,0:T(8,128)(2,1)} %refs_0_.1), channel_id=1, source_target_pairs={{0,16},{16,0},{32,48},{48,32},{64,80},{80,64},{96,112},{112,96},{1... | collective-permute-start | bytes 1572872 | tf_op jit(solution)/shard_map/ppermute | solution.py:428
  9.5 1.7 %collective-permute-start.3 = (bf16[272,128]{1,0:T(8,128)(2,1)}, bf16[272,128]{1,0:T(8,128)(2,1)S(1)}, u32[]{:S(2)}, u32[]{:S(2)}) collective-permute-start(bf16[272,128]{1,0:T(8,128)(2,1)} %get-tuple-element.34.p_own), channel_id=1, source_target_pairs={{0,4},{1,5},{2,6},{3,7},{4,0},{5,1},{6,2},{7,3},{8,12},{9,13},{10,... | collective-permute-start | bytes 208904 | tf_op jit(solution)/shard_map/ppermute | solution.py:409
  11.2 2.9 %collective-permute-start.4 = (bf16[272,128]{1,0:T(8,128)(2,1)}, bf16[272,128]{1,0:T(8,128)(2,1)S(1)}, u32[]{:S(2)}, u32[]{:S(2)}) collective-permute-start(bf16[272,128]{1,0:T(8,128)(2,1)} %get-tuple-element.34.p_own), channel_id=1, source_target_pairs={{0,8},{1,9},{2,10},{3,11},{4,12},{5,13},{6,14},{7,15},{8,0},{9,1},... | collective-permute-start | bytes 208904 | tf_op jit(solution)/shard_map/ppermute | solution.py:409
  18.4 2.9 %collective-permute-done.5.p_y3 = bf16[272,128]{1,0:T(8,128)(2,1)S(1)} collective-permute-done((bf16[272,128]{1,0:T(8,128)(2,1)}, bf16[272,128]{1,0:T(8,128)(2,1)S(1)}, u32[]{:S(2)}, u32[]{:S(2)}) %collective-permute-start.5) | collective-permute-done | bytes 69664 | tf_op jit(solution)/shard_map/ppermute | solution.py:409
  23.5 3.2 %collective-permute-start.7 = (bf16[256,512]{1,0:T(8,128)(2,1)}, bf16[256,512]{1,0:T(8,128)(2,1)S(1)}, u32[]{:S(2)}, u32[]{:S(2)}) collective-permute-start(bf16[256,512]{1,0:T(8,128)(2,1)} %slice.7), channel_id=1, source_target_pairs={{0,96},{16,112},{32,0},{48,16},{64,32},{80,48},{96,64},{112,80},{1... | collective-permute-start | bytes 786440 | tf_op jit(solution)/shard_map/ppermute | solution.py:455
  26.8 2.0 %collective-permute-done.13.p_x = bf16[1088,128]{1,0:T(8,128)(2,1)S(1)} collective-permute-done((bf16[1088,128]{1,0:T(8,128)(2,1)}, bf16[1088,128]{1,0:T(8,128)(2,1)S(1)}, u32[]{:S(2)}, u32[]{:S(2)}) %collective-permute-start.13) | collective-permute-done | bytes 278560 | tf_op jit(solution)/shard_map/ppermute | solution.py:409
  29.5 3.2 %collective-permute-start.9 = (bf16[256,1024]{1,0:T(8,128)(2,1)S(1)}, bf16[256,1024]{1,0:T(8,128)(2,1)S(1)}, u32[]{:S(2)}, u32[]{:S(2)}) collective-permute-start(bf16[256,1024]{1,0:T(8,128)(2,1)S(1)} %collective-permute-done.2.refs_3_), channel_id=1, source_target_pairs={{0,96},{16,112},{32,0},{48,16},{64,32},{80,48},{96,64},{112,80},{1... | collective-permute-start | bytes 1572872 | tf_op jit(solution)/shard_map/ppermute | solution.py:457
  33.5 2.8 %collective-permute-start.11 = (bf16[256,512]{1,0:T(8,128)(2,1)S(1)}, bf16[256,512]{1,0:T(8,128)(2,1)S(1)}, u32[]{:S(2)}, u32[]{:S(2)}) collective-permute-start(bf16[256,512]{1,0:T(8,128)(2,1)S(1)} %collective-permute-done.7.refs_1_), channel_id=1, source_target_pairs={{0,16},{16,0},{32,48},{48,32},{64,80},{80,64},{96,112},{112,96},{1... | collective-permute-start | bytes 786440 | tf_op jit(solution)/shard_map/ppermute | solution.py:459
  36.3 6.2 %project.1 = (f32[256,1024]{1,0:T(8,128)S(1)}, f32[256,256]{1,0:T(8,128)S(1)}) custom-call(s32[8]{0:T(128)S(1)} %stack.35.place, bf16[8192,1024]{1,0:T(8,128)(2,1)} %wq.5, bf16[8192,128]{1,0:T(8,128)(2,1)} %wk.5, bf16[8192,128]{1,0:T(8,128)(2,1)} %w.1, bf16[256,1024]{1,0:T(8,128)(2,1)S(1)} %copy-done.2, bf16[256,1024]{1,0:T(8,128)(2,1)S(1)} %collective-permute-done.refs_1_, ...), custom_call_target="tpu_custom_call" | custom-call | flops 17179869184 | tf_op jit(solution)/shard_map/project/pallas_call | solution.py:463
  45.1 3.0 %collective-permute-done.11.refs_5_ = bf16[256,512]{1,0:T(8,128)(2,1)S(1)} collective-permute-done((bf16[256,512]{1,0:T(8,128)(2,1)S(1)}, bf16[256,512]{1,0:T(8,128)(2,1)S(1)}, u32[]{:S(2)}, u32[]{:S(2)}) %collective-permute-start.11) | collective-permute-done | bytes 262176 | tf_op jit(solution)/shard_map/ppermute | solution.py:459
  48.0 2.7 %value.1.v_own = bf16[256,128]{1,0:T(8,128)(2,1)S(1)} custom-call(s32[8]{0:T(128)S(1)} %stack.35.place, bf16[8192,128]{1,0:T(8,128)(2,1)} %w.1, f32[256,256]{1,0:T(8,128)S(1)} %get-tuple-element.41.before.kv_before, bf16[256,512]{1,0:T(8,128)(2,1)S(1)} %collective-permute-done.6.refs_0_, bf16[256,512]{1,0:T(8,128)(2,1)S(1)} %collective-permute-done.7.refs_1_, ...), custom_call_target="tpu_custom_call" | custom-call | tf_op jit(solution)/shard_map/value/pallas_call | solution.py:482
  51.5 15.3 %prep.1 = (bf16[4096,128]{1,0:T(8,128)(2,1)S(1)}, f32[4096,128]{1,0:T(8,128)S(1)}, f32[4096,128]{1,0:T(8,128)S(1)}, bf16[4096,128]{1,0:T(8,128)(2,1)S(1)}, bf16[8,128,256]{2,1,0:T(8,128)(2,1)S(1)}) custom-call(f32[1,128]{1,0:T(1,128)S(1)} %fusion.2.inverse, f32[16,128]{1,0:T(8,128)S(1)} %bitcast.12, bf16[256,1024]{1,0:T(8,128)(2,1)S(1)} %copy-done.3, ...), custom_call_target="tpu_custom_call" | custom-call | flops 4294967296 | tf_op jit(solution)/shard_map/prep/pallas_call | solution.py:498
  70.5 2.9 %collective-permute-start.16 = (bf16[512,128]{1,0:T(8,128)(2,1)S(1)}, bf16[512,128]{1,0:T(8,128)(2,1)S(1)}, u32[]{:S(2)}, u32[]{:S(2)}) collective-permute-start(bf16[512,128]{1,0:T(8,128)(2,1)S(1)} %pad_maximum_fusion.1), channel_id=1, source_target_pairs={{0,8},{1,9},{2,10},{3,11},{4,12},{5,13},{6,14},{7,15},{8,0},{9,1},... | collective-permute-start | bytes 393224 | tf_op jit(solution)/shard_map/ppermute | solution.py:409
  73.5 1.7 %collective-permute-start.17 = (bf16[512,128]{1,0:T(8,128)(2,1)S(1)}, bf16[512,128]{1,0:T(8,128)(2,1)S(1)}, u32[]{:S(2)}, u32[]{:S(2)}) collective-permute-start(bf16[512,128]{1,0:T(8,128)(2,1)S(1)} %pad_maximum_fusion.1), channel_id=1, source_target_pairs={{0,12},{1,13},{2,14},{3,15},{4,8},{5,9},{6,10},{7,11},{8,4},{9,5},... | collective-permute-start | bytes 393224 | tf_op jit(solution)/shard_map/ppermute | solution.py:409
  75.2 6.1 %stats.2 = (bf16[4,256,128]{2,1,0:T(8,128)(2,1)S(1)}, bf16[4,128,256]{2,1,0:T(8,128)(2,1)S(1)}, f32[4,256]{1,0:T(4,128)S(1)}, f32[16,128]{1,0:T(8,128)S(1)}) custom-call(s32[8]{0:T(128)S(1)} %stack.35.place, s32[2]{0:T(128)S(1)} %copy-done.6, s32[1,256]{1,0:T(1,128)S(1)} %copy-done.5, s32[256,128]{1,0:T(8,128)S(1)} %copy-done, f32[16,128]{1,0:T(8,128)S(1)} %bitcast.13, ...), custom_call_target="tpu_custom_call" | custom-call | flops 17179869184 | tf_op jit(solution)/shard_map/stats/pallas_call | solution.py:524
  81.5 5.8 %stats.3 = (bf16[4,256,128]{2,1,0:T(8,128)(2,1)S(1)}, bf16[4,128,256]{2,1,0:T(8,128)(2,1)S(1)}, f32[4,256]{1,0:T(4,128)S(1)}, f32[16,128]{1,0:T(8,128)}) custom-call(s32[8]{0:T(128)S(1)} %stack.35.place, s32[2]{0:T(128)S(1)} %copy-done.6, s32[1,256]{1,0:T(1,128)S(1)} %copy-done.5, s32[256,128]{1,0:T(8,128)S(1)} %copy-done, f32[16,128]{1,0:T(8,128)S(1)} %bitcast.14, ...), custom_call_target="tpu_custom_call" | custom-call | flops 17179869184 | tf_op jit(solution)/shard_map/stats/pallas_call | solution.py:524
  87.3 7.3 %grad.1 = (bf16[256,1024]{1,0:T(8,128)(2,1)}, f32[16,128]{1,0:T(8,128)S(1)}) custom-call(s32[2]{0:T(128)S(1)} %copy-done.6, bf16[4,256,128]{2,1,0:T(8,128)(2,1)S(1)} %get-tuple-element.50.q_rot_0, bf16[4,128,256]{2,1,0:T(8,128)(2,1)S(1)} %get-tuple-element.51.q_t_0, f32[4,256]{1,0:T(4,128)S(1)} %get-tuple-element.52.log_total_0, ...), custom_call_target="tpu_custom_call" | custom-call | flops 8589934592 | bytes 8388608 | tf_op jit(solution)/shard_map/grad/pallas_call | solution.py:570
  95.9 6.4 %collective-permute-start.20 = (f32[16,128]{1,0:T(8,128)S(1)}, f32[16,128]{1,0:T(8,128)S(1)}, u32[]{:S(2)}, u32[]{:S(2)}) collective-permute-start(f32[16,128]{1,0:T(8,128)S(1)} %add.75), channel_id=1, source_target_pairs={{0,2},{1,3},{2,0},{3,1},{4,6},{5,7},{6,4},{7,5},{8,10},{9,11},{10,... | collective-permute-start | bytes 24584 | tf_op jit(solution)/shard_map/ppermute | solution.py:409
  102.3 1.6 %collective-permute-done.20 = f32[16,128]{1,0:T(8,128)S(1)} collective-permute-done((f32[16,128]{1,0:T(8,128)S(1)}, f32[16,128]{1,0:T(8,128)S(1)}, u32[]{:S(2)}, u32[]{:S(2)}) %collective-permute-start.20) | collective-permute-done | bytes 8224 | tf_op jit(solution)/shard_map/ppermute | solution.py:409
  103.9 8.3 %collective-permute-start.21 = (f32[16,128]{1,0:T(8,128)S(1)}, f32[16,128]{1,0:T(8,128)S(1)}, u32[]{:S(2)}, u32[]{:S(2)}) collective-permute-start(f32[16,128]{1,0:T(8,128)S(1)} %add.76), channel_id=1, source_target_pairs={{0,4},{1,5},{2,6},{3,7},{4,0},{5,1},{6,2},{7,3},{8,12},{9,13},{10,... | collective-permute-start | bytes 24584 | tf_op jit(solution)/shard_map/ppermute | solution.py:409
  112.2 1.6 %collective-permute-done.21 = f32[16,128]{1,0:T(8,128)S(1)} collective-permute-done((f32[16,128]{1,0:T(8,128)S(1)}, f32[16,128]{1,0:T(8,128)S(1)}, u32[]{:S(2)}, u32[]{:S(2)}) %collective-permute-start.21) | collective-permute-done | bytes 8224 | tf_op jit(solution)/shard_map/ppermute | solution.py:409
  113.9 19.3 %collective-permute-start.22 = (f32[16,128]{1,0:T(8,128)S(1)}, f32[16,128]{1,0:T(8,128)S(1)}, u32[]{:S(2)}, u32[]{:S(2)}) collective-permute-start(f32[16,128]{1,0:T(8,128)S(1)} %add.77), channel_id=1, source_target_pairs={{0,8},{1,9},{2,10},{3,11},{4,12},{5,13},{6,14},{7,15},{8,0},{9,1},... | collective-permute-start | bytes 24584 | tf_op jit(solution)/shard_map/ppermute | solution.py:409
  (74 shorter events, 20.2 us)
Async XLA Ops:
  0.6 35.7 %copy-start.2 = (bf16[256,1024]{1,0:T(8,128)(2,1)S(1)}, bf16[256,1024]{1,0:T(8,128)(2,1)}, u32[]{:S(2)}) copy-start(bf16[256,1024]{1,0:T(8,128)(2,1)} %refs_0_.1) | copy-start | bytes 1572868
  0.6 22.0 %collective-permute-start = (bf16[256,1024]{1,0:T(8,128)(2,1)}, bf16[256,1024]{1,0:T(8,128)(2,1)S(1)}, u32[]{:S(2)}, u32[]{:S(2)}) collective-permute-start(bf16[256,1024]{1,0:T(8,128)(2,1)} %refs_0_.1), channel_id=1, source_target_pairs={{0,32},{16,48},{32,64},{48,80},{64,96},{80,112},{96,0},{112,16},{1... | collective-permute-start | bytes 1572872 | tf_op jit(solution)/shard_map/ppermute | solution.py:426
  2.7 19.9 %collective-permute-start.1 = (bf16[256,1024]{1,0:T(8,128)(2,1)}, bf16[256,1024]{1,0:T(8,128)(2,1)S(1)}, u32[]{:S(2)}, u32[]{:S(2)}) collective-permute-start(bf16[256,1024]{1,0:T(8,128)(2,1)} %refs_0_.1), channel_id=1, source_target_pairs={{0,96},{16,112},{32,0},{48,16},{64,32},{80,48},{96,64},{112,80},{1... | collective-permute-start | bytes 1572872 | tf_op jit(solution)/shard_map/ppermute | solution.py:427
  4.9 17.7 %collective-permute-start.2 = (bf16[256,1024]{1,0:T(8,128)(2,1)}, bf16[256,1024]{1,0:T(8,128)(2,1)S(1)}, u32[]{:S(2)}, u32[]{:S(2)}) collective-permute-start(bf16[256,1024]{1,0:T(8,128)(2,1)} %refs_0_.1), channel_id=1, source_target_pairs={{0,16},{16,0},{32,48},{48,32},{64,80},{80,64},{96,112},{112,96},{1... | collective-permute-start | bytes 1572872 | tf_op jit(solution)/shard_map/ppermute | solution.py:428
  9.5 6.1 %collective-permute-start.3 = (bf16[272,128]{1,0:T(8,128)(2,1)}, bf16[272,128]{1,0:T(8,128)(2,1)S(1)}, u32[]{:S(2)}, u32[]{:S(2)}) collective-permute-start(bf16[272,128]{1,0:T(8,128)(2,1)} %get-tuple-element.34.p_own), channel_id=1, source_target_pairs={{0,4},{1,5},{2,6},{3,7},{4,0},{5,1},{6,2},{7,3},{8,12},{9,13},{10,... | collective-permute-start | bytes 208904 | tf_op jit(solution)/shard_map/ppermute | solution.py:409
  11.2 6.6 %collective-permute-start.4 = (bf16[272,128]{1,0:T(8,128)(2,1)}, bf16[272,128]{1,0:T(8,128)(2,1)S(1)}, u32[]{:S(2)}, u32[]{:S(2)}) collective-permute-start(bf16[272,128]{1,0:T(8,128)(2,1)} %get-tuple-element.34.p_own), channel_id=1, source_target_pairs={{0,8},{1,9},{2,10},{3,11},{4,12},{5,13},{6,14},{7,15},{8,0},{9,1},... | collective-permute-start | bytes 208904 | tf_op jit(solution)/shard_map/ppermute | solution.py:409
  15.6 5.7 %collective-permute-start.5 = (bf16[272,128]{1,0:T(8,128)(2,1)}, bf16[272,128]{1,0:T(8,128)(2,1)S(1)}, u32[]{:S(2)}, u32[]{:S(2)}) collective-permute-start(bf16[272,128]{1,0:T(8,128)(2,1)} %get-tuple-element.34.p_own), channel_id=1, source_target_pairs={{0,12},{1,13},{2,14},{3,15},{4,8},{5,9},{6,10},{7,11},{8,4},{9,5},... | collective-permute-start | bytes 208904 | tf_op jit(solution)/shard_map/ppermute | solution.py:409
  22.0 6.8 %collective-permute-start.13 = (bf16[1088,128]{1,0:T(8,128)(2,1)}, bf16[1088,128]{1,0:T(8,128)(2,1)S(1)}, u32[]{:S(2)}, u32[]{:S(2)}) collective-permute-start(bf16[1088,128]{1,0:T(8,128)(2,1)} %get-tuple-element.65), channel_id=1, source_target_pairs={{0,2},{1,3},{2,0},{3,1},{4,6},{5,7},{6,4},{7,5},{8,10},{9,11},{10,... | collective-permute-start | bytes 835592 | tf_op jit(solution)/shard_map/ppermute | solution.py:409
  22.6 10.1 %collective-permute-start.6 = (bf16[256,512]{1,0:T(8,128)(2,1)S(1)}, bf16[256,512]{1,0:T(8,128)(2,1)S(1)}, u32[]{:S(2)}, u32[]{:S(2)}) collective-permute-start(bf16[256,512]{1,0:T(8,128)(2,1)S(1)} %slice.6), channel_id=1, source_target_pairs={{0,32},{16,48},{32,64},{48,80},{64,96},{80,112},{96,0},{112,16},{1... | collective-permute-start | bytes 786440 | tf_op jit(solution)/shard_map/ppermute | solution.py:454
  23.5 9.3 %collective-permute-start.7 = (bf16[256,512]{1,0:T(8,128)(2,1)}, bf16[256,512]{1,0:T(8,128)(2,1)S(1)}, u32[]{:S(2)}, u32[]{:S(2)}) collective-permute-start(bf16[256,512]{1,0:T(8,128)(2,1)} %slice.7), channel_id=1, source_target_pairs={{0,96},{16,112},{32,0},{48,16},{64,32},{80,48},{96,64},{112,80},{1... | collective-permute-start | bytes 786440 | tf_op jit(solution)/shard_map/ppermute | solution.py:455
  29.5 21.9 %collective-permute-start.14 = (bf16[2176,128]{1,0:T(8,128)(2,1)}, bf16[2176,128]{1,0:T(8,128)(2,1)S(1)}, u32[]{:S(2)}, u32[]{:S(2)}) collective-permute-start(bf16[2176,128]{1,0:T(8,128)(2,1)} %constant_dynamic-update-slice_fusion.4), channel_id=1, source_target_pairs={{0,1},{1,0},{2,3},{3,2},{4,5},{5,4},{6,7},{7,6},{8,9},{9,8},{10,11... | collective-permute-start | bytes 1671176 | tf_op jit(solution)/shard_map/ppermute | solution.py:409
  29.5 15.5 %collective-permute-start.8 = (bf16[256,1024]{1,0:T(8,128)(2,1)S(1)}, bf16[256,1024]{1,0:T(8,128)(2,1)S(1)}, u32[]{:S(2)}, u32[]{:S(2)}) collective-permute-start(bf16[256,1024]{1,0:T(8,128)(2,1)S(1)} %collective-permute-done.2.refs_3_), channel_id=1, source_target_pairs={{0,32},{16,48},{32,64},{48,80},{64,96},{80,112},{96,0},{112,16},{1... | collective-permute-start | bytes 1572872 | tf_op jit(solution)/shard_map/ppermute | solution.py:456
  29.5 15.5 %collective-permute-start.9 = (bf16[256,1024]{1,0:T(8,128)(2,1)S(1)}, bf16[256,1024]{1,0:T(8,128)(2,1)S(1)}, u32[]{:S(2)}, u32[]{:S(2)}) collective-permute-start(bf16[256,1024]{1,0:T(8,128)(2,1)S(1)} %collective-permute-done.2.refs_3_), channel_id=1, source_target_pairs={{0,96},{16,112},{32,0},{48,16},{64,32},{80,48},{96,64},{112,80},{1... | collective-permute-start | bytes 1572872 | tf_op jit(solution)/shard_map/ppermute | solution.py:457
  32.8 12.3 %collective-permute-start.10 = (bf16[256,512]{1,0:T(8,128)(2,1)S(1)}, bf16[256,512]{1,0:T(8,128)(2,1)S(1)}, u32[]{:S(2)}, u32[]{:S(2)}) collective-permute-start(bf16[256,512]{1,0:T(8,128)(2,1)S(1)} %collective-permute-done.6.refs_0_), channel_id=1, source_target_pairs={{0,16},{16,0},{32,48},{48,32},{64,80},{80,64},{96,112},{112,96},{1... | collective-permute-start | bytes 786440 | tf_op jit(solution)/shard_map/ppermute | solution.py:458
  33.5 14.5 %collective-permute-start.11 = (bf16[256,512]{1,0:T(8,128)(2,1)S(1)}, bf16[256,512]{1,0:T(8,128)(2,1)S(1)}, u32[]{:S(2)}, u32[]{:S(2)}) collective-permute-start(bf16[256,512]{1,0:T(8,128)(2,1)S(1)} %collective-permute-done.7.refs_1_), channel_id=1, source_target_pairs={{0,16},{16,0},{32,48},{48,32},{64,80},{80,64},{96,112},{112,96},{1... | collective-permute-start | bytes 786440 | tf_op jit(solution)/shard_map/ppermute | solution.py:459
  50.8 19.7 %collective-permute-start.12 = (bf16[256,128]{1,0:T(8,128)(2,1)S(1)}, bf16[256,128]{1,0:T(8,128)(2,1)S(1)}, u32[]{:S(2)}, u32[]{:S(2)}) collective-permute-start(bf16[256,128]{1,0:T(8,128)(2,1)S(1)} %value.1.v_own), channel_id=1, source_target_pairs={{0,2},{1,3},{2,0},{3,1},{4,6},{5,7},{6,4},{7,5},{8,10},{9,11},{10,... | collective-permute-start | bytes 196616 | tf_op jit(solution)/shard_map/ppermute | solution.py:409
  70.4 10.9 %collective-permute-start.15 = (bf16[512,128]{1,0:T(8,128)(2,1)S(1)}, bf16[512,128]{1,0:T(8,128)(2,1)S(1)}, u32[]{:S(2)}, u32[]{:S(2)}) collective-permute-start(bf16[512,128]{1,0:T(8,128)(2,1)S(1)} %pad_maximum_fusion.1), channel_id=1, source_target_pairs={{0,4},{1,5},{2,6},{3,7},{4,0},{5,1},{6,2},{7,3},{8,12},{9,13},{10,... | collective-permute-start | bytes 393224 | tf_op jit(solution)/shard_map/ppermute | solution.py:409
  70.5 10.8 %collective-permute-start.16 = (bf16[512,128]{1,0:T(8,128)(2,1)S(1)}, bf16[512,128]{1,0:T(8,128)(2,1)S(1)}, u32[]{:S(2)}, u32[]{:S(2)}) collective-permute-start(bf16[512,128]{1,0:T(8,128)(2,1)S(1)} %pad_maximum_fusion.1), channel_id=1, source_target_pairs={{0,8},{1,9},{2,10},{3,11},{4,12},{5,13},{6,14},{7,15},{8,0},{9,1},... | collective-permute-start | bytes 393224 | tf_op jit(solution)/shard_map/ppermute | solution.py:409
  73.5 7.8 %collective-permute-start.17 = (bf16[512,128]{1,0:T(8,128)(2,1)S(1)}, bf16[512,128]{1,0:T(8,128)(2,1)S(1)}, u32[]{:S(2)}, u32[]{:S(2)}) collective-permute-start(bf16[512,128]{1,0:T(8,128)(2,1)S(1)} %pad_maximum_fusion.1), channel_id=1, source_target_pairs={{0,12},{1,13},{2,14},{3,15},{4,8},{5,9},{6,10},{7,11},{8,4},{9,5},... | collective-permute-start | bytes 393224 | tf_op jit(solution)/shard_map/ppermute | solution.py:409
  81.4 5.9 %collective-permute-start.18 = (bf16[2048,128]{1,0:T(8,128)(2,1)S(1)}, bf16[2048,128]{1,0:T(8,128)(2,1)S(1)}, u32[]{:S(2)}, u32[]{:S(2)}) collective-permute-start(bf16[2048,128]{1,0:T(8,128)(2,1)S(1)} %pad_maximum_fusion), channel_id=1, source_target_pairs={{0,1},{1,0},{2,3},{3,2},{4,5},{5,4},{6,7},{7,6},{8,9},{9,8},{10,11... | collective-permute-start | bytes 1572872 | tf_op jit(solution)/shard_map/ppermute | solution.py:409
  94.6 1.3 collective-permute-start.19
  95.9 8.0 %collective-permute-start.20 = (f32[16,128]{1,0:T(8,128)S(1)}, f32[16,128]{1,0:T(8,128)S(1)}, u32[]{:S(2)}, u32[]{:S(2)}) collective-permute-start(f32[16,128]{1,0:T(8,128)S(1)} %add.75), channel_id=1, source_target_pairs={{0,2},{1,3},{2,0},{3,1},{4,6},{5,7},{6,4},{7,5},{8,10},{9,11},{10,... | collective-permute-start | bytes 24584 | tf_op jit(solution)/shard_map/ppermute | solution.py:409
  103.9 9.9 %collective-permute-start.21 = (f32[16,128]{1,0:T(8,128)S(1)}, f32[16,128]{1,0:T(8,128)S(1)}, u32[]{:S(2)}, u32[]{:S(2)}) collective-permute-start(f32[16,128]{1,0:T(8,128)S(1)} %add.76), channel_id=1, source_target_pairs={{0,4},{1,5},{2,6},{3,7},{4,0},{5,1},{6,2},{7,3},{8,12},{9,13},{10,... | collective-permute-start | bytes 24584 | tf_op jit(solution)/shard_map/ppermute | solution.py:409
  113.9 20.9 %collective-permute-start.22 = (f32[16,128]{1,0:T(8,128)S(1)}, f32[16,128]{1,0:T(8,128)S(1)}, u32[]{:S(2)}, u32[]{:S(2)}) collective-permute-start(f32[16,128]{1,0:T(8,128)S(1)} %add.77), channel_id=1, source_target_pairs={{0,8},{1,9},{2,10},{3,11},{4,12},{5,13},{6,14},{7,15},{8,0},{9,1},... | collective-permute-start | bytes 24584 | tf_op jit(solution)/shard_map/ppermute | solution.py:409
  (14 other events, 105.3 us)

commit v4 on v3

v4 whole, which is shorter than its diff:
```python
import functools
import math

import jax
import jax.numpy as jnp
from jax import lax
from jax.experimental import pallas as pl
from jax.experimental.pallas import tpu as pltpu
from jax.sharding import PartitionSpec as P

HD = 128
ROPE_BASE = 500000.0
NEG_BIG = -1e30
LOG2E = math.log2(math.e)
SCALE = 1.0 / math.sqrt(HD)
BLOCK = 512
NN = (((1,), (0,)), ((), ()))
TN = (((0,), (0,)), ((), ()))
TAIL = 16
PARTNER = 15


def sincos(angle):
    turns = jnp.floor(angle * (2.0 / math.pi) + 0.5)
    r = angle - turns * 1.5703125
    r = r - turns * 4.837512969970703125e-4
    r = r - turns * 7.54978995489188216e-8
    z = r * r
    s = ((-1.9515295891e-4 * z + 8.3321608736e-3) * z - 1.6666654611e-1) * z * r + r
    c = ((2.443315711809948e-5 * z - 1.388731625493765e-3) * z + 4.166664568298827e-2) * z * z
    c = c - 0.5 * z + 1.0
    quadrant = turns.astype(jnp.int32)
    odd = (quadrant & 1) == 1
    sine = jnp.where(odd, c, s)
    cosine = jnp.where(odd, s, c)
    sine = jnp.where((quadrant & 2) == 0, sine, -sine)
    cosine = jnp.where(((quadrant + 1) & 2) == 0, cosine, -cosine)
    return sine, cosine


def slots_y_first(pieces):
    own, y1, y2, y3, x, core = pieces
    found = [(0, own, 0), (4, y1, 0), (8, y2, 0), (12, y3, 0)]
    found += [(2 | 4 * j, x, j) for j in range(4)]
    return found + [(1 | (4 * j if j < 4 else 2 | 4 * (j - 4)), core, j) for j in range(8)]


def slots(pieces):
    own, x, y1, y2, y3, core = pieces
    found = [(0, own, 0), (2, x, 0)]
    for y, ref in ((1, y1), (2, y2), (3, y3)):
        found += [(4 * y, ref, 0), (4 * y + 2, ref, 1)]
    return found + [(2 * j + 1, core, j) for j in range(8)]


def token_rank():
    return lax.axis_index("tokens")


def pack_kernel(rows, key_codes, positions, packed):
    packed[:rows, :] = key_codes[...].astype(jnp.float32).astype(jnp.bfloat16)
    place = positions[...]
    high, low = place & ~63, place & 63
    wide = [x[:, j * HD : (j + 1) * HD] for x in (high, low) for j in range(rows // HD)]
    blank = jnp.zeros((TAIL - len(wide), HD), jnp.int32)
    tail = jnp.concatenate(wide + [blank], axis=0)
    packed[rows:, :] = tail.astype(jnp.float32).astype(jnp.bfloat16)


def prep_kernel(
    rows, ranks, levels, heads,
    inverse, book, cot, cot_b, p_own, p_y1, p_y2, p_y3, p_x, p_core,
    keys_f, cos_f, sin_f, codes_f, cot_t, early, info, packed_s, keys, cos_k, sin_k, codes, sems, out_sems,
):
    me = token_rank()
    tall = rows + TAIL
    copies = []
    for j, (bits, ref, at) in enumerate(slots_y_first((p_own, p_y1, p_y2, p_y3, p_x, p_core))):
        start = pl.multiple_of((me ^ bits) * tall, TAIL)
        copies.append(
            pltpu.make_async_copy(
                ref.at[at * tall : (at + 1) * tall, :], packed_s.at[pl.ds(start, tall), :], sems.at[j]
            )
        )
    for copy in copies:
        copy.start()
    side = rows // 2
    for h in range(heads):
        columns, lanes = slice(h * HD, (h + 1) * HD), slice(h % 2 * side, (h % 2 + 1) * side)
        cot_t[h // 2, :, lanes] = cot[:side, columns].T
        cot_t[heads // 2 + h // 2, :, lanes] = cot_b[:, columns].T
    for copy in copies:
        copy.wait()
    for j, start in enumerate(segments(side)):
        rank = me if j == 0 else me ^ PARTNER
        tail = packed_s[pl.ds(pl.multiple_of(rank * tall + rows, TAIL), TAIL), :].astype(jnp.float32)
        place = tail[j : j + 1, :] + tail[2 + j : 3 + j, :]
        index = start + lax.broadcasted_iota(jnp.int32, (1, side), 1)
        first = index.astype(jnp.float32) - place
        early[j : j + 1, :] = jnp.concatenate([first, first], axis=1).astype(jnp.int32)
        info[2 * j] = jnp.min(first).astype(jnp.int32) // BLOCK
        info[2 * j + 1] = jnp.max(first).astype(jnp.int32)
    eye = lax.broadcasted_iota(jnp.int32, (HD, HD), 0) == lax.broadcasted_iota(
        jnp.int32, (HD, HD), 1
    )
    left = lax.broadcasted_iota(jnp.int32, (HD, HD), 1) < HD // 2
    ones = jnp.ones((2 * HD, HD), jnp.bfloat16)
    sides = rows // HD
    outs = [(keys, keys_f), (cos_k, cos_f), (sin_k, sin_f), (codes, codes_f)]

    @pl.loop(0, ranks)
    def _(i):
        source = pl.multiple_of(i * tall, TAIL)
        tail = packed_s[pl.ds(source + rows, TAIL), :].astype(jnp.float32)
        places = []
        for part in range(sides):
            high = jnp.where(eye, tail[part : part + 1, :], 0.0)
            low = jnp.where(eye, tail[sides + part : sides + part + 1, :], 0.0)
            digits = jnp.concatenate([high, low], axis=1).astype(jnp.bfloat16)
            places.append(lax.dot_general(digits, ones, NN, preferred_element_type=jnp.float32))
        for part in range(0, sides, 2):
            sine, cosine = sincos(jnp.where(left, places[part], places[part + 1]) * inverse[...])
            sine_r, cosine_r = pltpu.roll(sine, HD // 2, 1), pltpu.roll(cosine, HD // 2, 1)
            tables = (
                (jnp.where(left, cosine, cosine_r), jnp.where(left, -sine, sine_r)),
                (jnp.where(left, cosine_r, cosine), jnp.where(left, -sine_r, sine)),
            )
            for side, (cosine, sine) in enumerate(tables):
                at = part + side
                target = pl.multiple_of(i * rows + at * HD, HD)
                cos_k[pl.ds(target, HD), :] = cosine
                sin_k[pl.ds(target, HD), :] = sine
                raw = packed_s[pl.ds(source + at * HD, HD), :]
                codes[pl.ds(target, HD), :] = raw
                code = raw.astype(jnp.float32).astype(jnp.int32)
                layer = [book[e : e + 1, :] for e in range(levels)]
                bit = 1
                while len(layer) > 1:
                    on = (code & bit) != 0
                    layer = [jnp.where(on, layer[j + 1], layer[j]) for j in range(0, len(layer), 2)]
                    bit *= 2
                deq = layer[0]
                turned = deq * cosine + pltpu.roll(deq, HD // 2, 1) * sine
                keys[pl.ds(target, HD), :] = turned.astype(jnp.bfloat16)
        block = pl.ds(pl.multiple_of(i * rows, rows), rows)
        for j, (ref, full) in enumerate(outs):
            pltpu.make_async_copy(ref.at[block, :], full.at[block, :], out_sems.at[j]).start()

    for j, (ref, full) in enumerate(outs):
        pltpu.make_async_copy(ref, full, out_sems.at[j]).wait()


def shard_rows(place, n, part):
    return pl.ds(pl.multiple_of(place[n] * part, part), part)


def fetch(pieces, x_s, part, sem):
    copies = []
    for j, piece in enumerate(pieces):
        side = piece.shape[0]
        target = x_s.at[j % 2 * side : (j % 2 + 1) * side, j // 2 * part : (j // 2 + 1) * part]
        copies.append(pltpu.make_async_copy(piece, target, sem(j)))
    return copies


def project_kernel(
    count, part, place, wq, wk, wv, *refs,
):
    pieces, (q_out, kv_out, x_s, wq_s, wkv_s, sems) = refs[: 2 * count], refs[2 * count :]
    loads = fetch(pieces, x_s, part, lambda j: sems.at[3 * count + j])
    copies = []
    for n in range(count):
        rows = shard_rows(place, n, part)
        copies.append([
            loads[2 * n],
            loads[2 * n + 1],
            pltpu.make_async_copy(wq.at[rows, :], wq_s.at[n], sems.at[3 * n]),
            pltpu.make_async_copy(wk.at[rows, :], wkv_s.at[n, :, :HD], sems.at[3 * n + 1]),
            pltpu.make_async_copy(wv.at[rows, :], wkv_s.at[n, :, HD:], sems.at[3 * n + 2]),
        ])
        for copy in copies[-1]:
            copy.start()
    for n in range(count):
        for copy in copies[n]:
            copy.wait()
        x = x_s[:, n * part : (n + 1) * part]
        q = jnp.dot(x, wq_s[n], preferred_element_type=jnp.float32)
        kv = jnp.dot(x, wkv_s[n], preferred_element_type=jnp.float32)
        q_out[...] = q if n == 0 else q_out[...] + q
        kv_out[...] = kv if n == 0 else kv_out[...] + kv


def value_kernel(first, count, part, place, w, before, *refs):
    pieces, (value, x_s, w_s, before_s, sems) = refs[:-5], refs[-5:]
    copies = fetch(pieces, x_s, part, lambda j: sems.at[j])
    copies.append(pltpu.make_async_copy(before.at[:, HD:], before_s, sems.at[len(copies)]))
    for n in range(count):
        copies.append(
            pltpu.make_async_copy(w.at[shard_rows(place, first + n, part), :], w_s.at[n], sems.at[len(copies)])
        )
    for copy in copies:
        copy.start()
    for copy in copies:
        copy.wait()
    total = before_s[...]
    for n in range(count):
        total += jnp.dot(x_s[:, n * part : (n + 1) * part], w_s[n], preferred_element_type=jnp.float32)
    value[...] = total.astype(jnp.bfloat16)


def visible_block(base, block, own, earliest, side):
    key = base + lax.broadcasted_iota(jnp.int32, (block, 2 * side), 0)
    query = own + lax.broadcasted_iota(jnp.int32, (block, 2 * side), 1) % side
    return (key <= query) & (key >= earliest)


def segments(side):
    me = token_rank()
    return (2 * side * me, 2 * side * (me ^ PARTNER) + side)


def over_blocks(own, first, edge, side, body):
    last = (own + side + BLOCK - 1) // BLOCK

    @pl.loop(first, last)
    def _(b):
        masked = (b * BLOCK < edge) | (b * BLOCK + BLOCK > own)

        @pl.when(masked)
        def _():
            body(b, True)

        @pl.when(jnp.logical_not(masked))
        def _():
            body(b, False)


def stats_kernel(
    begin, heads, rows, levels, weight, first, count, part,
    place, info, early, book, cos_k, sin_k, codes_f, keys_k, q_before, kv_before, wq, wk, *refs,
):
    pieces = refs[:-18]
    (
        q_rot, q_t, log_total, bins,
        peak_s, mass_s, cos_q, sin_q, codes, keys, x_s, wq_s, wk_s, q_s, true_s, x_sems, w_sems, sems,
    ) = refs[-18:]
    side = rows // 2
    columns = pl.ds(begin * HD, heads * HD)
    loads = fetch(pieces, x_s, part, lambda j: x_sems.at[j])
    weights = []
    for n in range(count):
        at = shard_rows(place, first + n, part)
        row = [pltpu.make_async_copy(wq.at[at, columns], wq_s.at[n], w_sems.at[2 * n])]
        if begin == 0:
            row.append(pltpu.make_async_copy(wk.at[at, :], wk_s.at[n], w_sems.at[2 * n + 1]))
        weights.append(row)
    before = [pltpu.make_async_copy(q_before.at[:, columns], q_s, sems.at[0])]
    if begin == 0:
        before.append(pltpu.make_async_copy(kv_before.at[:, :HD], true_s, sems.at[1]))
    tables = [pltpu.make_async_copy(keys_k, keys, sems.at[2])]
    for j, start in enumerate(segments(side)):
        source = pl.ds(pl.multiple_of(start, side), side)
        target = slice(j * side, (j + 1) * side)
        for i, (full, ref) in enumerate(((cos_k, cos_q), (sin_k, sin_q), (codes_f, codes))):
            tables.append(
                pltpu.make_async_copy(full.at[source, :], ref.at[target, :], sems.at[3 + 3 * j + i])
            )
    for copy in before + loads + sum(weights, []) + tables:
        copy.start()
    peak_s[...] = jnp.full_like(peak_s, NEG_BIG)
    mass_s[...] = jnp.zeros_like(mass_s)
    for copy in before + loads:
        copy.wait()
    for n in range(count):
        for copy in weights[n]:
            copy.wait()
        x = x_s[:, n * part : (n + 1) * part]
        q_s[...] += jnp.dot(x, wq_s[n], preferred_element_type=jnp.float32)
        if begin == 0:
            true_s[...] += jnp.dot(x, wk_s[n], preferred_element_type=jnp.float32)
    for copy in tables:
        copy.wait()
    if begin == 0:
        code = codes[...].astype(jnp.float32)
        for level in range(levels):
            entry = weight * (book[level : level + 1, :] - true_s[...])
            bins[level : level + 1, :] = jnp.sum(
                jnp.where(code == level, entry, 0.0), axis=0, keepdims=True
            )
    else:
        bins[...] = jnp.zeros_like(bins)
    pairs = heads // 2
    for h in range(heads):
        x = q_s[:, h * HD : (h + 1) * HD]
        turned = (x * cos_q[...] + pltpu.roll(x, HD // 2, 1) * sin_q[...]).astype(jnp.bfloat16)
        lanes = slice(h % 2 * side, (h % 2 + 1) * side)
        for j in range(2):
            piece = turned[j * side : (j + 1) * side, :]
            q_rot[j * pairs + h // 2, lanes, :] = piece
            q_t[j * pairs + h // 2, :, lanes] = piece.T

    for j, own in enumerate(segments(side)):
        def body(b, masked):
            base = pl.multiple_of(b * BLOCK, BLOCK)
            k = keys[pl.ds(base, BLOCK), :]
            if masked:
                seen = visible_block(base, BLOCK, own, early[j : j + 1, :], side)
            for tile in range(j * pairs, (j + 1) * pairs):
                t = lax.dot_general(k, q_t[tile], NN, preferred_element_type=jnp.float32)
                t = t * (SCALE * LOG2E)
                if masked:
                    t = jnp.where(seen, t, NEG_BIG)
                old = peak_s[tile : tile + 1, :]
                new = jnp.maximum(old, jnp.max(t, axis=0, keepdims=True))
                fresh = jnp.sum(jnp.exp2(t - new), axis=0, keepdims=True)
                mass_s[tile : tile + 1, :] = mass_s[tile : tile + 1, :] * jnp.exp2(old - new) + fresh
                peak_s[tile : tile + 1, :] = new

        over_blocks(own, info[2 * j], info[2 * j + 1], side, body)

    log_total[...] = peak_s[...] + jnp.log(mass_s[...]) * LOG2E


def grad_kernel(
    heads, rows, levels,
    info, q_rot_0, q_t_0, log_total_0, q_rot_1, q_t_1, log_total_1, early, cot, cot_b, cot_t, init,
    keys_k, cos_f, sin_f, codes_f, v_own, v_x, v_y1, v_y2, v_y3, v_core,
    out, out_b, bins, probs_s, out_s, delta_s, acc_s, values, keys, cos_k, sin_k, codes, sems,
):
    me = token_rank()
    side, pairs = rows // 2, heads // 2
    part = pairs // 2

    def tiles(ref_0, ref_1):
        return [
            [(ref_0, ref_1)[p // part].at[j * part + p % part] for p in range(pairs)] for j in range(2)
        ]

    q_rot, q_t = tiles(q_rot_0, q_rot_1), tiles(q_t_0, q_t_1)
    log_total = [
        [(log_total_0, log_total_1)[p // part].at[pl.ds(j * part + p % part, 1), :] for p in range(pairs)]
        for j in range(2)
    ]
    copies = [pltpu.make_async_copy(keys_k, keys, sems.at[0])]
    for i, (bits, ref, at) in enumerate(slots((v_own, v_x, v_y1, v_y2, v_y3, v_core))):
        rank = me ^ bits
        for j, start in enumerate((rank * rows, (rank ^ PARTNER) * rows + side)):
            source = slice(at * rows + j * side, at * rows + (j + 1) * side)
            target = pl.ds(pl.multiple_of(start, side), side)
            copies.append(
                pltpu.make_async_copy(
                    ref.at[source, :], values.at[target, :], sems.at[1 + 2 * i + j]
                )
            )
    late = [
        pltpu.make_async_copy(cos_f, cos_k, sems.at[33]),
        pltpu.make_async_copy(sin_f, sin_k, sems.at[34]),
        pltpu.make_async_copy(codes_f, codes, sems.at[35]),
    ]
    for copy in copies + late:
        copy.start()
    acc_s[...] = jnp.zeros_like(acc_s)
    out_s[...] = jnp.zeros_like(out_s)
    for copy in copies:
        copy.wait()

    for j, own in enumerate(segments(side)):
        first, edge = info[2 * j], info[2 * j + 1]

        def forward(b, masked):
            base = pl.multiple_of(b * BLOCK, BLOCK)
            k = keys[pl.ds(base, BLOCK), :]
            v = values[pl.ds(base, BLOCK), :]
            if masked:
                seen = visible_block(base, BLOCK, own, early[j : j + 1, :], side)
            for p in range(pairs):
                s = lax.dot_general(k, q_t[j][p][...], NN, preferred_element_type=jnp.float32)
                w = jnp.exp2(s * (SCALE * LOG2E) - log_total[j][p][...])
                if masked:
                    w = jnp.where(seen, w, 0.0)
                probs_s[b - first, p] = w
                out_s[j * pairs + p] += lax.dot_general(
                    w.astype(jnp.bfloat16), v, TN, preferred_element_type=jnp.float32
                )

        over_blocks(own, first, edge, side, forward)
        for h in range(heads):
            columns = slice(h * HD, (h + 1) * HD)
            lanes = slice(h % 2 * side, (h % 2 + 1) * side)
            o = out_s[j * pairs + h // 2, lanes, :].astype(jnp.bfloat16)
            if j == 0:
                out[:, columns] = o
                grad = cot[:side, columns]
            else:
                out_b[:, columns] = o
                grad = cot_b[:, columns]
            prod = grad.astype(jnp.float32) * o.astype(jnp.float32)
            delta_s[h // 2 : h // 2 + 1, lanes] = jnp.sum(prod.T, axis=0, keepdims=True)
        if j == 0:
            for copy in late:
                copy.wait()

        @pl.loop(first, (own + side + BLOCK - 1) // BLOCK)
        def _(b):
            base = pl.multiple_of(b * BLOCK, BLOCK)
            v = values[pl.ds(base, BLOCK), :]
            dk = jnp.zeros((BLOCK, HD), jnp.float32)
            for p in range(pairs):
                dp = lax.dot_general(v, cot_t[j * pairs + p], NN, preferred_element_type=jnp.float32)
                ds = (probs_s[b - first, p] * (dp - delta_s[p : p + 1, :])).astype(jnp.bfloat16)
                dk = dk + lax.dot_general(ds, q_rot[j][p][...], NN, preferred_element_type=jnp.float32)
            dk = dk * SCALE
            g = dk * cos_k[pl.ds(base, BLOCK), :] - pltpu.roll(dk, HD // 2, 1) * sin_k[pl.ds(base, BLOCK), :]
            code = codes[pl.ds(base, BLOCK), :].astype(jnp.float32)
            for level in range(levels):
                chosen = jnp.where(code == level, g, 0.0)
                acc_s[level] += jnp.sum(chosen.reshape(BLOCK // 8, 8, HD), axis=0)

    bins[...] = init[...] + jnp.sum(acc_s[...], axis=1)


def anywhere():
    return pl.BlockSpec(memory_space=pl.ANY)


def vmem():
    return pl.BlockSpec(memory_space=pltpu.VMEM)


def smem():
    return pl.BlockSpec(memory_space=pltpu.SMEM)


def cost(flops, size):
    return pl.CostEstimate(flops=flops, bytes_accessed=size, transcendentals=0)


def shards(hidden, w_query, w_key, w_value, key_codes, codebook, positions, cotangent):
    rows, part = hidden.shape
    width = w_query.shape[1]
    heads = width // HD
    levels = codebook.shape[1]
    ranks = lax.axis_size("tokens")
    total = rows * ranks
    group = lax.axis_size("tensor")
    rank = lax.axis_index("tensor")
    me = lax.axis_index("tokens")
    own = me * rows
    bf16, f32 = jnp.bfloat16, jnp.float32

    cross = lambda x, d: lax.ppermute(x, "tokens", [(i, i ^ d) for i in range(ranks)])

    def everyone(x, first, second, third):
        x_side = first(cross(x, 2))
        pair = second(jnp.concatenate([x, x_side], axis=0))
        y_side = [cross(pair, 4 * y) for y in (1, 2, 3)]
        core = cross(third(jnp.concatenate([pair] + y_side, axis=0)), 1)
        return (x, x_side, *y_side, core)

    def after(*others):
        return lambda v: lax.optimization_barrier((v, others))[0]

    flip = [(i, i ^ 1) for i in range(group)]
    up = [(i, (i + 2) % group) for i in range(group)]
    down = [(i, (i - 2) % group) for i in range(group)]
    send = functools.partial(lax.ppermute, axis_name="tensor")
    side = rows // 2
    upper, lower, key_codes = lax.optimization_barrier((hidden[:side], hidden[side:], key_codes))
    hidden_b = cross(lower, PARTNER)
    mine = (upper, hidden_b)
    low_a, high_a, other_a = (send(mine[0], perm=perm) for perm in (up, down, flip))
    low_b, high_b, other_b = (send(mine[1], perm=perm) for perm in (up, down, flip))
    cot_b = cross(cotangent[side:], PARTNER)
    places = positions[None, :]
    packed = pl.pallas_call(
        functools.partial(pack_kernel, rows),
        out_shape=jax.ShapeDtypeStruct((rows + TAIL, HD), bf16),
        in_specs=[vmem()] * 2,
        out_specs=vmem(),
        name="pack",
    )(key_codes, places)
    book = codebook.T
    inverse = jnp.exp((jnp.arange(HD) % (HD // 2)).astype(f32) * (-2.0 * math.log(ROPE_BASE) / HD))

    mate = rank ^ 1
    turn = lambda x, by: (x + by) % group
    shard = [rank, turn(rank, -2), turn(rank, 2), mate]
    shard += [turn(rank, 4), turn(mate, -2), turn(mate, 2), turn(mate, 4)]
    place = jnp.stack(shard).astype(jnp.int32)

    packed = after(low_a, high_a, other_a)(packed)
    y_side = [cross(packed, 4 * y) for y in (1, 2, 3)]
    column = jnp.concatenate([packed] + y_side, axis=0)
    x_side = cross(column, 2)
    low_a, high_a, other_a = lax.optimization_barrier((low_a, high_a, other_a))
    far_a = send(low_a, perm=up)
    other_low_a = send(other_a, perm=up)
    other_high_a = send(other_a, perm=down)
    low_b, high_b, other_b = after(column)((low_b, high_b, other_b))
    far_b = send(high_b, perm=down)
    other_low_b = send(other_b, perm=up)
    other_high_b = send(other_b, perm=down)
    other_far_a = send(far_a, perm=flip)
    other_far_b = send(far_b, perm=flip)
    half = group // 2
    other_b = after(far_b)(other_b)
    q_sum, kv_sum = pl.pallas_call(
        functools.partial(project_kernel, half, part),
        out_shape=(jax.ShapeDtypeStruct((rows, width), f32), jax.ShapeDtypeStruct((rows, 2 * HD), f32)),
        in_specs=[smem()] + [anywhere()] * (3 + 2 * half),
        out_specs=(vmem(),) * 2,
        scratch_shapes=[
            pltpu.VMEM((rows, half * part), bf16),
            pltpu.VMEM((half, part, width), bf16),
            pltpu.VMEM((half, part, 2 * HD), bf16),
            pltpu.SemaphoreType.DMA((5 * half,)),
        ],
        compiler_params=pltpu.CompilerParams(vmem_limit_bytes=50 << 20),
        cost_estimate=cost(1 << 34, 0),
        name="project",
    )(place, w_query, w_key, w_value, *mine, low_a, low_b, high_a, high_b, other_a, other_b)
    core = cross(jnp.concatenate([column, x_side], axis=0), 1)
    packed = (packed, *y_side, x_side, core)

    rest = [far_a, far_b, other_low_a, other_low_b, other_high_a, other_high_b, other_far_a, other_far_b]
    value = pl.pallas_call(
        functools.partial(value_kernel, half, half, part),
        out_shape=jax.ShapeDtypeStruct((rows, HD), bf16),
        in_specs=[smem()] + [anywhere()] * (2 + len(rest)),
        out_specs=vmem(),
        scratch_shapes=[
            pltpu.VMEM((rows, half * part), bf16),
            pltpu.VMEM((half, part, HD), bf16),
            pltpu.VMEM((rows, HD), f32),
            pltpu.SemaphoreType.DMA((half + len(rest) + 1,)),
        ],
        compiler_params=pltpu.CompilerParams(vmem_limit_bytes=50 << 20),
        cost_estimate=cost(0, 0),
        name="value",
    )(place, w_value, kv_sum, *rest)

    keys, cos_k, sin_k, codes, cot_t, early, info = pl.pallas_call(
        functools.partial(prep_kernel, rows, ranks, levels, heads),
        out_shape=(
            jax.ShapeDtypeStruct((total, HD), bf16),
            jax.ShapeDtypeStruct((total, HD), f32),
            jax.ShapeDtypeStruct((total, HD), f32),
            jax.ShapeDtypeStruct((total, HD), bf16),
            jax.ShapeDtypeStruct((heads, HD, rows), bf16),
            jax.ShapeDtypeStruct((2, rows), jnp.int32),
            jax.ShapeDtypeStruct((4,), jnp.int32),
        ),
        in_specs=[vmem()] * 4 + [anywhere()] * 6,
        out_specs=(anywhere(),) * 4 + (vmem(), vmem(), smem()),
        scratch_shapes=[
            pltpu.VMEM((ranks * (rows + TAIL), HD), bf16),
            pltpu.VMEM((total, HD), bf16),
            pltpu.VMEM((total, HD), f32),
            pltpu.VMEM((total, HD), f32),
            pltpu.VMEM((total, HD), bf16),
            pltpu.SemaphoreType.DMA((ranks,)),
            pltpu.SemaphoreType.DMA((4,)),
        ],
        compiler_params=pltpu.CompilerParams(vmem_limit_bytes=58 << 20),
        cost_estimate=cost(1 << 32, 0),
        name="prep",
    )(after(value)(inverse[None, :]), book, cotangent, cot_b, *packed)

    def log_totals(begin, count, place):
        return pl.pallas_call(
            functools.partial(
                stats_kernel, begin, count, rows, levels, levels / total, half, half, part
            ),
            out_shape=(
                jax.ShapeDtypeStruct((count, rows, HD), bf16),
                jax.ShapeDtypeStruct((count, HD, rows), bf16),
                jax.ShapeDtypeStruct((count, rows), f32),
                jax.ShapeDtypeStruct((levels, HD), f32),
            ),
            in_specs=[smem()] * 2 + [vmem()] * 2 + [anywhere()] * (8 + len(rest)),
            out_specs=(vmem(),) * 4,
            scratch_shapes=[pltpu.VMEM((count, rows), f32)] * 2
            + [pltpu.VMEM((rows, HD), f32)] * 2
            + [
                pltpu.VMEM((rows, HD), bf16),
                pltpu.VMEM((total, HD), bf16),
                pltpu.VMEM((rows, half * part), bf16),
                pltpu.VMEM((half, part, count * HD), bf16),
                pltpu.VMEM((half, part, HD), bf16),
                pltpu.VMEM((rows, count * HD), f32),
                pltpu.VMEM((rows, HD), f32),
                pltpu.SemaphoreType.DMA((len(rest),)),
                pltpu.SemaphoreType.DMA((2 * half,)),
                pltpu.SemaphoreType.DMA((9,)),
            ],
            compiler_params=pltpu.CompilerParams(vmem_limit_bytes=50 << 20),
            cost_estimate=cost(1 << 34, 0),
            name="stats",
        )(
            place, info, early, book, cos_k, sin_k, codes, keys,
            q_sum, kv_sum, w_query, w_key, *rest,
        )

    totals = []

    def second(pair):
        pair, ready = lax.optimization_barrier((pair, place))
        totals.extend(log_totals(0, heads // 2, ready))
        return pair

    values = everyone(value, after(keys), second, lambda v: after(totals[2])(v))
    q_rot_0, q_t_0, log_total_0, init = totals
    late, _ = lax.optimization_barrier((place, values[2:5]))
    q_rot_1, q_t_1, log_total_1, _ = log_totals(heads // 2, heads // 2, late)

    most = total // BLOCK
    out, out_b, local = pl.pallas_call(
        functools.partial(grad_kernel, heads, rows, levels),
        out_shape=(
            jax.ShapeDtypeStruct((side, width), bf16),
            jax.ShapeDtypeStruct((side, width), bf16),
            jax.ShapeDtypeStruct((levels, HD), f32),
        ),
        in_specs=[smem()] + [vmem()] * 11 + [anywhere()] * 10,
        out_specs=(vmem(),) * 3,
        scratch_shapes=[
            pltpu.VMEM((min(most, 7), heads // 2, BLOCK, rows), f32),
            pltpu.VMEM((heads, rows, HD), f32),
            pltpu.VMEM((heads // 2, rows), f32),
            pltpu.VMEM((levels, 8, HD), f32),
            pltpu.VMEM((total, HD), bf16),
            pltpu.VMEM((total, HD), bf16),
            pltpu.VMEM((total, HD), f32),
            pltpu.VMEM((total, HD), f32),
            pltpu.VMEM((total, HD), bf16),
            pltpu.SemaphoreType.DMA((36,)),
        ],
        compiler_params=pltpu.CompilerParams(vmem_limit_bytes=44 << 20),
        cost_estimate=cost(8 * rows * width * total, 8 << 20),
        name="grad",
    )(
        info, q_rot_0, q_t_0, log_total_0, q_rot_1, q_t_1, log_total_1, early, cotangent, cot_b, cot_t, init,
        keys, cos_k, sin_k, codes, *values,
    )
    back = cross(out_b, PARTNER)
    for d in (1, 2, 4, 8):
        local = local + cross(local, d)
    return (jnp.concatenate([out, back], axis=0), local.T)


def solution(mesh):
    placed = (
        P("tokens", "tensor"),
        P(None, "tensor"),
        P(None, "tensor"),
        P(None, "tensor"),
        P("tokens", "tensor"),
        P("tensor", None),
        P("tokens"),
        P("tokens", "tensor"),
    )
    return jax.shard_map(
        shards,
        mesh=mesh,
        in_specs=placed,
        out_specs=(P("tokens", "tensor"), P("tensor", None)),
        check_vma=False,
    )
```

time: 137 us -> 152 us (1.11); the launches traced: 135 us -> 154 us
  waiting for transfers between devices: 15.4 us -> 37.6 us
  Pallas kernels: 44.9 us -> 40.8 us
  starting transfers between devices: 63.7 us -> 62 us
    ppermute x7 -> x12, waiting for transfers between devices: 1.57 us -> 12.1 us  [the longest x3 4.97 us: shards(): send(mine[1], perm=perm)]
    ppermute x14 -> x17, waiting for transfers between devices: 10.9 us -> 18.5 us  [shards(): lax.ppermute(x, 'tokens', [(i, i ^ d) for i in range(ranks)])]
    ppermute x14 -> x17, starting transfers between devices: 46.4 us -> 39.3 us  [shards(): lax.ppermute(x, 'tokens', [(i, i ^ d) for i in range(ranks)])]
    pallas_call x1, Pallas kernels: 15.3 us -> 9.54 us  [shards(): pl.pallas_call(functools.partial(prep_kernel, rows, ranks, levels, heads)...]
    ppermute x7 -> x12, starting transfers between devices: 13.8 us -> 19 us  [the longest x3 7.29 us: shards(): send(mine[0], perm=perm)]
    ppermute x1, waiting for transfers between devices: 2.97 us -> 5.52 us  [shards(): other_far_b = send(far_b, perm=flip)]
    ppermute x1, waiting for transfers between devices: 0.01 us -> 1.57 us  [shards(): other_far_a = send(far_a, perm=flip)]
    unnamed x34 -> x42, local copies, waits for them, and re-layouts: 8.18 us -> 6.82 us
  transfers between devices with their start and end apart: 23 -> 31, of which waited for: 8 -> 12; matrix products, arithmetic and copies ran while one was open for 4% -> 3% of each run, Pallas kernels for 28% -> 21%
where the time goes in v4:
time: 152 us; the launch traced here: 154 us
  starting transfers between devices  62 us (41%)
  Pallas kernels  40.8 us (27%)
  waiting for transfers between devices  37.6 us (25%)
  local copies, waits for them, and re-layouts  10.4 us (7%)
  other arithmetic  2.02 us (1%)
    ppermute x17, starting transfers between devices, shards(): lax.ppermute(x, 'tokens', [(i, i ^ d) for i in range(ranks)])  39.3 us
    ppermute x17, waiting for transfers between devices, shards(): lax.ppermute(x, 'tokens', [(i, i ^ d) for i in range(ranks)])  18.5 us
    pallas_call x2, Pallas kernels, log_totals(): pl.pallas_call(functools.partial(stats_kernel, begin, count, rows, levels...  12.7 us
    pallas_call x1, Pallas kernels, shards(): pl.pallas_call(functools.partial(prep_kernel, rows, ranks, levels, heads)...  9.54 us
    pallas_call x1, Pallas kernels, shards(): pl.pallas_call(functools.partial(grad_kernel, heads, rows, levels), out_s...  8.07 us
    ppermute x3, starting transfers between devices, shards(): send(mine[0], perm=perm)  7.29 us
    unnamed x42, local copies, waits for them, and re-layouts  6.82 us
    pallas_call x1, Pallas kernels, shards(): pl.pallas_call(functools.partial(project_kernel, half, part), out_shape=(...  6.27 us
  transfers between devices with their start and end apart: 31, of which 12 were waited for; matrix products, arithmetic and copies ran while one was open for 3% of the time, Pallas kernels for 21%

profile of v4, /device:TPU:0, one launch (start us, length us, event | category | flops | bytes accessed | tf_op | source)
XLA Modules:
  0.0 153.9 jit_solution(2680891911434015284)
XLA Ops:
  3.8 2.2 %collective-permute-start.2 = (bf16[128,1024]{1,0:T(8,128)(2,1)S(1)}, bf16[128,1024]{1,0:T(8,128)(2,1)S(1)}, u32[]{:S(2)}, u32[]{:S(2)}) collective-permute-start(bf16[128,1024]{1,0:T(8,128)(2,1)S(1)} %get-tuple-element.38.refs_0_), channel_id=1, source_target_pairs={{0,96},{16,112},{32,0},{48,16},{64,32},{80,48},{96,64},{112,80},{1... | collective-permute-start | bytes 786440 | tf_op jit(solution)/shard_map/ppermute | solution.py:471
  6.0 3.0 %collective-permute-start.3 = (bf16[128,1024]{1,0:T(8,128)(2,1)S(1)}, bf16[128,1024]{1,0:T(8,128)(2,1)S(1)}, u32[]{:S(2)}, u32[]{:S(2)}) collective-permute-start(bf16[128,1024]{1,0:T(8,128)(2,1)S(1)} %get-tuple-element.38.refs_0_), channel_id=1, source_target_pairs={{0,16},{16,0},{32,48},{48,32},{64,80},{80,64},{96,112},{112,96},{1... | collective-permute-start | bytes 786440 | tf_op jit(solution)/shard_map/ppermute | solution.py:471
  12.5 3.3 %collective-permute-done.3.refs_6_ = bf16[128,1024]{1,0:T(8,128)(2,1)S(1)} collective-permute-done((bf16[128,1024]{1,0:T(8,128)(2,1)S(1)}, bf16[128,1024]{1,0:T(8,128)(2,1)S(1)}, u32[]{:S(2)}, u32[]{:S(2)}) %collective-permute-start.3) | collective-permute-done | bytes 262176 | tf_op jit(solution)/shard_map/ppermute | solution.py:471
  15.8 2.5 %collective-permute-start.7 = (bf16[272,128]{1,0:T(8,128)(2,1)}, bf16[272,128]{1,0:T(8,128)(2,1)S(1)}, u32[]{:S(2)}, u32[]{:S(2)}) collective-permute-start(bf16[272,128]{1,0:T(8,128)(2,1)} %pack.1.p_own), channel_id=1, source_target_pairs={{0,4},{1,5},{2,6},{3,7},{4,0},{5,1},{6,2},{7,3},{8,12},{9,13},{10,... | collective-permute-start | bytes 208904 | tf_op jit(solution)/shard_map/ppermute | solution.py:451
  18.3 2.9 %collective-permute-start.8 = (bf16[272,128]{1,0:T(8,128)(2,1)}, bf16[272,128]{1,0:T(8,128)(2,1)S(1)}, u32[]{:S(2)}, u32[]{:S(2)}) collective-permute-start(bf16[272,128]{1,0:T(8,128)(2,1)} %pack.1.p_own), channel_id=1, source_target_pairs={{0,8},{1,9},{2,10},{3,11},{4,12},{5,13},{6,14},{7,15},{8,0},{9,1},... | collective-permute-start | bytes 208904 | tf_op jit(solution)/shard_map/ppermute | solution.py:451
  22.3 2.8 %collective-permute-done.8.p_y2 = bf16[272,128]{1,0:T(8,128)(2,1)S(1)} collective-permute-done((bf16[272,128]{1,0:T(8,128)(2,1)}, bf16[272,128]{1,0:T(8,128)(2,1)S(1)}, u32[]{:S(2)}, u32[]{:S(2)}) %collective-permute-start.8) | collective-permute-done | bytes 69664 | tf_op jit(solution)/shard_map/ppermute | solution.py:451
  28.6 3.2 %collective-permute-start.5 = (bf16[128,1024]{1,0:T(8,128)(2,1)S(1)}, bf16[128,1024]{1,0:T(8,128)(2,1)}, u32[]{:S(2)}, u32[]{:S(2)}) collective-permute-start(bf16[128,1024]{1,0:T(8,128)(2,1)S(1)} %collective-permute-done.refs_1_), channel_id=1, source_target_pairs={{0,96},{16,112},{32,0},{48,16},{64,32},{80,48},{96,64},{112,80},{1... | collective-permute-start | bytes 786440 | tf_op jit(solution)/shard_map/ppermute | solution.py:472
  31.8 2.7 %collective-permute-start.6 = (bf16[128,1024]{1,0:T(8,128)(2,1)S(1)}, bf16[128,1024]{1,0:T(8,128)(2,1)}, u32[]{:S(2)}, u32[]{:S(2)}) collective-permute-start(bf16[128,1024]{1,0:T(8,128)(2,1)S(1)} %collective-permute-done.refs_1_), channel_id=1, source_target_pairs={{0,16},{16,0},{32,48},{48,32},{64,80},{80,64},{96,112},{112,96},{1... | collective-permute-start | bytes 786440 | tf_op jit(solution)/shard_map/ppermute | solution.py:472
  34.6 3.9 %collective-permute-done.4.refs_3_ = bf16[128,1024]{1,0:T(8,128)(2,1)S(1)} collective-permute-done((bf16[128,1024]{1,0:T(8,128)(2,1)S(1)}, bf16[128,1024]{1,0:T(8,128)(2,1)S(1)}, u32[]{:S(2)}, u32[]{:S(2)}) %collective-permute-start.4) | collective-permute-done | bytes 262176 | tf_op jit(solution)/shard_map/ppermute | solution.py:472
  46.6 3.8 %collective-permute-done.10.refs_1_ = bf16[128,1024]{1,0:T(8,128)(2,1)S(1)} collective-permute-done((bf16[128,1024]{1,0:T(8,128)(2,1)}, bf16[128,1024]{1,0:T(8,128)(2,1)S(1)}, u32[]{:S(2)}, u32[]{:S(2)}) %collective-permute-start.10) | collective-permute-done | bytes 262176 | tf_op jit(solution)/shard_map/ppermute | solution.py:500
  52.1 2.1 %collective-permute-start.16 = (bf16[128,1024]{1,0:T(8,128)(2,1)S(1)}, bf16[128,1024]{1,0:T(8,128)(2,1)S(1)}, u32[]{:S(2)}, u32[]{:S(2)}) collective-permute-start(bf16[128,1024]{1,0:T(8,128)(2,1)S(1)} %collective-permute-done.11.refs_0_), channel_id=1, source_target_pairs={{0,16},{16,0},{32,48},{48,32},{64,80},{80,64},{96,112},{112,96},{1... | collective-permute-start | bytes 786440 | tf_op jit(solution)/shard_map/ppermute | solution.py:503
  55.8 6.3 %project.1 = (f32[256,1024]{1,0:T(8,128)S(1)}, f32[256,256]{1,0:T(8,128)S(1)}) custom-call(s32[8]{0:T(128)S(1)} %stack.35.place, bf16[8192,1024]{1,0:T(8,128)(2,1)} %wq.5, bf16[8192,128]{1,0:T(8,128)(2,1)} %wk.5, bf16[8192,128]{1,0:T(8,128)(2,1)} %w.1, bf16[128,1024]{1,0:T(8,128)(2,1)S(1)} %get-tuple-element.38.refs_0_, ...), custom_call_target="tpu_custom_call" | custom-call | flops 17179869184 | tf_op jit(solution)/shard_map/project/pallas_call | solution.py:507
  64.7 5.5 %collective-permute-done.17.refs_7_ = bf16[128,1024]{1,0:T(8,128)(2,1)S(1)} collective-permute-done((bf16[128,1024]{1,0:T(8,128)(2,1)S(1)}, bf16[128,1024]{1,0:T(8,128)(2,1)S(1)}, u32[]{:S(2)}, u32[]{:S(2)}) %collective-permute-start.17) | collective-permute-done | bytes 262176 | tf_op jit(solution)/shard_map/ppermute | solution.py:504
  70.2 2.7 %value.1.v_own = bf16[256,128]{1,0:T(8,128)(2,1)S(1)} custom-call(s32[8]{0:T(128)S(1)} %stack.35.place, bf16[8192,128]{1,0:T(8,128)(2,1)} %w.1, f32[256,256]{1,0:T(8,128)S(1)} %get-tuple-element.49.before.kv_before, bf16[128,1024]{1,0:T(8,128)(2,1)S(1)} %collective-permute-done.11.refs_0_, bf16[128,1024]{1,0:T(8,128)(2,1)S(1)} %collective-permute-done.10.refs_1_, ...), custom_call_target="tpu_custom_call" | custom-call | tf_op jit(solution)/shard_map/value/pallas_call | solution.py:526
  74.1 9.5 %prep.1 = (bf16[4096,128]{1,0:T(8,128)(2,1)}, f32[4096,128]{1,0:T(8,128)}, f32[4096,128]{1,0:T(8,128)}, bf16[4096,128]{1,0:T(8,128)(2,1)}, bf16[8,128,256]{2,1,0...) custom-call(f32[1,128]{1,0:T(1,128)} %fusion.2.inverse, f32[16,128]{1,0:T(8,128)} %bitcast.12, bf16[256,1024]{1,0:T(8,128)(2,1)} %cot.3, ...), custom_call_target="tpu_custom_call" | custom-call | flops 4294967296 | tf_op jit(solution)/shard_map/prep/pallas_call | solution.py:542
  84.5 3.9 %collective-permute-start.24 = (bf16[512,128]{1,0:T(8,128)(2,1)S(1)}, bf16[512,128]{1,0:T(8,128)(2,1)S(1)}, u32[]{:S(2)}, u32[]{:S(2)}) collective-permute-start(bf16[512,128]{1,0:T(8,128)(2,1)S(1)} %pad_maximum_fusion.2), channel_id=1, source_target_pairs={{0,12},{1,13},{2,14},{3,15},{4,8},{5,9},{6,10},{7,11},{8,4},{9,5},... | collective-permute-start | bytes 393224 | tf_op jit(solution)/shard_map/ppermute | solution.py:451
  91.1 6.3 %stats.2 = (bf16[4,256,128]{2,1,0:T(8,128)(2,1)S(1)}, bf16[4,128,256]{2,1,0:T(8,128)(2,1)S(1)}, f32[4,256]{1,0:T(4,128)S(1)}, f32[16,128]{1,0:T(8,128)S(1)}) custom-call(s32[8]{0:T(128)S(1)} %stack.35.place, s32[4]{0:T(128)S(1)} %copy-done.13, s32[2,256]{1,0:T(2,128)S(1)} %copy-done.12, f32[16,128]{1,0:T(8,128)S(1)} %bitcast.13, ...), custom_call_target="tpu_custom_call" | custom-call | flops 17179869184 | tf_op jit(solution)/shard_map/stats/pallas_call | solution.py:570
  97.7 6.3 %stats.3 = (bf16[4,256,128]{2,1,0:T(8,128)(2,1)S(1)}, bf16[4,128,256]{2,1,0:T(8,128)(2,1)S(1)}, f32[4,256]{1,0:T(4,128)S(1)}, f32[16,128]{1,0:T(8,128)}) custom-call(s32[8]{0:T(128)S(1)} %stack.35.place, s32[4]{0:T(128)S(1)} %copy-done.13, s32[2,256]{1,0:T(2,128)S(1)} %copy-done.12, f32[16,128]{1,0:T(8,128)S(1)} %bitcast.14, ...), custom_call_target="tpu_custom_call" | custom-call | flops 17179869184 | tf_op jit(solution)/shard_map/stats/pallas_call | solution.py:570
  105.3 8.1 %grad.1 = (bf16[128,1024]{1,0:T(8,128)(2,1)S(1)}, bf16[128,1024]{1,0:T(8,128)(2,1)S(1)}, f32[16,128]{1,0:T(8,128)S(1)}) custom-call(s32[4]{0:T(128)S(1)} %copy-done.13, bf16[4,256,128]{2,1,0:T(8,128)(2,1)S(1)} %get-tuple-element.60.q_rot_0, bf16[4,128,256]{2,1,0:T(8,128)(2,1)S(1)} %get-tuple-element.61.q_t_0, f32[4,256]{1,0:T(4,128)S(1)} %get-tuple-element.62.log_total_0, ...), custom_call_target="tpu_custom_call" | custom-call | flops 8589934592 | bytes 8388608 | tf_op jit(solution)/shard_map/grad/pallas_call | solution.py:617
  115.1 3.1 %collective-permute-start.27 = (f32[16,128]{1,0:T(8,128)S(1)}, f32[16,128]{1,0:T(8,128)S(1)}, u32[]{:S(2)}, u32[]{:S(2)}) collective-permute-start(f32[16,128]{1,0:T(8,128)S(1)} %get-tuple-element.73), channel_id=1, source_target_pairs={{0,1},{1,0},{2,3},{3,2},{4,5},{5,4},{6,7},{7,6},{8,9},{9,8},{10,11... | collective-permute-start | bytes 24584 | tf_op jit(solution)/shard_map/ppermute | solution.py:451
  119.1 19.5 %collective-permute-start.28 = (f32[16,128]{1,0:T(8,128)S(1)}, f32[16,128]{1,0:T(8,128)S(1)}, u32[]{:S(2)}, u32[]{:S(2)}) collective-permute-start(f32[16,128]{1,0:T(8,128)S(1)} %add.75), channel_id=1, source_target_pairs={{0,2},{1,3},{2,0},{3,1},{4,6},{5,7},{6,4},{7,5},{8,10},{9,11},{10,... | collective-permute-start | bytes 24584 | tf_op jit(solution)/shard_map/ppermute | solution.py:451
  138.6 5.1 %collective-permute-done.28 = f32[16,128]{1,0:T(8,128)S(1)} collective-permute-done((f32[16,128]{1,0:T(8,128)S(1)}, f32[16,128]{1,0:T(8,128)S(1)}, u32[]{:S(2)}, u32[]{:S(2)}) %collective-permute-start.28) | collective-permute-done | bytes 8224 | tf_op jit(solution)/shard_map/ppermute | solution.py:451
  143.7 3.6 %collective-permute-done.29 = f32[16,128]{1,0:T(8,128)S(1)} collective-permute-done((f32[16,128]{1,0:T(8,128)S(1)}, f32[16,128]{1,0:T(8,128)S(1)}, u32[]{:S(2)}, u32[]{:S(2)}) %collective-permute-start.29) | collective-permute-done | bytes 8224 | tf_op jit(solution)/shard_map/ppermute | solution.py:451
  148.2 4.2 %collective-permute-done.30 = f32[16,128]{1,0:T(8,128)S(1)} collective-permute-done((f32[16,128]{1,0:T(8,128)S(1)}, f32[16,128]{1,0:T(8,128)S(1)}, u32[]{:S(2)}, u32[]{:S(2)}) %collective-permute-start.30) | collective-permute-done | bytes 8224 | tf_op jit(solution)/shard_map/ppermute | solution.py:451
  (99 shorter events, 36.1 us)
Async XLA Ops:
  1.8 10.8 %collective-permute-start.1 = (bf16[128,1024]{1,0:T(8,128)(2,1)S(1)}, bf16[128,1024]{1,0:T(8,128)(2,1)S(1)}, u32[]{:S(2)}, u32[]{:S(2)}) collective-permute-start(bf16[128,1024]{1,0:T(8,128)(2,1)S(1)} %get-tuple-element.38.refs_0_), channel_id=1, source_target_pairs={{0,32},{16,48},{32,64},{48,80},{64,96},{80,112},{96,0},{112,16},{1... | collective-permute-start | bytes 786440 | tf_op jit(solution)/shard_map/ppermute | solution.py:471
  3.8 8.7 %collective-permute-start.2 = (bf16[128,1024]{1,0:T(8,128)(2,1)S(1)}, bf16[128,1024]{1,0:T(8,128)(2,1)S(1)}, u32[]{:S(2)}, u32[]{:S(2)}) collective-permute-start(bf16[128,1024]{1,0:T(8,128)(2,1)S(1)} %get-tuple-element.38.refs_0_), channel_id=1, source_target_pairs={{0,96},{16,112},{32,0},{48,16},{64,32},{80,48},{96,64},{112,80},{1... | collective-permute-start | bytes 786440 | tf_op jit(solution)/shard_map/ppermute | solution.py:471
  6.0 9.8 %collective-permute-start.3 = (bf16[128,1024]{1,0:T(8,128)(2,1)S(1)}, bf16[128,1024]{1,0:T(8,128)(2,1)S(1)}, u32[]{:S(2)}, u32[]{:S(2)}) collective-permute-start(bf16[128,1024]{1,0:T(8,128)(2,1)S(1)} %get-tuple-element.38.refs_0_), channel_id=1, source_target_pairs={{0,16},{16,0},{32,48},{48,32},{64,80},{80,64},{96,112},{112,96},{1... | collective-permute-start | bytes 786440 | tf_op jit(solution)/shard_map/ppermute | solution.py:471
  9.1 19.5 %collective-permute-start = (bf16[128,1024]{1,0:T(8,128)(2,1)S(1)}, bf16[128,1024]{1,0:T(8,128)(2,1)S(1)}, u32[]{:S(2)}, u32[]{:S(2)}) collective-permute-start(bf16[128,1024]{1,0:T(8,128)(2,1)S(1)} %get-tuple-element.39), channel_id=1, source_target_pairs={{0,15},{1,14},{2,13},{3,12},{4,11},{5,10},{6,9},{7,8},{8,7},{9,6},... | collective-permute-start | bytes 786440 | tf_op jit(solution)/shard_map/ppermute | solution.py:451
  27.0 16.0 %collective-permute-start.19 = (bf16[1088,128]{1,0:T(8,128)(2,1)S(1)}, bf16[1088,128]{1,0:T(8,128)(2,1)}, u32[]{:S(2)}, u32[]{:S(2)}) collective-permute-start(bf16[1088,128]{1,0:T(8,128)(2,1)S(1)} %get-tuple-element.77), channel_id=1, source_target_pairs={{0,2},{1,3},{2,0},{3,1},{4,6},{5,7},{6,4},{7,5},{8,10},{9,11},{10,... | collective-permute-start | bytes 835592 | tf_op jit(solution)/shard_map/ppermute | solution.py:451
  28.6 9.8 %collective-permute-start.4 = (bf16[128,1024]{1,0:T(8,128)(2,1)S(1)}, bf16[128,1024]{1,0:T(8,128)(2,1)S(1)}, u32[]{:S(2)}, u32[]{:S(2)}) collective-permute-start(bf16[128,1024]{1,0:T(8,128)(2,1)S(1)} %collective-permute-done.refs_1_), channel_id=1, source_target_pairs={{0,32},{16,48},{32,64},{48,80},{64,96},{80,112},{96,0},{112,16},{1... | collective-permute-start | bytes 786440 | tf_op jit(solution)/shard_map/ppermute | solution.py:472
  28.6 11.2 %collective-permute-start.5 = (bf16[128,1024]{1,0:T(8,128)(2,1)S(1)}, bf16[128,1024]{1,0:T(8,128)(2,1)}, u32[]{:S(2)}, u32[]{:S(2)}) collective-permute-start(bf16[128,1024]{1,0:T(8,128)(2,1)S(1)} %collective-permute-done.refs_1_), channel_id=1, source_target_pairs={{0,96},{16,112},{32,0},{48,16},{64,32},{80,48},{96,64},{112,80},{1... | collective-permute-start | bytes 786440 | tf_op jit(solution)/shard_map/ppermute | solution.py:472
  31.8 9.7 %collective-permute-start.6 = (bf16[128,1024]{1,0:T(8,128)(2,1)S(1)}, bf16[128,1024]{1,0:T(8,128)(2,1)}, u32[]{:S(2)}, u32[]{:S(2)}) collective-permute-start(bf16[128,1024]{1,0:T(8,128)(2,1)S(1)} %collective-permute-done.refs_1_), channel_id=1, source_target_pairs={{0,16},{16,0},{32,48},{48,32},{64,80},{80,64},{96,112},{112,96},{1... | collective-permute-start | bytes 786440 | tf_op jit(solution)/shard_map/ppermute | solution.py:472
  34.6 17.5 %collective-permute-start.12 = (bf16[128,1024]{1,0:T(8,128)(2,1)S(1)}, bf16[128,1024]{1,0:T(8,128)(2,1)S(1)}, u32[]{:S(2)}, u32[]{:S(2)}) collective-permute-start(bf16[128,1024]{1,0:T(8,128)(2,1)S(1)} %collective-permute-done.3.refs_6_), channel_id=1, source_target_pairs={{0,32},{16,48},{32,64},{48,80},{64,96},{80,112},{96,0},{112,16},{1... | collective-permute-start | bytes 786440 | tf_op jit(solution)/shard_map/ppermute | solution.py:497
  38.4 15.8 %collective-permute-start.14 = (bf16[128,1024]{1,0:T(8,128)(2,1)S(1)}, bf16[128,1024]{1,0:T(8,128)(2,1)S(1)}, u32[]{:S(2)}, u32[]{:S(2)}) collective-permute-start(bf16[128,1024]{1,0:T(8,128)(2,1)S(1)} %collective-permute-done.3.refs_6_), channel_id=1, source_target_pairs={{0,96},{16,112},{32,0},{48,16},{64,32},{80,48},{96,64},{112,80},{1... | collective-permute-start | bytes 786440 | tf_op jit(solution)/shard_map/ppermute | solution.py:498
  39.8 10.6 %collective-permute-start.11 = (bf16[128,1024]{1,0:T(8,128)(2,1)S(1)}, bf16[128,1024]{1,0:T(8,128)(2,1)S(1)}, u32[]{:S(2)}, u32[]{:S(2)}) collective-permute-start(bf16[128,1024]{1,0:T(8,128)(2,1)S(1)} %collective-permute-done.1.refs_2_), channel_id=1, source_target_pairs={{0,32},{16,48},{32,64},{48,80},{64,96},{80,112},{96,0},{112,16},{1... | collective-permute-start | bytes 786440 | tf_op jit(solution)/shard_map/ppermute | solution.py:496
  41.6 8.9 %collective-permute-start.10 = (bf16[128,1024]{1,0:T(8,128)(2,1)}, bf16[128,1024]{1,0:T(8,128)(2,1)S(1)}, u32[]{:S(2)}, u32[]{:S(2)}) collective-permute-start(bf16[128,1024]{1,0:T(8,128)(2,1)} %collective-permute-done.5.refs_5_), channel_id=1, source_target_pairs={{0,96},{16,112},{32,0},{48,16},{64,32},{80,48},{96,64},{112,80},{1... | collective-permute-start | bytes 786440 | tf_op jit(solution)/shard_map/ppermute | solution.py:500
  43.1 11.2 %collective-permute-start.13 = (bf16[128,1024]{1,0:T(8,128)(2,1)}, bf16[128,1024]{1,0:T(8,128)(2,1)S(1)}, u32[]{:S(2)}, u32[]{:S(2)}) collective-permute-start(bf16[128,1024]{1,0:T(8,128)(2,1)} %collective-permute-done.6.refs_7_), channel_id=1, source_target_pairs={{0,32},{16,48},{32,64},{48,80},{64,96},{80,112},{96,0},{112,16},{1... | collective-permute-start | bytes 786440 | tf_op jit(solution)/shard_map/ppermute | solution.py:501
  50.4 22.7 %collective-permute-start.18 = (bf16[128,1024]{1,0:T(8,128)(2,1)}, bf16[128,1024]{1,0:T(8,128)(2,1)S(1)}, u32[]{:S(2)}, u32[]{:S(2)}) collective-permute-start(bf16[128,1024]{1,0:T(8,128)(2,1)} %slice.11), channel_id=1, source_target_pairs={{0,15},{1,14},{2,13},{3,12},{4,11},{5,10},{6,9},{7,8},{8,7},{9,6},... | collective-permute-start | bytes 786440 | tf_op jit(solution)/shard_map/ppermute | solution.py:451
  50.4 12.7 %collective-permute-start.15 = (bf16[128,1024]{1,0:T(8,128)(2,1)}, bf16[128,1024]{1,0:T(8,128)(2,1)S(1)}, u32[]{:S(2)}, u32[]{:S(2)}) collective-permute-start(bf16[128,1024]{1,0:T(8,128)(2,1)} %collective-permute-done.6.refs_7_), channel_id=1, source_target_pairs={{0,96},{16,112},{32,0},{48,16},{64,32},{80,48},{96,64},{112,80},{1... | collective-permute-start | bytes 786440 | tf_op jit(solution)/shard_map/ppermute | solution.py:502
  52.1 12.6 %collective-permute-start.16 = (bf16[128,1024]{1,0:T(8,128)(2,1)S(1)}, bf16[128,1024]{1,0:T(8,128)(2,1)S(1)}, u32[]{:S(2)}, u32[]{:S(2)}) collective-permute-start(bf16[128,1024]{1,0:T(8,128)(2,1)S(1)} %collective-permute-done.11.refs_0_), channel_id=1, source_target_pairs={{0,16},{16,0},{32,48},{48,32},{64,80},{80,64},{96,112},{112,96},{1... | collective-permute-start | bytes 786440 | tf_op jit(solution)/shard_map/ppermute | solution.py:503
  54.2 18.9 %collective-permute-start.20 = (bf16[2176,128]{1,0:T(8,128)(2,1)}, bf16[2176,128]{1,0:T(8,128)(2,1)S(1)}, u32[]{:S(2)}, u32[]{:S(2)}) collective-permute-start(bf16[2176,128]{1,0:T(8,128)(2,1)} %constant_dynamic-update-slice_fusion.4), channel_id=1, source_target_pairs={{0,1},{1,0},{2,3},{3,2},{4,5},{5,4},{6,7},{7,6},{8,9},{9,8},{10,11... | collective-permute-start | bytes 1671176 | tf_op jit(solution)/shard_map/ppermute | solution.py:451
  54.3 15.9 %collective-permute-start.17 = (bf16[128,1024]{1,0:T(8,128)(2,1)S(1)}, bf16[128,1024]{1,0:T(8,128)(2,1)S(1)}, u32[]{:S(2)}, u32[]{:S(2)}) collective-permute-start(bf16[128,1024]{1,0:T(8,128)(2,1)S(1)} %collective-permute-done.10.refs_1_), channel_id=1, source_target_pairs={{0,16},{16,0},{32,48},{48,32},{64,80},{80,64},{96,112},{112,96},{1... | collective-permute-start | bytes 786440 | tf_op jit(solution)/shard_map/ppermute | solution.py:504
  72.9 10.8 %collective-permute-start.21 = (bf16[256,128]{1,0:T(8,128)(2,1)S(1)}, bf16[256,128]{1,0:T(8,128)(2,1)S(1)}, u32[]{:S(2)}, u32[]{:S(2)}) collective-permute-start(bf16[256,128]{1,0:T(8,128)(2,1)S(1)} %value.1.v_own), channel_id=1, source_target_pairs={{0,2},{1,3},{2,0},{3,1},{4,6},{5,7},{6,4},{7,5},{8,10},{9,11},{10,... | collective-permute-start | bytes 196616 | tf_op jit(solution)/shard_map/ppermute | solution.py:451
  83.7 13.7 %collective-permute-start.22 = (bf16[512,128]{1,0:T(8,128)(2,1)S(1)}, bf16[512,128]{1,0:T(8,128)(2,1)S(1)}, u32[]{:S(2)}, u32[]{:S(2)}) collective-permute-start(bf16[512,128]{1,0:T(8,128)(2,1)S(1)} %pad_maximum_fusion.2), channel_id=1, source_target_pairs={{0,4},{1,5},{2,6},{3,7},{4,0},{5,1},{6,2},{7,3},{8,12},{9,13},{10,... | collective-permute-start | bytes 393224 | tf_op jit(solution)/shard_map/ppermute | solution.py:451
  83.8 13.6 %collective-permute-start.23 = (bf16[512,128]{1,0:T(8,128)(2,1)S(1)}, bf16[512,128]{1,0:T(8,128)(2,1)S(1)}, u32[]{:S(2)}, u32[]{:S(2)}) collective-permute-start(bf16[512,128]{1,0:T(8,128)(2,1)S(1)} %pad_maximum_fusion.2), channel_id=1, source_target_pairs={{0,8},{1,9},{2,10},{3,11},{4,12},{5,13},{6,14},{7,15},{8,0},{9,1},... | collective-permute-start | bytes 393224 | tf_op jit(solution)/shard_map/ppermute | solution.py:451
  84.5 12.9 %collective-permute-start.24 = (bf16[512,128]{1,0:T(8,128)(2,1)S(1)}, bf16[512,128]{1,0:T(8,128)(2,1)S(1)}, u32[]{:S(2)}, u32[]{:S(2)}) collective-permute-start(bf16[512,128]{1,0:T(8,128)(2,1)S(1)} %pad_maximum_fusion.2), channel_id=1, source_target_pairs={{0,12},{1,13},{2,14},{3,15},{4,8},{5,9},{6,10},{7,11},{8,4},{9,5},... | collective-permute-start | bytes 393224 | tf_op jit(solution)/shard_map/ppermute | solution.py:451
  113.4 39.7 %collective-permute-start.26 = (bf16[128,1024]{1,0:T(8,128)(2,1)S(1)}, bf16[128,1024]{1,0:T(8,128)(2,1)S(1)}, u32[]{:S(2)}, u32[]{:S(2)}) collective-permute-start(bf16[128,1024]{1,0:T(8,128)(2,1)S(1)} %get-tuple-element.72), channel_id=1, source_target_pairs={{0,15},{1,14},{2,13},{3,12},{4,11},{5,10},{6,9},{7,8},{8,7},{9,6},... | collective-permute-start | bytes 786440 | tf_op jit(solution)/shard_map/ppermute | solution.py:451
  119.1 24.6 %collective-permute-start.28 = (f32[16,128]{1,0:T(8,128)S(1)}, f32[16,128]{1,0:T(8,128)S(1)}, u32[]{:S(2)}, u32[]{:S(2)}) collective-permute-start(f32[16,128]{1,0:T(8,128)S(1)} %add.75), channel_id=1, source_target_pairs={{0,2},{1,3},{2,0},{3,1},{4,6},{5,7},{6,4},{7,5},{8,10},{9,11},{10,... | collective-permute-start | bytes 24584 | tf_op jit(solution)/shard_map/ppermute | solution.py:451
  (26 other events, 242.0 us)

commit v5 on v3

--- a/solution.py
+++ b/solution.py
@@ -37,13 +37,6 @@
     return sine, cosine
 
 
-def slots_y_first(pieces):
-    own, y1, y2, y3, x, core = pieces
-    found = [(0, own, 0), (4, y1, 0), (8, y2, 0), (12, y3, 0)]
-    found += [(2 | 4 * j, x, j) for j in range(4)]
-    return found + [(1 | (4 * j if j < 4 else 2 | 4 * (j - 4)), core, j) for j in range(8)]
-
-
 def slots(pieces):
     own, x, y1, y2, y3, core = pieces
     found = [(0, own, 0), (2, x, 0)]
@@ -73,15 +66,26 @@
 
 
 def prep_kernel(
-    rows, ranks, levels, heads,
-    inverse, book, cot, p_own, p_y1, p_y2, p_y3, p_x, p_core,
-    keys_f, cos_f, sin_f, codes_f, cot_t, packed_s, keys, cos_k, sin_k, codes, sems, out_sems,
+    near, rows, ranks, levels,
+    inverse, book, *refs,
 ):
+    pieces = refs[:5] if near else refs[:1]
+    if near:
+        cot, cot_t = refs[5], refs[10]
+        for h in range(cot_t.shape[0]):
+            cot_t[h] = cot[:, h * HD : (h + 1) * HD].T
+        refs = refs[:10] + refs[11:]
+    keys_f, cos_f, sin_f, codes_f, packed_s, keys, cos_k, sin_k, codes, sems, out_sems = refs[-11:]
     me = token_rank()
     tall = rows + TAIL
+    if near:
+        found = [(2 * j, ref, 0) for j, ref in enumerate(pieces[:4])]
+        found += [(2 * j + 1, pieces[4], j) for j in range(4)]
+    else:
+        found = [(2 * j if j < 4 else 2 * (j - 4) + 1, pieces[0], j) for j in range(8)]
     copies = []
-    for j, (bits, ref, at) in enumerate(slots_y_first((p_own, p_y1, p_y2, p_y3, p_x, p_core))):
-        start = pl.multiple_of((me ^ bits) * tall, TAIL)
+    for j, (bits, ref, at) in enumerate(found):
+        start = pl.multiple_of(((me // 2) ^ bits) * tall, TAIL)
         copies.append(
             pltpu.make_async_copy(
                 ref.at[at * tall : (at + 1) * tall, :], packed_s.at[pl.ds(start, tall), :], sems.at[j]
@@ -89,8 +93,6 @@
         )
     for copy in copies:
         copy.start()
-    for h in range(heads):
-        cot_t[h] = cot[:, h * HD : (h + 1) * HD].T
     for copy in copies:
         copy.wait()
     eye = lax.broadcasted_iota(jnp.int32, (HD, HD), 0) == lax.broadcasted_iota(
@@ -120,11 +122,11 @@
             )
             for side, (cosine, sine) in enumerate(tables):
                 at = part + side
-                target = pl.multiple_of(i * rows + at * HD, HD)
-                cos_k[pl.ds(target, HD), :] = cosine
-                sin_k[pl.ds(target, HD), :] = sine
+                target = pl.ds(at * HD, HD)
+                cos_k[i, target, :] = cosine
+                sin_k[i, target, :] = sine
                 raw = packed_s[pl.ds(source + at * HD, HD), :]
-                codes[pl.ds(target, HD), :] = raw
+                codes[i, target, :] = raw
                 code = raw.astype(jnp.float32).astype(jnp.int32)
                 layer = [book[e : e + 1, :] for e in range(levels)]
                 bit = 1
@@ -134,10 +136,9 @@
                     bit *= 2
                 deq = layer[0]
                 turned = deq * cosine + pltpu.roll(deq, HD // 2, 1) * sine
-                keys[pl.ds(target, HD), :] = turned.astype(jnp.bfloat16)
-        block = pl.ds(pl.multiple_of(i * rows, rows), rows)
+                keys[i, target, :] = turned.astype(jnp.bfloat16)
         for j, (ref, full) in enumerate(outs):
-            pltpu.make_async_copy(ref.at[block, :], full.at[block, :], out_sems.at[j]).start()
+            pltpu.make_async_copy(ref.at[i], full.at[i], out_sems.at[j]).start()
 
     for j, (ref, full) in enumerate(outs):
         pltpu.make_async_copy(ref, full, out_sems.at[j]).wait()
@@ -145,6 +146,14 @@
 
 def shard_rows(place, n, part):
     return pl.ds(pl.multiple_of(place[n] * part, part), part)
+
+
+def interleave(near, distant, ref, sem):
+    core = token_rank() % 2
+    return [
+        pltpu.make_async_copy(half, ref.at[:, core ^ j], sem(j))
+        for j, half in enumerate((near, distant))
+    ]
 
 
 def fetch(pieces, x_s, sem):
@@ -224,7 +233,7 @@
 
 def stats_kernel(
     begin, heads, rows, levels, weight, first, count, part,
-    place, info, early, codes, book, cos_k, sin_k, keys_k, q_before, kv_before, wq, wk, *refs,
+    place, info, early, codes, book, cos_k, sin_k, keys_n, keys_d, q_before, kv_before, wq, wk, *refs,
 ):
     pieces = refs[:-17]
     (
@@ -232,7 +241,7 @@
         peak_s, mass_s, cos_q, sin_q, keys, x_s, wq_s, wk_s, q_s, true_s, x_sems, w_sems, sems,
     ) = refs[-17:]
     own = token_rank() * rows
-    mine = pl.ds(pl.multiple_of(own, rows), rows)
+    mine = token_rank() // 2
     columns = pl.ds(begin * HD, heads * HD)
     loads = fetch(pieces, x_s, lambda j: x_sems.at[j])
     weights = []
@@ -246,10 +255,9 @@
     if begin == 0:
         before.append(pltpu.make_async_copy(kv_before.at[:, :HD], true_s, sems.at[1]))
     tables = [
-        pltpu.make_async_copy(cos_k.at[mine, :], cos_q, sems.at[2]),
-        pltpu.make_async_copy(sin_k.at[mine, :], sin_q, sems.at[3]),
-        pltpu.make_async_copy(keys_k, keys, sems.at[4]),
-    ]
+        pltpu.make_async_copy(cos_k.at[mine], cos_q, sems.at[2]),
+        pltpu.make_async_copy(sin_k.at[mine], sin_q, sems.at[3]),
+    ] + interleave(keys_n, keys_d, keys, lambda j: sems.at[4 + j])
     for copy in before + loads + sum(weights, []) + tables:
         copy.start()
     peak_s[...] = jnp.full_like(peak_s, NEG_BIG)
@@ -282,7 +290,7 @@
 
     def body(b, masked):
         base = pl.multiple_of(b * BLOCK, BLOCK)
-        k = keys[pl.ds(base, BLOCK), :]
+        k = keys[b].reshape(BLOCK, HD)
         if masked:
             seen = visible_block(base, BLOCK, own, early[...], rows)
         for h in range(heads):
@@ -303,7 +311,7 @@
 def grad_kernel(
     heads, rows, levels,
     info, q_rot_0, q_t_0, log_total_0, q_rot_1, q_t_1, log_total_1, early, cot, cot_t, init,
-    keys_k, cos_f, sin_f, codes_f, v_own, v_x, v_y1, v_y2, v_y3, v_core,
+    keys_n, keys_d, cos_n, cos_d, sin_n, sin_d, codes_n, codes_d, v_own, v_x, v_y1, v_y2, v_y3, v_core,
     out, bins, probs_s, out_s, delta_s, acc_s, values, keys, cos_k, sin_k, codes, sems,
 ):
     me = token_rank()
@@ -312,19 +320,17 @@
     q_rot = [q_rot_0.at[h] for h in range(part)] + [q_rot_1.at[h] for h in range(part)]
     q_t = [q_t_0.at[h] for h in range(part)] + [q_t_1.at[h] for h in range(part)]
     log_total = [ref.at[h : h + 1, :] for ref in (log_total_0, log_total_1) for h in range(part)]
-    copies = [pltpu.make_async_copy(keys_k, keys, sems.at[0])]
+    copies = interleave(keys_n, keys_d, keys, lambda j: sems.at[16 + j])
     for j, (bits, ref, at) in enumerate(slots((v_own, v_x, v_y1, v_y2, v_y3, v_core))):
         start = pl.multiple_of((me ^ bits) * rows, rows)
         copies.append(
             pltpu.make_async_copy(
-                ref.at[at * rows : (at + 1) * rows, :], values.at[pl.ds(start, rows), :], sems.at[1 + j]
+                ref.at[at * rows : (at + 1) * rows, :], values.at[pl.ds(start, rows), :], sems.at[j]
             )
         )
-    late = [
-        pltpu.make_async_copy(cos_f, cos_k, sems.at[17]),
-        pltpu.make_async_copy(sin_f, sin_k, sems.at[18]),
-        pltpu.make_async_copy(codes_f, codes, sems.at[19]),
-    ]
+    late = interleave(cos_n, cos_d, cos_k, lambda j: sems.at[18 + j])
+    late += interleave(sin_n, sin_d, sin_k, lambda j: sems.at[20 + j])
+    late += interleave(codes_n, codes_d, codes, lambda j: sems.at[22 + j])
     for copy in copies + late:
         copy.start()
     out_s[...] = jnp.zeros_like(out_s)
@@ -333,7 +339,7 @@
 
     def forward(b, masked):
         base = pl.multiple_of(b * BLOCK, BLOCK)
-        k = keys[pl.ds(base, BLOCK), :]
+        k = keys[b].reshape(BLOCK, HD)
         v = values[pl.ds(base, BLOCK), :]
         if masked:
             seen = visible_block(base, BLOCK, own, early[...], rows)
@@ -368,8 +374,9 @@
             ds = (probs_s[b - first, h] * (dp - delta_s[h : h + 1, :])).astype(jnp.bfloat16)
             dk = dk + lax.dot_general(ds, q_rot[h][...], NN, preferred_element_type=jnp.float32)
         dk = dk * SCALE
-        g = dk * cos_k[pl.ds(base, BLOCK), :] - pltpu.roll(dk, HD // 2, 1) * sin_k[pl.ds(base, BLOCK), :]
-        code = codes[pl.ds(base, BLOCK), :].astype(jnp.float32)
+        cosine, sine = cos_k[b].reshape(BLOCK, HD), sin_k[b].reshape(BLOCK, HD)
+        g = dk * cosine - pltpu.roll(dk, HD // 2, 1) * sine
+        code = codes[b].reshape(BLOCK, HD).astype(jnp.float32)
         for level in range(levels):
             chosen = jnp.where(code == level, g, 0.0)
             acc_s[level] += jnp.sum(chosen.reshape(BLOCK // 8, 8, HD), axis=0)
@@ -495,30 +502,27 @@
         name="value",
     )(place, w_value, kv_sum, *rest)
 
-    keys, cos_k, sin_k, codes, cot_t = pl.pallas_call(
-        functools.partial(prep_kernel, rows, ranks, levels, heads),
-        out_shape=(
-            jax.ShapeDtypeStruct((total, HD), bf16),
-            jax.ShapeDtypeStruct((total, HD), f32),
-            jax.ShapeDtypeStruct((total, HD), f32),
-            jax.ShapeDtypeStruct((total, HD), bf16),
-            jax.ShapeDtypeStruct((heads, HD, rows), bf16),
-        ),
-        in_specs=[vmem()] * 3 + [anywhere()] * 6,
-        out_specs=(anywhere(),) * 4 + (vmem(),),
-        scratch_shapes=[
-            pltpu.VMEM((ranks * (rows + TAIL), HD), bf16),
-            pltpu.VMEM((total, HD), bf16),
-            pltpu.VMEM((total, HD), f32),
-            pltpu.VMEM((total, HD), f32),
-            pltpu.VMEM((total, HD), bf16),
-            pltpu.SemaphoreType.DMA((ranks,)),
-            pltpu.SemaphoreType.DMA((4,)),
-        ],
-        compiler_params=pltpu.CompilerParams(vmem_limit_bytes=14 << 20),
-        cost_estimate=cost(1 << 32, 0),
-        name="prep",
-    )(after(value)(inverse[None, :]), book, cotangent, *packed)
+    def prep(near, inverse, *pieces):
+        few = ranks // 2
+        shapes = [(few, rows, HD)] * 4
+        kinds = [bf16, f32, f32, bf16]
+        return pl.pallas_call(
+            functools.partial(prep_kernel, near, rows, few, levels),
+            out_shape=[jax.ShapeDtypeStruct(size, kind) for size, kind in zip(shapes, kinds)]
+            + [jax.ShapeDtypeStruct((heads, HD, rows), bf16)] * near,
+            in_specs=[vmem()] * 2 + [anywhere()] * (5 if near else 1) + [vmem()] * near,
+            out_specs=[anywhere()] * 4 + [vmem()] * near,
+            scratch_shapes=[pltpu.VMEM((few * (rows + TAIL), HD), bf16)]
+            + [pltpu.VMEM(size, kind) for size, kind in zip(shapes, kinds)]
+            + [pltpu.SemaphoreType.DMA((few,)), pltpu.SemaphoreType.DMA((4,))],
+            compiler_params=pltpu.CompilerParams(vmem_limit_bytes=58 << 20),
+            cost_estimate=cost(1 << 32, 0),
+            name="prep",
+        )(inverse, book, *pieces)
+
+    *near, cot_t = prep(True, after(kv_sum)(inverse[None, :]), *packed[:5], cotangent)
+    distant = prep(False, after(value)(inverse[None, :]), packed[5])
+    keys = distant[0]
 
     def log_totals(begin, count, place):
         return pl.pallas_call(
@@ -531,12 +535,12 @@
                 jax.ShapeDtypeStruct((count, rows), f32),
                 jax.ShapeDtypeStruct((levels, HD), f32),
             ),
-            in_specs=[smem()] * 2 + [vmem()] * 3 + [anywhere()] * (7 + len(rest)),
+            in_specs=[smem()] * 2 + [vmem()] * 3 + [anywhere()] * (8 + len(rest)),
             out_specs=(vmem(),) * 4,
             scratch_shapes=[pltpu.VMEM((count, rows), f32)] * 2
             + [pltpu.VMEM((rows, HD), f32)] * 2
             + [
-                pltpu.VMEM((total, HD), bf16),
+                pltpu.VMEM((ranks // 2, 2, rows, HD), bf16),
                 pltpu.VMEM((rows, half * part), bf16),
                 pltpu.VMEM((half, part, count * HD), bf16),
                 pltpu.VMEM((half, part, HD), bf16),
@@ -544,13 +548,13 @@
                 pltpu.VMEM((rows, HD), f32),
                 pltpu.SemaphoreType.DMA((len(rest),)),
                 pltpu.SemaphoreType.DMA((2 * half,)),
-                pltpu.SemaphoreType.DMA((5,)),
+                pltpu.SemaphoreType.DMA((6,)),
             ],
             compiler_params=pltpu.CompilerParams(vmem_limit_bytes=50 << 20),
             cost_estimate=cost(1 << 34, 0),
             name="stats",
         )(
-            place, info, early, key_codes, book, cos_k, sin_k, keys,
+            place, info, early, key_codes, book, near[1], near[2], near[0], distant[0],
             q_sum, kv_sum, w_query, w_key, *rest,
         )
 
@@ -573,7 +577,7 @@
             jax.ShapeDtypeStruct((rows, width), bf16),
             jax.ShapeDtypeStruct((levels, HD), f32),
         ),
-        in_specs=[smem()] + [vmem()] * 10 + [anywhere()] * 10,
+        in_specs=[smem()] + [vmem()] * 10 + [anywhere()] * 14,
         out_specs=(vmem(),) * 2,
         scratch_shapes=[
             pltpu.VMEM((min(most, 7), heads, BLOCK, rows), f32),
@@ -581,20 +585,20 @@
             pltpu.VMEM((heads, rows), f32),
             pltpu.VMEM((levels, 8, HD), f32),
             pltpu.VMEM((total, HD), bf16),
-            pltpu.VMEM((total, HD), bf16),
-            pltpu.VMEM((total, HD), f32),
-            pltpu.VMEM((total, HD), f32),
-            pltpu.VMEM((total, HD), bf16),
-            pltpu.SemaphoreType.DMA((20,)),
+            pltpu.VMEM((ranks // 2, 2, rows, HD), bf16),
+            pltpu.VMEM((ranks // 2, 2, rows, HD), f32),
+            pltpu.VMEM((ranks // 2, 2, rows, HD), f32),
+            pltpu.VMEM((ranks // 2, 2, rows, HD), bf16),
+            pltpu.SemaphoreType.DMA((24,)),
         ],
         compiler_params=pltpu.CompilerParams(vmem_limit_bytes=44 << 20),
         cost_estimate=cost(8 * rows * width * total, 8 << 20),
         name="grad",
     )(
         info, q_rot_0, q_t_0, log_total_0, q_rot_1, q_t_1, log_total_1, early, cotangent, cot_t, init,
-        keys, cos_k, sin_k, codes, *values,
+        *[table for both in zip(near, distant) for table in both], *values,
     )
-    for d in (1, 2, 4, 8):
+    for d in (1, 2, 4, 12):
         local = local + cross(local, d)
     return (attention_out, local.T)
 

time: 137 us -> 132 us (0.964)
  Pallas kernels: 44.9 us -> 41.6 us
  local copies, waits for them, and re-layouts: 9.76 us -> 6.5 us
    pallas_call x1 -> x2, Pallas kernels: 15.3 us -> 11.7 us  [prep(): pl.pallas_call(functools.partial(prep_kernel, near, rows, few, levels), o...]
    unnamed x34 -> x48, local copies, waits for them, and re-layouts: 8.18 us -> 5.61 us
    ppermute x1, waiting for transfers between devices: 2.97 us -> 4.55 us  [shards(): other_far_b = send(far_b, perm=flip)]
    ppermute x1, waiting for transfers between devices: 1.55 us -> 0.01 us  [shards(): other_low = send(other, perm=up)]
  transfers between devices with their start and end apart: 23 -> 23, of which waited for: 8 -> 8; matrix products, arithmetic and copies ran while one was open for 4% -> 4% of each run, Pallas kernels for 28% -> 26%
where the time goes in v5:
time: 132 us
  starting transfers between devices  65 us (49%)
  Pallas kernels  41.6 us (32%)
  waiting for transfers between devices  16.2 us (12%)
  local copies, waits for them, and re-layouts  6.5 us (5%)
    ppermute x14, starting transfers between devices, shards(): lax.ppermute(x, 'tokens', [(i, i ^ d) for i in range(ranks)])  47.6 us
    pallas_call x2, Pallas kernels, log_totals(): pl.pallas_call(functools.partial(stats_kernel, begin, count, rows, levels...  11.9 us
    pallas_call x2, Pallas kernels, prep(): pl.pallas_call(functools.partial(prep_kernel, near, rows, few, levels), o...  11.7 us
    ppermute x14, waiting for transfers between devices, shards(): lax.ppermute(x, 'tokens', [(i, i ^ d) for i in range(ranks)])  11 us
    pallas_call x1, Pallas kernels, shards(): pl.pallas_call(functools.partial(grad_kernel, heads, rows, levels), out_s...  7.54 us
    pallas_call x1, Pallas kernels, shards(): pl.pallas_call(functools.partial(project_kernel, half, part), out_shape=(...  6.22 us
    unnamed x48, local copies, waits for them, and re-layouts  5.61 us
    ppermute x1, waiting for transfers between devices, shards(): other_far_b = send(far_b, perm=flip)  4.55 us
  transfers between devices with their start and end apart: 23, of which 8 were waited for; matrix products, arithmetic and copies ran while one was open for 4% of the time, Pallas kernels for 26%

profile of v5, /device:TPU:0, one launch (start us, length us, event | category | flops | bytes accessed | tf_op | source)
XLA Modules:
  0.0 131.7 jit_solution(12749919591763898193)
XLA Ops:
  0.6 2.1 %collective-permute-start = (bf16[256,1024]{1,0:T(8,128)(2,1)}, bf16[256,1024]{1,0:T(8,128)(2,1)S(1)}, u32[]{:S(2)}, u32[]{:S(2)}) collective-permute-start(bf16[256,1024]{1,0:T(8,128)(2,1)} %refs_0_.1), channel_id=1, source_target_pairs={{0,32},{16,48},{32,64},{48,80},{64,96},{80,112},{96,0},{112,16},{1... | collective-permute-start | bytes 1572872 | tf_op jit(solution)/shard_map/ppermute | solution.py:433
  2.7 2.2 %collective-permute-start.1 = (bf16[256,1024]{1,0:T(8,128)(2,1)}, bf16[256,1024]{1,0:T(8,128)(2,1)S(1)}, u32[]{:S(2)}, u32[]{:S(2)}) collective-permute-start(bf16[256,1024]{1,0:T(8,128)(2,1)} %refs_0_.1), channel_id=1, source_target_pairs={{0,96},{16,112},{32,0},{48,16},{64,32},{80,48},{96,64},{112,80},{1... | collective-permute-start | bytes 1572872 | tf_op jit(solution)/shard_map/ppermute | solution.py:434
  4.9 3.0 %collective-permute-start.2 = (bf16[256,1024]{1,0:T(8,128)(2,1)}, bf16[256,1024]{1,0:T(8,128)(2,1)S(1)}, u32[]{:S(2)}, u32[]{:S(2)}) collective-permute-start(bf16[256,1024]{1,0:T(8,128)(2,1)} %refs_0_.1), channel_id=1, source_target_pairs={{0,16},{16,0},{32,48},{48,32},{64,80},{80,64},{96,112},{112,96},{1... | collective-permute-start | bytes 1572872 | tf_op jit(solution)/shard_map/ppermute | solution.py:435
  9.5 1.7 %collective-permute-start.3 = (bf16[272,128]{1,0:T(8,128)(2,1)}, bf16[272,128]{1,0:T(8,128)(2,1)S(1)}, u32[]{:S(2)}, u32[]{:S(2)}) collective-permute-start(bf16[272,128]{1,0:T(8,128)(2,1)} %get-tuple-element.39.refs_0_), channel_id=1, source_target_pairs={{0,4},{1,5},{2,6},{3,7},{4,0},{5,1},{6,2},{7,3},{8,12},{9,13},{10,... | collective-permute-start | bytes 208904 | tf_op jit(solution)/shard_map/ppermute | solution.py:416
  11.2 2.9 %collective-permute-start.4 = (bf16[272,128]{1,0:T(8,128)(2,1)}, bf16[272,128]{1,0:T(8,128)(2,1)S(1)}, u32[]{:S(2)}, u32[]{:S(2)}) collective-permute-start(bf16[272,128]{1,0:T(8,128)(2,1)} %get-tuple-element.39.refs_0_), channel_id=1, source_target_pairs={{0,8},{1,9},{2,10},{3,11},{4,12},{5,13},{6,14},{7,15},{8,0},{9,1},... | collective-permute-start | bytes 208904 | tf_op jit(solution)/shard_map/ppermute | solution.py:416
  18.4 2.9 %collective-permute-done.5.refs_3_ = bf16[272,128]{1,0:T(8,128)(2,1)S(1)} collective-permute-done((bf16[272,128]{1,0:T(8,128)(2,1)}, bf16[272,128]{1,0:T(8,128)(2,1)S(1)}, u32[]{:S(2)}, u32[]{:S(2)}) %collective-permute-start.5) | collective-permute-done | bytes 69664 | tf_op jit(solution)/shard_map/ppermute | solution.py:416
  22.8 3.3 %collective-permute-start.7 = (bf16[256,512]{1,0:T(8,128)(2,1)S(1)}, bf16[256,512]{1,0:T(8,128)(2,1)S(1)}, u32[]{:S(2)}, u32[]{:S(2)}) collective-permute-start(bf16[256,512]{1,0:T(8,128)(2,1)S(1)} %slice.7), channel_id=1, source_target_pairs={{0,96},{16,112},{32,0},{48,16},{64,32},{80,48},{96,64},{112,80},{1... | collective-permute-start | bytes 786440 | tf_op jit(solution)/shard_map/ppermute | solution.py:462
  26.8 2.0 %collective-permute-done.13.refs_4_ = bf16[1088,128]{1,0:T(8,128)(2,1)S(1)} collective-permute-done((bf16[1088,128]{1,0:T(8,128)(2,1)}, bf16[1088,128]{1,0:T(8,128)(2,1)S(1)}, u32[]{:S(2)}, u32[]{:S(2)}) %collective-permute-start.13) | collective-permute-done | bytes 278560 | tf_op jit(solution)/shard_map/ppermute | solution.py:416
  29.6 3.2 %collective-permute-start.9 = (bf16[256,1024]{1,0:T(8,128)(2,1)S(1)}, bf16[256,1024]{1,0:T(8,128)(2,1)S(1)}, u32[]{:S(2)}, u32[]{:S(2)}) collective-permute-start(bf16[256,1024]{1,0:T(8,128)(2,1)S(1)} %collective-permute-done.2.refs_3_), channel_id=1, source_target_pairs={{0,96},{16,112},{32,0},{48,16},{64,32},{80,48},{96,64},{112,80},{1... | collective-permute-start | bytes 1572872 | tf_op jit(solution)/shard_map/ppermute | solution.py:464
  32.8 6.2 %project.1 = (f32[256,1024]{1,0:T(8,128)S(1)}, f32[256,256]{1,0:T(8,128)S(1)}) custom-call(s32[8]{0:T(128)S(1)} %stack.35.place, bf16[8192,1024]{1,0:T(8,128)(2,1)} %wq.5, bf16[8192,128]{1,0:T(8,128)(2,1)} %wk.5, bf16[8192,128]{1,0:T(8,128)(2,1)} %w.1, bf16[256,1024]{1,0:T(8,128)(2,1)S(1)} %copy-done.1, bf16[256,1024]{1,0:T(8,128)(2,1)S(1)} %collective-permute-done.refs_1_, ...), custom_call_target="tpu_custom_call" | custom-call | flops 17179869184 | tf_op jit(solution)/shard_map/project/pallas_call | solution.py:470
  40.8 2.8 %collective-permute-start.11 = (bf16[256,512]{1,0:T(8,128)(2,1)S(1)}, bf16[256,512]{1,0:T(8,128)(2,1)S(1)}, u32[]{:S(2)}, u32[]{:S(2)}) collective-permute-start(bf16[256,512]{1,0:T(8,128)(2,1)S(1)} %collective-permute-done.7.refs_1_), channel_id=1, source_target_pairs={{0,16},{16,0},{32,48},{48,32},{64,80},{80,64},{96,112},{112,96},{1... | collective-permute-start | bytes 786440 | tf_op jit(solution)/shard_map/ppermute | solution.py:466
  43.6 6.4 %prep.3 = (bf16[8,256,128]{2,1,0:T(8,128)(2,1)}, f32[8,256,128]{2,1,0:T(8,128)}, f32[8,256,128]{2,1,0:T(8,128)}, bf16[8,256,128]{2,1,0:T(8,128)(2,1)}, bf16[8,128,256]{2,1,0:T(8,128)(2,1)}) custom-call(f32[1,128]{1,0:T(1,128)} %fusion.2.inverse, f32[16,128]{1,0:T(8,128)} %bitcast.12, bf16[272,128]{1,0:T(8,128)(2,1)} %get-tuple-element.39.refs_0_, ...), custom_call_target="tpu_custom_call" | custom-call | flops 4294967296 | tf_op jit(solution)/shard_map/prep/pallas_call | solution.py:509
  50.8 4.6 %collective-permute-done.11.refs_5_ = bf16[256,512]{1,0:T(8,128)(2,1)S(1)} collective-permute-done((bf16[256,512]{1,0:T(8,128)(2,1)S(1)}, bf16[256,512]{1,0:T(8,128)(2,1)S(1)}, u32[]{:S(2)}, u32[]{:S(2)}) %collective-permute-start.11) | collective-permute-done | bytes 262176 | tf_op jit(solution)/shard_map/ppermute | solution.py:466
  55.3 2.7 %value.1.v_own = bf16[256,128]{1,0:T(8,128)(2,1)S(1)} custom-call(s32[8]{0:T(128)S(1)} %stack.35.place, bf16[8192,128]{1,0:T(8,128)(2,1)} %w.1, f32[256,256]{1,0:T(8,128)S(1)} %get-tuple-element.46.before.kv_before, bf16[256,512]{1,0:T(8,128)(2,1)S(1)} %collective-permute-done.6.refs_0_, bf16[256,512]{1,0:T(8,128)(2,1)S(1)} %collective-permute-done.7.refs_1_, ...), custom_call_target="tpu_custom_call" | custom-call | tf_op jit(solution)/shard_map/value/pallas_call | solution.py:489
  58.7 5.3 %prep.2 = (bf16[8,256,128]{2,1,0:T(8,128)(2,1)}, f32[8,256,128]{2,1,0:T(8,128)}, f32[8,256,128]{2,1,0:T(8,128)}, bf16[8,256,128]{2,1,0:T(8,128)(2,1)}) custom-call(f32[1,128]{1,0:T(1,128)} %fusion.2.inverse, f32[16,128]{1,0:T(8,128)} %bitcast.13, bf16[2176,128]{1,0:T(8,128)(2,1)} %collective-permute-done.14.refs_0_), custom_call_target="tpu_custom_call" | custom-call | flops 4294967296 | tf_op jit(solution)/shard_map/prep/pallas_call | solution.py:509
  64.1 2.9 %collective-permute-start.16 = (bf16[512,128]{1,0:T(8,128)(2,1)S(1)}, bf16[512,128]{1,0:T(8,128)(2,1)S(1)}, u32[]{:S(2)}, u32[]{:S(2)}) collective-permute-start(bf16[512,128]{1,0:T(8,128)(2,1)S(1)} %pad_maximum_fusion.1), channel_id=1, source_target_pairs={{0,8},{1,9},{2,10},{3,11},{4,12},{5,13},{6,14},{7,15},{8,0},{9,1},... | collective-permute-start | bytes 393224 | tf_op jit(solution)/shard_map/ppermute | solution.py:416
  67.1 1.7 %collective-permute-start.17 = (bf16[512,128]{1,0:T(8,128)(2,1)S(1)}, bf16[512,128]{1,0:T(8,128)(2,1)S(1)}, u32[]{:S(2)}, u32[]{:S(2)}) collective-permute-start(bf16[512,128]{1,0:T(8,128)(2,1)S(1)} %pad_maximum_fusion.1), channel_id=1, source_target_pairs={{0,12},{1,13},{2,14},{3,15},{4,8},{5,9},{6,10},{7,11},{8,4},{9,5},... | collective-permute-start | bytes 393224 | tf_op jit(solution)/shard_map/ppermute | solution.py:416
  69.9 6.1 %stats.2 = (bf16[4,256,128]{2,1,0:T(8,128)(2,1)S(1)}, bf16[4,128,256]{2,1,0:T(8,128)(2,1)S(1)}, f32[4,256]{1,0:T(4,128)S(1)}, f32[16,128]{1,0:T(8,128)S(1)}) custom-call(s32[8]{0:T(128)S(1)} %stack.35.place, s32[2]{0:T(128)S(1)} %copy-done.5, s32[1,256]{1,0:T(1,128)S(1)} %copy-done.4, s32[256,128]{1,0:T(8,128)S(1)} %copy-done, f32[16,128]{1,0:T(8,128)S(1)} %bitcast.14, ...), custom_call_target="tpu_custom_call" | custom-call | flops 17179869184 | tf_op jit(solution)/shard_map/stats/pallas_call | solution.py:528
  76.2 5.8 %stats.3 = (bf16[4,256,128]{2,1,0:T(8,128)(2,1)S(1)}, bf16[4,128,256]{2,1,0:T(8,128)(2,1)S(1)}, f32[4,256]{1,0:T(4,128)S(1)}, f32[16,128]{1,0:T(8,128)}) custom-call(s32[8]{0:T(128)S(1)} %stack.35.place, s32[2]{0:T(128)S(1)} %copy-done.5, s32[1,256]{1,0:T(1,128)S(1)} %copy-done.4, s32[256,128]{1,0:T(8,128)S(1)} %copy-done, f32[16,128]{1,0:T(8,128)S(1)} %bitcast.15, ...), custom_call_target="tpu_custom_call" | custom-call | flops 17179869184 | tf_op jit(solution)/shard_map/stats/pallas_call | solution.py:528
  82.2 7.5 %grad.1 = (bf16[256,1024]{1,0:T(8,128)(2,1)}, f32[16,128]{1,0:T(8,128)S(1)}) custom-call(s32[2]{0:T(128)S(1)} %copy-done.5, bf16[4,256,128]{2,1,0:T(8,128)(2,1)S(1)} %get-tuple-element.57.q_rot_0, bf16[4,128,256]{2,1,0:T(8,128)(2,1)S(1)} %get-tuple-element.58.q_t_0, f32[4,256]{1,0:T(4,128)S(1)} %get-tuple-element.59.log_total_0, ...), custom_call_target="tpu_custom_call" | custom-call | flops 8589934592 | bytes 8388608 | tf_op jit(solution)/shard_map/grad/pallas_call | solution.py:574
  91.0 6.4 %collective-permute-start.20 = (f32[16,128]{1,0:T(8,128)S(1)}, f32[16,128]{1,0:T(8,128)S(1)}, u32[]{:S(2)}, u32[]{:S(2)}) collective-permute-start(f32[16,128]{1,0:T(8,128)S(1)} %add.77), channel_id=1, source_target_pairs={{0,2},{1,3},{2,0},{3,1},{4,6},{5,7},{6,4},{7,5},{8,10},{9,11},{10,... | collective-permute-start | bytes 24584 | tf_op jit(solution)/shard_map/ppermute | solution.py:416
  97.3 1.6 %collective-permute-done.20 = f32[16,128]{1,0:T(8,128)S(1)} collective-permute-done((f32[16,128]{1,0:T(8,128)S(1)}, f32[16,128]{1,0:T(8,128)S(1)}, u32[]{:S(2)}, u32[]{:S(2)}) %collective-permute-start.20) | collective-permute-done | bytes 8224 | tf_op jit(solution)/shard_map/ppermute | solution.py:416
  99.0 8.3 %collective-permute-start.21 = (f32[16,128]{1,0:T(8,128)S(1)}, f32[16,128]{1,0:T(8,128)S(1)}, u32[]{:S(2)}, u32[]{:S(2)}) collective-permute-start(f32[16,128]{1,0:T(8,128)S(1)} %add.78), channel_id=1, source_target_pairs={{0,4},{1,5},{2,6},{3,7},{4,0},{5,1},{6,2},{7,3},{8,12},{9,13},{10,... | collective-permute-start | bytes 24584 | tf_op jit(solution)/shard_map/ppermute | solution.py:416
  108.9 20.5 %collective-permute-start.22 = (f32[16,128]{1,0:T(8,128)S(1)}, f32[16,128]{1,0:T(8,128)S(1)}, u32[]{:S(2)}, u32[]{:S(2)}) collective-permute-start(f32[16,128]{1,0:T(8,128)S(1)} %add.79), channel_id=1, source_target_pairs={{0,12},{1,13},{2,14},{3,15},{4,8},{5,9},{6,10},{7,11},{8,4},{9,5},... | collective-permute-start | bytes 24584 | tf_op jit(solution)/shard_map/ppermute | solution.py:416
  (89 shorter events, 18.3 us)
Async XLA Ops:
  0.6 32.2 %copy-start.1 = (bf16[256,1024]{1,0:T(8,128)(2,1)S(1)}, bf16[256,1024]{1,0:T(8,128)(2,1)}, u32[]{:S(2)}) copy-start(bf16[256,1024]{1,0:T(8,128)(2,1)} %refs_0_.1) | copy-start | bytes 1572868
  0.6 22.0 %collective-permute-start = (bf16[256,1024]{1,0:T(8,128)(2,1)}, bf16[256,1024]{1,0:T(8,128)(2,1)S(1)}, u32[]{:S(2)}, u32[]{:S(2)}) collective-permute-start(bf16[256,1024]{1,0:T(8,128)(2,1)} %refs_0_.1), channel_id=1, source_target_pairs={{0,32},{16,48},{32,64},{48,80},{64,96},{80,112},{96,0},{112,16},{1... | collective-permute-start | bytes 1572872 | tf_op jit(solution)/shard_map/ppermute | solution.py:433
  2.7 19.9 %collective-permute-start.1 = (bf16[256,1024]{1,0:T(8,128)(2,1)}, bf16[256,1024]{1,0:T(8,128)(2,1)S(1)}, u32[]{:S(2)}, u32[]{:S(2)}) collective-permute-start(bf16[256,1024]{1,0:T(8,128)(2,1)} %refs_0_.1), channel_id=1, source_target_pairs={{0,96},{16,112},{32,0},{48,16},{64,32},{80,48},{96,64},{112,80},{1... | collective-permute-start | bytes 1572872 | tf_op jit(solution)/shard_map/ppermute | solution.py:434
  4.9 17.7 %collective-permute-start.2 = (bf16[256,1024]{1,0:T(8,128)(2,1)}, bf16[256,1024]{1,0:T(8,128)(2,1)S(1)}, u32[]{:S(2)}, u32[]{:S(2)}) collective-permute-start(bf16[256,1024]{1,0:T(8,128)(2,1)} %refs_0_.1), channel_id=1, source_target_pairs={{0,16},{16,0},{32,48},{48,32},{64,80},{80,64},{96,112},{112,96},{1... | collective-permute-start | bytes 1572872 | tf_op jit(solution)/shard_map/ppermute | solution.py:435
  9.5 6.1 %collective-permute-start.3 = (bf16[272,128]{1,0:T(8,128)(2,1)}, bf16[272,128]{1,0:T(8,128)(2,1)S(1)}, u32[]{:S(2)}, u32[]{:S(2)}) collective-permute-start(bf16[272,128]{1,0:T(8,128)(2,1)} %get-tuple-element.39.refs_0_), channel_id=1, source_target_pairs={{0,4},{1,5},{2,6},{3,7},{4,0},{5,1},{6,2},{7,3},{8,12},{9,13},{10,... | collective-permute-start | bytes 208904 | tf_op jit(solution)/shard_map/ppermute | solution.py:416
  11.2 6.6 %collective-permute-start.4 = (bf16[272,128]{1,0:T(8,128)(2,1)}, bf16[272,128]{1,0:T(8,128)(2,1)S(1)}, u32[]{:S(2)}, u32[]{:S(2)}) collective-permute-start(bf16[272,128]{1,0:T(8,128)(2,1)} %get-tuple-element.39.refs_0_), channel_id=1, source_target_pairs={{0,8},{1,9},{2,10},{3,11},{4,12},{5,13},{6,14},{7,15},{8,0},{9,1},... | collective-permute-start | bytes 208904 | tf_op jit(solution)/shard_map/ppermute | solution.py:416
  15.6 5.7 %collective-permute-start.5 = (bf16[272,128]{1,0:T(8,128)(2,1)}, bf16[272,128]{1,0:T(8,128)(2,1)S(1)}, u32[]{:S(2)}, u32[]{:S(2)}) collective-permute-start(bf16[272,128]{1,0:T(8,128)(2,1)} %get-tuple-element.39.refs_0_), channel_id=1, source_target_pairs={{0,12},{1,13},{2,14},{3,15},{4,8},{5,9},{6,10},{7,11},{8,4},{9,5},... | collective-permute-start | bytes 208904 | tf_op jit(solution)/shard_map/ppermute | solution.py:416
  22.0 6.8 %collective-permute-start.13 = (bf16[1088,128]{1,0:T(8,128)(2,1)}, bf16[1088,128]{1,0:T(8,128)(2,1)S(1)}, u32[]{:S(2)}, u32[]{:S(2)}) collective-permute-start(bf16[1088,128]{1,0:T(8,128)(2,1)} %get-tuple-element.75), channel_id=1, source_target_pairs={{0,2},{1,3},{2,0},{3,1},{4,6},{5,7},{6,4},{7,5},{8,10},{9,11},{10,... | collective-permute-start | bytes 835592 | tf_op jit(solution)/shard_map/ppermute | solution.py:416
  22.7 10.1 %collective-permute-start.6 = (bf16[256,512]{1,0:T(8,128)(2,1)S(1)}, bf16[256,512]{1,0:T(8,128)(2,1)S(1)}, u32[]{:S(2)}, u32[]{:S(2)}) collective-permute-start(bf16[256,512]{1,0:T(8,128)(2,1)S(1)} %slice.6), channel_id=1, source_target_pairs={{0,32},{16,48},{32,64},{48,80},{64,96},{80,112},{96,0},{112,16},{1... | collective-permute-start | bytes 786440 | tf_op jit(solution)/shard_map/ppermute | solution.py:461
  22.8 10.0 %collective-permute-start.7 = (bf16[256,512]{1,0:T(8,128)(2,1)S(1)}, bf16[256,512]{1,0:T(8,128)(2,1)S(1)}, u32[]{:S(2)}, u32[]{:S(2)}) collective-permute-start(bf16[256,512]{1,0:T(8,128)(2,1)S(1)} %slice.7), channel_id=1, source_target_pairs={{0,96},{16,112},{32,0},{48,16},{64,32},{80,48},{96,64},{112,80},{1... | collective-permute-start | bytes 786440 | tf_op jit(solution)/shard_map/ppermute | solution.py:462
  29.6 29.2 %collective-permute-start.14 = (bf16[2176,128]{1,0:T(8,128)(2,1)}, bf16[2176,128]{1,0:T(8,128)(2,1)}, u32[]{:S(2)}, u32[]{:S(2)}) collective-permute-start(bf16[2176,128]{1,0:T(8,128)(2,1)} %constant_dynamic-update-slice_fusion.4), channel_id=1, source_target_pairs={{0,1},{1,0},{2,3},{3,2},{4,5},{5,4},{6,7},{7,6},{8,9},{9,8},{10,11... | collective-permute-start | bytes 1671176 | tf_op jit(solution)/shard_map/ppermute | solution.py:416
  29.6 20.5 %collective-permute-start.8 = (bf16[256,1024]{1,0:T(8,128)(2,1)S(1)}, bf16[256,1024]{1,0:T(8,128)(2,1)S(1)}, u32[]{:S(2)}, u32[]{:S(2)}) collective-permute-start(bf16[256,1024]{1,0:T(8,128)(2,1)S(1)} %collective-permute-done.2.refs_3_), channel_id=1, source_target_pairs={{0,32},{16,48},{32,64},{48,80},{64,96},{80,112},{96,0},{112,16},{1... | collective-permute-start | bytes 1572872 | tf_op jit(solution)/shard_map/ppermute | solution.py:463
  29.6 20.5 %collective-permute-start.9 = (bf16[256,1024]{1,0:T(8,128)(2,1)S(1)}, bf16[256,1024]{1,0:T(8,128)(2,1)S(1)}, u32[]{:S(2)}, u32[]{:S(2)}) collective-permute-start(bf16[256,1024]{1,0:T(8,128)(2,1)S(1)} %collective-permute-done.2.refs_3_), channel_id=1, source_target_pairs={{0,96},{16,112},{32,0},{48,16},{64,32},{80,48},{96,64},{112,80},{1... | collective-permute-start | bytes 1572872 | tf_op jit(solution)/shard_map/ppermute | solution.py:464
  40.0 10.7 %collective-permute-start.10 = (bf16[256,512]{1,0:T(8,128)(2,1)S(1)}, bf16[256,512]{1,0:T(8,128)(2,1)S(1)}, u32[]{:S(2)}, u32[]{:S(2)}) collective-permute-start(bf16[256,512]{1,0:T(8,128)(2,1)S(1)} %collective-permute-done.6.refs_0_), channel_id=1, source_target_pairs={{0,16},{16,0},{32,48},{48,32},{64,80},{80,64},{96,112},{112,96},{1... | collective-permute-start | bytes 786440 | tf_op jit(solution)/shard_map/ppermute | solution.py:465
  40.8 14.5 %collective-permute-start.11 = (bf16[256,512]{1,0:T(8,128)(2,1)S(1)}, bf16[256,512]{1,0:T(8,128)(2,1)S(1)}, u32[]{:S(2)}, u32[]{:S(2)}) collective-permute-start(bf16[256,512]{1,0:T(8,128)(2,1)S(1)} %collective-permute-done.7.refs_1_), channel_id=1, source_target_pairs={{0,16},{16,0},{32,48},{48,32},{64,80},{80,64},{96,112},{112,96},{1... | collective-permute-start | bytes 786440 | tf_op jit(solution)/shard_map/ppermute | solution.py:466
  58.1 5.9 %collective-permute-start.12 = (bf16[256,128]{1,0:T(8,128)(2,1)S(1)}, bf16[256,128]{1,0:T(8,128)(2,1)S(1)}, u32[]{:S(2)}, u32[]{:S(2)}) collective-permute-start(bf16[256,128]{1,0:T(8,128)(2,1)S(1)} %value.1.v_own), channel_id=1, source_target_pairs={{0,2},{1,3},{2,0},{3,1},{4,6},{5,7},{6,4},{7,5},{8,10},{9,11},{10,... | collective-permute-start | bytes 196616 | tf_op jit(solution)/shard_map/ppermute | solution.py:416
  64.0 11.9 %collective-permute-start.15 = (bf16[512,128]{1,0:T(8,128)(2,1)S(1)}, bf16[512,128]{1,0:T(8,128)(2,1)S(1)}, u32[]{:S(2)}, u32[]{:S(2)}) collective-permute-start(bf16[512,128]{1,0:T(8,128)(2,1)S(1)} %pad_maximum_fusion.1), channel_id=1, source_target_pairs={{0,4},{1,5},{2,6},{3,7},{4,0},{5,1},{6,2},{7,3},{8,12},{9,13},{10,... | collective-permute-start | bytes 393224 | tf_op jit(solution)/shard_map/ppermute | solution.py:416
  64.1 11.8 %collective-permute-start.16 = (bf16[512,128]{1,0:T(8,128)(2,1)S(1)}, bf16[512,128]{1,0:T(8,128)(2,1)S(1)}, u32[]{:S(2)}, u32[]{:S(2)}) collective-permute-start(bf16[512,128]{1,0:T(8,128)(2,1)S(1)} %pad_maximum_fusion.1), channel_id=1, source_target_pairs={{0,8},{1,9},{2,10},{3,11},{4,12},{5,13},{6,14},{7,15},{8,0},{9,1},... | collective-permute-start | bytes 393224 | tf_op jit(solution)/shard_map/ppermute | solution.py:416
  67.1 8.9 %collective-permute-start.17 = (bf16[512,128]{1,0:T(8,128)(2,1)S(1)}, bf16[512,128]{1,0:T(8,128)(2,1)S(1)}, u32[]{:S(2)}, u32[]{:S(2)}) collective-permute-start(bf16[512,128]{1,0:T(8,128)(2,1)S(1)} %pad_maximum_fusion.1), channel_id=1, source_target_pairs={{0,12},{1,13},{2,14},{3,15},{4,8},{5,9},{6,10},{7,11},{8,4},{9,5},... | collective-permute-start | bytes 393224 | tf_op jit(solution)/shard_map/ppermute | solution.py:416
  76.1 5.9 %collective-permute-start.18 = (bf16[2048,128]{1,0:T(8,128)(2,1)S(1)}, bf16[2048,128]{1,0:T(8,128)(2,1)S(1)}, u32[]{:S(2)}, u32[]{:S(2)}) collective-permute-start(bf16[2048,128]{1,0:T(8,128)(2,1)S(1)} %pad_maximum_fusion), channel_id=1, source_target_pairs={{0,1},{1,0},{2,3},{3,2},{4,5},{5,4},{6,7},{7,6},{8,9},{9,8},{10,11... | collective-permute-start | bytes 1572872 | tf_op jit(solution)/shard_map/ppermute | solution.py:416
  89.7 1.3 collective-permute-start.19
  91.0 8.0 %collective-permute-start.20 = (f32[16,128]{1,0:T(8,128)S(1)}, f32[16,128]{1,0:T(8,128)S(1)}, u32[]{:S(2)}, u32[]{:S(2)}) collective-permute-start(f32[16,128]{1,0:T(8,128)S(1)} %add.77), channel_id=1, source_target_pairs={{0,2},{1,3},{2,0},{3,1},{4,6},{5,7},{6,4},{7,5},{8,10},{9,11},{10,... | collective-permute-start | bytes 24584 | tf_op jit(solution)/shard_map/ppermute | solution.py:416
  99.0 9.9 %collective-permute-start.21 = (f32[16,128]{1,0:T(8,128)S(1)}, f32[16,128]{1,0:T(8,128)S(1)}, u32[]{:S(2)}, u32[]{:S(2)}) collective-permute-start(f32[16,128]{1,0:T(8,128)S(1)} %add.78), channel_id=1, source_target_pairs={{0,4},{1,5},{2,6},{3,7},{4,0},{5,1},{6,2},{7,3},{8,12},{9,13},{10,... | collective-permute-start | bytes 24584 | tf_op jit(solution)/shard_map/ppermute | solution.py:416
  108.9 22.2 %collective-permute-start.22 = (f32[16,128]{1,0:T(8,128)S(1)}, f32[16,128]{1,0:T(8,128)S(1)}, u32[]{:S(2)}, u32[]{:S(2)}) collective-permute-start(f32[16,128]{1,0:T(8,128)S(1)} %add.79), channel_id=1, source_target_pairs={{0,12},{1,13},{2,14},{3,15},{4,8},{5,9},{6,10},{7,11},{8,4},{9,5},... | collective-permute-start | bytes 24584 | tf_op jit(solution)/shard_map/ppermute | solution.py:416
  (21 other events, 153.1 us)

commit v6 on v5

--- a/solution.py
+++ b/solution.py
@@ -516,7 +516,7 @@
             + [pltpu.VMEM(size, kind) for size, kind in zip(shapes, kinds)]
             + [pltpu.SemaphoreType.DMA((few,)), pltpu.SemaphoreType.DMA((4,))],
             compiler_params=pltpu.CompilerParams(vmem_limit_bytes=58 << 20),
-            cost_estimate=cost(1 << 32, 0),
+            cost_estimate=cost(0 if near else 1 << 32, 0),
             name="prep",
         )(inverse, book, *pieces)
 

time: 132 us -> 127 us (0.962)
  waiting for transfers between devices: 16.2 us -> 10.3 us
    ppermute x1, waiting for transfers between devices: 4.55 us -> 0.01 us  [shards(): other_far_b = send(far_b, perm=flip)]
    unnamed x48 -> x46, local copies, waits for them, and re-layouts: 5.61 us -> 5.67 us
  transfers between devices with their start and end apart: 23 -> 23, of which waited for: 8 -> 6; matrix products, arithmetic and copies ran while one was open for 4% -> 5% of each run, Pallas kernels for 26% -> 27%
where the time goes in v6:
time: 127 us; the launch traced here: 126 us
  starting transfers between devices  64.3 us (51%)
  Pallas kernels  41.6 us (33%)
  waiting for transfers between devices  10.3 us (8%)
  local copies, waits for them, and re-layouts  7.27 us (6%)
    ppermute x14, starting transfers between devices, shards(): lax.ppermute(x, 'tokens', [(i, i ^ d) for i in range(ranks)])  47.1 us
    pallas_call x2, Pallas kernels, log_totals(): pl.pallas_call(functools.partial(stats_kernel, begin, count, rows, levels...  11.9 us
    pallas_call x2, Pallas kernels, prep(): pl.pallas_call(functools.partial(prep_kernel, near, rows, few, levels), o...  11.7 us
    ppermute x14, waiting for transfers between devices, shards(): lax.ppermute(x, 'tokens', [(i, i ^ d) for i in range(ranks)])  10.3 us
    pallas_call x1, Pallas kernels, shards(): pl.pallas_call(functools.partial(grad_kernel, heads, rows, levels), out_s...  7.55 us
    pallas_call x1, Pallas kernels, shards(): pl.pallas_call(functools.partial(project_kernel, half, part), out_shape=(...  6.2 us
    unnamed x46, local copies, waits for them, and re-layouts  5.67 us
    ppermute x1, starting transfers between devices, shards(): other_high = send(other, perm=down)  3.23 us
  transfers between devices with their start and end apart: 23, of which 6 were waited for; matrix products, arithmetic and copies ran while one was open for 5% of the time, Pallas kernels for 27%

profile of v6, /device:TPU:0, one launch (start us, length us, event | category | flops | bytes accessed | tf_op | source)
XLA Modules:
  0.0 125.9 jit_solution(17809428623203524835)
XLA Ops:
  0.6 2.1 %collective-permute-start = (bf16[256,1024]{1,0:T(8,128)(2,1)}, bf16[256,1024]{1,0:T(8,128)(2,1)S(1)}, u32[]{:S(2)}, u32[]{:S(2)}) collective-permute-start(bf16[256,1024]{1,0:T(8,128)(2,1)} %refs_0_.1), channel_id=1, source_target_pairs={{0,32},{16,48},{32,64},{48,80},{64,96},{80,112},{96,0},{112,16},{1... | collective-permute-start | bytes 1572872 | tf_op jit(solution)/shard_map/ppermute | solution.py:433
  2.7 2.2 %collective-permute-start.1 = (bf16[256,1024]{1,0:T(8,128)(2,1)}, bf16[256,1024]{1,0:T(8,128)(2,1)S(1)}, u32[]{:S(2)}, u32[]{:S(2)}) collective-permute-start(bf16[256,1024]{1,0:T(8,128)(2,1)} %refs_0_.1), channel_id=1, source_target_pairs={{0,96},{16,112},{32,0},{48,16},{64,32},{80,48},{96,64},{112,80},{1... | collective-permute-start | bytes 1572872 | tf_op jit(solution)/shard_map/ppermute | solution.py:434
  4.9 3.0 %collective-permute-start.2 = (bf16[256,1024]{1,0:T(8,128)(2,1)}, bf16[256,1024]{1,0:T(8,128)(2,1)S(1)}, u32[]{:S(2)}, u32[]{:S(2)}) collective-permute-start(bf16[256,1024]{1,0:T(8,128)(2,1)} %refs_0_.1), channel_id=1, source_target_pairs={{0,16},{16,0},{32,48},{48,32},{64,80},{80,64},{96,112},{112,96},{1... | collective-permute-start | bytes 1572872 | tf_op jit(solution)/shard_map/ppermute | solution.py:435
  9.5 1.7 %collective-permute-start.3 = (bf16[272,128]{1,0:T(8,128)(2,1)}, bf16[272,128]{1,0:T(8,128)(2,1)S(1)}, u32[]{:S(2)}, u32[]{:S(2)}) collective-permute-start(bf16[272,128]{1,0:T(8,128)(2,1)} %get-tuple-element.39.refs_0_), channel_id=1, source_target_pairs={{0,4},{1,5},{2,6},{3,7},{4,0},{5,1},{6,2},{7,3},{8,12},{9,13},{10,... | collective-permute-start | bytes 208904 | tf_op jit(solution)/shard_map/ppermute | solution.py:416
  11.2 2.9 %collective-permute-start.4 = (bf16[272,128]{1,0:T(8,128)(2,1)}, bf16[272,128]{1,0:T(8,128)(2,1)S(1)}, u32[]{:S(2)}, u32[]{:S(2)}) collective-permute-start(bf16[272,128]{1,0:T(8,128)(2,1)} %get-tuple-element.39.refs_0_), channel_id=1, source_target_pairs={{0,8},{1,9},{2,10},{3,11},{4,12},{5,13},{6,14},{7,15},{8,0},{9,1},... | collective-permute-start | bytes 208904 | tf_op jit(solution)/shard_map/ppermute | solution.py:416
  18.4 2.9 %collective-permute-done.5.refs_3_ = bf16[272,128]{1,0:T(8,128)(2,1)S(1)} collective-permute-done((bf16[272,128]{1,0:T(8,128)(2,1)}, bf16[272,128]{1,0:T(8,128)(2,1)S(1)}, u32[]{:S(2)}, u32[]{:S(2)}) %collective-permute-start.5) | collective-permute-done | bytes 69664 | tf_op jit(solution)/shard_map/ppermute | solution.py:416
  23.5 3.1 %collective-permute-start.7 = (bf16[256,512]{1,0:T(8,128)(2,1)}, bf16[256,512]{1,0:T(8,128)(2,1)S(1)}, u32[]{:S(2)}, u32[]{:S(2)}) collective-permute-start(bf16[256,512]{1,0:T(8,128)(2,1)} %slice.7), channel_id=1, source_target_pairs={{0,96},{16,112},{32,0},{48,16},{64,32},{80,48},{96,64},{112,80},{1... | collective-permute-start | bytes 786440 | tf_op jit(solution)/shard_map/ppermute | solution.py:462
  29.6 3.2 %collective-permute-start.9 = (bf16[256,1024]{1,0:T(8,128)(2,1)S(1)}, bf16[256,1024]{1,0:T(8,128)(2,1)S(1)}, u32[]{:S(2)}, u32[]{:S(2)}) collective-permute-start(bf16[256,1024]{1,0:T(8,128)(2,1)S(1)} %collective-permute-done.2.refs_3_), channel_id=1, source_target_pairs={{0,96},{16,112},{32,0},{48,16},{64,32},{80,48},{96,64},{112,80},{1... | collective-permute-start | bytes 1572872 | tf_op jit(solution)/shard_map/ppermute | solution.py:464
  33.5 2.8 %collective-permute-start.11 = (bf16[256,512]{1,0:T(8,128)(2,1)S(1)}, bf16[256,512]{1,0:T(8,128)(2,1)S(1)}, u32[]{:S(2)}, u32[]{:S(2)}) collective-permute-start(bf16[256,512]{1,0:T(8,128)(2,1)S(1)} %collective-permute-done.7.refs_1_), channel_id=1, source_target_pairs={{0,16},{16,0},{32,48},{48,32},{64,80},{80,64},{96,112},{112,96},{1... | collective-permute-start | bytes 786440 | tf_op jit(solution)/shard_map/ppermute | solution.py:466
  36.3 6.2 %project.1 = (f32[256,1024]{1,0:T(8,128)S(1)}, f32[256,256]{1,0:T(8,128)S(1)}) custom-call(s32[8]{0:T(128)S(1)} %stack.35.place, bf16[8192,1024]{1,0:T(8,128)(2,1)} %wq.5, bf16[8192,128]{1,0:T(8,128)(2,1)} %wk.5, bf16[8192,128]{1,0:T(8,128)(2,1)} %w.1, bf16[256,1024]{1,0:T(8,128)(2,1)S(1)} %copy-done.5, bf16[256,1024]{1,0:T(8,128)(2,1)S(1)} %collective-permute-done.refs_1_, ...), custom_call_target="tpu_custom_call" | custom-call | flops 17179869184 | tf_op jit(solution)/shard_map/project/pallas_call | solution.py:470
  43.6 6.4 %prep.3 = (bf16[8,256,128]{2,1,0:T(8,128)(2,1)}, f32[8,256,128]{2,1,0:T(8,128)}, f32[8,256,128]{2,1,0:T(8,128)}, bf16[8,256,128]{2,1,0:T(8,128)(2,1)}, bf16[8,128,256]{2,1,0:T(8,128)(2,1)}) custom-call(f32[1,128]{1,0:T(1,128)} %fusion.2.inverse, f32[16,128]{1,0:T(8,128)} %bitcast.12, bf16[272,128]{1,0:T(8,128)(2,1)} %get-tuple-element.39.refs_0_, ...), custom_call_target="tpu_custom_call" | custom-call | tf_op jit(solution)/shard_map/prep/pallas_call | solution.py:509
  50.0 2.7 %value.1.v_own = bf16[256,128]{1,0:T(8,128)(2,1)S(1)} custom-call(s32[8]{0:T(128)S(1)} %stack.35.place, bf16[8192,128]{1,0:T(8,128)(2,1)} %w.1, f32[256,256]{1,0:T(8,128)S(1)} %get-tuple-element.46.before.kv_before, bf16[256,512]{1,0:T(8,128)(2,1)S(1)} %collective-permute-done.6.refs_0_, bf16[256,512]{1,0:T(8,128)(2,1)S(1)} %collective-permute-done.7.refs_1_, ...), custom_call_target="tpu_custom_call" | custom-call | tf_op jit(solution)/shard_map/value/pallas_call | solution.py:489
  53.5 5.3 %prep.2 = (bf16[8,256,128]{2,1,0:T(8,128)(2,1)}, f32[8,256,128]{2,1,0:T(8,128)}, f32[8,256,128]{2,1,0:T(8,128)}, bf16[8,256,128]{2,1,0:T(8,128)(2,1)}) custom-call(f32[1,128]{1,0:T(1,128)} %fusion.2.inverse, f32[16,128]{1,0:T(8,128)} %bitcast.13, bf16[2176,128]{1,0:T(8,128)(2,1)} %collective-permute-done.14.refs_0_), custom_call_target="tpu_custom_call" | custom-call | flops 4294967296 | tf_op jit(solution)/shard_map/prep/pallas_call | solution.py:509
  58.9 2.9 %collective-permute-start.16 = (bf16[512,128]{1,0:T(8,128)(2,1)S(1)}, bf16[512,128]{1,0:T(8,128)(2,1)S(1)}, u32[]{:S(2)}, u32[]{:S(2)}) collective-permute-start(bf16[512,128]{1,0:T(8,128)(2,1)S(1)} %pad_maximum_fusion.1), channel_id=1, source_target_pairs={{0,8},{1,9},{2,10},{3,11},{4,12},{5,13},{6,14},{7,15},{8,0},{9,1},... | collective-permute-start | bytes 393224 | tf_op jit(solution)/shard_map/ppermute | solution.py:416
  61.9 1.7 %collective-permute-start.17 = (bf16[512,128]{1,0:T(8,128)(2,1)S(1)}, bf16[512,128]{1,0:T(8,128)(2,1)S(1)}, u32[]{:S(2)}, u32[]{:S(2)}) collective-permute-start(bf16[512,128]{1,0:T(8,128)(2,1)S(1)} %pad_maximum_fusion.1), channel_id=1, source_target_pairs={{0,12},{1,13},{2,14},{3,15},{4,8},{5,9},{6,10},{7,11},{8,4},{9,5},... | collective-permute-start | bytes 393224 | tf_op jit(solution)/shard_map/ppermute | solution.py:416
  64.7 6.1 %stats.2 = (bf16[4,256,128]{2,1,0:T(8,128)(2,1)S(1)}, bf16[4,128,256]{2,1,0:T(8,128)(2,1)S(1)}, f32[4,256]{1,0:T(4,128)S(1)}, f32[16,128]{1,0:T(8,128)S(1)}) custom-call(s32[8]{0:T(128)S(1)} %stack.35.place, s32[2]{0:T(128)S(1)} %copy-done.10, s32[1,256]{1,0:T(1,128)S(1)} %copy-done.9, s32[256,128]{1,0:T(8,128)S(1)} %copy-done.1, f32[16,128]{1,0:T(8,128)S(1)} %bitcast.14, ...), custom_call_target="tpu_custom_call" | custom-call | flops 17179869184 | tf_op jit(solution)/shard_map/stats/pallas_call | solution.py:528
  71.0 5.8 %stats.3 = (bf16[4,256,128]{2,1,0:T(8,128)(2,1)S(1)}, bf16[4,128,256]{2,1,0:T(8,128)(2,1)S(1)}, f32[4,256]{1,0:T(4,128)S(1)}, f32[16,128]{1,0:T(8,128)}) custom-call(s32[8]{0:T(128)S(1)} %stack.35.place, s32[2]{0:T(128)S(1)} %copy-done.10, s32[1,256]{1,0:T(1,128)S(1)} %copy-done.9, s32[256,128]{1,0:T(8,128)S(1)} %copy-done.1, f32[16,128]{1,0:T(8,128)S(1)} %bitcast.15, ...), custom_call_target="tpu_custom_call" | custom-call | flops 17179869184 | tf_op jit(solution)/shard_map/stats/pallas_call | solution.py:528
  76.9 7.5 %grad.1 = (bf16[256,1024]{1,0:T(8,128)(2,1)}, f32[16,128]{1,0:T(8,128)S(1)}) custom-call(s32[2]{0:T(128)S(1)} %copy-done.10, bf16[4,256,128]{2,1,0:T(8,128)(2,1)S(1)} %get-tuple-element.57.q_rot_0, bf16[4,128,256]{2,1,0:T(8,128)(2,1)S(1)} %get-tuple-element.58.q_t_0, f32[4,256]{1,0:T(4,128)S(1)} %get-tuple-element.59.log_total_0, ...), custom_call_target="tpu_custom_call" | custom-call | flops 8589934592 | bytes 8388608 | tf_op jit(solution)/shard_map/grad/pallas_call | solution.py:574
  85.7 6.4 %collective-permute-start.20 = (f32[16,128]{1,0:T(8,128)S(1)}, f32[16,128]{1,0:T(8,128)S(1)}, u32[]{:S(2)}, u32[]{:S(2)}) collective-permute-start(f32[16,128]{1,0:T(8,128)S(1)} %add.77), channel_id=1, source_target_pairs={{0,2},{1,3},{2,0},{3,1},{4,6},{5,7},{6,4},{7,5},{8,10},{9,11},{10,... | collective-permute-start | bytes 24584 | tf_op jit(solution)/shard_map/ppermute | solution.py:416
  92.1 1.6 %collective-permute-done.20 = f32[16,128]{1,0:T(8,128)S(1)} collective-permute-done((f32[16,128]{1,0:T(8,128)S(1)}, f32[16,128]{1,0:T(8,128)S(1)}, u32[]{:S(2)}, u32[]{:S(2)}) %collective-permute-start.20) | collective-permute-done | bytes 8224 | tf_op jit(solution)/shard_map/ppermute | solution.py:416
  93.7 3.6 %collective-permute-start.21 = (f32[16,128]{1,0:T(8,128)S(1)}, f32[16,128]{1,0:T(8,128)S(1)}, u32[]{:S(2)}, u32[]{:S(2)}) collective-permute-start(f32[16,128]{1,0:T(8,128)S(1)} %add.78), channel_id=1, source_target_pairs={{0,4},{1,5},{2,6},{3,7},{4,0},{5,1},{6,2},{7,3},{8,12},{9,13},{10,... | collective-permute-start | bytes 24584 | tf_op jit(solution)/shard_map/ppermute | solution.py:416
  97.3 1.6 %collective-permute-done.21 = f32[16,128]{1,0:T(8,128)S(1)} collective-permute-done((f32[16,128]{1,0:T(8,128)S(1)}, f32[16,128]{1,0:T(8,128)S(1)}, u32[]{:S(2)}, u32[]{:S(2)}) %collective-permute-start.21) | collective-permute-done | bytes 8224 | tf_op jit(solution)/shard_map/ppermute | solution.py:416
  99.0 24.7 %collective-permute-start.22 = (f32[16,128]{1,0:T(8,128)S(1)}, f32[16,128]{1,0:T(8,128)S(1)}, u32[]{:S(2)}, u32[]{:S(2)}) collective-permute-start(f32[16,128]{1,0:T(8,128)S(1)} %add.79), channel_id=1, source_target_pairs={{0,12},{1,13},{2,14},{3,15},{4,8},{5,9},{6,10},{7,11},{8,4},{9,5},... | collective-permute-start | bytes 24584 | tf_op jit(solution)/shard_map/ppermute | solution.py:416
  123.7 1.6 %collective-permute-done.22 = f32[16,128]{1,0:T(8,128)S(1)} collective-permute-done((f32[16,128]{1,0:T(8,128)S(1)}, f32[16,128]{1,0:T(8,128)S(1)}, u32[]{:S(2)}, u32[]{:S(2)}) %collective-permute-start.22) | collective-permute-done | bytes 8224 | tf_op jit(solution)/shard_map/ppermute | solution.py:416
  (87 shorter events, 16.6 us)
Async XLA Ops:
  0.6 35.7 %copy-start.5 = (bf16[256,1024]{1,0:T(8,128)(2,1)S(1)}, bf16[256,1024]{1,0:T(8,128)(2,1)}, u32[]{:S(2)}) copy-start(bf16[256,1024]{1,0:T(8,128)(2,1)} %refs_0_.1) | copy-start | bytes 1572868
  0.6 22.0 %collective-permute-start = (bf16[256,1024]{1,0:T(8,128)(2,1)}, bf16[256,1024]{1,0:T(8,128)(2,1)S(1)}, u32[]{:S(2)}, u32[]{:S(2)}) collective-permute-start(bf16[256,1024]{1,0:T(8,128)(2,1)} %refs_0_.1), channel_id=1, source_target_pairs={{0,32},{16,48},{32,64},{48,80},{64,96},{80,112},{96,0},{112,16},{1... | collective-permute-start | bytes 1572872 | tf_op jit(solution)/shard_map/ppermute | solution.py:433
  2.7 19.9 %collective-permute-start.1 = (bf16[256,1024]{1,0:T(8,128)(2,1)}, bf16[256,1024]{1,0:T(8,128)(2,1)S(1)}, u32[]{:S(2)}, u32[]{:S(2)}) collective-permute-start(bf16[256,1024]{1,0:T(8,128)(2,1)} %refs_0_.1), channel_id=1, source_target_pairs={{0,96},{16,112},{32,0},{48,16},{64,32},{80,48},{96,64},{112,80},{1... | collective-permute-start | bytes 1572872 | tf_op jit(solution)/shard_map/ppermute | solution.py:434
  4.9 17.7 %collective-permute-start.2 = (bf16[256,1024]{1,0:T(8,128)(2,1)}, bf16[256,1024]{1,0:T(8,128)(2,1)S(1)}, u32[]{:S(2)}, u32[]{:S(2)}) collective-permute-start(bf16[256,1024]{1,0:T(8,128)(2,1)} %refs_0_.1), channel_id=1, source_target_pairs={{0,16},{16,0},{32,48},{48,32},{64,80},{80,64},{96,112},{112,96},{1... | collective-permute-start | bytes 1572872 | tf_op jit(solution)/shard_map/ppermute | solution.py:435
  9.5 6.1 %collective-permute-start.3 = (bf16[272,128]{1,0:T(8,128)(2,1)}, bf16[272,128]{1,0:T(8,128)(2,1)S(1)}, u32[]{:S(2)}, u32[]{:S(2)}) collective-permute-start(bf16[272,128]{1,0:T(8,128)(2,1)} %get-tuple-element.39.refs_0_), channel_id=1, source_target_pairs={{0,4},{1,5},{2,6},{3,7},{4,0},{5,1},{6,2},{7,3},{8,12},{9,13},{10,... | collective-permute-start | bytes 208904 | tf_op jit(solution)/shard_map/ppermute | solution.py:416
  11.2 6.6 %collective-permute-start.4 = (bf16[272,128]{1,0:T(8,128)(2,1)}, bf16[272,128]{1,0:T(8,128)(2,1)S(1)}, u32[]{:S(2)}, u32[]{:S(2)}) collective-permute-start(bf16[272,128]{1,0:T(8,128)(2,1)} %get-tuple-element.39.refs_0_), channel_id=1, source_target_pairs={{0,8},{1,9},{2,10},{3,11},{4,12},{5,13},{6,14},{7,15},{8,0},{9,1},... | collective-permute-start | bytes 208904 | tf_op jit(solution)/shard_map/ppermute | solution.py:416
  15.6 5.7 %collective-permute-start.5 = (bf16[272,128]{1,0:T(8,128)(2,1)}, bf16[272,128]{1,0:T(8,128)(2,1)S(1)}, u32[]{:S(2)}, u32[]{:S(2)}) collective-permute-start(bf16[272,128]{1,0:T(8,128)(2,1)} %get-tuple-element.39.refs_0_), channel_id=1, source_target_pairs={{0,12},{1,13},{2,14},{3,15},{4,8},{5,9},{6,10},{7,11},{8,4},{9,5},... | collective-permute-start | bytes 208904 | tf_op jit(solution)/shard_map/ppermute | solution.py:416
  22.0 6.8 %collective-permute-start.13 = (bf16[1088,128]{1,0:T(8,128)(2,1)}, bf16[1088,128]{1,0:T(8,128)(2,1)S(1)}, u32[]{:S(2)}, u32[]{:S(2)}) collective-permute-start(bf16[1088,128]{1,0:T(8,128)(2,1)} %get-tuple-element.75), channel_id=1, source_target_pairs={{0,2},{1,3},{2,0},{3,1},{4,6},{5,7},{6,4},{7,5},{8,10},{9,11},{10,... | collective-permute-start | bytes 835592 | tf_op jit(solution)/shard_map/ppermute | solution.py:416
  22.7 10.2 %collective-permute-start.6 = (bf16[256,512]{1,0:T(8,128)(2,1)S(1)}, bf16[256,512]{1,0:T(8,128)(2,1)S(1)}, u32[]{:S(2)}, u32[]{:S(2)}) collective-permute-start(bf16[256,512]{1,0:T(8,128)(2,1)S(1)} %slice.6), channel_id=1, source_target_pairs={{0,32},{16,48},{32,64},{48,80},{64,96},{80,112},{96,0},{112,16},{1... | collective-permute-start | bytes 786440 | tf_op jit(solution)/shard_map/ppermute | solution.py:461
  23.5 9.3 %collective-permute-start.7 = (bf16[256,512]{1,0:T(8,128)(2,1)}, bf16[256,512]{1,0:T(8,128)(2,1)S(1)}, u32[]{:S(2)}, u32[]{:S(2)}) collective-permute-start(bf16[256,512]{1,0:T(8,128)(2,1)} %slice.7), channel_id=1, source_target_pairs={{0,96},{16,112},{32,0},{48,16},{64,32},{80,48},{96,64},{112,80},{1... | collective-permute-start | bytes 786440 | tf_op jit(solution)/shard_map/ppermute | solution.py:462
  29.6 23.9 %collective-permute-start.14 = (bf16[2176,128]{1,0:T(8,128)(2,1)}, bf16[2176,128]{1,0:T(8,128)(2,1)}, u32[]{:S(2)}, u32[]{:S(2)}) collective-permute-start(bf16[2176,128]{1,0:T(8,128)(2,1)} %constant_dynamic-update-slice_fusion.4), channel_id=1, source_target_pairs={{0,1},{1,0},{2,3},{3,2},{4,5},{5,4},{6,7},{7,6},{8,9},{9,8},{10,11... | collective-permute-start | bytes 1671176 | tf_op jit(solution)/shard_map/ppermute | solution.py:416
  29.6 20.4 %collective-permute-start.8 = (bf16[256,1024]{1,0:T(8,128)(2,1)S(1)}, bf16[256,1024]{1,0:T(8,128)(2,1)S(1)}, u32[]{:S(2)}, u32[]{:S(2)}) collective-permute-start(bf16[256,1024]{1,0:T(8,128)(2,1)S(1)} %collective-permute-done.2.refs_3_), channel_id=1, source_target_pairs={{0,32},{16,48},{32,64},{48,80},{64,96},{80,112},{96,0},{112,16},{1... | collective-permute-start | bytes 1572872 | tf_op jit(solution)/shard_map/ppermute | solution.py:463
  29.6 20.4 %collective-permute-start.9 = (bf16[256,1024]{1,0:T(8,128)(2,1)S(1)}, bf16[256,1024]{1,0:T(8,128)(2,1)S(1)}, u32[]{:S(2)}, u32[]{:S(2)}) collective-permute-start(bf16[256,1024]{1,0:T(8,128)(2,1)S(1)} %collective-permute-done.2.refs_3_), channel_id=1, source_target_pairs={{0,96},{16,112},{32,0},{48,16},{64,32},{80,48},{96,64},{112,80},{1... | collective-permute-start | bytes 1572872 | tf_op jit(solution)/shard_map/ppermute | solution.py:464
  32.8 17.2 %collective-permute-start.10 = (bf16[256,512]{1,0:T(8,128)(2,1)S(1)}, bf16[256,512]{1,0:T(8,128)(2,1)S(1)}, u32[]{:S(2)}, u32[]{:S(2)}) collective-permute-start(bf16[256,512]{1,0:T(8,128)(2,1)S(1)} %collective-permute-done.6.refs_0_), channel_id=1, source_target_pairs={{0,16},{16,0},{32,48},{48,32},{64,80},{80,64},{96,112},{112,96},{1... | collective-permute-start | bytes 786440 | tf_op jit(solution)/shard_map/ppermute | solution.py:465
  33.5 16.5 %collective-permute-start.11 = (bf16[256,512]{1,0:T(8,128)(2,1)S(1)}, bf16[256,512]{1,0:T(8,128)(2,1)S(1)}, u32[]{:S(2)}, u32[]{:S(2)}) collective-permute-start(bf16[256,512]{1,0:T(8,128)(2,1)S(1)} %collective-permute-done.7.refs_1_), channel_id=1, source_target_pairs={{0,16},{16,0},{32,48},{48,32},{64,80},{80,64},{96,112},{112,96},{1... | collective-permute-start | bytes 786440 | tf_op jit(solution)/shard_map/ppermute | solution.py:466
  52.8 6.0 %collective-permute-start.12 = (bf16[256,128]{1,0:T(8,128)(2,1)S(1)}, bf16[256,128]{1,0:T(8,128)(2,1)S(1)}, u32[]{:S(2)}, u32[]{:S(2)}) collective-permute-start(bf16[256,128]{1,0:T(8,128)(2,1)S(1)} %value.1.v_own), channel_id=1, source_target_pairs={{0,2},{1,3},{2,0},{3,1},{4,6},{5,7},{6,4},{7,5},{8,10},{9,11},{10,... | collective-permute-start | bytes 196616 | tf_op jit(solution)/shard_map/ppermute | solution.py:416
  58.8 11.9 %collective-permute-start.15 = (bf16[512,128]{1,0:T(8,128)(2,1)S(1)}, bf16[512,128]{1,0:T(8,128)(2,1)S(1)}, u32[]{:S(2)}, u32[]{:S(2)}) collective-permute-start(bf16[512,128]{1,0:T(8,128)(2,1)S(1)} %pad_maximum_fusion.1), channel_id=1, source_target_pairs={{0,4},{1,5},{2,6},{3,7},{4,0},{5,1},{6,2},{7,3},{8,12},{9,13},{10,... | collective-permute-start | bytes 393224 | tf_op jit(solution)/shard_map/ppermute | solution.py:416
  58.9 11.8 %collective-permute-start.16 = (bf16[512,128]{1,0:T(8,128)(2,1)S(1)}, bf16[512,128]{1,0:T(8,128)(2,1)S(1)}, u32[]{:S(2)}, u32[]{:S(2)}) collective-permute-start(bf16[512,128]{1,0:T(8,128)(2,1)S(1)} %pad_maximum_fusion.1), channel_id=1, source_target_pairs={{0,8},{1,9},{2,10},{3,11},{4,12},{5,13},{6,14},{7,15},{8,0},{9,1},... | collective-permute-start | bytes 393224 | tf_op jit(solution)/shard_map/ppermute | solution.py:416
  61.9 8.9 %collective-permute-start.17 = (bf16[512,128]{1,0:T(8,128)(2,1)S(1)}, bf16[512,128]{1,0:T(8,128)(2,1)S(1)}, u32[]{:S(2)}, u32[]{:S(2)}) collective-permute-start(bf16[512,128]{1,0:T(8,128)(2,1)S(1)} %pad_maximum_fusion.1), channel_id=1, source_target_pairs={{0,12},{1,13},{2,14},{3,15},{4,8},{5,9},{6,10},{7,11},{8,4},{9,5},... | collective-permute-start | bytes 393224 | tf_op jit(solution)/shard_map/ppermute | solution.py:416
  70.9 5.9 %collective-permute-start.18 = (bf16[2048,128]{1,0:T(8,128)(2,1)S(1)}, bf16[2048,128]{1,0:T(8,128)(2,1)S(1)}, u32[]{:S(2)}, u32[]{:S(2)}) collective-permute-start(bf16[2048,128]{1,0:T(8,128)(2,1)S(1)} %pad_maximum_fusion), channel_id=1, source_target_pairs={{0,1},{1,0},{2,3},{3,2},{4,5},{5,4},{6,7},{7,6},{8,9},{9,8},{10,11... | collective-permute-start | bytes 1572872 | tf_op jit(solution)/shard_map/ppermute | solution.py:416
  84.5 1.3 collective-permute-start.19
  85.7 8.0 %collective-permute-start.20 = (f32[16,128]{1,0:T(8,128)S(1)}, f32[16,128]{1,0:T(8,128)S(1)}, u32[]{:S(2)}, u32[]{:S(2)}) collective-permute-start(f32[16,128]{1,0:T(8,128)S(1)} %add.77), channel_id=1, source_target_pairs={{0,2},{1,3},{2,0},{3,1},{4,6},{5,7},{6,4},{7,5},{8,10},{9,11},{10,... | collective-permute-start | bytes 24584 | tf_op jit(solution)/shard_map/ppermute | solution.py:416
  93.7 5.2 %collective-permute-start.21 = (f32[16,128]{1,0:T(8,128)S(1)}, f32[16,128]{1,0:T(8,128)S(1)}, u32[]{:S(2)}, u32[]{:S(2)}) collective-permute-start(f32[16,128]{1,0:T(8,128)S(1)} %add.78), channel_id=1, source_target_pairs={{0,4},{1,5},{2,6},{3,7},{4,0},{5,1},{6,2},{7,3},{8,12},{9,13},{10,... | collective-permute-start | bytes 24584 | tf_op jit(solution)/shard_map/ppermute | solution.py:416
  99.0 26.3 %collective-permute-start.22 = (f32[16,128]{1,0:T(8,128)S(1)}, f32[16,128]{1,0:T(8,128)S(1)}, u32[]{:S(2)}, u32[]{:S(2)}) collective-permute-start(f32[16,128]{1,0:T(8,128)S(1)} %add.79), channel_id=1, source_target_pairs={{0,12},{1,13},{2,14},{3,15},{4,8},{5,9},{6,10},{7,11},{8,4},{9,5},... | collective-permute-start | bytes 24584 | tf_op jit(solution)/shard_map/ppermute | solution.py:416
  (20 other events, 191.8 us)

commit v7 on v6

--- a/solution.py
+++ b/solution.py
@@ -232,7 +232,7 @@
 
 
 def stats_kernel(
-    begin, heads, rows, levels, weight, first, count, part,
+    heads, wide, rows, levels, weight, first, count, part,
     place, info, early, codes, book, cos_k, sin_k, keys_n, keys_d, q_before, kv_before, wq, wk, *refs,
 ):
     pieces = refs[:-17]
@@ -242,26 +242,24 @@
     ) = refs[-17:]
     own = token_rank() * rows
     mine = token_rank() // 2
-    columns = pl.ds(begin * HD, heads * HD)
     loads = fetch(pieces, x_s, lambda j: x_sems.at[j])
     weights = []
     for n in range(count):
         at = shard_rows(place, first + n, part)
-        row = [pltpu.make_async_copy(wq.at[at, columns], wq_s.at[n], w_sems.at[2 * n])]
-        if begin == 0:
-            row.append(pltpu.make_async_copy(wk.at[at, :], wk_s.at[n], w_sems.at[2 * n + 1]))
-        weights.append(row)
-    before = [pltpu.make_async_copy(q_before.at[:, columns], q_s, sems.at[0])]
-    if begin == 0:
-        before.append(pltpu.make_async_copy(kv_before.at[:, :HD], true_s, sems.at[1]))
+        weights.append([
+            pltpu.make_async_copy(wq.at[at, :], wq_s.at[n], w_sems.at[2 * n]),
+            pltpu.make_async_copy(wk.at[at, :], wk_s.at[n], w_sems.at[2 * n + 1]),
+        ])
+    before = [
+        pltpu.make_async_copy(q_before, q_s, sems.at[0]),
+        pltpu.make_async_copy(kv_before.at[:, :HD], true_s, sems.at[1]),
+    ]
     tables = [
         pltpu.make_async_copy(cos_k.at[mine], cos_q, sems.at[2]),
         pltpu.make_async_copy(sin_k.at[mine], sin_q, sems.at[3]),
     ] + interleave(keys_n, keys_d, keys, lambda j: sems.at[4 + j])
     for copy in before + loads + sum(weights, []) + tables:
         copy.start()
-    peak_s[...] = jnp.full_like(peak_s, NEG_BIG)
-    mass_s[...] = jnp.zeros_like(mass_s)
     for copy in before + loads:
         copy.wait()
     for n in range(count):
@@ -269,24 +267,26 @@
             copy.wait()
         x = x_s[:, n * part : (n + 1) * part]
         q_s[...] += jnp.dot(x, wq_s[n], preferred_element_type=jnp.float32)
-        if begin == 0:
-            true_s[...] += jnp.dot(x, wk_s[n], preferred_element_type=jnp.float32)
-    if begin == 0:
-        code = codes[...]
-        for level in range(levels):
-            entry = weight * (book[level : level + 1, :] - true_s[...])
-            bins[level : level + 1, :] = jnp.sum(
-                jnp.where(code == level, entry, 0.0), axis=0, keepdims=True
-            )
-    else:
-        bins[...] = jnp.zeros_like(bins)
+        true_s[...] += jnp.dot(x, wk_s[n], preferred_element_type=jnp.float32)
+    code = codes[...]
+    for level in range(levels):
+        entry = weight * (book[level : level + 1, :] - true_s[...])
+        bins[level : level + 1, :] = jnp.sum(
+            jnp.where(code == level, entry, 0.0), axis=0, keepdims=True
+        )
     for copy in tables:
         copy.wait()
-    for h in range(heads):
+    for h in range(wide):
         x = q_s[:, h * HD : (h + 1) * HD]
         turned = (x * cos_q[...] + pltpu.roll(x, HD // 2, 1) * sin_q[...]).astype(jnp.bfloat16)
         q_rot[h] = turned
         q_t[h] = turned.T
+    scan_totals(own, info, early, rows, 0, heads, q_t, keys, peak_s, mass_s, log_total)
+
+
+def scan_totals(own, info, early, rows, begin, heads, q_t, keys, peak_s, mass_s, log_total):
+    peak_s[...] = jnp.full_like(peak_s, NEG_BIG)
+    mass_s[...] = jnp.zeros_like(mass_s)
 
     def body(b, masked):
         base = pl.multiple_of(b * BLOCK, BLOCK)
@@ -294,7 +294,7 @@
         if masked:
             seen = visible_block(base, BLOCK, own, early[...], rows)
         for h in range(heads):
-            t = lax.dot_general(k, q_t[h], NN, preferred_element_type=jnp.float32)
+            t = lax.dot_general(k, q_t[begin + h], NN, preferred_element_type=jnp.float32)
             t = t * (SCALE * LOG2E)
             if masked:
                 t = jnp.where(seen, t, NEG_BIG)
@@ -308,18 +308,30 @@
     log_total[...] = peak_s[...] + jnp.log(mass_s[...]) * LOG2E
 
 
+def late_stats_kernel(
+    begin, heads, rows, info, early, q_t, keys_n, keys_d, log_total, peak_s, mass_s, keys, sems,
+):
+    copies = interleave(keys_n, keys_d, keys, lambda j: sems.at[j])
+    for copy in copies:
+        copy.start()
+    for copy in copies:
+        copy.wait()
+    own = token_rank() * rows
+    scan_totals(own, info, early, rows, begin, heads, q_t, keys, peak_s, mass_s, log_total)
+
+
 def grad_kernel(
     heads, rows, levels,
-    info, q_rot_0, q_t_0, log_total_0, q_rot_1, q_t_1, log_total_1, early, cot, cot_t, init,
+    info, q_rot, q_t, log_total_0, log_total_1, early, cot, cot_t, init,
     keys_n, keys_d, cos_n, cos_d, sin_n, sin_d, codes_n, codes_d, v_own, v_x, v_y1, v_y2, v_y3, v_core,
-    out, bins, probs_s, out_s, delta_s, acc_s, values, keys, cos_k, sin_k, codes, sems,
+    out, bins, probs_s, out_s, delta_s, acc_s, values, keys, cos_k, sin_k, codes, held, sems,
 ):
     me = token_rank()
     own, first = me * rows, info[0]
     part = heads // 2
-    q_rot = [q_rot_0.at[h] for h in range(part)] + [q_rot_1.at[h] for h in range(part)]
-    q_t = [q_t_0.at[h] for h in range(part)] + [q_t_1.at[h] for h in range(part)]
-    log_total = [ref.at[h : h + 1, :] for ref in (log_total_0, log_total_1) for h in range(part)]
+    early_heads = log_total_0.shape[0]
+    log_total = [log_total_0.at[h : h + 1, :] for h in range(early_heads)]
+    log_total += [log_total_1.at[h : h + 1, :] for h in range(heads - early_heads)]
     copies = interleave(keys_n, keys_d, keys, lambda j: sems.at[16 + j])
     for j, (bits, ref, at) in enumerate(slots((v_own, v_x, v_y1, v_y2, v_y3, v_core))):
         start = pl.multiple_of((me ^ bits) * rows, rows)
@@ -344,7 +356,7 @@
         if masked:
             seen = visible_block(base, BLOCK, own, early[...], rows)
         for h in range(heads):
-            s = lax.dot_general(k, q_t[h][...], NN, preferred_element_type=jnp.float32)
+            s = lax.dot_general(k, q_t[h], NN, preferred_element_type=jnp.float32)
             p = jnp.exp2(s * (SCALE * LOG2E) - log_total[h][...])
             if masked:
                 p = jnp.where(seen, p, 0.0)
@@ -364,15 +376,7 @@
     for copy in late:
         copy.wait()
 
-    @pl.loop(first, last)
-    def _(b):
-        base = pl.multiple_of(b * BLOCK, BLOCK)
-        v = values[pl.ds(base, BLOCK), :]
-        dk = jnp.zeros((BLOCK, HD), jnp.float32)
-        for h in range(heads):
-            dp = lax.dot_general(v, cot_t[h], NN, preferred_element_type=jnp.float32)
-            ds = (probs_s[b - first, h] * (dp - delta_s[h : h + 1, :])).astype(jnp.bfloat16)
-            dk = dk + lax.dot_general(ds, q_rot[h][...], NN, preferred_element_type=jnp.float32)
+    def add_bins(b, dk):
         dk = dk * SCALE
         cosine, sine = cos_k[b].reshape(BLOCK, HD), sin_k[b].reshape(BLOCK, HD)
         g = dk * cosine - pltpu.roll(dk, HD // 2, 1) * sine
@@ -381,6 +385,21 @@
             chosen = jnp.where(code == level, g, 0.0)
             acc_s[level] += jnp.sum(chosen.reshape(BLOCK // 8, 8, HD), axis=0)
 
+    held[...] = jnp.zeros_like(held)
+
+    @pl.loop(first, last)
+    def _(b):
+        base = pl.multiple_of(b * BLOCK, BLOCK)
+        v = values[pl.ds(base, BLOCK), :]
+        add_bins(jnp.maximum(b - 1, first), held[...])
+        dk = jnp.zeros((BLOCK, HD), jnp.float32)
+        for h in range(heads):
+            dp = lax.dot_general(v, cot_t[h], NN, preferred_element_type=jnp.float32)
+            ds = (probs_s[b - first, h] * (dp - delta_s[h : h + 1, :])).astype(jnp.bfloat16)
+            dk = dk + lax.dot_general(ds, q_rot[h], NN, preferred_element_type=jnp.float32)
+        held[...] = dk
+
+    add_bins(last - 1, held[...])
     bins[...] = init[...] + jnp.sum(acc_s[...], axis=1)
 
 
@@ -524,14 +543,18 @@
     distant = prep(False, after(value)(inverse[None, :]), packed[5])
     keys = distant[0]
 
-    def log_totals(begin, count, place):
-        return pl.pallas_call(
+    count = heads * 3 // 8
+    totals = []
+
+    def second(pair):
+        pair, ready = lax.optimization_barrier((pair, place))
+        found = pl.pallas_call(
             functools.partial(
-                stats_kernel, begin, count, rows, levels, levels / total, half, half, part
+                stats_kernel, count, heads, rows, levels, levels / total, half, half, part
             ),
             out_shape=(
-                jax.ShapeDtypeStruct((count, rows, HD), bf16),
-                jax.ShapeDtypeStruct((count, HD, rows), bf16),
+                jax.ShapeDtypeStruct((heads, rows, HD), bf16),
+                jax.ShapeDtypeStruct((heads, HD, rows), bf16),
                 jax.ShapeDtypeStruct((count, rows), f32),
                 jax.ShapeDtypeStruct((levels, HD), f32),
             ),
@@ -542,9 +565,9 @@
             + [
                 pltpu.VMEM((ranks // 2, 2, rows, HD), bf16),
                 pltpu.VMEM((rows, half * part), bf16),
-                pltpu.VMEM((half, part, count * HD), bf16),
+                pltpu.VMEM((half, part, width), bf16),
                 pltpu.VMEM((half, part, HD), bf16),
-                pltpu.VMEM((rows, count * HD), f32),
+                pltpu.VMEM((rows, width), f32),
                 pltpu.VMEM((rows, HD), f32),
                 pltpu.SemaphoreType.DMA((len(rest),)),
                 pltpu.SemaphoreType.DMA((2 * half,)),
@@ -554,21 +577,26 @@
             cost_estimate=cost(1 << 34, 0),
             name="stats",
         )(
-            place, info, early, key_codes, book, near[1], near[2], near[0], distant[0],
+            ready, info, early, key_codes, book, near[1], near[2], near[0], distant[0],
             q_sum, kv_sum, w_query, w_key, *rest,
         )
-
-    totals = []
-
-    def second(pair):
-        pair, ready = lax.optimization_barrier((pair, place))
-        totals.extend(log_totals(0, heads // 2, ready))
+        totals.extend(found)
         return pair
 
     values = everyone(value, after(keys), second, lambda v: after(totals[2])(v))
-    q_rot_0, q_t_0, log_total_0, init = totals
-    late, _ = lax.optimization_barrier((place, values[2:5]))
-    q_rot_1, q_t_1, log_total_1, _ = log_totals(heads // 2, heads // 2, late)
+    q_rot, q_t, log_total_0, init = totals
+    late, _ = lax.optimization_barrier((q_t, values[2:5]))
+    log_total_1 = pl.pallas_call(
+        functools.partial(late_stats_kernel, count, heads - count, rows),
+        out_shape=jax.ShapeDtypeStruct((heads - count, rows), f32),
+        in_specs=[smem()] + [vmem()] * 2 + [anywhere()] * 2,
+        out_specs=vmem(),
+        scratch_shapes=[pltpu.VMEM((heads - count, rows), f32)] * 2
+        + [pltpu.VMEM((ranks // 2, 2, rows, HD), bf16), pltpu.SemaphoreType.DMA((2,))],
+        compiler_params=pltpu.CompilerParams(vmem_limit_bytes=32 << 20),
+        cost_estimate=cost(1 << 34, 0),
+        name="stats_late",
+    )(info, early, late, near[0], distant[0])
 
     most = total // BLOCK
     attention_out, local = pl.pallas_call(
@@ -577,7 +605,7 @@
             jax.ShapeDtypeStruct((rows, width), bf16),
             jax.ShapeDtypeStruct((levels, HD), f32),
         ),
-        in_specs=[smem()] + [vmem()] * 10 + [anywhere()] * 14,
+        in_specs=[smem()] + [vmem()] * 8 + [anywhere()] * 14,
         out_specs=(vmem(),) * 2,
         scratch_shapes=[
             pltpu.VMEM((min(most, 7), heads, BLOCK, rows), f32),
@@ -589,13 +617,14 @@
             pltpu.VMEM((ranks // 2, 2, rows, HD), f32),
             pltpu.VMEM((ranks // 2, 2, rows, HD), f32),
             pltpu.VMEM((ranks // 2, 2, rows, HD), bf16),
+            pltpu.VMEM((BLOCK, HD), f32),
             pltpu.SemaphoreType.DMA((24,)),
         ],
         compiler_params=pltpu.CompilerParams(vmem_limit_bytes=44 << 20),
         cost_estimate=cost(8 * rows * width * total, 8 << 20),
         name="grad",
     )(
-        info, q_rot_0, q_t_0, log_total_0, q_rot_1, q_t_1, log_total_1, early, cotangent, cot_t, init,
+        info, q_rot, q_t, log_total_0, log_total_1, early, cotangent, cot_t, init,
         *[table for both in zip(near, distant) for table in both], *values,
     )
     for d in (1, 2, 4, 12):

time: 127 us -> 124 us (0.976)
  Pallas kernels: 41.6 us -> 39.1 us
  starting transfers between devices: 64.3 us -> 62.9 us
    pallas_call x2, Pallas kernels: 11.9 us -> 9.69 us  [the longest x1 8.06 us: second(): pl.pallas_call(functools.partial(stats_kernel, count, heads, rows, levels...]
    ppermute x14, starting transfers between devices: 47.1 us -> 45.6 us  [shards(): lax.ppermute(x, 'tokens', [(i, i ^ d) for i in range(ranks)])]
    unnamed x46 -> x48, local copies, waits for them, and re-layouts: 5.67 us -> 6.35 us
  transfers between devices with their start and end apart: 23 -> 23, of which waited for: 6 -> 7; matrix products, arithmetic and copies ran while one was open for 5% -> 5% of each run, Pallas kernels for 27% -> 26%
where the time goes in v7:
time: 124 us; the launch traced here: 123 us
  starting transfers between devices  62.9 us (51%)
  Pallas kernels  39.1 us (32%)
  waiting for transfers between devices  10.8 us (9%)
  local copies, waits for them, and re-layouts  7.96 us (6%)
    ppermute x14, starting transfers between devices, shards(): lax.ppermute(x, 'tokens', [(i, i ^ d) for i in range(ranks)])  45.6 us
    pallas_call x2, Pallas kernels, prep(): pl.pallas_call(functools.partial(prep_kernel, near, rows, few, levels), o...  11.7 us
    ppermute x14, waiting for transfers between devices, shards(): lax.ppermute(x, 'tokens', [(i, i ^ d) for i in range(ranks)])  10.7 us
    pallas_call x1, Pallas kernels, second(): pl.pallas_call(functools.partial(stats_kernel, count, heads, rows, levels...  8.06 us
    pallas_call x1, Pallas kernels, shards(): pl.pallas_call(functools.partial(grad_kernel, heads, rows, levels), out_s...  7.26 us
    unnamed x48, local copies, waits for them, and re-layouts  6.35 us
    pallas_call x1, Pallas kernels, shards(): pl.pallas_call(functools.partial(project_kernel, half, part), out_shape=(...  6.2 us
    ppermute x1, starting transfers between devices, shards(): other_high = send(other, perm=down)  3.23 us
  transfers between devices with their start and end apart: 23, of which 7 were waited for; matrix products, arithmetic and copies ran while one was open for 5% of the time, Pallas kernels for 26%

profile of v7, /device:TPU:0, one launch (start us, length us, event | category | flops | bytes accessed | tf_op | source)
XLA Modules:
  0.0 123.0 jit_solution(9663227349235758992)
XLA Ops:
  0.6 2.1 %collective-permute-start = (bf16[256,1024]{1,0:T(8,128)(2,1)}, bf16[256,1024]{1,0:T(8,128)(2,1)S(1)}, u32[]{:S(2)}, u32[]{:S(2)}) collective-permute-start(bf16[256,1024]{1,0:T(8,128)(2,1)} %refs_0_.1), channel_id=1, source_target_pairs={{0,32},{16,48},{32,64},{48,80},{64,96},{80,112},{96,0},{112,16},{1... | collective-permute-start | bytes 1572872 | tf_op jit(solution)/shard_map/ppermute | solution.py:452
  2.7 2.2 %collective-permute-start.1 = (bf16[256,1024]{1,0:T(8,128)(2,1)}, bf16[256,1024]{1,0:T(8,128)(2,1)S(1)}, u32[]{:S(2)}, u32[]{:S(2)}) collective-permute-start(bf16[256,1024]{1,0:T(8,128)(2,1)} %refs_0_.1), channel_id=1, source_target_pairs={{0,96},{16,112},{32,0},{48,16},{64,32},{80,48},{96,64},{112,80},{1... | collective-permute-start | bytes 1572872 | tf_op jit(solution)/shard_map/ppermute | solution.py:453
  4.9 3.0 %collective-permute-start.2 = (bf16[256,1024]{1,0:T(8,128)(2,1)}, bf16[256,1024]{1,0:T(8,128)(2,1)S(1)}, u32[]{:S(2)}, u32[]{:S(2)}) collective-permute-start(bf16[256,1024]{1,0:T(8,128)(2,1)} %refs_0_.1), channel_id=1, source_target_pairs={{0,16},{16,0},{32,48},{48,32},{64,80},{80,64},{96,112},{112,96},{1... | collective-permute-start | bytes 1572872 | tf_op jit(solution)/shard_map/ppermute | solution.py:454
  9.5 1.7 %collective-permute-start.3 = (bf16[272,128]{1,0:T(8,128)(2,1)}, bf16[272,128]{1,0:T(8,128)(2,1)S(1)}, u32[]{:S(2)}, u32[]{:S(2)}) collective-permute-start(bf16[272,128]{1,0:T(8,128)(2,1)} %get-tuple-element.36.refs_0_), channel_id=1, source_target_pairs={{0,4},{1,5},{2,6},{3,7},{4,0},{5,1},{6,2},{7,3},{8,12},{9,13},{10,... | collective-permute-start | bytes 208904 | tf_op jit(solution)/shard_map/ppermute | solution.py:435
  11.2 2.9 %collective-permute-start.4 = (bf16[272,128]{1,0:T(8,128)(2,1)}, bf16[272,128]{1,0:T(8,128)(2,1)S(1)}, u32[]{:S(2)}, u32[]{:S(2)}) collective-permute-start(bf16[272,128]{1,0:T(8,128)(2,1)} %get-tuple-element.36.refs_0_), channel_id=1, source_target_pairs={{0,8},{1,9},{2,10},{3,11},{4,12},{5,13},{6,14},{7,15},{8,0},{9,1},... | collective-permute-start | bytes 208904 | tf_op jit(solution)/shard_map/ppermute | solution.py:435
  18.4 2.9 %collective-permute-done.5.refs_3_ = bf16[272,128]{1,0:T(8,128)(2,1)S(1)} collective-permute-done((bf16[272,128]{1,0:T(8,128)(2,1)}, bf16[272,128]{1,0:T(8,128)(2,1)S(1)}, u32[]{:S(2)}, u32[]{:S(2)}) %collective-permute-start.5) | collective-permute-done | bytes 69664 | tf_op jit(solution)/shard_map/ppermute | solution.py:435
  23.5 3.1 %collective-permute-start.7 = (bf16[256,512]{1,0:T(8,128)(2,1)}, bf16[256,512]{1,0:T(8,128)(2,1)S(1)}, u32[]{:S(2)}, u32[]{:S(2)}) collective-permute-start(bf16[256,512]{1,0:T(8,128)(2,1)} %slice.7), channel_id=1, source_target_pairs={{0,96},{16,112},{32,0},{48,16},{64,32},{80,48},{96,64},{112,80},{1... | collective-permute-start | bytes 786440 | tf_op jit(solution)/shard_map/ppermute | solution.py:481
  29.6 3.2 %collective-permute-start.9 = (bf16[256,1024]{1,0:T(8,128)(2,1)S(1)}, bf16[256,1024]{1,0:T(8,128)(2,1)S(1)}, u32[]{:S(2)}, u32[]{:S(2)}) collective-permute-start(bf16[256,1024]{1,0:T(8,128)(2,1)S(1)} %collective-permute-done.2.refs_3_), channel_id=1, source_target_pairs={{0,96},{16,112},{32,0},{48,16},{64,32},{80,48},{96,64},{112,80},{1... | collective-permute-start | bytes 1572872 | tf_op jit(solution)/shard_map/ppermute | solution.py:483
  33.5 2.8 %collective-permute-start.11 = (bf16[256,512]{1,0:T(8,128)(2,1)S(1)}, bf16[256,512]{1,0:T(8,128)(2,1)S(1)}, u32[]{:S(2)}, u32[]{:S(2)}) collective-permute-start(bf16[256,512]{1,0:T(8,128)(2,1)S(1)} %collective-permute-done.7.refs_1_), channel_id=1, source_target_pairs={{0,16},{16,0},{32,48},{48,32},{64,80},{80,64},{96,112},{112,96},{1... | collective-permute-start | bytes 786440 | tf_op jit(solution)/shard_map/ppermute | solution.py:485
  36.3 6.2 %project.1 = (f32[256,1024]{1,0:T(8,128)S(1)}, f32[256,256]{1,0:T(8,128)S(1)}) custom-call(s32[8]{0:T(128)S(1)} %stack.35.place, bf16[8192,1024]{1,0:T(8,128)(2,1)} %wq.3, bf16[8192,128]{1,0:T(8,128)(2,1)} %wk.3, bf16[8192,128]{1,0:T(8,128)(2,1)} %w.1, bf16[256,1024]{1,0:T(8,128)(2,1)S(1)} %copy-done.6, bf16[256,1024]{1,0:T(8,128)(2,1)S(1)} %collective-permute-done.refs_1_, ...), custom_call_target="tpu_custom_call" | custom-call | flops 17179869184 | tf_op jit(solution)/shard_map/project/pallas_call | solution.py:489
  43.6 6.4 %prep.3 = (bf16[8,256,128]{2,1,0:T(8,128)(2,1)}, f32[8,256,128]{2,1,0:T(8,128)}, f32[8,256,128]{2,1,0:T(8,128)}, bf16[8,256,128]{2,1,0:T(8,128)(2,1)}, bf16[8,128,256]{2,1,0:T(8,128)(2,1)}) custom-call(f32[1,128]{1,0:T(1,128)} %fusion.2.inverse, f32[16,128]{1,0:T(8,128)} %bitcast.12, bf16[272,128]{1,0:T(8,128)(2,1)} %get-tuple-element.36.refs_0_, ...), custom_call_target="tpu_custom_call" | custom-call | tf_op jit(solution)/shard_map/prep/pallas_call | solution.py:528
  50.1 2.7 %value.1.v_own = bf16[256,128]{1,0:T(8,128)(2,1)S(1)} custom-call(s32[8]{0:T(128)S(1)} %stack.35.place, bf16[8192,128]{1,0:T(8,128)(2,1)} %w.1, f32[256,256]{1,0:T(8,128)S(1)} %get-tuple-element.43.before.kv_before, bf16[256,512]{1,0:T(8,128)(2,1)S(1)} %collective-permute-done.6.refs_0_, bf16[256,512]{1,0:T(8,128)(2,1)S(1)} %collective-permute-done.7.refs_1_, ...), custom_call_target="tpu_custom_call" | custom-call | tf_op jit(solution)/shard_map/value/pallas_call | solution.py:508
  53.5 5.3 %prep.2 = (bf16[8,256,128]{2,1,0:T(8,128)(2,1)}, f32[8,256,128]{2,1,0:T(8,128)}, f32[8,256,128]{2,1,0:T(8,128)}, bf16[8,256,128]{2,1,0:T(8,128)(2,1)}) custom-call(f32[1,128]{1,0:T(1,128)} %fusion.2.inverse, f32[16,128]{1,0:T(8,128)} %bitcast.13, bf16[2176,128]{1,0:T(8,128)(2,1)} %collective-permute-done.14.refs_0_), custom_call_target="tpu_custom_call" | custom-call | flops 4294967296 | tf_op jit(solution)/shard_map/prep/pallas_call | solution.py:528
  58.9 2.9 %collective-permute-start.16 = (bf16[512,128]{1,0:T(8,128)(2,1)S(1)}, bf16[512,128]{1,0:T(8,128)(2,1)S(1)}, u32[]{:S(2)}, u32[]{:S(2)}) collective-permute-start(bf16[512,128]{1,0:T(8,128)(2,1)S(1)} %pad_maximum_fusion.1), channel_id=1, source_target_pairs={{0,8},{1,9},{2,10},{3,11},{4,12},{5,13},{6,14},{7,15},{8,0},{9,1},... | collective-permute-start | bytes 393224 | tf_op jit(solution)/shard_map/ppermute | solution.py:435
  61.9 1.7 %collective-permute-start.17 = (bf16[512,128]{1,0:T(8,128)(2,1)S(1)}, bf16[512,128]{1,0:T(8,128)(2,1)S(1)}, u32[]{:S(2)}, u32[]{:S(2)}) collective-permute-start(bf16[512,128]{1,0:T(8,128)(2,1)S(1)} %pad_maximum_fusion.1), channel_id=1, source_target_pairs={{0,12},{1,13},{2,14},{3,15},{4,8},{5,9},{6,10},{7,11},{8,4},{9,5},... | collective-permute-start | bytes 393224 | tf_op jit(solution)/shard_map/ppermute | solution.py:435
  64.7 8.1 %stats.1 = (bf16[8,256,128]{2,1,0:T(8,128)(2,1)S(1)}, bf16[8,128,256]{2,1,0:T(8,128)(2,1)S(1)}, f32[3,256]{1,0:T(4,128)S(1)}, f32[16,128]{1,0:T(8,128)S(1)}) custom-call(s32[8]{0:T(128)S(1)} %stack.35.place, s32[2]{0:T(128)S(1)} %copy-done.11, s32[1,256]{1,0:T(1,128)S(1)} %copy-done.10, s32[256,128]{1,0:T(8,128)S(1)} %copy-done.2, f32[16,128]{1,0:T(8,128)S(1)} %bitcast.14, ...), custom_call_target="tpu_custom_call" | custom-call | flops 17179869184 | tf_op jit(solution)/shard_map/stats/pallas_call | solution.py:551
  73.0 1.6 %stats_late.1.log_total_1 = f32[5,256]{1,0:T(8,128)S(1)} custom-call(s32[2]{0:T(128)S(1)} %copy-done.11, s32[1,256]{1,0:T(1,128)S(1)} %copy-done.10, bf16[8,128,256]{2,1,0:T(8,128)(2,1)S(1)} %get-tuple-element.58.q_t, bf16[8,256,128]{2,1,0:T(8,128)(2,1)S(1)} %copy-done.7, bf16[8,256,128]{2,1,0:T(8,128)(2,1)S(1)} %copy-done.14), custom_call_target="tpu_custom_call" | custom-call | flops 17179869184 | tf_op jit(solution)/shard_map/stats_late/pallas_call | solution.py:589
  75.6 7.3 %grad.1 = (bf16[256,1024]{1,0:T(8,128)(2,1)}, f32[16,128]{1,0:T(8,128)S(1)}) custom-call(s32[2]{0:T(128)S(1)} %copy-done.11, bf16[8,256,128]{2,1,0:T(8,128)(2,1)S(1)} %get-tuple-element.54.q_rot, bf16[8,128,256]{2,1,0:T(8,128)(2,1)S(1)} %get-tuple-element.58.q_t, f32[3,256]{1,0:T(4,128)S(1)} %get-tuple-element.56.log_total_0, ...), custom_call_target="tpu_custom_call" | custom-call | flops 8589934592 | bytes 8388608 | tf_op jit(solution)/shard_map/grad/pallas_call | solution.py:602
  84.2 5.6 %collective-permute-start.20 = (f32[16,128]{1,0:T(8,128)S(1)}, f32[16,128]{1,0:T(8,128)S(1)}, u32[]{:S(2)}, u32[]{:S(2)}) collective-permute-start(f32[16,128]{1,0:T(8,128)S(1)} %add.77), channel_id=1, source_target_pairs={{0,2},{1,3},{2,0},{3,1},{4,6},{5,7},{6,4},{7,5},{8,10},{9,11},{10,... | collective-permute-start | bytes 24584 | tf_op jit(solution)/shard_map/ppermute | solution.py:435
  89.7 1.6 %collective-permute-done.20 = f32[16,128]{1,0:T(8,128)S(1)} collective-permute-done((f32[16,128]{1,0:T(8,128)S(1)}, f32[16,128]{1,0:T(8,128)S(1)}, u32[]{:S(2)}, u32[]{:S(2)}) %collective-permute-start.20) | collective-permute-done | bytes 8224 | tf_op jit(solution)/shard_map/ppermute | solution.py:435
  91.4 8.0 %collective-permute-start.21 = (f32[16,128]{1,0:T(8,128)S(1)}, f32[16,128]{1,0:T(8,128)S(1)}, u32[]{:S(2)}, u32[]{:S(2)}) collective-permute-start(f32[16,128]{1,0:T(8,128)S(1)} %add.78), channel_id=1, source_target_pairs={{0,4},{1,5},{2,6},{3,7},{4,0},{5,1},{6,2},{7,3},{8,12},{9,13},{10,... | collective-permute-start | bytes 24584 | tf_op jit(solution)/shard_map/ppermute | solution.py:435
  99.3 1.6 %collective-permute-done.21 = f32[16,128]{1,0:T(8,128)S(1)} collective-permute-done((f32[16,128]{1,0:T(8,128)S(1)}, f32[16,128]{1,0:T(8,128)S(1)}, u32[]{:S(2)}, u32[]{:S(2)}) %collective-permute-start.21) | collective-permute-done | bytes 8224 | tf_op jit(solution)/shard_map/ppermute | solution.py:435
  100.9 19.9 %collective-permute-start.22 = (f32[16,128]{1,0:T(8,128)S(1)}, f32[16,128]{1,0:T(8,128)S(1)}, u32[]{:S(2)}, u32[]{:S(2)}) collective-permute-start(f32[16,128]{1,0:T(8,128)S(1)} %add.79), channel_id=1, source_target_pairs={{0,12},{1,13},{2,14},{3,15},{4,8},{5,9},{6,10},{7,11},{8,4},{9,5},... | collective-permute-start | bytes 24584 | tf_op jit(solution)/shard_map/ppermute | solution.py:435
  120.8 1.6 %collective-permute-done.22 = f32[16,128]{1,0:T(8,128)S(1)} collective-permute-done((f32[16,128]{1,0:T(8,128)S(1)}, f32[16,128]{1,0:T(8,128)S(1)}, u32[]{:S(2)}, u32[]{:S(2)}) %collective-permute-start.22) | collective-permute-done | bytes 8224 | tf_op jit(solution)/shard_map/ppermute | solution.py:435
  (89 shorter events, 17.5 us)
Async XLA Ops:
  0.6 35.7 %copy-start.6 = (bf16[256,1024]{1,0:T(8,128)(2,1)S(1)}, bf16[256,1024]{1,0:T(8,128)(2,1)}, u32[]{:S(2)}) copy-start(bf16[256,1024]{1,0:T(8,128)(2,1)} %refs_0_.1) | copy-start | bytes 1572868
  0.6 22.0 %collective-permute-start = (bf16[256,1024]{1,0:T(8,128)(2,1)}, bf16[256,1024]{1,0:T(8,128)(2,1)S(1)}, u32[]{:S(2)}, u32[]{:S(2)}) collective-permute-start(bf16[256,1024]{1,0:T(8,128)(2,1)} %refs_0_.1), channel_id=1, source_target_pairs={{0,32},{16,48},{32,64},{48,80},{64,96},{80,112},{96,0},{112,16},{1... | collective-permute-start | bytes 1572872 | tf_op jit(solution)/shard_map/ppermute | solution.py:452
  2.7 19.9 %collective-permute-start.1 = (bf16[256,1024]{1,0:T(8,128)(2,1)}, bf16[256,1024]{1,0:T(8,128)(2,1)S(1)}, u32[]{:S(2)}, u32[]{:S(2)}) collective-permute-start(bf16[256,1024]{1,0:T(8,128)(2,1)} %refs_0_.1), channel_id=1, source_target_pairs={{0,96},{16,112},{32,0},{48,16},{64,32},{80,48},{96,64},{112,80},{1... | collective-permute-start | bytes 1572872 | tf_op jit(solution)/shard_map/ppermute | solution.py:453
  4.9 17.7 %collective-permute-start.2 = (bf16[256,1024]{1,0:T(8,128)(2,1)}, bf16[256,1024]{1,0:T(8,128)(2,1)S(1)}, u32[]{:S(2)}, u32[]{:S(2)}) collective-permute-start(bf16[256,1024]{1,0:T(8,128)(2,1)} %refs_0_.1), channel_id=1, source_target_pairs={{0,16},{16,0},{32,48},{48,32},{64,80},{80,64},{96,112},{112,96},{1... | collective-permute-start | bytes 1572872 | tf_op jit(solution)/shard_map/ppermute | solution.py:454
  9.5 6.1 %collective-permute-start.3 = (bf16[272,128]{1,0:T(8,128)(2,1)}, bf16[272,128]{1,0:T(8,128)(2,1)S(1)}, u32[]{:S(2)}, u32[]{:S(2)}) collective-permute-start(bf16[272,128]{1,0:T(8,128)(2,1)} %get-tuple-element.36.refs_0_), channel_id=1, source_target_pairs={{0,4},{1,5},{2,6},{3,7},{4,0},{5,1},{6,2},{7,3},{8,12},{9,13},{10,... | collective-permute-start | bytes 208904 | tf_op jit(solution)/shard_map/ppermute | solution.py:435
  11.2 6.6 %collective-permute-start.4 = (bf16[272,128]{1,0:T(8,128)(2,1)}, bf16[272,128]{1,0:T(8,128)(2,1)S(1)}, u32[]{:S(2)}, u32[]{:S(2)}) collective-permute-start(bf16[272,128]{1,0:T(8,128)(2,1)} %get-tuple-element.36.refs_0_), channel_id=1, source_target_pairs={{0,8},{1,9},{2,10},{3,11},{4,12},{5,13},{6,14},{7,15},{8,0},{9,1},... | collective-permute-start | bytes 208904 | tf_op jit(solution)/shard_map/ppermute | solution.py:435
  15.6 5.7 %collective-permute-start.5 = (bf16[272,128]{1,0:T(8,128)(2,1)}, bf16[272,128]{1,0:T(8,128)(2,1)S(1)}, u32[]{:S(2)}, u32[]{:S(2)}) collective-permute-start(bf16[272,128]{1,0:T(8,128)(2,1)} %get-tuple-element.36.refs_0_), channel_id=1, source_target_pairs={{0,12},{1,13},{2,14},{3,15},{4,8},{5,9},{6,10},{7,11},{8,4},{9,5},... | collective-permute-start | bytes 208904 | tf_op jit(solution)/shard_map/ppermute | solution.py:435
  22.0 6.8 %collective-permute-start.13 = (bf16[1088,128]{1,0:T(8,128)(2,1)}, bf16[1088,128]{1,0:T(8,128)(2,1)S(1)}, u32[]{:S(2)}, u32[]{:S(2)}) collective-permute-start(bf16[1088,128]{1,0:T(8,128)(2,1)} %get-tuple-element.69), channel_id=1, source_target_pairs={{0,2},{1,3},{2,0},{3,1},{4,6},{5,7},{6,4},{7,5},{8,10},{9,11},{10,... | collective-permute-start | bytes 835592 | tf_op jit(solution)/shard_map/ppermute | solution.py:435
  22.7 10.2 %collective-permute-start.6 = (bf16[256,512]{1,0:T(8,128)(2,1)S(1)}, bf16[256,512]{1,0:T(8,128)(2,1)S(1)}, u32[]{:S(2)}, u32[]{:S(2)}) collective-permute-start(bf16[256,512]{1,0:T(8,128)(2,1)S(1)} %slice.6), channel_id=1, source_target_pairs={{0,32},{16,48},{32,64},{48,80},{64,96},{80,112},{96,0},{112,16},{1... | collective-permute-start | bytes 786440 | tf_op jit(solution)/shard_map/ppermute | solution.py:480
  23.5 9.3 %collective-permute-start.7 = (bf16[256,512]{1,0:T(8,128)(2,1)}, bf16[256,512]{1,0:T(8,128)(2,1)S(1)}, u32[]{:S(2)}, u32[]{:S(2)}) collective-permute-start(bf16[256,512]{1,0:T(8,128)(2,1)} %slice.7), channel_id=1, source_target_pairs={{0,96},{16,112},{32,0},{48,16},{64,32},{80,48},{96,64},{112,80},{1... | collective-permute-start | bytes 786440 | tf_op jit(solution)/shard_map/ppermute | solution.py:481
  29.6 24.0 %collective-permute-start.14 = (bf16[2176,128]{1,0:T(8,128)(2,1)}, bf16[2176,128]{1,0:T(8,128)(2,1)}, u32[]{:S(2)}, u32[]{:S(2)}) collective-permute-start(bf16[2176,128]{1,0:T(8,128)(2,1)} %constant_dynamic-update-slice_fusion.4), channel_id=1, source_target_pairs={{0,1},{1,0},{2,3},{3,2},{4,5},{5,4},{6,7},{7,6},{8,9},{9,8},{10,11... | collective-permute-start | bytes 1671176 | tf_op jit(solution)/shard_map/ppermute | solution.py:435
  29.6 20.4 %collective-permute-start.8 = (bf16[256,1024]{1,0:T(8,128)(2,1)S(1)}, bf16[256,1024]{1,0:T(8,128)(2,1)S(1)}, u32[]{:S(2)}, u32[]{:S(2)}) collective-permute-start(bf16[256,1024]{1,0:T(8,128)(2,1)S(1)} %collective-permute-done.2.refs_3_), channel_id=1, source_target_pairs={{0,32},{16,48},{32,64},{48,80},{64,96},{80,112},{96,0},{112,16},{1... | collective-permute-start | bytes 1572872 | tf_op jit(solution)/shard_map/ppermute | solution.py:482
  29.6 20.4 %collective-permute-start.9 = (bf16[256,1024]{1,0:T(8,128)(2,1)S(1)}, bf16[256,1024]{1,0:T(8,128)(2,1)S(1)}, u32[]{:S(2)}, u32[]{:S(2)}) collective-permute-start(bf16[256,1024]{1,0:T(8,128)(2,1)S(1)} %collective-permute-done.2.refs_3_), channel_id=1, source_target_pairs={{0,96},{16,112},{32,0},{48,16},{64,32},{80,48},{96,64},{112,80},{1... | collective-permute-start | bytes 1572872 | tf_op jit(solution)/shard_map/ppermute | solution.py:483
  32.8 17.2 %collective-permute-start.10 = (bf16[256,512]{1,0:T(8,128)(2,1)S(1)}, bf16[256,512]{1,0:T(8,128)(2,1)S(1)}, u32[]{:S(2)}, u32[]{:S(2)}) collective-permute-start(bf16[256,512]{1,0:T(8,128)(2,1)S(1)} %collective-permute-done.6.refs_0_), channel_id=1, source_target_pairs={{0,16},{16,0},{32,48},{48,32},{64,80},{80,64},{96,112},{112,96},{1... | collective-permute-start | bytes 786440 | tf_op jit(solution)/shard_map/ppermute | solution.py:484
  33.5 16.5 %collective-permute-start.11 = (bf16[256,512]{1,0:T(8,128)(2,1)S(1)}, bf16[256,512]{1,0:T(8,128)(2,1)S(1)}, u32[]{:S(2)}, u32[]{:S(2)}) collective-permute-start(bf16[256,512]{1,0:T(8,128)(2,1)S(1)} %collective-permute-done.7.refs_1_), channel_id=1, source_target_pairs={{0,16},{16,0},{32,48},{48,32},{64,80},{80,64},{96,112},{112,96},{1... | collective-permute-start | bytes 786440 | tf_op jit(solution)/shard_map/ppermute | solution.py:485
  52.8 6.0 %collective-permute-start.12 = (bf16[256,128]{1,0:T(8,128)(2,1)S(1)}, bf16[256,128]{1,0:T(8,128)(2,1)S(1)}, u32[]{:S(2)}, u32[]{:S(2)}) collective-permute-start(bf16[256,128]{1,0:T(8,128)(2,1)S(1)} %value.1.v_own), channel_id=1, source_target_pairs={{0,2},{1,3},{2,0},{3,1},{4,6},{5,7},{6,4},{7,5},{8,10},{9,11},{10,... | collective-permute-start | bytes 196616 | tf_op jit(solution)/shard_map/ppermute | solution.py:435
  58.9 13.9 %collective-permute-start.15 = (bf16[512,128]{1,0:T(8,128)(2,1)S(1)}, bf16[512,128]{1,0:T(8,128)(2,1)S(1)}, u32[]{:S(2)}, u32[]{:S(2)}) collective-permute-start(bf16[512,128]{1,0:T(8,128)(2,1)S(1)} %pad_maximum_fusion.1), channel_id=1, source_target_pairs={{0,4},{1,5},{2,6},{3,7},{4,0},{5,1},{6,2},{7,3},{8,12},{9,13},{10,... | collective-permute-start | bytes 393224 | tf_op jit(solution)/shard_map/ppermute | solution.py:435
  58.9 13.8 %collective-permute-start.16 = (bf16[512,128]{1,0:T(8,128)(2,1)S(1)}, bf16[512,128]{1,0:T(8,128)(2,1)S(1)}, u32[]{:S(2)}, u32[]{:S(2)}) collective-permute-start(bf16[512,128]{1,0:T(8,128)(2,1)S(1)} %pad_maximum_fusion.1), channel_id=1, source_target_pairs={{0,8},{1,9},{2,10},{3,11},{4,12},{5,13},{6,14},{7,15},{8,0},{9,1},... | collective-permute-start | bytes 393224 | tf_op jit(solution)/shard_map/ppermute | solution.py:435
  61.9 10.9 %collective-permute-start.17 = (bf16[512,128]{1,0:T(8,128)(2,1)S(1)}, bf16[512,128]{1,0:T(8,128)(2,1)S(1)}, u32[]{:S(2)}, u32[]{:S(2)}) collective-permute-start(bf16[512,128]{1,0:T(8,128)(2,1)S(1)} %pad_maximum_fusion.1), channel_id=1, source_target_pairs={{0,12},{1,13},{2,14},{3,15},{4,8},{5,9},{6,10},{7,11},{8,4},{9,5},... | collective-permute-start | bytes 393224 | tf_op jit(solution)/shard_map/ppermute | solution.py:435
  72.9 2.0 %collective-permute-start.18 = (bf16[2048,128]{1,0:T(8,128)(2,1)S(1)}, bf16[2048,128]{1,0:T(8,128)(2,1)S(1)}, u32[]{:S(2)}, u32[]{:S(2)}) collective-permute-start(bf16[2048,128]{1,0:T(8,128)(2,1)S(1)} %pad_maximum_fusion), channel_id=1, source_target_pairs={{0,1},{1,0},{2,3},{3,2},{4,5},{5,4},{6,7},{7,6},{8,9},{9,8},{10,11... | collective-permute-start | bytes 1572872 | tf_op jit(solution)/shard_map/ppermute | solution.py:435
  82.9 1.3 %collective-permute-start.19 = (f32[16,128]{1,0:T(8,128)S(1)}, f32[16,128]{1,0:T(8,128)S(1)}, u32[]{:S(2)}, u32[]{:S(2)}) collective-permute-start(f32[16,128]{1,0:T(8,128)S(1)} %get-tuple-element.67), channel_id=1, source_target_pairs={{0,1},{1,0},{2,3},{3,2},{4,5},{5,4},{6,7},{7,6},{8,9},{9,8},{10,11... | collective-permute-start | bytes 24584 | tf_op jit(solution)/shard_map/ppermute | solution.py:435
  84.2 7.2 %collective-permute-start.20 = (f32[16,128]{1,0:T(8,128)S(1)}, f32[16,128]{1,0:T(8,128)S(1)}, u32[]{:S(2)}, u32[]{:S(2)}) collective-permute-start(f32[16,128]{1,0:T(8,128)S(1)} %add.77), channel_id=1, source_target_pairs={{0,2},{1,3},{2,0},{3,1},{4,6},{5,7},{6,4},{7,5},{8,10},{9,11},{10,... | collective-permute-start | bytes 24584 | tf_op jit(solution)/shard_map/ppermute | solution.py:435
  91.4 9.6 %collective-permute-start.21 = (f32[16,128]{1,0:T(8,128)S(1)}, f32[16,128]{1,0:T(8,128)S(1)}, u32[]{:S(2)}, u32[]{:S(2)}) collective-permute-start(f32[16,128]{1,0:T(8,128)S(1)} %add.78), channel_id=1, source_target_pairs={{0,4},{1,5},{2,6},{3,7},{4,0},{5,1},{6,2},{7,3},{8,12},{9,13},{10,... | collective-permute-start | bytes 24584 | tf_op jit(solution)/shard_map/ppermute | solution.py:435
  100.9 21.5 %collective-permute-start.22 = (f32[16,128]{1,0:T(8,128)S(1)}, f32[16,128]{1,0:T(8,128)S(1)}, u32[]{:S(2)}, u32[]{:S(2)}) collective-permute-start(f32[16,128]{1,0:T(8,128)S(1)} %add.79), channel_id=1, source_target_pairs={{0,12},{1,13},{2,14},{3,15},{4,8},{5,9},{6,10},{7,11},{8,4},{9,5},... | collective-permute-start | bytes 24584 | tf_op jit(solution)/shard_map/ppermute | solution.py:435
  (21 other events, 164.4 us)

commit v8 on v7

--- a/solution.py
+++ b/solution.py
@@ -17,6 +17,7 @@
 NN = (((1,), (0,)), ((), ()))
 TN = (((0,), (0,)), ((), ()))
 TAIL = 16
+STRIP = 32
 
 
 def sincos(angle):
@@ -67,17 +68,18 @@
 
 def prep_kernel(
     near, rows, ranks, levels,
-    inverse, book, *refs,
+    book, *refs,
 ):
     pieces = refs[:5] if near else refs[:1]
     if near:
-        cot, cot_t = refs[5], refs[10]
-        for h in range(cot_t.shape[0]):
-            cot_t[h] = cot[:, h * HD : (h + 1) * HD].T
-        refs = refs[:10] + refs[11:]
+        cot_f, cot_t, cot = refs[5], refs[10], refs[-1]
+        refs = refs[:10] + refs[11:-1]
     keys_f, cos_f, sin_f, codes_f, packed_s, keys, cos_k, sin_k, codes, sems, out_sems = refs[-11:]
     me = token_rank()
     tall = rows + TAIL
+    if near:
+        loading = pltpu.make_async_copy(cot_f, cot, sems.at[ranks])
+        loading.start()
     if near:
         found = [(2 * j, ref, 0) for j, ref in enumerate(pieces[:4])]
         found += [(2 * j + 1, pieces[4], j) for j in range(4)]
@@ -98,10 +100,42 @@
     eye = lax.broadcasted_iota(jnp.int32, (HD, HD), 0) == lax.broadcasted_iota(
         jnp.int32, (HD, HD), 1
     )
-    left = lax.broadcasted_iota(jnp.int32, (HD, HD), 1) < HD // 2
+    left = lax.broadcasted_iota(jnp.int32, (STRIP, HD), 1) < HD // 2
     ones = jnp.ones((2 * HD, HD), jnp.bfloat16)
     sides = rows // HD
     outs = [(keys, keys_f), (cos_k, cos_f), (sin_k, sin_f), (codes, codes_f)]
+
+    inverse = jnp.exp(
+        (lax.broadcasted_iota(jnp.int32, (1, HD), 1) % (HD // 2)).astype(jnp.float32)
+        * (-2.0 * math.log(ROPE_BASE) / HD)
+    )
+
+    def prep_strip(i, part, strip, places, source):
+        rows_of = slice(strip, strip + STRIP)
+        place = jnp.where(left, places[part][rows_of, :], places[part + 1][rows_of, :])
+        sine, cosine = sincos(place * inverse)
+        sine_r, cosine_r = pltpu.roll(sine, HD // 2, 1), pltpu.roll(cosine, HD // 2, 1)
+        tables = (
+            (jnp.where(left, cosine, cosine_r), jnp.where(left, -sine, sine_r)),
+            (jnp.where(left, cosine_r, cosine), jnp.where(left, -sine_r, sine)),
+        )
+        for side, (cosine, sine) in enumerate(tables):
+            at = (part + side) * HD + strip
+            target = pl.ds(at, STRIP)
+            cos_k[i, target, :] = cosine
+            sin_k[i, target, :] = sine
+            raw = packed_s[pl.ds(source + at, STRIP), :]
+            codes[i, target, :] = raw
+            code = raw.astype(jnp.float32).astype(jnp.int32)
+            layer = [book[e : e + 1, :] for e in range(levels)]
+            bit = 1
+            while len(layer) > 1:
+                on = (code & bit) != 0
+                layer = [jnp.where(on, layer[j + 1], layer[j]) for j in range(0, len(layer), 2)]
+                bit *= 2
+            deq = layer[0]
+            turned = deq * cosine + pltpu.roll(deq, HD // 2, 1) * sine
+            keys[i, target, :] = turned.astype(jnp.bfloat16)
 
     @pl.loop(0, ranks)
     def _(i):
@@ -114,32 +148,15 @@
             digits = jnp.concatenate([high, low], axis=1).astype(jnp.bfloat16)
             places.append(lax.dot_general(digits, ones, NN, preferred_element_type=jnp.float32))
         for part in range(0, sides, 2):
-            sine, cosine = sincos(jnp.where(left, places[part], places[part + 1]) * inverse[...])
-            sine_r, cosine_r = pltpu.roll(sine, HD // 2, 1), pltpu.roll(cosine, HD // 2, 1)
-            tables = (
-                (jnp.where(left, cosine, cosine_r), jnp.where(left, -sine, sine_r)),
-                (jnp.where(left, cosine_r, cosine), jnp.where(left, -sine_r, sine)),
-            )
-            for side, (cosine, sine) in enumerate(tables):
-                at = part + side
-                target = pl.ds(at * HD, HD)
-                cos_k[i, target, :] = cosine
-                sin_k[i, target, :] = sine
-                raw = packed_s[pl.ds(source + at * HD, HD), :]
-                codes[i, target, :] = raw
-                code = raw.astype(jnp.float32).astype(jnp.int32)
-                layer = [book[e : e + 1, :] for e in range(levels)]
-                bit = 1
-                while len(layer) > 1:
-                    on = (code & bit) != 0
-                    layer = [jnp.where(on, layer[j + 1], layer[j]) for j in range(0, len(layer), 2)]
-                    bit *= 2
-                deq = layer[0]
-                turned = deq * cosine + pltpu.roll(deq, HD // 2, 1) * sine
-                keys[i, target, :] = turned.astype(jnp.bfloat16)
+            for strip in range(0, HD, STRIP):
+                prep_strip(i, part, strip, places, source)
         for j, (ref, full) in enumerate(outs):
             pltpu.make_async_copy(ref.at[i], full.at[i], out_sems.at[j]).start()
 
+    if near:
+        loading.wait()
+        for h in range(cot_t.shape[0]):
+            cot_t[h] = cot[:, h * HD : (h + 1) * HD].T
     for j, (ref, full) in enumerate(outs):
         pltpu.make_async_copy(ref, full, out_sems.at[j]).wait()
 
@@ -465,7 +482,6 @@
         name="pack",
     )(key_codes, places)
     book = codebook.T
-    inverse = jnp.exp((jnp.arange(HD) % (HD // 2)).astype(f32) * (-2.0 * math.log(ROPE_BASE) / HD))
 
     mate = rank ^ 1
     turn = lambda x, by: (x + by) % group
@@ -521,7 +537,7 @@
         name="value",
     )(place, w_value, kv_sum, *rest)
 
-    def prep(near, inverse, *pieces):
+    def prep(near, book, *pieces):
         few = ranks // 2
         shapes = [(few, rows, HD)] * 4
         kinds = [bf16, f32, f32, bf16]
@@ -529,18 +545,19 @@
             functools.partial(prep_kernel, near, rows, few, levels),
             out_shape=[jax.ShapeDtypeStruct(size, kind) for size, kind in zip(shapes, kinds)]
             + [jax.ShapeDtypeStruct((heads, HD, rows), bf16)] * near,
-            in_specs=[vmem()] * 2 + [anywhere()] * (5 if near else 1) + [vmem()] * near,
+            in_specs=[vmem()] + [anywhere()] * len(pieces),
             out_specs=[anywhere()] * 4 + [vmem()] * near,
             scratch_shapes=[pltpu.VMEM((few * (rows + TAIL), HD), bf16)]
             + [pltpu.VMEM(size, kind) for size, kind in zip(shapes, kinds)]
-            + [pltpu.SemaphoreType.DMA((few,)), pltpu.SemaphoreType.DMA((4,))],
+            + [pltpu.SemaphoreType.DMA((few + 1,)), pltpu.SemaphoreType.DMA((4,))]
+            + [pltpu.VMEM((rows, width), bf16)] * near,
             compiler_params=pltpu.CompilerParams(vmem_limit_bytes=58 << 20),
             cost_estimate=cost(0 if near else 1 << 32, 0),
             name="prep",
-        )(inverse, book, *pieces)
-
-    *near, cot_t = prep(True, after(kv_sum)(inverse[None, :]), *packed[:5], cotangent)
-    distant = prep(False, after(value)(inverse[None, :]), packed[5])
+        )(book, *pieces)
+
+    *near, cot_t = prep(True, after(kv_sum)(book), *packed[:5], cotangent)
+    distant = prep(False, after(value)(book), packed[5])
     keys = distant[0]
 
     count = heads * 3 // 8

time: 124 us -> 124 us (level)
  transfers between devices with their start and end apart: 23 -> 23, of which waited for: 7 -> 7; matrix products, arithmetic and copies ran while one was open for 5% -> 4% of each run, Pallas kernels for 26% -> 26%
where the time goes in v8:
time: 124 us; the launch traced here: 123 us
  starting transfers between devices  63.4 us (51%)
  Pallas kernels  38.9 us (31%)
  waiting for transfers between devices  11.3 us (9%)
  local copies, waits for them, and re-layouts  7.96 us (6%)
    ppermute x14, starting transfers between devices, shards(): lax.ppermute(x, 'tokens', [(i, i ^ d) for i in range(ranks)])  46.1 us
    pallas_call x2, Pallas kernels, prep(): pl.pallas_call(functools.partial(prep_kernel, near, rows, few, levels), o...  11.5 us
    ppermute x14, waiting for transfers between devices, shards(): lax.ppermute(x, 'tokens', [(i, i ^ d) for i in range(ranks)])  11.3 us
    pallas_call x1, Pallas kernels, second(): pl.pallas_call(functools.partial(stats_kernel, count, heads, rows, levels...  8.06 us
    pallas_call x1, Pallas kernels, shards(): pl.pallas_call(functools.partial(grad_kernel, heads, rows, levels), out_s...  7.26 us
    unnamed x48, local copies, waits for them, and re-layouts  6.35 us
    pallas_call x1, Pallas kernels, shards(): pl.pallas_call(functools.partial(project_kernel, half, part), out_shape=(...  6.2 us
    ppermute x1, starting transfers between devices, shards(): other_high = send(other, perm=down)  3.23 us
  transfers between devices with their start and end apart: 23, of which 7 were waited for; matrix products, arithmetic and copies ran while one was open for 4% of the time, Pallas kernels for 26%

profile of v8, /device:TPU:0, one launch (start us, length us, event | category | flops | bytes accessed | tf_op | source)
XLA Modules:
  0.0 123.2 jit_solution(264931441727637935)
XLA Ops:
  0.6 2.1 %collective-permute-start = (bf16[256,1024]{1,0:T(8,128)(2,1)}, bf16[256,1024]{1,0:T(8,128)(2,1)S(1)}, u32[]{:S(2)}, u32[]{:S(2)}) collective-permute-start(bf16[256,1024]{1,0:T(8,128)(2,1)} %refs_0_.1), channel_id=1, source_target_pairs={{0,32},{16,48},{32,64},{48,80},{64,96},{80,112},{96,0},{112,16},{1... | collective-permute-start | bytes 1572872 | tf_op jit(solution)/shard_map/ppermute | solution.py:469
  2.7 2.2 %collective-permute-start.1 = (bf16[256,1024]{1,0:T(8,128)(2,1)}, bf16[256,1024]{1,0:T(8,128)(2,1)S(1)}, u32[]{:S(2)}, u32[]{:S(2)}) collective-permute-start(bf16[256,1024]{1,0:T(8,128)(2,1)} %refs_0_.1), channel_id=1, source_target_pairs={{0,96},{16,112},{32,0},{48,16},{64,32},{80,48},{96,64},{112,80},{1... | collective-permute-start | bytes 1572872 | tf_op jit(solution)/shard_map/ppermute | solution.py:470
  4.9 3.0 %collective-permute-start.2 = (bf16[256,1024]{1,0:T(8,128)(2,1)}, bf16[256,1024]{1,0:T(8,128)(2,1)S(1)}, u32[]{:S(2)}, u32[]{:S(2)}) collective-permute-start(bf16[256,1024]{1,0:T(8,128)(2,1)} %refs_0_.1), channel_id=1, source_target_pairs={{0,16},{16,0},{32,48},{48,32},{64,80},{80,64},{96,112},{112,96},{1... | collective-permute-start | bytes 1572872 | tf_op jit(solution)/shard_map/ppermute | solution.py:471
  9.5 1.7 %collective-permute-start.3 = (bf16[272,128]{1,0:T(8,128)(2,1)}, bf16[272,128]{1,0:T(8,128)(2,1)S(1)}, u32[]{:S(2)}, u32[]{:S(2)}) collective-permute-start(bf16[272,128]{1,0:T(8,128)(2,1)} %get-tuple-element.36.refs_0_), channel_id=1, source_target_pairs={{0,4},{1,5},{2,6},{3,7},{4,0},{5,1},{6,2},{7,3},{8,12},{9,13},{10,... | collective-permute-start | bytes 208904 | tf_op jit(solution)/shard_map/ppermute | solution.py:452
  11.2 2.9 %collective-permute-start.4 = (bf16[272,128]{1,0:T(8,128)(2,1)}, bf16[272,128]{1,0:T(8,128)(2,1)S(1)}, u32[]{:S(2)}, u32[]{:S(2)}) collective-permute-start(bf16[272,128]{1,0:T(8,128)(2,1)} %get-tuple-element.36.refs_0_), channel_id=1, source_target_pairs={{0,8},{1,9},{2,10},{3,11},{4,12},{5,13},{6,14},{7,15},{8,0},{9,1},... | collective-permute-start | bytes 208904 | tf_op jit(solution)/shard_map/ppermute | solution.py:452
  18.4 2.9 %collective-permute-done.5.refs_3_ = bf16[272,128]{1,0:T(8,128)(2,1)S(1)} collective-permute-done((bf16[272,128]{1,0:T(8,128)(2,1)}, bf16[272,128]{1,0:T(8,128)(2,1)S(1)}, u32[]{:S(2)}, u32[]{:S(2)}) %collective-permute-start.5) | collective-permute-done | bytes 69664 | tf_op jit(solution)/shard_map/ppermute | solution.py:452
  23.5 3.1 %collective-permute-start.7 = (bf16[256,512]{1,0:T(8,128)(2,1)}, bf16[256,512]{1,0:T(8,128)(2,1)S(1)}, u32[]{:S(2)}, u32[]{:S(2)}) collective-permute-start(bf16[256,512]{1,0:T(8,128)(2,1)} %slice.7), channel_id=1, source_target_pairs={{0,96},{16,112},{32,0},{48,16},{64,32},{80,48},{96,64},{112,80},{1... | collective-permute-start | bytes 786440 | tf_op jit(solution)/shard_map/ppermute | solution.py:497
  26.8 2.0 %collective-permute-done.13.refs_4_ = bf16[1088,128]{1,0:T(8,128)(2,1)S(1)} collective-permute-done((bf16[1088,128]{1,0:T(8,128)(2,1)}, bf16[1088,128]{1,0:T(8,128)(2,1)S(1)}, u32[]{:S(2)}, u32[]{:S(2)}) %collective-permute-start.13) | collective-permute-done | bytes 278560 | tf_op jit(solution)/shard_map/ppermute | solution.py:452
  29.6 3.2 %collective-permute-start.9 = (bf16[256,1024]{1,0:T(8,128)(2,1)S(1)}, bf16[256,1024]{1,0:T(8,128)(2,1)S(1)}, u32[]{:S(2)}, u32[]{:S(2)}) collective-permute-start(bf16[256,1024]{1,0:T(8,128)(2,1)S(1)} %collective-permute-done.2.refs_3_), channel_id=1, source_target_pairs={{0,96},{16,112},{32,0},{48,16},{64,32},{80,48},{96,64},{112,80},{1... | collective-permute-start | bytes 1572872 | tf_op jit(solution)/shard_map/ppermute | solution.py:499
  33.5 2.8 %collective-permute-start.11 = (bf16[256,512]{1,0:T(8,128)(2,1)S(1)}, bf16[256,512]{1,0:T(8,128)(2,1)S(1)}, u32[]{:S(2)}, u32[]{:S(2)}) collective-permute-start(bf16[256,512]{1,0:T(8,128)(2,1)S(1)} %collective-permute-done.7.refs_1_), channel_id=1, source_target_pairs={{0,16},{16,0},{32,48},{48,32},{64,80},{80,64},{96,112},{112,96},{1... | collective-permute-start | bytes 786440 | tf_op jit(solution)/shard_map/ppermute | solution.py:501
  36.3 6.2 %project.1 = (f32[256,1024]{1,0:T(8,128)S(1)}, f32[256,256]{1,0:T(8,128)S(1)}) custom-call(s32[8]{0:T(128)S(1)} %stack.35.place, bf16[8192,1024]{1,0:T(8,128)(2,1)} %wq.3, bf16[8192,128]{1,0:T(8,128)(2,1)} %wk.3, bf16[8192,128]{1,0:T(8,128)(2,1)} %w.1, bf16[256,1024]{1,0:T(8,128)(2,1)S(1)} %copy-done.6, bf16[256,1024]{1,0:T(8,128)(2,1)S(1)} %collective-permute-done.refs_1_, ...), custom_call_target="tpu_custom_call" | custom-call | flops 17179869184 | tf_op jit(solution)/shard_map/project/pallas_call | solution.py:505
  43.6 6.1 %prep.3 = (bf16[8,256,128]{2,1,0:T(8,128)(2,1)}, f32[8,256,128]{2,1,0:T(8,128)}, f32[8,256,128]{2,1,0:T(8,128)}, bf16[8,256,128]{2,1,0:T(8,128)(2,1)}, bf16[8,128,256]{2,1,0:T(8,128)(2,1)}) custom-call(f32[16,128]{1,0:T(8,128)} %bitcast.12, bf16[272,128]{1,0:T(8,128)(2,1)} %get-tuple-element.36.refs_0_, bf16[272,128]{1,0:T(8,128)(2,1)} %copy-done.18, ...), custom_call_target="tpu_custom_call" | custom-call | tf_op jit(solution)/shard_map/prep/pallas_call | solution.py:544
  49.7 2.7 %value.1.v_own = bf16[256,128]{1,0:T(8,128)(2,1)S(1)} custom-call(s32[8]{0:T(128)S(1)} %stack.35.place, bf16[8192,128]{1,0:T(8,128)(2,1)} %w.1, f32[256,256]{1,0:T(8,128)S(1)} %get-tuple-element.43.before.kv_before, bf16[256,512]{1,0:T(8,128)(2,1)S(1)} %collective-permute-done.6.refs_0_, bf16[256,512]{1,0:T(8,128)(2,1)S(1)} %collective-permute-done.7.refs_1_, ...), custom_call_target="tpu_custom_call" | custom-call | tf_op jit(solution)/shard_map/value/pallas_call | solution.py:524
  53.2 5.3 %prep.2 = (bf16[8,256,128]{2,1,0:T(8,128)(2,1)}, f32[8,256,128]{2,1,0:T(8,128)}, f32[8,256,128]{2,1,0:T(8,128)}, bf16[8,256,128]{2,1,0:T(8,128)(2,1)}) custom-call(f32[16,128]{1,0:T(8,128)} %bitcast.13, bf16[2176,128]{1,0:T(8,128)(2,1)} %collective-permute-done.14.refs_0_), custom_call_target="tpu_custom_call" | custom-call | flops 4294967296 | tf_op jit(solution)/shard_map/prep/pallas_call | solution.py:544
  58.7 2.9 %collective-permute-start.16 = (bf16[512,128]{1,0:T(8,128)(2,1)S(1)}, bf16[512,128]{1,0:T(8,128)(2,1)S(1)}, u32[]{:S(2)}, u32[]{:S(2)}) collective-permute-start(bf16[512,128]{1,0:T(8,128)(2,1)S(1)} %pad_maximum_fusion.1), channel_id=1, source_target_pairs={{0,8},{1,9},{2,10},{3,11},{4,12},{5,13},{6,14},{7,15},{8,0},{9,1},... | collective-permute-start | bytes 393224 | tf_op jit(solution)/shard_map/ppermute | solution.py:452
  61.6 1.7 %collective-permute-start.17 = (bf16[512,128]{1,0:T(8,128)(2,1)S(1)}, bf16[512,128]{1,0:T(8,128)(2,1)S(1)}, u32[]{:S(2)}, u32[]{:S(2)}) collective-permute-start(bf16[512,128]{1,0:T(8,128)(2,1)S(1)} %pad_maximum_fusion.1), channel_id=1, source_target_pairs={{0,12},{1,13},{2,14},{3,15},{4,8},{5,9},{6,10},{7,11},{8,4},{9,5},... | collective-permute-start | bytes 393224 | tf_op jit(solution)/shard_map/ppermute | solution.py:452
  64.4 8.1 %stats.1 = (bf16[8,256,128]{2,1,0:T(8,128)(2,1)S(1)}, bf16[8,128,256]{2,1,0:T(8,128)(2,1)S(1)}, f32[3,256]{1,0:T(4,128)S(1)}, f32[16,128]{1,0:T(8,128)S(1)}) custom-call(s32[8]{0:T(128)S(1)} %stack.35.place, s32[2]{0:T(128)S(1)} %copy-done.11, s32[1,256]{1,0:T(1,128)S(1)} %copy-done.10, s32[256,128]{1,0:T(8,128)S(1)} %copy-done.2, f32[16,128]{1,0:T(8,128)S(1)} %bitcast.14, ...), custom_call_target="tpu_custom_call" | custom-call | flops 17179869184 | tf_op jit(solution)/shard_map/stats/pallas_call | solution.py:568
  72.7 1.6 %stats_late.1.log_total_1 = f32[5,256]{1,0:T(8,128)S(1)} custom-call(s32[2]{0:T(128)S(1)} %copy-done.11, s32[1,256]{1,0:T(1,128)S(1)} %copy-done.10, bf16[8,128,256]{2,1,0:T(8,128)(2,1)S(1)} %get-tuple-element.58.q_t, bf16[8,256,128]{2,1,0:T(8,128)(2,1)S(1)} %copy-done.7, bf16[8,256,128]{2,1,0:T(8,128)(2,1)S(1)} %copy-done.14), custom_call_target="tpu_custom_call" | custom-call | flops 17179869184 | tf_op jit(solution)/shard_map/stats_late/pallas_call | solution.py:606
  75.3 7.3 %grad.1 = (bf16[256,1024]{1,0:T(8,128)(2,1)}, f32[16,128]{1,0:T(8,128)S(1)}) custom-call(s32[2]{0:T(128)S(1)} %copy-done.11, bf16[8,256,128]{2,1,0:T(8,128)(2,1)S(1)} %get-tuple-element.54.q_rot, bf16[8,128,256]{2,1,0:T(8,128)(2,1)S(1)} %get-tuple-element.58.q_t, f32[3,256]{1,0:T(4,128)S(1)} %get-tuple-element.56.log_total_0, ...), custom_call_target="tpu_custom_call" | custom-call | flops 8589934592 | bytes 8388608 | tf_op jit(solution)/shard_map/grad/pallas_call | solution.py:619
  83.9 5.6 %collective-permute-start.20 = (f32[16,128]{1,0:T(8,128)S(1)}, f32[16,128]{1,0:T(8,128)S(1)}, u32[]{:S(2)}, u32[]{:S(2)}) collective-permute-start(f32[16,128]{1,0:T(8,128)S(1)} %add.61), channel_id=1, source_target_pairs={{0,2},{1,3},{2,0},{3,1},{4,6},{5,7},{6,4},{7,5},{8,10},{9,11},{10,... | collective-permute-start | bytes 24584 | tf_op jit(solution)/shard_map/ppermute | solution.py:452
  91.1 8.0 %collective-permute-start.21 = (f32[16,128]{1,0:T(8,128)S(1)}, f32[16,128]{1,0:T(8,128)S(1)}, u32[]{:S(2)}, u32[]{:S(2)}) collective-permute-start(f32[16,128]{1,0:T(8,128)S(1)} %add.62), channel_id=1, source_target_pairs={{0,4},{1,5},{2,6},{3,7},{4,0},{5,1},{6,2},{7,3},{8,12},{9,13},{10,... | collective-permute-start | bytes 24584 | tf_op jit(solution)/shard_map/ppermute | solution.py:452
  99.0 1.6 %collective-permute-done.21 = f32[16,128]{1,0:T(8,128)S(1)} collective-permute-done((f32[16,128]{1,0:T(8,128)S(1)}, f32[16,128]{1,0:T(8,128)S(1)}, u32[]{:S(2)}, u32[]{:S(2)}) %collective-permute-start.21) | collective-permute-done | bytes 8224 | tf_op jit(solution)/shard_map/ppermute | solution.py:452
  100.7 20.3 %collective-permute-start.22 = (f32[16,128]{1,0:T(8,128)S(1)}, f32[16,128]{1,0:T(8,128)S(1)}, u32[]{:S(2)}, u32[]{:S(2)}) collective-permute-start(f32[16,128]{1,0:T(8,128)S(1)} %add.63), channel_id=1, source_target_pairs={{0,12},{1,13},{2,14},{3,15},{4,8},{5,9},{6,10},{7,11},{8,4},{9,5},... | collective-permute-start | bytes 24584 | tf_op jit(solution)/shard_map/ppermute | solution.py:452
  121.0 1.6 %collective-permute-done.22 = f32[16,128]{1,0:T(8,128)S(1)} collective-permute-done((f32[16,128]{1,0:T(8,128)S(1)}, f32[16,128]{1,0:T(8,128)S(1)}, u32[]{:S(2)}, u32[]{:S(2)}) %collective-permute-start.22) | collective-permute-done | bytes 8224 | tf_op jit(solution)/shard_map/ppermute | solution.py:452
  (88 shorter events, 17.1 us)
Async XLA Ops:
  0.6 35.7 %copy-start.6 = (bf16[256,1024]{1,0:T(8,128)(2,1)S(1)}, bf16[256,1024]{1,0:T(8,128)(2,1)}, u32[]{:S(2)}) copy-start(bf16[256,1024]{1,0:T(8,128)(2,1)} %refs_0_.1) | copy-start | bytes 1572868
  0.6 22.0 %collective-permute-start = (bf16[256,1024]{1,0:T(8,128)(2,1)}, bf16[256,1024]{1,0:T(8,128)(2,1)S(1)}, u32[]{:S(2)}, u32[]{:S(2)}) collective-permute-start(bf16[256,1024]{1,0:T(8,128)(2,1)} %refs_0_.1), channel_id=1, source_target_pairs={{0,32},{16,48},{32,64},{48,80},{64,96},{80,112},{96,0},{112,16},{1... | collective-permute-start | bytes 1572872 | tf_op jit(solution)/shard_map/ppermute | solution.py:469
  2.7 19.9 %collective-permute-start.1 = (bf16[256,1024]{1,0:T(8,128)(2,1)}, bf16[256,1024]{1,0:T(8,128)(2,1)S(1)}, u32[]{:S(2)}, u32[]{:S(2)}) collective-permute-start(bf16[256,1024]{1,0:T(8,128)(2,1)} %refs_0_.1), channel_id=1, source_target_pairs={{0,96},{16,112},{32,0},{48,16},{64,32},{80,48},{96,64},{112,80},{1... | collective-permute-start | bytes 1572872 | tf_op jit(solution)/shard_map/ppermute | solution.py:470
  4.9 17.7 %collective-permute-start.2 = (bf16[256,1024]{1,0:T(8,128)(2,1)}, bf16[256,1024]{1,0:T(8,128)(2,1)S(1)}, u32[]{:S(2)}, u32[]{:S(2)}) collective-permute-start(bf16[256,1024]{1,0:T(8,128)(2,1)} %refs_0_.1), channel_id=1, source_target_pairs={{0,16},{16,0},{32,48},{48,32},{64,80},{80,64},{96,112},{112,96},{1... | collective-permute-start | bytes 1572872 | tf_op jit(solution)/shard_map/ppermute | solution.py:471
  9.5 6.1 %collective-permute-start.3 = (bf16[272,128]{1,0:T(8,128)(2,1)}, bf16[272,128]{1,0:T(8,128)(2,1)S(1)}, u32[]{:S(2)}, u32[]{:S(2)}) collective-permute-start(bf16[272,128]{1,0:T(8,128)(2,1)} %get-tuple-element.36.refs_0_), channel_id=1, source_target_pairs={{0,4},{1,5},{2,6},{3,7},{4,0},{5,1},{6,2},{7,3},{8,12},{9,13},{10,... | collective-permute-start | bytes 208904 | tf_op jit(solution)/shard_map/ppermute | solution.py:452
  11.2 6.6 %collective-permute-start.4 = (bf16[272,128]{1,0:T(8,128)(2,1)}, bf16[272,128]{1,0:T(8,128)(2,1)S(1)}, u32[]{:S(2)}, u32[]{:S(2)}) collective-permute-start(bf16[272,128]{1,0:T(8,128)(2,1)} %get-tuple-element.36.refs_0_), channel_id=1, source_target_pairs={{0,8},{1,9},{2,10},{3,11},{4,12},{5,13},{6,14},{7,15},{8,0},{9,1},... | collective-permute-start | bytes 208904 | tf_op jit(solution)/shard_map/ppermute | solution.py:452
  15.6 5.7 %collective-permute-start.5 = (bf16[272,128]{1,0:T(8,128)(2,1)}, bf16[272,128]{1,0:T(8,128)(2,1)S(1)}, u32[]{:S(2)}, u32[]{:S(2)}) collective-permute-start(bf16[272,128]{1,0:T(8,128)(2,1)} %get-tuple-element.36.refs_0_), channel_id=1, source_target_pairs={{0,12},{1,13},{2,14},{3,15},{4,8},{5,9},{6,10},{7,11},{8,4},{9,5},... | collective-permute-start | bytes 208904 | tf_op jit(solution)/shard_map/ppermute | solution.py:452
  22.0 6.8 %collective-permute-start.13 = (bf16[1088,128]{1,0:T(8,128)(2,1)}, bf16[1088,128]{1,0:T(8,128)(2,1)S(1)}, u32[]{:S(2)}, u32[]{:S(2)}) collective-permute-start(bf16[1088,128]{1,0:T(8,128)(2,1)} %get-tuple-element.69), channel_id=1, source_target_pairs={{0,2},{1,3},{2,0},{3,1},{4,6},{5,7},{6,4},{7,5},{8,10},{9,11},{10,... | collective-permute-start | bytes 835592 | tf_op jit(solution)/shard_map/ppermute | solution.py:452
  22.7 10.2 %collective-permute-start.6 = (bf16[256,512]{1,0:T(8,128)(2,1)S(1)}, bf16[256,512]{1,0:T(8,128)(2,1)S(1)}, u32[]{:S(2)}, u32[]{:S(2)}) collective-permute-start(bf16[256,512]{1,0:T(8,128)(2,1)S(1)} %slice.6), channel_id=1, source_target_pairs={{0,32},{16,48},{32,64},{48,80},{64,96},{80,112},{96,0},{112,16},{1... | collective-permute-start | bytes 786440 | tf_op jit(solution)/shard_map/ppermute | solution.py:496
  23.5 9.3 %collective-permute-start.7 = (bf16[256,512]{1,0:T(8,128)(2,1)}, bf16[256,512]{1,0:T(8,128)(2,1)S(1)}, u32[]{:S(2)}, u32[]{:S(2)}) collective-permute-start(bf16[256,512]{1,0:T(8,128)(2,1)} %slice.7), channel_id=1, source_target_pairs={{0,96},{16,112},{32,0},{48,16},{64,32},{80,48},{96,64},{112,80},{1... | collective-permute-start | bytes 786440 | tf_op jit(solution)/shard_map/ppermute | solution.py:497
  29.6 23.7 %collective-permute-start.14 = (bf16[2176,128]{1,0:T(8,128)(2,1)}, bf16[2176,128]{1,0:T(8,128)(2,1)}, u32[]{:S(2)}, u32[]{:S(2)}) collective-permute-start(bf16[2176,128]{1,0:T(8,128)(2,1)} %constant_dynamic-update-slice_fusion.4), channel_id=1, source_target_pairs={{0,1},{1,0},{2,3},{3,2},{4,5},{5,4},{6,7},{7,6},{8,9},{9,8},{10,11... | collective-permute-start | bytes 1671176 | tf_op jit(solution)/shard_map/ppermute | solution.py:452
  29.6 20.1 %collective-permute-start.8 = (bf16[256,1024]{1,0:T(8,128)(2,1)S(1)}, bf16[256,1024]{1,0:T(8,128)(2,1)S(1)}, u32[]{:S(2)}, u32[]{:S(2)}) collective-permute-start(bf16[256,1024]{1,0:T(8,128)(2,1)S(1)} %collective-permute-done.2.refs_3_), channel_id=1, source_target_pairs={{0,32},{16,48},{32,64},{48,80},{64,96},{80,112},{96,0},{112,16},{1... | collective-permute-start | bytes 1572872 | tf_op jit(solution)/shard_map/ppermute | solution.py:498
  29.6 20.1 %collective-permute-start.9 = (bf16[256,1024]{1,0:T(8,128)(2,1)S(1)}, bf16[256,1024]{1,0:T(8,128)(2,1)S(1)}, u32[]{:S(2)}, u32[]{:S(2)}) collective-permute-start(bf16[256,1024]{1,0:T(8,128)(2,1)S(1)} %collective-permute-done.2.refs_3_), channel_id=1, source_target_pairs={{0,96},{16,112},{32,0},{48,16},{64,32},{80,48},{96,64},{112,80},{1... | collective-permute-start | bytes 1572872 | tf_op jit(solution)/shard_map/ppermute | solution.py:499
  32.8 16.9 %collective-permute-start.10 = (bf16[256,512]{1,0:T(8,128)(2,1)S(1)}, bf16[256,512]{1,0:T(8,128)(2,1)S(1)}, u32[]{:S(2)}, u32[]{:S(2)}) collective-permute-start(bf16[256,512]{1,0:T(8,128)(2,1)S(1)} %collective-permute-done.6.refs_0_), channel_id=1, source_target_pairs={{0,16},{16,0},{32,48},{48,32},{64,80},{80,64},{96,112},{112,96},{1... | collective-permute-start | bytes 786440 | tf_op jit(solution)/shard_map/ppermute | solution.py:500
  33.5 16.2 %collective-permute-start.11 = (bf16[256,512]{1,0:T(8,128)(2,1)S(1)}, bf16[256,512]{1,0:T(8,128)(2,1)S(1)}, u32[]{:S(2)}, u32[]{:S(2)}) collective-permute-start(bf16[256,512]{1,0:T(8,128)(2,1)S(1)} %collective-permute-done.7.refs_1_), channel_id=1, source_target_pairs={{0,16},{16,0},{32,48},{48,32},{64,80},{80,64},{96,112},{112,96},{1... | collective-permute-start | bytes 786440 | tf_op jit(solution)/shard_map/ppermute | solution.py:501
  52.5 6.0 %collective-permute-start.12 = (bf16[256,128]{1,0:T(8,128)(2,1)S(1)}, bf16[256,128]{1,0:T(8,128)(2,1)S(1)}, u32[]{:S(2)}, u32[]{:S(2)}) collective-permute-start(bf16[256,128]{1,0:T(8,128)(2,1)S(1)} %value.1.v_own), channel_id=1, source_target_pairs={{0,2},{1,3},{2,0},{3,1},{4,6},{5,7},{6,4},{7,5},{8,10},{9,11},{10,... | collective-permute-start | bytes 196616 | tf_op jit(solution)/shard_map/ppermute | solution.py:452
  58.6 13.9 %collective-permute-start.15 = (bf16[512,128]{1,0:T(8,128)(2,1)S(1)}, bf16[512,128]{1,0:T(8,128)(2,1)S(1)}, u32[]{:S(2)}, u32[]{:S(2)}) collective-permute-start(bf16[512,128]{1,0:T(8,128)(2,1)S(1)} %pad_maximum_fusion.1), channel_id=1, source_target_pairs={{0,4},{1,5},{2,6},{3,7},{4,0},{5,1},{6,2},{7,3},{8,12},{9,13},{10,... | collective-permute-start | bytes 393224 | tf_op jit(solution)/shard_map/ppermute | solution.py:452
  58.7 13.8 %collective-permute-start.16 = (bf16[512,128]{1,0:T(8,128)(2,1)S(1)}, bf16[512,128]{1,0:T(8,128)(2,1)S(1)}, u32[]{:S(2)}, u32[]{:S(2)}) collective-permute-start(bf16[512,128]{1,0:T(8,128)(2,1)S(1)} %pad_maximum_fusion.1), channel_id=1, source_target_pairs={{0,8},{1,9},{2,10},{3,11},{4,12},{5,13},{6,14},{7,15},{8,0},{9,1},... | collective-permute-start | bytes 393224 | tf_op jit(solution)/shard_map/ppermute | solution.py:452
  61.6 10.9 %collective-permute-start.17 = (bf16[512,128]{1,0:T(8,128)(2,1)S(1)}, bf16[512,128]{1,0:T(8,128)(2,1)S(1)}, u32[]{:S(2)}, u32[]{:S(2)}) collective-permute-start(bf16[512,128]{1,0:T(8,128)(2,1)S(1)} %pad_maximum_fusion.1), channel_id=1, source_target_pairs={{0,12},{1,13},{2,14},{3,15},{4,8},{5,9},{6,10},{7,11},{8,4},{9,5},... | collective-permute-start | bytes 393224 | tf_op jit(solution)/shard_map/ppermute | solution.py:452
  72.6 2.0 %collective-permute-start.18 = (bf16[2048,128]{1,0:T(8,128)(2,1)S(1)}, bf16[2048,128]{1,0:T(8,128)(2,1)S(1)}, u32[]{:S(2)}, u32[]{:S(2)}) collective-permute-start(bf16[2048,128]{1,0:T(8,128)(2,1)S(1)} %pad_maximum_fusion), channel_id=1, source_target_pairs={{0,1},{1,0},{2,3},{3,2},{4,5},{5,4},{6,7},{7,6},{8,9},{9,8},{10,11... | collective-permute-start | bytes 1572872 | tf_op jit(solution)/shard_map/ppermute | solution.py:452
  82.6 1.3 %collective-permute-start.19 = (f32[16,128]{1,0:T(8,128)S(1)}, f32[16,128]{1,0:T(8,128)S(1)}, u32[]{:S(2)}, u32[]{:S(2)}) collective-permute-start(f32[16,128]{1,0:T(8,128)S(1)} %get-tuple-element.67), channel_id=1, source_target_pairs={{0,1},{1,0},{2,3},{3,2},{4,5},{5,4},{6,7},{7,6},{8,9},{9,8},{10,11... | collective-permute-start | bytes 24584 | tf_op jit(solution)/shard_map/ppermute | solution.py:452
  83.9 7.2 %collective-permute-start.20 = (f32[16,128]{1,0:T(8,128)S(1)}, f32[16,128]{1,0:T(8,128)S(1)}, u32[]{:S(2)}, u32[]{:S(2)}) collective-permute-start(f32[16,128]{1,0:T(8,128)S(1)} %add.61), channel_id=1, source_target_pairs={{0,2},{1,3},{2,0},{3,1},{4,6},{5,7},{6,4},{7,5},{8,10},{9,11},{10,... | collective-permute-start | bytes 24584 | tf_op jit(solution)/shard_map/ppermute | solution.py:452
  91.1 9.6 %collective-permute-start.21 = (f32[16,128]{1,0:T(8,128)S(1)}, f32[16,128]{1,0:T(8,128)S(1)}, u32[]{:S(2)}, u32[]{:S(2)}) collective-permute-start(f32[16,128]{1,0:T(8,128)S(1)} %add.62), channel_id=1, source_target_pairs={{0,4},{1,5},{2,6},{3,7},{4,0},{5,1},{6,2},{7,3},{8,12},{9,13},{10,... | collective-permute-start | bytes 24584 | tf_op jit(solution)/shard_map/ppermute | solution.py:452
  100.7 21.9 %collective-permute-start.22 = (f32[16,128]{1,0:T(8,128)S(1)}, f32[16,128]{1,0:T(8,128)S(1)}, u32[]{:S(2)}, u32[]{:S(2)}) collective-permute-start(f32[16,128]{1,0:T(8,128)S(1)} %add.63), channel_id=1, source_target_pairs={{0,12},{1,13},{2,14},{3,15},{4,8},{5,9},{6,10},{7,11},{8,4},{9,5},... | collective-permute-start | bytes 24584 | tf_op jit(solution)/shard_map/ppermute | solution.py:452
  (21 other events, 164.5 us)

commit v9 on v8

--- a/solution.py
+++ b/solution.py
@@ -517,6 +517,7 @@
         cost_estimate=cost(1 << 34, 0),
         name="project",
     )(place, w_query, w_key, w_value, hidden, low, high, other)
+    x_side = after(far_a, far_b)(x_side)
     core = cross(jnp.concatenate([column, x_side], axis=0), 1)
     packed = (packed, *y_side, x_side, core)
 

time: 124 us -> 125 us (level)
  waiting for transfers between devices: 11.3 us -> 13 us
    ppermute x1, waiting for transfers between devices: 0.01 us -> 3.1 us  [shards(): far_a = send(low[:, :n], perm=up)]
    ppermute x14, waiting for transfers between devices: 11.3 us -> 9.26 us  [shards(): lax.ppermute(x, 'tokens', [(i, i ^ d) for i in range(ranks)])]
    ppermute x1, starting transfers between devices: 2.8 us -> 1.52 us  [shards(): other_far_b = send(far_b, perm=flip)]
    ppermute x1, starting transfers between devices: 0.74 us -> 2.01 us  [shards(): other_far_a = send(far_a, perm=flip)]
  transfers between devices with their start and end apart: 23 -> 23, of which waited for: 7 -> 8; matrix products, arithmetic and copies ran while one was open for 4% -> 4% of each run, Pallas kernels for 26% -> 25%
where the time goes in v9:
time: 125 us
  starting transfers between devices  63.7 us (51%)
  Pallas kernels  38.9 us (31%)
  waiting for transfers between devices  13 us (10%)
  local copies, waits for them, and re-layouts  7.95 us (6%)
    ppermute x14, starting transfers between devices, shards(): lax.ppermute(x, 'tokens', [(i, i ^ d) for i in range(ranks)])  46.4 us
    pallas_call x2, Pallas kernels, prep(): pl.pallas_call(functools.partial(prep_kernel, near, rows, few, levels), o...  11.5 us
    ppermute x14, waiting for transfers between devices, shards(): lax.ppermute(x, 'tokens', [(i, i ^ d) for i in range(ranks)])  9.26 us
    pallas_call x1, Pallas kernels, second(): pl.pallas_call(functools.partial(stats_kernel, count, heads, rows, levels...  8.06 us
    pallas_call x1, Pallas kernels, shards(): pl.pallas_call(functools.partial(grad_kernel, heads, rows, levels), out_s...  7.26 us
    unnamed x48, local copies, waits for them, and re-layouts  6.35 us
    pallas_call x1, Pallas kernels, shards(): pl.pallas_call(functools.partial(project_kernel, half, part), out_shape=(...  6.21 us
    ppermute x1, starting transfers between devices, shards(): other_high = send(other, perm=down)  3.22 us
  transfers between devices with their start and end apart: 23, of which 8 were waited for; matrix products, arithmetic and copies ran while one was open for 4% of the time, Pallas kernels for 25%

profile of v9, /device:TPU:0, one launch (start us, length us, event | category | flops | bytes accessed | tf_op | source)
XLA Modules:
  0.0 125.3 jit_solution(6876947608946132946)
XLA Ops:
  0.6 2.1 %collective-permute-start = (bf16[256,1024]{1,0:T(8,128)(2,1)}, bf16[256,1024]{1,0:T(8,128)(2,1)S(1)}, u32[]{:S(2)}, u32[]{:S(2)}) collective-permute-start(bf16[256,1024]{1,0:T(8,128)(2,1)} %refs_0_.1), channel_id=1, source_target_pairs={{0,32},{16,48},{32,64},{48,80},{64,96},{80,112},{96,0},{112,16},{1... | collective-permute-start | bytes 1572872 | tf_op jit(solution)/shard_map/ppermute | solution.py:469
  2.7 2.2 %collective-permute-start.1 = (bf16[256,1024]{1,0:T(8,128)(2,1)}, bf16[256,1024]{1,0:T(8,128)(2,1)S(1)}, u32[]{:S(2)}, u32[]{:S(2)}) collective-permute-start(bf16[256,1024]{1,0:T(8,128)(2,1)} %refs_0_.1), channel_id=1, source_target_pairs={{0,96},{16,112},{32,0},{48,16},{64,32},{80,48},{96,64},{112,80},{1... | collective-permute-start | bytes 1572872 | tf_op jit(solution)/shard_map/ppermute | solution.py:470
  4.9 3.0 %collective-permute-start.2 = (bf16[256,1024]{1,0:T(8,128)(2,1)}, bf16[256,1024]{1,0:T(8,128)(2,1)S(1)}, u32[]{:S(2)}, u32[]{:S(2)}) collective-permute-start(bf16[256,1024]{1,0:T(8,128)(2,1)} %refs_0_.1), channel_id=1, source_target_pairs={{0,16},{16,0},{32,48},{48,32},{64,80},{80,64},{96,112},{112,96},{1... | collective-permute-start | bytes 1572872 | tf_op jit(solution)/shard_map/ppermute | solution.py:471
  9.5 1.7 %collective-permute-start.3 = (bf16[272,128]{1,0:T(8,128)(2,1)}, bf16[272,128]{1,0:T(8,128)(2,1)S(1)}, u32[]{:S(2)}, u32[]{:S(2)}) collective-permute-start(bf16[272,128]{1,0:T(8,128)(2,1)} %get-tuple-element.37.refs_0_), channel_id=1, source_target_pairs={{0,4},{1,5},{2,6},{3,7},{4,0},{5,1},{6,2},{7,3},{8,12},{9,13},{10,... | collective-permute-start | bytes 208904 | tf_op jit(solution)/shard_map/ppermute | solution.py:452
  11.2 2.9 %collective-permute-start.4 = (bf16[272,128]{1,0:T(8,128)(2,1)}, bf16[272,128]{1,0:T(8,128)(2,1)S(1)}, u32[]{:S(2)}, u32[]{:S(2)}) collective-permute-start(bf16[272,128]{1,0:T(8,128)(2,1)} %get-tuple-element.37.refs_0_), channel_id=1, source_target_pairs={{0,8},{1,9},{2,10},{3,11},{4,12},{5,13},{6,14},{7,15},{8,0},{9,1},... | collective-permute-start | bytes 208904 | tf_op jit(solution)/shard_map/ppermute | solution.py:452
  18.4 2.9 %collective-permute-done.5.refs_3_ = bf16[272,128]{1,0:T(8,128)(2,1)S(1)} collective-permute-done((bf16[272,128]{1,0:T(8,128)(2,1)}, bf16[272,128]{1,0:T(8,128)(2,1)S(1)}, u32[]{:S(2)}, u32[]{:S(2)}) %collective-permute-start.5) | collective-permute-done | bytes 69664 | tf_op jit(solution)/shard_map/ppermute | solution.py:452
  23.5 3.1 %collective-permute-start.7 = (bf16[256,512]{1,0:T(8,128)(2,1)}, bf16[256,512]{1,0:T(8,128)(2,1)S(1)}, u32[]{:S(2)}, u32[]{:S(2)}) collective-permute-start(bf16[256,512]{1,0:T(8,128)(2,1)} %slice.7), channel_id=1, source_target_pairs={{0,96},{16,112},{32,0},{48,16},{64,32},{80,48},{96,64},{112,80},{1... | collective-permute-start | bytes 786440 | tf_op jit(solution)/shard_map/ppermute | solution.py:497
  26.8 3.2 %collective-permute-start.9 = (bf16[256,1024]{1,0:T(8,128)(2,1)S(1)}, bf16[256,1024]{1,0:T(8,128)(2,1)S(1)}, u32[]{:S(2)}, u32[]{:S(2)}) collective-permute-start(bf16[256,1024]{1,0:T(8,128)(2,1)S(1)} %collective-permute-done.2.refs_3_), channel_id=1, source_target_pairs={{0,96},{16,112},{32,0},{48,16},{64,32},{80,48},{96,64},{112,80},{1... | collective-permute-start | bytes 1572872 | tf_op jit(solution)/shard_map/ppermute | solution.py:499
  30.0 3.1 %collective-permute-done.6.refs_0_ = bf16[256,512]{1,0:T(8,128)(2,1)S(1)} collective-permute-done((bf16[256,512]{1,0:T(8,128)(2,1)S(1)}, bf16[256,512]{1,0:T(8,128)(2,1)S(1)}, u32[]{:S(2)}, u32[]{:S(2)}) %collective-permute-start.6) | collective-permute-done | bytes 262176 | tf_op jit(solution)/shard_map/ppermute | solution.py:496
  34.5 2.0 %collective-permute-start.10 = (bf16[256,512]{1,0:T(8,128)(2,1)S(1)}, bf16[256,512]{1,0:T(8,128)(2,1)S(1)}, u32[]{:S(2)}, u32[]{:S(2)}) collective-permute-start(bf16[256,512]{1,0:T(8,128)(2,1)S(1)} %collective-permute-done.6.refs_0_), channel_id=1, source_target_pairs={{0,16},{16,0},{32,48},{48,32},{64,80},{80,64},{96,112},{112,96},{1... | collective-permute-start | bytes 786440 | tf_op jit(solution)/shard_map/ppermute | solution.py:500
  38.1 6.2 %project.1 = (f32[256,1024]{1,0:T(8,128)S(1)}, f32[256,256]{1,0:T(8,128)S(1)}) custom-call(s32[8]{0:T(128)S(1)} %stack.35.place, bf16[8192,1024]{1,0:T(8,128)(2,1)} %wq.3, bf16[8192,128]{1,0:T(8,128)(2,1)} %wk.3, bf16[8192,128]{1,0:T(8,128)(2,1)} %w.1, bf16[256,1024]{1,0:T(8,128)(2,1)S(1)} %copy-done.6, bf16[256,1024]{1,0:T(8,128)(2,1)S(1)} %collective-permute-done.refs_1_, ...), custom_call_target="tpu_custom_call" | custom-call | flops 17179869184 | tf_op jit(solution)/shard_map/project/pallas_call | solution.py:505
  45.3 6.1 %prep.3 = (bf16[8,256,128]{2,1,0:T(8,128)(2,1)}, f32[8,256,128]{2,1,0:T(8,128)}, f32[8,256,128]{2,1,0:T(8,128)}, bf16[8,256,128]{2,1,0:T(8,128)(2,1)}, bf16[8,128,256]{2,1,0:T(8,128)(2,1)}) custom-call(f32[16,128]{1,0:T(8,128)} %bitcast.12, bf16[272,128]{1,0:T(8,128)(2,1)} %get-tuple-element.37.refs_0_, bf16[272,128]{1,0:T(8,128)(2,1)} %copy-done.18, ...), custom_call_target="tpu_custom_call" | custom-call | tf_op jit(solution)/shard_map/prep/pallas_call | solution.py:545
  51.5 2.7 %value.1.v_own = bf16[256,128]{1,0:T(8,128)(2,1)S(1)} custom-call(s32[8]{0:T(128)S(1)} %stack.35.place, bf16[8192,128]{1,0:T(8,128)(2,1)} %w.1, f32[256,256]{1,0:T(8,128)S(1)} %get-tuple-element.44.before.kv_before, bf16[256,512]{1,0:T(8,128)(2,1)S(1)} %collective-permute-done.6.refs_0_, bf16[256,512]{1,0:T(8,128)(2,1)S(1)} %collective-permute-done.7.refs_1_, ...), custom_call_target="tpu_custom_call" | custom-call | tf_op jit(solution)/shard_map/value/pallas_call | solution.py:525
  55.8 5.3 %prep.2 = (bf16[8,256,128]{2,1,0:T(8,128)(2,1)}, f32[8,256,128]{2,1,0:T(8,128)}, f32[8,256,128]{2,1,0:T(8,128)}, bf16[8,256,128]{2,1,0:T(8,128)(2,1)}) custom-call(f32[16,128]{1,0:T(8,128)} %bitcast.13, bf16[2176,128]{1,0:T(8,128)(2,1)} %collective-permute-done.14.refs_0_), custom_call_target="tpu_custom_call" | custom-call | flops 4294967296 | tf_op jit(solution)/shard_map/prep/pallas_call | solution.py:545
  61.2 2.9 %collective-permute-start.16 = (bf16[512,128]{1,0:T(8,128)(2,1)S(1)}, bf16[512,128]{1,0:T(8,128)(2,1)S(1)}, u32[]{:S(2)}, u32[]{:S(2)}) collective-permute-start(bf16[512,128]{1,0:T(8,128)(2,1)S(1)} %pad_maximum_fusion.1), channel_id=1, source_target_pairs={{0,8},{1,9},{2,10},{3,11},{4,12},{5,13},{6,14},{7,15},{8,0},{9,1},... | collective-permute-start | bytes 393224 | tf_op jit(solution)/shard_map/ppermute | solution.py:452
  64.2 1.8 %collective-permute-start.17 = (bf16[512,128]{1,0:T(8,128)(2,1)S(1)}, bf16[512,128]{1,0:T(8,128)(2,1)S(1)}, u32[]{:S(2)}, u32[]{:S(2)}) collective-permute-start(bf16[512,128]{1,0:T(8,128)(2,1)S(1)} %pad_maximum_fusion.1), channel_id=1, source_target_pairs={{0,12},{1,13},{2,14},{3,15},{4,8},{5,9},{6,10},{7,11},{8,4},{9,5},... | collective-permute-start | bytes 393224 | tf_op jit(solution)/shard_map/ppermute | solution.py:452
  67.0 8.1 %stats.1 = (bf16[8,256,128]{2,1,0:T(8,128)(2,1)S(1)}, bf16[8,128,256]{2,1,0:T(8,128)(2,1)S(1)}, f32[3,256]{1,0:T(4,128)S(1)}, f32[16,128]{1,0:T(8,128)S(1)}) custom-call(s32[8]{0:T(128)S(1)} %stack.35.place, s32[2]{0:T(128)S(1)} %copy-done.11, s32[1,256]{1,0:T(1,128)S(1)} %copy-done.10, s32[256,128]{1,0:T(8,128)S(1)} %copy-done.2, f32[16,128]{1,0:T(8,128)S(1)} %bitcast.14, ...), custom_call_target="tpu_custom_call" | custom-call | flops 17179869184 | tf_op jit(solution)/shard_map/stats/pallas_call | solution.py:569
  75.3 1.6 %stats_late.1.log_total_1 = f32[5,256]{1,0:T(8,128)S(1)} custom-call(s32[2]{0:T(128)S(1)} %copy-done.11, s32[1,256]{1,0:T(1,128)S(1)} %copy-done.10, bf16[8,128,256]{2,1,0:T(8,128)(2,1)S(1)} %get-tuple-element.60.q_t, bf16[8,256,128]{2,1,0:T(8,128)(2,1)S(1)} %copy-done.7, bf16[8,256,128]{2,1,0:T(8,128)(2,1)S(1)} %copy-done.14), custom_call_target="tpu_custom_call" | custom-call | flops 17179869184 | tf_op jit(solution)/shard_map/stats_late/pallas_call | solution.py:607
  77.9 7.3 %grad.1 = (bf16[256,1024]{1,0:T(8,128)(2,1)}, f32[16,128]{1,0:T(8,128)S(1)}) custom-call(s32[2]{0:T(128)S(1)} %copy-done.11, bf16[8,256,128]{2,1,0:T(8,128)(2,1)S(1)} %get-tuple-element.56.q_rot, bf16[8,128,256]{2,1,0:T(8,128)(2,1)S(1)} %get-tuple-element.60.q_t, f32[3,256]{1,0:T(4,128)S(1)} %get-tuple-element.58.log_total_0, ...), custom_call_target="tpu_custom_call" | custom-call | flops 8589934592 | bytes 8388608 | tf_op jit(solution)/shard_map/grad/pallas_call | solution.py:620
  86.4 4.8 %collective-permute-start.20 = (f32[16,128]{1,0:T(8,128)S(1)}, f32[16,128]{1,0:T(8,128)S(1)}, u32[]{:S(2)}, u32[]{:S(2)}) collective-permute-start(f32[16,128]{1,0:T(8,128)S(1)} %add.61), channel_id=1, source_target_pairs={{0,2},{1,3},{2,0},{3,1},{4,6},{5,7},{6,4},{7,5},{8,10},{9,11},{10,... | collective-permute-start | bytes 24584 | tf_op jit(solution)/shard_map/ppermute | solution.py:452
  92.8 8.0 %collective-permute-start.21 = (f32[16,128]{1,0:T(8,128)S(1)}, f32[16,128]{1,0:T(8,128)S(1)}, u32[]{:S(2)}, u32[]{:S(2)}) collective-permute-start(f32[16,128]{1,0:T(8,128)S(1)} %add.62), channel_id=1, source_target_pairs={{0,4},{1,5},{2,6},{3,7},{4,0},{5,1},{6,2},{7,3},{8,12},{9,13},{10,... | collective-permute-start | bytes 24584 | tf_op jit(solution)/shard_map/ppermute | solution.py:452
  100.8 1.6 %collective-permute-done.21 = f32[16,128]{1,0:T(8,128)S(1)} collective-permute-done((f32[16,128]{1,0:T(8,128)S(1)}, f32[16,128]{1,0:T(8,128)S(1)}, u32[]{:S(2)}, u32[]{:S(2)}) %collective-permute-start.21) | collective-permute-done | bytes 8224 | tf_op jit(solution)/shard_map/ppermute | solution.py:452
  102.4 20.7 %collective-permute-start.22 = (f32[16,128]{1,0:T(8,128)S(1)}, f32[16,128]{1,0:T(8,128)S(1)}, u32[]{:S(2)}, u32[]{:S(2)}) collective-permute-start(f32[16,128]{1,0:T(8,128)S(1)} %add.63), channel_id=1, source_target_pairs={{0,12},{1,13},{2,14},{3,15},{4,8},{5,9},{6,10},{7,11},{8,4},{9,5},... | collective-permute-start | bytes 24584 | tf_op jit(solution)/shard_map/ppermute | solution.py:452
  123.1 1.6 %collective-permute-done.22 = f32[16,128]{1,0:T(8,128)S(1)} collective-permute-done((f32[16,128]{1,0:T(8,128)S(1)}, f32[16,128]{1,0:T(8,128)S(1)}, u32[]{:S(2)}, u32[]{:S(2)}) %collective-permute-start.22) | collective-permute-done | bytes 8224 | tf_op jit(solution)/shard_map/ppermute | solution.py:452
  (88 shorter events, 19.3 us)
Async XLA Ops:
  0.6 37.4 %copy-start.6 = (bf16[256,1024]{1,0:T(8,128)(2,1)S(1)}, bf16[256,1024]{1,0:T(8,128)(2,1)}, u32[]{:S(2)}) copy-start(bf16[256,1024]{1,0:T(8,128)(2,1)} %refs_0_.1) | copy-start | bytes 1572868
  0.6 22.0 %collective-permute-start = (bf16[256,1024]{1,0:T(8,128)(2,1)}, bf16[256,1024]{1,0:T(8,128)(2,1)S(1)}, u32[]{:S(2)}, u32[]{:S(2)}) collective-permute-start(bf16[256,1024]{1,0:T(8,128)(2,1)} %refs_0_.1), channel_id=1, source_target_pairs={{0,32},{16,48},{32,64},{48,80},{64,96},{80,112},{96,0},{112,16},{1... | collective-permute-start | bytes 1572872 | tf_op jit(solution)/shard_map/ppermute | solution.py:469
  2.7 19.9 %collective-permute-start.1 = (bf16[256,1024]{1,0:T(8,128)(2,1)}, bf16[256,1024]{1,0:T(8,128)(2,1)S(1)}, u32[]{:S(2)}, u32[]{:S(2)}) collective-permute-start(bf16[256,1024]{1,0:T(8,128)(2,1)} %refs_0_.1), channel_id=1, source_target_pairs={{0,96},{16,112},{32,0},{48,16},{64,32},{80,48},{96,64},{112,80},{1... | collective-permute-start | bytes 1572872 | tf_op jit(solution)/shard_map/ppermute | solution.py:470
  4.9 17.7 %collective-permute-start.2 = (bf16[256,1024]{1,0:T(8,128)(2,1)}, bf16[256,1024]{1,0:T(8,128)(2,1)S(1)}, u32[]{:S(2)}, u32[]{:S(2)}) collective-permute-start(bf16[256,1024]{1,0:T(8,128)(2,1)} %refs_0_.1), channel_id=1, source_target_pairs={{0,16},{16,0},{32,48},{48,32},{64,80},{80,64},{96,112},{112,96},{1... | collective-permute-start | bytes 1572872 | tf_op jit(solution)/shard_map/ppermute | solution.py:471
  9.5 6.1 %collective-permute-start.3 = (bf16[272,128]{1,0:T(8,128)(2,1)}, bf16[272,128]{1,0:T(8,128)(2,1)S(1)}, u32[]{:S(2)}, u32[]{:S(2)}) collective-permute-start(bf16[272,128]{1,0:T(8,128)(2,1)} %get-tuple-element.37.refs_0_), channel_id=1, source_target_pairs={{0,4},{1,5},{2,6},{3,7},{4,0},{5,1},{6,2},{7,3},{8,12},{9,13},{10,... | collective-permute-start | bytes 208904 | tf_op jit(solution)/shard_map/ppermute | solution.py:452
  11.2 6.6 %collective-permute-start.4 = (bf16[272,128]{1,0:T(8,128)(2,1)}, bf16[272,128]{1,0:T(8,128)(2,1)S(1)}, u32[]{:S(2)}, u32[]{:S(2)}) collective-permute-start(bf16[272,128]{1,0:T(8,128)(2,1)} %get-tuple-element.37.refs_0_), channel_id=1, source_target_pairs={{0,8},{1,9},{2,10},{3,11},{4,12},{5,13},{6,14},{7,15},{8,0},{9,1},... | collective-permute-start | bytes 208904 | tf_op jit(solution)/shard_map/ppermute | solution.py:452
  15.6 5.7 %collective-permute-start.5 = (bf16[272,128]{1,0:T(8,128)(2,1)}, bf16[272,128]{1,0:T(8,128)(2,1)S(1)}, u32[]{:S(2)}, u32[]{:S(2)}) collective-permute-start(bf16[272,128]{1,0:T(8,128)(2,1)} %get-tuple-element.37.refs_0_), channel_id=1, source_target_pairs={{0,12},{1,13},{2,14},{3,15},{4,8},{5,9},{6,10},{7,11},{8,4},{9,5},... | collective-permute-start | bytes 208904 | tf_op jit(solution)/shard_map/ppermute | solution.py:452
  22.0 11.7 %collective-permute-start.13 = (bf16[1088,128]{1,0:T(8,128)(2,1)}, bf16[1088,128]{1,0:T(8,128)(2,1)S(1)}, u32[]{:S(2)}, u32[]{:S(2)}) collective-permute-start(bf16[1088,128]{1,0:T(8,128)(2,1)} %get-tuple-element.71), channel_id=1, source_target_pairs={{0,2},{1,3},{2,0},{3,1},{4,6},{5,7},{6,4},{7,5},{8,10},{9,11},{10,... | collective-permute-start | bytes 835592 | tf_op jit(solution)/shard_map/ppermute | solution.py:452
  22.6 10.5 %collective-permute-start.6 = (bf16[256,512]{1,0:T(8,128)(2,1)S(1)}, bf16[256,512]{1,0:T(8,128)(2,1)S(1)}, u32[]{:S(2)}, u32[]{:S(2)}) collective-permute-start(bf16[256,512]{1,0:T(8,128)(2,1)S(1)} %slice.6), channel_id=1, source_target_pairs={{0,32},{16,48},{32,64},{48,80},{64,96},{80,112},{96,0},{112,16},{1... | collective-permute-start | bytes 786440 | tf_op jit(solution)/shard_map/ppermute | solution.py:496
  23.5 10.2 %collective-permute-start.7 = (bf16[256,512]{1,0:T(8,128)(2,1)}, bf16[256,512]{1,0:T(8,128)(2,1)S(1)}, u32[]{:S(2)}, u32[]{:S(2)}) collective-permute-start(bf16[256,512]{1,0:T(8,128)(2,1)} %slice.7), channel_id=1, source_target_pairs={{0,96},{16,112},{32,0},{48,16},{64,32},{80,48},{96,64},{112,80},{1... | collective-permute-start | bytes 786440 | tf_op jit(solution)/shard_map/ppermute | solution.py:497
  26.8 24.7 %collective-permute-start.8 = (bf16[256,1024]{1,0:T(8,128)(2,1)S(1)}, bf16[256,1024]{1,0:T(8,128)(2,1)S(1)}, u32[]{:S(2)}, u32[]{:S(2)}) collective-permute-start(bf16[256,1024]{1,0:T(8,128)(2,1)S(1)} %collective-permute-done.2.refs_3_), channel_id=1, source_target_pairs={{0,32},{16,48},{32,64},{48,80},{64,96},{80,112},{96,0},{112,16},{1... | collective-permute-start | bytes 1572872 | tf_op jit(solution)/shard_map/ppermute | solution.py:498
  26.8 24.7 %collective-permute-start.9 = (bf16[256,1024]{1,0:T(8,128)(2,1)S(1)}, bf16[256,1024]{1,0:T(8,128)(2,1)S(1)}, u32[]{:S(2)}, u32[]{:S(2)}) collective-permute-start(bf16[256,1024]{1,0:T(8,128)(2,1)S(1)} %collective-permute-done.2.refs_3_), channel_id=1, source_target_pairs={{0,96},{16,112},{32,0},{48,16},{64,32},{80,48},{96,64},{112,80},{1... | collective-permute-start | bytes 1572872 | tf_op jit(solution)/shard_map/ppermute | solution.py:499
  34.5 21.2 %collective-permute-start.14 = (bf16[2176,128]{1,0:T(8,128)(2,1)}, bf16[2176,128]{1,0:T(8,128)(2,1)}, u32[]{:S(2)}, u32[]{:S(2)}) collective-permute-start(bf16[2176,128]{1,0:T(8,128)(2,1)} %constant_dynamic-update-slice_fusion.4), channel_id=1, source_target_pairs={{0,1},{1,0},{2,3},{3,2},{4,5},{5,4},{6,7},{7,6},{8,9},{9,8},{10,11... | collective-permute-start | bytes 1671176 | tf_op jit(solution)/shard_map/ppermute | solution.py:452
  34.5 16.9 %collective-permute-start.10 = (bf16[256,512]{1,0:T(8,128)(2,1)S(1)}, bf16[256,512]{1,0:T(8,128)(2,1)S(1)}, u32[]{:S(2)}, u32[]{:S(2)}) collective-permute-start(bf16[256,512]{1,0:T(8,128)(2,1)S(1)} %collective-permute-done.6.refs_0_), channel_id=1, source_target_pairs={{0,16},{16,0},{32,48},{48,32},{64,80},{80,64},{96,112},{112,96},{1... | collective-permute-start | bytes 786440 | tf_op jit(solution)/shard_map/ppermute | solution.py:500
  36.5 14.9 %collective-permute-start.11 = (bf16[256,512]{1,0:T(8,128)(2,1)S(1)}, bf16[256,512]{1,0:T(8,128)(2,1)S(1)}, u32[]{:S(2)}, u32[]{:S(2)}) collective-permute-start(bf16[256,512]{1,0:T(8,128)(2,1)S(1)} %collective-permute-done.7.refs_1_), channel_id=1, source_target_pairs={{0,16},{16,0},{32,48},{48,32},{64,80},{80,64},{96,112},{112,96},{1... | collective-permute-start | bytes 786440 | tf_op jit(solution)/shard_map/ppermute | solution.py:501
  54.3 6.8 %collective-permute-start.12 = (bf16[256,128]{1,0:T(8,128)(2,1)S(1)}, bf16[256,128]{1,0:T(8,128)(2,1)S(1)}, u32[]{:S(2)}, u32[]{:S(2)}) collective-permute-start(bf16[256,128]{1,0:T(8,128)(2,1)S(1)} %value.1.v_own), channel_id=1, source_target_pairs={{0,2},{1,3},{2,0},{3,1},{4,6},{5,7},{6,4},{7,5},{8,10},{9,11},{10,... | collective-permute-start | bytes 196616 | tf_op jit(solution)/shard_map/ppermute | solution.py:452
  61.1 13.9 %collective-permute-start.15 = (bf16[512,128]{1,0:T(8,128)(2,1)S(1)}, bf16[512,128]{1,0:T(8,128)(2,1)S(1)}, u32[]{:S(2)}, u32[]{:S(2)}) collective-permute-start(bf16[512,128]{1,0:T(8,128)(2,1)S(1)} %pad_maximum_fusion.1), channel_id=1, source_target_pairs={{0,4},{1,5},{2,6},{3,7},{4,0},{5,1},{6,2},{7,3},{8,12},{9,13},{10,... | collective-permute-start | bytes 393224 | tf_op jit(solution)/shard_map/ppermute | solution.py:452
  61.2 13.8 %collective-permute-start.16 = (bf16[512,128]{1,0:T(8,128)(2,1)S(1)}, bf16[512,128]{1,0:T(8,128)(2,1)S(1)}, u32[]{:S(2)}, u32[]{:S(2)}) collective-permute-start(bf16[512,128]{1,0:T(8,128)(2,1)S(1)} %pad_maximum_fusion.1), channel_id=1, source_target_pairs={{0,8},{1,9},{2,10},{3,11},{4,12},{5,13},{6,14},{7,15},{8,0},{9,1},... | collective-permute-start | bytes 393224 | tf_op jit(solution)/shard_map/ppermute | solution.py:452
  64.2 10.9 %collective-permute-start.17 = (bf16[512,128]{1,0:T(8,128)(2,1)S(1)}, bf16[512,128]{1,0:T(8,128)(2,1)S(1)}, u32[]{:S(2)}, u32[]{:S(2)}) collective-permute-start(bf16[512,128]{1,0:T(8,128)(2,1)S(1)} %pad_maximum_fusion.1), channel_id=1, source_target_pairs={{0,12},{1,13},{2,14},{3,15},{4,8},{5,9},{6,10},{7,11},{8,4},{9,5},... | collective-permute-start | bytes 393224 | tf_op jit(solution)/shard_map/ppermute | solution.py:452
  75.2 2.0 %collective-permute-start.18 = (bf16[2048,128]{1,0:T(8,128)(2,1)S(1)}, bf16[2048,128]{1,0:T(8,128)(2,1)S(1)}, u32[]{:S(2)}, u32[]{:S(2)}) collective-permute-start(bf16[2048,128]{1,0:T(8,128)(2,1)S(1)} %pad_maximum_fusion), channel_id=1, source_target_pairs={{0,1},{1,0},{2,3},{3,2},{4,5},{5,4},{6,7},{7,6},{8,9},{9,8},{10,11... | collective-permute-start | bytes 1572872 | tf_op jit(solution)/shard_map/ppermute | solution.py:452
  85.2 1.3 collective-permute-start.19
  86.4 6.4 %collective-permute-start.20 = (f32[16,128]{1,0:T(8,128)S(1)}, f32[16,128]{1,0:T(8,128)S(1)}, u32[]{:S(2)}, u32[]{:S(2)}) collective-permute-start(f32[16,128]{1,0:T(8,128)S(1)} %add.61), channel_id=1, source_target_pairs={{0,2},{1,3},{2,0},{3,1},{4,6},{5,7},{6,4},{7,5},{8,10},{9,11},{10,... | collective-permute-start | bytes 24584 | tf_op jit(solution)/shard_map/ppermute | solution.py:452
  92.8 9.6 %collective-permute-start.21 = (f32[16,128]{1,0:T(8,128)S(1)}, f32[16,128]{1,0:T(8,128)S(1)}, u32[]{:S(2)}, u32[]{:S(2)}) collective-permute-start(f32[16,128]{1,0:T(8,128)S(1)} %add.62), channel_id=1, source_target_pairs={{0,4},{1,5},{2,6},{3,7},{4,0},{5,1},{6,2},{7,3},{8,12},{9,13},{10,... | collective-permute-start | bytes 24584 | tf_op jit(solution)/shard_map/ppermute | solution.py:452
  102.4 22.3 %collective-permute-start.22 = (f32[16,128]{1,0:T(8,128)S(1)}, f32[16,128]{1,0:T(8,128)S(1)}, u32[]{:S(2)}, u32[]{:S(2)}) collective-permute-start(f32[16,128]{1,0:T(8,128)S(1)} %add.63), channel_id=1, source_target_pairs={{0,12},{1,13},{2,14},{3,15},{4,8},{5,9},{6,10},{7,11},{8,4},{9,5},... | collective-permute-start | bytes 24584 | tf_op jit(solution)/shard_map/ppermute | solution.py:452
  (21 other events, 170.6 us)

commit v10 on v9

--- a/solution.py
+++ b/solution.py
@@ -497,6 +497,27 @@
     far_b = send(high[:, n:], perm=down)
     other_low = send(other, perm=up)
     other_high = send(other, perm=down)
+    def prep(near, book, *pieces):
+        few = ranks // 2
+        shapes = [(few, rows, HD)] * 4
+        kinds = [bf16, f32, f32, bf16]
+        return pl.pallas_call(
+            functools.partial(prep_kernel, near, rows, few, levels),
+            out_shape=[jax.ShapeDtypeStruct(size, kind) for size, kind in zip(shapes, kinds)]
+            + [jax.ShapeDtypeStruct((heads, HD, rows), bf16)] * near,
+            in_specs=[vmem()] + [anywhere()] * len(pieces),
+            out_specs=[anywhere()] * 4 + [vmem()] * near,
+            scratch_shapes=[pltpu.VMEM((few * (rows + TAIL), HD), bf16)]
+            + [pltpu.VMEM(size, kind) for size, kind in zip(shapes, kinds)]
+            + [pltpu.SemaphoreType.DMA((few + 1,)), pltpu.SemaphoreType.DMA((4,))]
+            + [pltpu.VMEM((rows, width), bf16)] * near,
+            compiler_params=pltpu.CompilerParams(vmem_limit_bytes=58 << 20),
+            cost_estimate=cost(0 if near else 1 << 32, 0),
+            name="prep",
+        )(book, *pieces)
+
+    *near, cot_t = prep(True, book, packed, *y_side, x_side, cotangent)
+    far_a, far_b = after(cot_t)((far_a, far_b))
     other_far_a = send(far_a, perm=flip)
     other_far_b = send(far_b, perm=flip)
 
@@ -538,26 +559,6 @@
         name="value",
     )(place, w_value, kv_sum, *rest)
 
-    def prep(near, book, *pieces):
-        few = ranks // 2
-        shapes = [(few, rows, HD)] * 4
-        kinds = [bf16, f32, f32, bf16]
-        return pl.pallas_call(
-            functools.partial(prep_kernel, near, rows, few, levels),
-            out_shape=[jax.ShapeDtypeStruct(size, kind) for size, kind in zip(shapes, kinds)]
-            + [jax.ShapeDtypeStruct((heads, HD, rows), bf16)] * near,
-            in_specs=[vmem()] + [anywhere()] * len(pieces),
-            out_specs=[anywhere()] * 4 + [vmem()] * near,
-            scratch_shapes=[pltpu.VMEM((few * (rows + TAIL), HD), bf16)]
-            + [pltpu.VMEM(size, kind) for size, kind in zip(shapes, kinds)]
-            + [pltpu.SemaphoreType.DMA((few + 1,)), pltpu.SemaphoreType.DMA((4,))]
-            + [pltpu.VMEM((rows, width), bf16)] * near,
-            compiler_params=pltpu.CompilerParams(vmem_limit_bytes=58 << 20),
-            cost_estimate=cost(0 if near else 1 << 32, 0),
-            name="prep",
-        )(book, *pieces)
-
-    *near, cot_t = prep(True, after(kv_sum)(book), *packed[:5], cotangent)
     distant = prep(False, after(value)(book), packed[5])
     keys = distant[0]
 

time: 125 us -> 125 us (level); the launches traced: 125 us -> 123 us
  starting transfers between devices: 63.7 us -> 58.6 us
  waiting for transfers between devices: 13 us -> 15.8 us
    ppermute x14, waiting for transfers between devices: 9.26 us -> 15.8 us  [shards(): lax.ppermute(x, 'tokens', [(i, i ^ d) for i in range(ranks)])]
    ppermute x14, starting transfers between devices: 46.4 us -> 40.9 us  [shards(): lax.ppermute(x, 'tokens', [(i, i ^ d) for i in range(ranks)])]
    ppermute x1, waiting for transfers between devices: 3.1 us -> 0.01 us  [shards(): far_a = send(low[:, :n], perm=up)]
    ppermute x1, starting transfers between devices: 2.07 us -> 0.01 us  [shards(): low = send(hidden, perm=up)]
    ppermute x1, starting transfers between devices: 2.2 us -> 4.19 us  [shards(): high = send(hidden, perm=down)]
    ppermute x1, starting transfers between devices: 1.52 us -> 2.95 us  [shards(): other_far_b = send(far_b, perm=flip)]
    ppermute x1, starting transfers between devices: 2.01 us -> 0.66 us  [shards(): other_far_a = send(far_a, perm=flip)]
  transfers between devices with their start and end apart: 23 -> 23, of which waited for: 8 -> 8; matrix products, arithmetic and copies ran while one was open for 4% -> 5% of each run, Pallas kernels for 25% -> 26%
where the time goes in v10:
time: 125 us; the launch traced here: 123 us
  starting transfers between devices  58.6 us (47%)
  Pallas kernels  38.9 us (31%)
  waiting for transfers between devices  15.8 us (13%)
  local copies, waits for them, and re-layouts  8.52 us (7%)
    ppermute x14, starting transfers between devices, shards(): lax.ppermute(x, 'tokens', [(i, i ^ d) for i in range(ranks)])  40.9 us
    ppermute x14, waiting for transfers between devices, shards(): lax.ppermute(x, 'tokens', [(i, i ^ d) for i in range(ranks)])  15.8 us
    pallas_call x2, Pallas kernels, prep(): pl.pallas_call(functools.partial(prep_kernel, near, rows, few, levels), o...  11.4 us
    pallas_call x1, Pallas kernels, second(): pl.pallas_call(functools.partial(stats_kernel, count, heads, rows, levels...  8.06 us
    pallas_call x1, Pallas kernels, shards(): pl.pallas_call(functools.partial(grad_kernel, heads, rows, levels), out_s...  7.26 us
    pallas_call x1, Pallas kernels, shards(): pl.pallas_call(functools.partial(project_kernel, half, part), out_shape=(...  6.21 us
    unnamed x48, local copies, waits for them, and re-layouts  6.01 us
    ppermute x1, starting transfers between devices, shards(): high = send(hidden, perm=down)  4.19 us
  transfers between devices with their start and end apart: 23, of which 8 were waited for; matrix products, arithmetic and copies ran while one was open for 5% of the time, Pallas kernels for 26%

profile of v10, /device:TPU:0, one launch (start us, length us, event | category | flops | bytes accessed | tf_op | source)
XLA Modules:
  0.0 123.4 jit_solution(15486913688822814413)
XLA Ops:
  0.6 4.2 %collective-permute-start.1 = (bf16[256,1024]{1,0:T(8,128)(2,1)}, bf16[256,1024]{1,0:T(8,128)(2,1)S(1)}, u32[]{:S(2)}, u32[]{:S(2)}) collective-permute-start(bf16[256,1024]{1,0:T(8,128)(2,1)} %refs_0_.1), channel_id=1, source_target_pairs={{0,96},{16,112},{32,0},{48,16},{64,32},{80,48},{96,64},{112,80},{1... | collective-permute-start | bytes 1572872 | tf_op jit(solution)/shard_map/ppermute | solution.py:470
  4.8 3.0 %collective-permute-start.2 = (bf16[256,1024]{1,0:T(8,128)(2,1)}, bf16[256,1024]{1,0:T(8,128)(2,1)S(1)}, u32[]{:S(2)}, u32[]{:S(2)}) collective-permute-start(bf16[256,1024]{1,0:T(8,128)(2,1)} %refs_0_.1), channel_id=1, source_target_pairs={{0,16},{16,0},{32,48},{48,32},{64,80},{80,64},{96,112},{112,96},{1... | collective-permute-start | bytes 1572872 | tf_op jit(solution)/shard_map/ppermute | solution.py:471
  9.4 3.1 %collective-permute-start.5 = (bf16[272,128]{1,0:T(8,128)(2,1)}, bf16[272,128]{1,0:T(8,128)(2,1)S(1)}, u32[]{:S(2)}, u32[]{:S(2)}) collective-permute-start(bf16[272,128]{1,0:T(8,128)(2,1)} %get-tuple-element.38.refs_0_), channel_id=1, source_target_pairs={{0,12},{1,13},{2,14},{3,15},{4,8},{5,9},{6,10},{7,11},{8,4},{9,5},... | collective-permute-start | bytes 208904 | tf_op jit(solution)/shard_map/ppermute | solution.py:452
  14.2 2.8 %collective-permute-done.3.refs_1_ = bf16[272,128]{1,0:T(8,128)(2,1)S(1)} collective-permute-done((bf16[272,128]{1,0:T(8,128)(2,1)}, bf16[272,128]{1,0:T(8,128)(2,1)S(1)}, u32[]{:S(2)}, u32[]{:S(2)}) %collective-permute-start.3) | collective-permute-done | bytes 69664 | tf_op jit(solution)/shard_map/ppermute | solution.py:452
  18.3 4.7 %collective-permute-done.4.refs_2_ = bf16[272,128]{1,0:T(8,128)(2,1)S(1)} collective-permute-done((bf16[272,128]{1,0:T(8,128)(2,1)}, bf16[272,128]{1,0:T(8,128)(2,1)S(1)}, u32[]{:S(2)}, u32[]{:S(2)}) %collective-permute-start.4) | collective-permute-done | bytes 69664 | tf_op jit(solution)/shard_map/ppermute | solution.py:452
  25.7 3.4 %collective-permute-start.7 = (bf16[256,512]{1,0:T(8,128)(2,1)}, bf16[256,512]{1,0:T(8,128)(2,1)S(1)}, u32[]{:S(2)}, u32[]{:S(2)}) collective-permute-start(bf16[256,512]{1,0:T(8,128)(2,1)} %slice.7), channel_id=1, source_target_pairs={{0,96},{16,112},{32,0},{48,16},{64,32},{80,48},{96,64},{112,80},{1... | collective-permute-start | bytes 786440 | tf_op jit(solution)/shard_map/ppermute | solution.py:497
  29.2 1.9 %collective-permute-done.8.refs_4_ = bf16[1088,128]{1,0:T(8,128)(2,1)S(1)} collective-permute-done((bf16[1088,128]{1,0:T(8,128)(2,1)}, bf16[1088,128]{1,0:T(8,128)(2,1)S(1)}, u32[]{:S(2)}, u32[]{:S(2)}) %collective-permute-start.8) | collective-permute-done | bytes 278560 | tf_op jit(solution)/shard_map/ppermute | solution.py:452
  31.9 6.1 %prep.2 = (bf16[8,256,128]{2,1,0:T(8,128)(2,1)}, f32[8,256,128]{2,1,0:T(8,128)}, f32[8,256,128]{2,1,0:T(8,128)}, bf16[8,256,128]{2,1,0:T(8,128)(2,1)}, bf16[8,128,256]{2,1,0:T(8,128)(2,1)}) custom-call(f32[16,128]{1,0:T(8,128)} %bitcast.12, bf16[272,128]{1,0:T(8,128)(2,1)} %get-tuple-element.38.refs_0_, bf16[272,128]{1,0:T(8,128)(2,1)} %copy-done.19, ...), custom_call_target="tpu_custom_call" | custom-call | tf_op jit(solution)/shard_map/prep/pallas_call | solution.py:504
  38.0 3.5 %collective-permute-start.10 = (bf16[256,1024]{1,0:T(8,128)(2,1)S(1)}, bf16[256,1024]{1,0:T(8,128)(2,1)S(1)}, u32[]{:S(2)}, u32[]{:S(2)}) collective-permute-start(bf16[256,1024]{1,0:T(8,128)(2,1)S(1)} %collective-permute-done.2.refs_3_), channel_id=1, source_target_pairs={{0,96},{16,112},{32,0},{48,16},{64,32},{80,48},{96,64},{112,80},{1... | collective-permute-start | bytes 1572872 | tf_op jit(solution)/shard_map/ppermute | solution.py:499
  42.2 3.0 %collective-permute-start.12 = (bf16[256,512]{1,0:T(8,128)(2,1)S(1)}, bf16[256,512]{1,0:T(8,128)(2,1)S(1)}, u32[]{:S(2)}, u32[]{:S(2)}) collective-permute-start(bf16[256,512]{1,0:T(8,128)(2,1)S(1)} %collective-permute-done.7.refs_1_), channel_id=1, source_target_pairs={{0,16},{16,0},{32,48},{48,32},{64,80},{80,64},{96,112},{112,96},{1... | collective-permute-start | bytes 786440 | tf_op jit(solution)/shard_map/ppermute | solution.py:522
  45.1 1.7 %constant_dynamic-update-slice_fusion.4 = bf16[2176,128]{1,0:T(8,128)(2,1)} fusion(bf16[2176,128]{1,0:T(8,128)(2,1)} %copy-done.21, bf16[1088,128]{1,0:T(8,128)(2,1)} %copy-done.17), kind=kLoop, calls=%fused_computation.6 | loop fusion | bytes 557056 | tf_op jit(solution)/shard_map/concatenate | solution.py:542
  46.8 6.2 %project.1 = (f32[256,1024]{1,0:T(8,128)S(1)}, f32[256,256]{1,0:T(8,128)S(1)}) custom-call(s32[8]{0:T(128)S(1)} %stack.35.place, bf16[8192,1024]{1,0:T(8,128)(2,1)} %wq.3, bf16[8192,128]{1,0:T(8,128)(2,1)} %wk.3, bf16[8192,128]{1,0:T(8,128)(2,1)} %w.1, bf16[256,1024]{1,0:T(8,128)(2,1)S(1)} %copy-done.6, bf16[256,1024]{1,0:T(8,128)(2,1)S(1)} %collective-permute-done.refs_1_, ...), custom_call_target="tpu_custom_call" | custom-call | flops 17179869184 | tf_op jit(solution)/shard_map/project/pallas_call | solution.py:526
  53.1 2.7 %value.1.v_own = bf16[256,128]{1,0:T(8,128)(2,1)S(1)} custom-call(s32[8]{0:T(128)S(1)} %stack.35.place, bf16[8192,128]{1,0:T(8,128)(2,1)} %w.1, f32[256,256]{1,0:T(8,128)S(1)} %get-tuple-element.48.before.kv_before, bf16[256,512]{1,0:T(8,128)(2,1)S(1)} %collective-permute-done.6.refs_0_, bf16[256,512]{1,0:T(8,128)(2,1)S(1)} %collective-permute-done.7.refs_1_, ...), custom_call_target="tpu_custom_call" | custom-call | tf_op jit(solution)/shard_map/value/pallas_call | solution.py:546
  56.5 5.3 %prep.3 = (bf16[8,256,128]{2,1,0:T(8,128)(2,1)}, f32[8,256,128]{2,1,0:T(8,128)}, f32[8,256,128]{2,1,0:T(8,128)}, bf16[8,256,128]{2,1,0:T(8,128)(2,1)}) custom-call(f32[16,128]{1,0:T(8,128)} %bitcast.13, bf16[2176,128]{1,0:T(8,128)(2,1)} %collective-permute-done.14.refs_0_), custom_call_target="tpu_custom_call" | custom-call | flops 4294967296 | tf_op jit(solution)/shard_map/prep/pallas_call | solution.py:504
  62.0 2.0 %collective-permute-start.16 = (bf16[512,128]{1,0:T(8,128)(2,1)S(1)}, bf16[512,128]{1,0:T(8,128)(2,1)S(1)}, u32[]{:S(2)}, u32[]{:S(2)}) collective-permute-start(bf16[512,128]{1,0:T(8,128)(2,1)S(1)} %pad_maximum_fusion.1), channel_id=1, source_target_pairs={{0,8},{1,9},{2,10},{3,11},{4,12},{5,13},{6,14},{7,15},{8,0},{9,1},... | collective-permute-start | bytes 393224 | tf_op jit(solution)/shard_map/ppermute | solution.py:452
  64.0 2.1 %collective-permute-start.15 = (bf16[512,128]{1,0:T(8,128)(2,1)S(1)}, bf16[512,128]{1,0:T(8,128)(2,1)S(1)}, u32[]{:S(2)}, u32[]{:S(2)}) collective-permute-start(bf16[512,128]{1,0:T(8,128)(2,1)S(1)} %pad_maximum_fusion.1), channel_id=1, source_target_pairs={{0,4},{1,5},{2,6},{3,7},{4,0},{5,1},{6,2},{7,3},{8,12},{9,13},{10,... | collective-permute-start | bytes 393224 | tf_op jit(solution)/shard_map/ppermute | solution.py:452
  67.1 8.1 %stats.1 = (bf16[8,256,128]{2,1,0:T(8,128)(2,1)S(1)}, bf16[8,128,256]{2,1,0:T(8,128)(2,1)S(1)}, f32[3,256]{1,0:T(4,128)S(1)}, f32[16,128]{1,0:T(8,128)S(1)}) custom-call(s32[8]{0:T(128)S(1)} %stack.35.place, s32[2]{0:T(128)S(1)} %copy-done.11, s32[1,256]{1,0:T(1,128)S(1)} %copy-done.10, s32[256,128]{1,0:T(8,128)S(1)} %copy-done.2, f32[16,128]{1,0:T(8,128)S(1)} %bitcast.14, ...), custom_call_target="tpu_custom_call" | custom-call | flops 17179869184 | tf_op jit(solution)/shard_map/stats/pallas_call | solution.py:570
  75.4 1.6 %stats_late.1.log_total_1 = f32[5,256]{1,0:T(8,128)S(1)} custom-call(s32[2]{0:T(128)S(1)} %copy-done.11, s32[1,256]{1,0:T(1,128)S(1)} %copy-done.10, bf16[8,128,256]{2,1,0:T(8,128)(2,1)S(1)} %get-tuple-element.63.q_t, bf16[8,256,128]{2,1,0:T(8,128)(2,1)S(1)} %copy-done.7, bf16[8,256,128]{2,1,0:T(8,128)(2,1)S(1)} %copy-done.14), custom_call_target="tpu_custom_call" | custom-call | flops 17179869184 | tf_op jit(solution)/shard_map/stats_late/pallas_call | solution.py:608
  78.0 7.3 %grad.1 = (bf16[256,1024]{1,0:T(8,128)(2,1)}, f32[16,128]{1,0:T(8,128)S(1)}) custom-call(s32[2]{0:T(128)S(1)} %copy-done.11, bf16[8,256,128]{2,1,0:T(8,128)(2,1)S(1)} %get-tuple-element.59.q_rot, bf16[8,128,256]{2,1,0:T(8,128)(2,1)S(1)} %get-tuple-element.63.q_t, f32[3,256]{1,0:T(4,128)S(1)} %get-tuple-element.61.log_total_0, ...), custom_call_target="tpu_custom_call" | custom-call | flops 8589934592 | bytes 8388608 | tf_op jit(solution)/shard_map/grad/pallas_call | solution.py:621
  86.6 5.4 %collective-permute-start.20 = (f32[16,128]{1,0:T(8,128)S(1)}, f32[16,128]{1,0:T(8,128)S(1)}, u32[]{:S(2)}, u32[]{:S(2)}) collective-permute-start(f32[16,128]{1,0:T(8,128)S(1)} %add.61), channel_id=1, source_target_pairs={{0,2},{1,3},{2,0},{3,1},{4,6},{5,7},{6,4},{7,5},{8,10},{9,11},{10,... | collective-permute-start | bytes 24584 | tf_op jit(solution)/shard_map/ppermute | solution.py:452
  92.0 1.6 %collective-permute-done.20 = f32[16,128]{1,0:T(8,128)S(1)} collective-permute-done((f32[16,128]{1,0:T(8,128)S(1)}, f32[16,128]{1,0:T(8,128)S(1)}, u32[]{:S(2)}, u32[]{:S(2)}) %collective-permute-start.20) | collective-permute-done | bytes 8224 | tf_op jit(solution)/shard_map/ppermute | solution.py:452
  93.6 4.7 %collective-permute-start.21 = (f32[16,128]{1,0:T(8,128)S(1)}, f32[16,128]{1,0:T(8,128)S(1)}, u32[]{:S(2)}, u32[]{:S(2)}) collective-permute-start(f32[16,128]{1,0:T(8,128)S(1)} %add.62), channel_id=1, source_target_pairs={{0,4},{1,5},{2,6},{3,7},{4,0},{5,1},{6,2},{7,3},{8,12},{9,13},{10,... | collective-permute-start | bytes 24584 | tf_op jit(solution)/shard_map/ppermute | solution.py:452
  100.0 21.3 %collective-permute-start.22 = (f32[16,128]{1,0:T(8,128)S(1)}, f32[16,128]{1,0:T(8,128)S(1)}, u32[]{:S(2)}, u32[]{:S(2)}) collective-permute-start(f32[16,128]{1,0:T(8,128)S(1)} %add.63), channel_id=1, source_target_pairs={{0,12},{1,13},{2,14},{3,15},{4,8},{5,9},{6,10},{7,11},{8,4},{9,5},... | collective-permute-start | bytes 24584 | tf_op jit(solution)/shard_map/ppermute | solution.py:452
  121.2 1.6 %collective-permute-done.22 = f32[16,128]{1,0:T(8,128)S(1)} collective-permute-done((f32[16,128]{1,0:T(8,128)S(1)}, f32[16,128]{1,0:T(8,128)S(1)}, u32[]{:S(2)}, u32[]{:S(2)}) %collective-permute-start.22) | collective-permute-done | bytes 8224 | tf_op jit(solution)/shard_map/ppermute | solution.py:452
  (88 shorter events, 15.1 us)
Async XLA Ops:
  0.6 46.2 %copy-start.6 = (bf16[256,1024]{1,0:T(8,128)(2,1)S(1)}, bf16[256,1024]{1,0:T(8,128)(2,1)}, u32[]{:S(2)}) copy-start(bf16[256,1024]{1,0:T(8,128)(2,1)} %refs_0_.1) | copy-start | bytes 1572868
  0.6 24.3 %collective-permute-start.1 = (bf16[256,1024]{1,0:T(8,128)(2,1)}, bf16[256,1024]{1,0:T(8,128)(2,1)S(1)}, u32[]{:S(2)}, u32[]{:S(2)}) collective-permute-start(bf16[256,1024]{1,0:T(8,128)(2,1)} %refs_0_.1), channel_id=1, source_target_pairs={{0,96},{16,112},{32,0},{48,16},{64,32},{80,48},{96,64},{112,80},{1... | collective-permute-start | bytes 1572872 | tf_op jit(solution)/shard_map/ppermute | solution.py:470
  4.8 20.2 %collective-permute-start = (bf16[256,1024]{1,0:T(8,128)(2,1)}, bf16[256,1024]{1,0:T(8,128)(2,1)S(1)}, u32[]{:S(2)}, u32[]{:S(2)}) collective-permute-start(bf16[256,1024]{1,0:T(8,128)(2,1)} %refs_0_.1), channel_id=1, source_target_pairs={{0,32},{16,48},{32,64},{48,80},{64,96},{80,112},{96,0},{112,16},{1... | collective-permute-start | bytes 1572872 | tf_op jit(solution)/shard_map/ppermute | solution.py:469
  4.8 20.2 %collective-permute-start.2 = (bf16[256,1024]{1,0:T(8,128)(2,1)}, bf16[256,1024]{1,0:T(8,128)(2,1)S(1)}, u32[]{:S(2)}, u32[]{:S(2)}) collective-permute-start(bf16[256,1024]{1,0:T(8,128)(2,1)} %refs_0_.1), channel_id=1, source_target_pairs={{0,16},{16,0},{32,48},{48,32},{64,80},{80,64},{96,112},{112,96},{1... | collective-permute-start | bytes 1572872 | tf_op jit(solution)/shard_map/ppermute | solution.py:471
  9.4 14.3 %collective-permute-start.5 = (bf16[272,128]{1,0:T(8,128)(2,1)}, bf16[272,128]{1,0:T(8,128)(2,1)S(1)}, u32[]{:S(2)}, u32[]{:S(2)}) collective-permute-start(bf16[272,128]{1,0:T(8,128)(2,1)} %get-tuple-element.38.refs_0_), channel_id=1, source_target_pairs={{0,12},{1,13},{2,14},{3,15},{4,8},{5,9},{6,10},{7,11},{8,4},{9,5},... | collective-permute-start | bytes 208904 | tf_op jit(solution)/shard_map/ppermute | solution.py:452
  12.5 4.5 %collective-permute-start.3 = (bf16[272,128]{1,0:T(8,128)(2,1)}, bf16[272,128]{1,0:T(8,128)(2,1)S(1)}, u32[]{:S(2)}, u32[]{:S(2)}) collective-permute-start(bf16[272,128]{1,0:T(8,128)(2,1)} %get-tuple-element.38.refs_0_), channel_id=1, source_target_pairs={{0,4},{1,5},{2,6},{3,7},{4,0},{5,1},{6,2},{7,3},{8,12},{9,13},{10,... | collective-permute-start | bytes 208904 | tf_op jit(solution)/shard_map/ppermute | solution.py:452
  17.0 6.0 %collective-permute-start.4 = (bf16[272,128]{1,0:T(8,128)(2,1)}, bf16[272,128]{1,0:T(8,128)(2,1)S(1)}, u32[]{:S(2)}, u32[]{:S(2)}) collective-permute-start(bf16[272,128]{1,0:T(8,128)(2,1)} %get-tuple-element.38.refs_0_), channel_id=1, source_target_pairs={{0,8},{1,9},{2,10},{3,11},{4,12},{5,13},{6,14},{7,15},{8,0},{9,1},... | collective-permute-start | bytes 208904 | tf_op jit(solution)/shard_map/ppermute | solution.py:452
  24.4 6.8 %collective-permute-start.8 = (bf16[1088,128]{1,0:T(8,128)(2,1)}, bf16[1088,128]{1,0:T(8,128)(2,1)S(1)}, u32[]{:S(2)}, u32[]{:S(2)}) collective-permute-start(bf16[1088,128]{1,0:T(8,128)(2,1)} %get-tuple-element.73), channel_id=1, source_target_pairs={{0,2},{1,3},{2,0},{3,1},{4,6},{5,7},{6,4},{7,5},{8,10},{9,11},{10,... | collective-permute-start | bytes 835592 | tf_op jit(solution)/shard_map/ppermute | solution.py:452
  25.7 15.8 %collective-permute-start.7 = (bf16[256,512]{1,0:T(8,128)(2,1)}, bf16[256,512]{1,0:T(8,128)(2,1)S(1)}, u32[]{:S(2)}, u32[]{:S(2)}) collective-permute-start(bf16[256,512]{1,0:T(8,128)(2,1)} %slice.7), channel_id=1, source_target_pairs={{0,96},{16,112},{32,0},{48,16},{64,32},{80,48},{96,64},{112,80},{1... | collective-permute-start | bytes 786440 | tf_op jit(solution)/shard_map/ppermute | solution.py:497
  29.2 12.3 %collective-permute-start.6 = (bf16[256,512]{1,0:T(8,128)(2,1)S(1)}, bf16[256,512]{1,0:T(8,128)(2,1)S(1)}, u32[]{:S(2)}, u32[]{:S(2)}) collective-permute-start(bf16[256,512]{1,0:T(8,128)(2,1)S(1)} %slice.6), channel_id=1, source_target_pairs={{0,32},{16,48},{32,64},{48,80},{64,96},{80,112},{96,0},{112,16},{1... | collective-permute-start | bytes 786440 | tf_op jit(solution)/shard_map/ppermute | solution.py:496
  38.0 15.0 %collective-permute-start.10 = (bf16[256,1024]{1,0:T(8,128)(2,1)S(1)}, bf16[256,1024]{1,0:T(8,128)(2,1)S(1)}, u32[]{:S(2)}, u32[]{:S(2)}) collective-permute-start(bf16[256,1024]{1,0:T(8,128)(2,1)S(1)} %collective-permute-done.2.refs_3_), channel_id=1, source_target_pairs={{0,96},{16,112},{32,0},{48,16},{64,32},{80,48},{96,64},{112,80},{1... | collective-permute-start | bytes 1572872 | tf_op jit(solution)/shard_map/ppermute | solution.py:499
  41.5 11.6 %collective-permute-start.9 = (bf16[256,1024]{1,0:T(8,128)(2,1)S(1)}, bf16[256,1024]{1,0:T(8,128)(2,1)S(1)}, u32[]{:S(2)}, u32[]{:S(2)}) collective-permute-start(bf16[256,1024]{1,0:T(8,128)(2,1)S(1)} %collective-permute-done.2.refs_3_), channel_id=1, source_target_pairs={{0,32},{16,48},{32,64},{48,80},{64,96},{80,112},{96,0},{112,16},{1... | collective-permute-start | bytes 1572872 | tf_op jit(solution)/shard_map/ppermute | solution.py:498
  41.5 11.6 %collective-permute-start.11 = (bf16[256,512]{1,0:T(8,128)(2,1)S(1)}, bf16[256,512]{1,0:T(8,128)(2,1)S(1)}, u32[]{:S(2)}, u32[]{:S(2)}) collective-permute-start(bf16[256,512]{1,0:T(8,128)(2,1)S(1)} %collective-permute-done.6.refs_0_), channel_id=1, source_target_pairs={{0,16},{16,0},{32,48},{48,32},{64,80},{80,64},{96,112},{112,96},{1... | collective-permute-start | bytes 786440 | tf_op jit(solution)/shard_map/ppermute | solution.py:521
  42.2 10.9 %collective-permute-start.12 = (bf16[256,512]{1,0:T(8,128)(2,1)S(1)}, bf16[256,512]{1,0:T(8,128)(2,1)S(1)}, u32[]{:S(2)}, u32[]{:S(2)}) collective-permute-start(bf16[256,512]{1,0:T(8,128)(2,1)S(1)} %collective-permute-done.7.refs_1_), channel_id=1, source_target_pairs={{0,16},{16,0},{32,48},{48,32},{64,80},{80,64},{96,112},{112,96},{1... | collective-permute-start | bytes 786440 | tf_op jit(solution)/shard_map/ppermute | solution.py:522
  46.8 9.7 %collective-permute-start.14 = (bf16[2176,128]{1,0:T(8,128)(2,1)}, bf16[2176,128]{1,0:T(8,128)(2,1)}, u32[]{:S(2)}, u32[]{:S(2)}) collective-permute-start(bf16[2176,128]{1,0:T(8,128)(2,1)} %constant_dynamic-update-slice_fusion.4), channel_id=1, source_target_pairs={{0,1},{1,0},{2,3},{3,2},{4,5},{5,4},{6,7},{7,6},{8,9},{9,8},{10,11... | collective-permute-start | bytes 1671176 | tf_op jit(solution)/shard_map/ppermute | solution.py:452
  55.9 6.0 %collective-permute-start.13 = (bf16[256,128]{1,0:T(8,128)(2,1)S(1)}, bf16[256,128]{1,0:T(8,128)(2,1)S(1)}, u32[]{:S(2)}, u32[]{:S(2)}) collective-permute-start(bf16[256,128]{1,0:T(8,128)(2,1)S(1)} %value.1.v_own), channel_id=1, source_target_pairs={{0,2},{1,3},{2,0},{3,1},{4,6},{5,7},{6,4},{7,5},{8,10},{9,11},{10,... | collective-permute-start | bytes 196616 | tf_op jit(solution)/shard_map/ppermute | solution.py:452
  61.9 13.3 %collective-permute-start.17 = (bf16[512,128]{1,0:T(8,128)(2,1)S(1)}, bf16[512,128]{1,0:T(8,128)(2,1)S(1)}, u32[]{:S(2)}, u32[]{:S(2)}) collective-permute-start(bf16[512,128]{1,0:T(8,128)(2,1)S(1)} %pad_maximum_fusion.1), channel_id=1, source_target_pairs={{0,12},{1,13},{2,14},{3,15},{4,8},{5,9},{6,10},{7,11},{8,4},{9,5},... | collective-permute-start | bytes 393224 | tf_op jit(solution)/shard_map/ppermute | solution.py:452
  62.0 13.2 %collective-permute-start.16 = (bf16[512,128]{1,0:T(8,128)(2,1)S(1)}, bf16[512,128]{1,0:T(8,128)(2,1)S(1)}, u32[]{:S(2)}, u32[]{:S(2)}) collective-permute-start(bf16[512,128]{1,0:T(8,128)(2,1)S(1)} %pad_maximum_fusion.1), channel_id=1, source_target_pairs={{0,8},{1,9},{2,10},{3,11},{4,12},{5,13},{6,14},{7,15},{8,0},{9,1},... | collective-permute-start | bytes 393224 | tf_op jit(solution)/shard_map/ppermute | solution.py:452
  64.0 11.2 %collective-permute-start.15 = (bf16[512,128]{1,0:T(8,128)(2,1)S(1)}, bf16[512,128]{1,0:T(8,128)(2,1)S(1)}, u32[]{:S(2)}, u32[]{:S(2)}) collective-permute-start(bf16[512,128]{1,0:T(8,128)(2,1)S(1)} %pad_maximum_fusion.1), channel_id=1, source_target_pairs={{0,4},{1,5},{2,6},{3,7},{4,0},{5,1},{6,2},{7,3},{8,12},{9,13},{10,... | collective-permute-start | bytes 393224 | tf_op jit(solution)/shard_map/ppermute | solution.py:452
  75.3 2.0 %collective-permute-start.18 = (bf16[2048,128]{1,0:T(8,128)(2,1)S(1)}, bf16[2048,128]{1,0:T(8,128)(2,1)S(1)}, u32[]{:S(2)}, u32[]{:S(2)}) collective-permute-start(bf16[2048,128]{1,0:T(8,128)(2,1)S(1)} %pad_maximum_fusion), channel_id=1, source_target_pairs={{0,1},{1,0},{2,3},{3,2},{4,5},{5,4},{6,7},{7,6},{8,9},{9,8},{10,11... | collective-permute-start | bytes 1572872 | tf_op jit(solution)/shard_map/ppermute | solution.py:452
  85.3 1.3 %collective-permute-start.19 = (f32[16,128]{1,0:T(8,128)S(1)}, f32[16,128]{1,0:T(8,128)S(1)}, u32[]{:S(2)}, u32[]{:S(2)}) collective-permute-start(f32[16,128]{1,0:T(8,128)S(1)} %get-tuple-element.71), channel_id=1, source_target_pairs={{0,1},{1,0},{2,3},{3,2},{4,5},{5,4},{6,7},{7,6},{8,9},{9,8},{10,11... | collective-permute-start | bytes 24584 | tf_op jit(solution)/shard_map/ppermute | solution.py:452
  86.6 7.1 %collective-permute-start.20 = (f32[16,128]{1,0:T(8,128)S(1)}, f32[16,128]{1,0:T(8,128)S(1)}, u32[]{:S(2)}, u32[]{:S(2)}) collective-permute-start(f32[16,128]{1,0:T(8,128)S(1)} %add.61), channel_id=1, source_target_pairs={{0,2},{1,3},{2,0},{3,1},{4,6},{5,7},{6,4},{7,5},{8,10},{9,11},{10,... | collective-permute-start | bytes 24584 | tf_op jit(solution)/shard_map/ppermute | solution.py:452
  93.6 6.3 %collective-permute-start.21 = (f32[16,128]{1,0:T(8,128)S(1)}, f32[16,128]{1,0:T(8,128)S(1)}, u32[]{:S(2)}, u32[]{:S(2)}) collective-permute-start(f32[16,128]{1,0:T(8,128)S(1)} %add.62), channel_id=1, source_target_pairs={{0,4},{1,5},{2,6},{3,7},{4,0},{5,1},{6,2},{7,3},{8,12},{9,13},{10,... | collective-permute-start | bytes 24584 | tf_op jit(solution)/shard_map/ppermute | solution.py:452
  100.0 22.9 %collective-permute-start.22 = (f32[16,128]{1,0:T(8,128)S(1)}, f32[16,128]{1,0:T(8,128)S(1)}, u32[]{:S(2)}, u32[]{:S(2)}) collective-permute-start(f32[16,128]{1,0:T(8,128)S(1)} %add.63), channel_id=1, source_target_pairs={{0,12},{1,13},{2,14},{3,15},{4,8},{5,9},{6,10},{7,11},{8,4},{9,5},... | collective-permute-start | bytes 24584 | tf_op jit(solution)/shard_map/ppermute | solution.py:452
  (21 other events, 110.7 us)

commit v11 on v8

--- a/solution.py
+++ b/solution.py
@@ -495,13 +495,7 @@
     low, high, other = after(column)((low, high, other))
     far_a = send(low[:, :n], perm=up)
     far_b = send(high[:, n:], perm=down)
-    other_low = send(other, perm=up)
-    other_high = send(other, perm=down)
-    other_far_a = send(far_a, perm=flip)
-    other_far_b = send(far_b, perm=flip)
-
     half = group // 2
-    low, high, other = after(far_a, far_b)((low, high, other))
     q_sum, kv_sum = pl.pallas_call(
         functools.partial(project_kernel, half, part),
         out_shape=(jax.ShapeDtypeStruct((rows, width), f32), jax.ShapeDtypeStruct((rows, 2 * HD), f32)),
@@ -517,6 +511,11 @@
         cost_estimate=cost(1 << 34, 0),
         name="project",
     )(place, w_query, w_key, w_value, hidden, low, high, other)
+    far_a, far_b, other, x_side = after(kv_sum)((far_a, far_b, other, x_side))
+    other_low = send(other, perm=up)
+    other_high = send(other, perm=down)
+    other_far_a = send(far_a, perm=flip)
+    other_far_b = send(far_b, perm=flip)
     core = cross(jnp.concatenate([column, x_side], axis=0), 1)
     packed = (packed, *y_side, x_side, core)
 
@@ -552,7 +551,7 @@
             + [pltpu.SemaphoreType.DMA((few + 1,)), pltpu.SemaphoreType.DMA((4,))]
             + [pltpu.VMEM((rows, width), bf16)] * near,
             compiler_params=pltpu.CompilerParams(vmem_limit_bytes=58 << 20),
-            cost_estimate=cost(0 if near else 1 << 32, 0),
+            cost_estimate=cost(1 << 34 if near else 1 << 32, 0),
             name="prep",
         )(book, *pieces)
 

time: 124 us -> 123 us (level)
  local copies, waits for them, and re-layouts: 7.96 us -> 3.9 us
  starting transfers between devices: 63.4 us -> 65.9 us
    unnamed x48 -> x46, local copies, waits for them, and re-layouts: 6.35 us -> 3.74 us
    ppermute x14, starting transfers between devices: 46.1 us -> 48.4 us  [shards(): lax.ppermute(x, 'tokens', [(i, i ^ d) for i in range(ranks)])]
    ppermute x1, waiting for transfers between devices: 0.01 us -> 1.8 us  [shards(): other_far_b = send(far_b, perm=flip)]
    ppermute x1, starting transfers between devices: 2.8 us -> 1.52 us  [shards(): other_far_b = send(far_b, perm=flip)]
    ppermute x1, starting transfers between devices: 0.74 us -> 2.01 us  [shards(): other_far_a = send(far_a, perm=flip)]
    ppermute x14, waiting for transfers between devices: 11.3 us -> 10 us  [shards(): lax.ppermute(x, 'tokens', [(i, i ^ d) for i in range(ranks)])]
  transfers between devices with their start and end apart: 23 -> 23, of which waited for: 7 -> 8; matrix products, arithmetic and copies ran while one was open for 4% -> 1% of each run, Pallas kernels for 26% -> 26%
where the time goes in v11:
time: 123 us; the launch traced here: 122 us
  starting transfers between devices  65.9 us (54%)
  Pallas kernels  38.9 us (32%)
  waiting for transfers between devices  11.8 us (10%)
  local copies, waits for them, and re-layouts  3.9 us (3%)
    ppermute x14, starting transfers between devices, shards(): lax.ppermute(x, 'tokens', [(i, i ^ d) for i in range(ranks)])  48.4 us
    pallas_call x2, Pallas kernels, prep(): pl.pallas_call(functools.partial(prep_kernel, near, rows, few, levels), o...  11.5 us
    ppermute x14, waiting for transfers between devices, shards(): lax.ppermute(x, 'tokens', [(i, i ^ d) for i in range(ranks)])  10 us
    pallas_call x1, Pallas kernels, second(): pl.pallas_call(functools.partial(stats_kernel, count, heads, rows, levels...  8.06 us
    pallas_call x1, Pallas kernels, shards(): pl.pallas_call(functools.partial(grad_kernel, heads, rows, levels), out_s...  7.27 us
    pallas_call x1, Pallas kernels, shards(): pl.pallas_call(functools.partial(project_kernel, half, part), out_shape=(...  6.2 us
    unnamed x46, local copies, waits for them, and re-layouts  3.74 us
    ppermute x1, starting transfers between devices, shards(): far_b = send(high[:, n:], perm=down)  3.29 us
  transfers between devices with their start and end apart: 23, of which 8 were waited for; matrix products, arithmetic and copies ran while one was open for 1% of the time, Pallas kernels for 26%

profile of v11, /device:TPU:0, one launch (start us, length us, event | category | flops | bytes accessed | tf_op | source)
XLA Modules:
  0.0 122.2 jit_solution(4592818603591491459)
XLA Ops:
  0.6 2.1 %collective-permute-start = (bf16[256,1024]{1,0:T(8,128)(2,1)}, bf16[256,1024]{1,0:T(8,128)(2,1)S(1)}, u32[]{:S(2)}, u32[]{:S(2)}) collective-permute-start(bf16[256,1024]{1,0:T(8,128)(2,1)} %refs_0_.1), channel_id=1, source_target_pairs={{0,32},{16,48},{32,64},{48,80},{64,96},{80,112},{96,0},{112,16},{1... | collective-permute-start | bytes 1572872 | tf_op jit(solution)/shard_map/ppermute | solution.py:469
  2.7 2.2 %collective-permute-start.1 = (bf16[256,1024]{1,0:T(8,128)(2,1)}, bf16[256,1024]{1,0:T(8,128)(2,1)S(1)}, u32[]{:S(2)}, u32[]{:S(2)}) collective-permute-start(bf16[256,1024]{1,0:T(8,128)(2,1)} %refs_0_.1), channel_id=1, source_target_pairs={{0,96},{16,112},{32,0},{48,16},{64,32},{80,48},{96,64},{112,80},{1... | collective-permute-start | bytes 1572872 | tf_op jit(solution)/shard_map/ppermute | solution.py:470
  4.9 3.0 %collective-permute-start.2 = (bf16[256,1024]{1,0:T(8,128)(2,1)}, bf16[256,1024]{1,0:T(8,128)(2,1)S(1)}, u32[]{:S(2)}, u32[]{:S(2)}) collective-permute-start(bf16[256,1024]{1,0:T(8,128)(2,1)} %refs_0_.1), channel_id=1, source_target_pairs={{0,16},{16,0},{32,48},{48,32},{64,80},{80,64},{96,112},{112,96},{1... | collective-permute-start | bytes 1572872 | tf_op jit(solution)/shard_map/ppermute | solution.py:471
  9.5 1.7 %collective-permute-start.3 = (bf16[272,128]{1,0:T(8,128)(2,1)}, bf16[272,128]{1,0:T(8,128)(2,1)S(1)}, u32[]{:S(2)}, u32[]{:S(2)}) collective-permute-start(bf16[272,128]{1,0:T(8,128)(2,1)} %get-tuple-element.37.refs_0_), channel_id=1, source_target_pairs={{0,4},{1,5},{2,6},{3,7},{4,0},{5,1},{6,2},{7,3},{8,12},{9,13},{10,... | collective-permute-start | bytes 208904 | tf_op jit(solution)/shard_map/ppermute | solution.py:452
  11.2 2.9 %collective-permute-start.4 = (bf16[272,128]{1,0:T(8,128)(2,1)}, bf16[272,128]{1,0:T(8,128)(2,1)S(1)}, u32[]{:S(2)}, u32[]{:S(2)}) collective-permute-start(bf16[272,128]{1,0:T(8,128)(2,1)} %get-tuple-element.37.refs_0_), channel_id=1, source_target_pairs={{0,8},{1,9},{2,10},{3,11},{4,12},{5,13},{6,14},{7,15},{8,0},{9,1},... | collective-permute-start | bytes 208904 | tf_op jit(solution)/shard_map/ppermute | solution.py:452
  15.1 2.0 %collective-permute-start.5 = (bf16[272,128]{1,0:T(8,128)(2,1)}, bf16[272,128]{1,0:T(8,128)(2,1)S(1)}, u32[]{:S(2)}, u32[]{:S(2)}) collective-permute-start(bf16[272,128]{1,0:T(8,128)(2,1)} %get-tuple-element.37.refs_0_), channel_id=1, source_target_pairs={{0,12},{1,13},{2,14},{3,15},{4,8},{5,9},{6,10},{7,11},{8,4},{9,5},... | collective-permute-start | bytes 208904 | tf_op jit(solution)/shard_map/ppermute | solution.py:452
  17.3 3.6 %collective-permute-done.5.refs_3_ = bf16[272,128]{1,0:T(8,128)(2,1)S(1)} collective-permute-done((bf16[272,128]{1,0:T(8,128)(2,1)}, bf16[272,128]{1,0:T(8,128)(2,1)S(1)}, u32[]{:S(2)}, u32[]{:S(2)}) %collective-permute-start.5) | collective-permute-done | bytes 69664 | tf_op jit(solution)/shard_map/ppermute | solution.py:452
  21.7 3.3 %collective-permute-start.7 = (bf16[256,512]{1,0:T(8,128)(2,1)S(1)}, bf16[256,512]{1,0:T(8,128)(2,1)S(1)}, u32[]{:S(2)}, u32[]{:S(2)}) collective-permute-start(bf16[256,512]{1,0:T(8,128)(2,1)S(1)} %slice.7), channel_id=1, source_target_pairs={{0,96},{16,112},{32,0},{48,16},{64,32},{80,48},{96,64},{112,80},{1... | collective-permute-start | bytes 786440 | tf_op jit(solution)/shard_map/ppermute | solution.py:497
  25.0 6.2 %project.1 = (f32[256,1024]{1,0:T(8,128)S(1)}, f32[256,256]{1,0:T(8,128)S(1)}) custom-call(s32[8]{0:T(128)S(1)} %stack.35.place, bf16[8192,1024]{1,0:T(8,128)(2,1)} %wq.3, bf16[8192,128]{1,0:T(8,128)(2,1)} %wk.3, bf16[8192,128]{1,0:T(8,128)(2,1)} %w.1, bf16[256,1024]{1,0:T(8,128)(2,1)S(1)} %copy-done.2, bf16[256,1024]{1,0:T(8,128)(2,1)S(1)} %collective-permute-done.refs_1_, ...), custom_call_target="tpu_custom_call" | custom-call | flops 17179869184 | tf_op jit(solution)/shard_map/project/pallas_call | solution.py:499
  32.3 3.2 %collective-permute-start.10 = (bf16[256,1024]{1,0:T(8,128)(2,1)S(1)}, bf16[256,1024]{1,0:T(8,128)(2,1)S(1)}, u32[]{:S(2)}, u32[]{:S(2)}) collective-permute-start(bf16[256,1024]{1,0:T(8,128)(2,1)S(1)} %collective-permute-done.2.refs_3_), channel_id=1, source_target_pairs={{0,96},{16,112},{32,0},{48,16},{64,32},{80,48},{96,64},{112,80},{1... | collective-permute-start | bytes 1572872 | tf_op jit(solution)/shard_map/ppermute | solution.py:516
  35.6 2.0 %collective-permute-start.11 = (bf16[256,512]{1,0:T(8,128)(2,1)S(1)}, bf16[256,512]{1,0:T(8,128)(2,1)S(1)}, u32[]{:S(2)}, u32[]{:S(2)}) collective-permute-start(bf16[256,512]{1,0:T(8,128)(2,1)S(1)} %collective-permute-done.6.refs_0_), channel_id=1, source_target_pairs={{0,16},{16,0},{32,48},{48,32},{64,80},{80,64},{96,112},{112,96},{1... | collective-permute-start | bytes 786440 | tf_op jit(solution)/shard_map/ppermute | solution.py:517
  39.2 6.1 %prep.3 = (bf16[8,256,128]{2,1,0:T(8,128)(2,1)}, f32[8,256,128]{2,1,0:T(8,128)}, f32[8,256,128]{2,1,0:T(8,128)}, bf16[8,256,128]{2,1,0:T(8,128)(2,1)}, bf16[8,128,256]{2,1,0:T(8,128)(2,1)}) custom-call(f32[16,128]{1,0:T(8,128)} %bitcast.12, bf16[272,128]{1,0:T(8,128)(2,1)} %get-tuple-element.37.refs_0_, bf16[272,128]{1,0:T(8,128)(2,1)} %copy-done.18, ...), custom_call_target="tpu_custom_call" | custom-call | flops 17179869184 | tf_op jit(solution)/shard_map/prep/pallas_call | solution.py:543
  45.4 1.8 %collective-permute-done.12.refs_5_ = bf16[256,512]{1,0:T(8,128)(2,1)S(1)} collective-permute-done((bf16[256,512]{1,0:T(8,128)(2,1)S(1)}, bf16[256,512]{1,0:T(8,128)(2,1)S(1)}, u32[]{:S(2)}, u32[]{:S(2)}) %collective-permute-start.12) | collective-permute-done | bytes 262176 | tf_op jit(solution)/shard_map/ppermute | solution.py:518
  47.2 2.7 %value.1.v_own = bf16[256,128]{1,0:T(8,128)(2,1)S(1)} custom-call(s32[8]{0:T(128)S(1)} %stack.35.place, bf16[8192,128]{1,0:T(8,128)(2,1)} %w.1, f32[256,256]{1,0:T(8,128)S(1)} %get-tuple-element.41.before.kv_before, bf16[256,512]{1,0:T(8,128)(2,1)S(1)} %collective-permute-done.6.refs_0_, bf16[256,512]{1,0:T(8,128)(2,1)S(1)} %collective-permute-done.7.refs_1_, ...), custom_call_target="tpu_custom_call" | custom-call | tf_op jit(solution)/shard_map/value/pallas_call | solution.py:523
  50.0 1.7 %collective-permute-start.13 = (bf16[256,128]{1,0:T(8,128)(2,1)S(1)}, bf16[256,128]{1,0:T(8,128)(2,1)S(1)}, u32[]{:S(2)}, u32[]{:S(2)}) collective-permute-start(bf16[256,128]{1,0:T(8,128)(2,1)S(1)} %value.1.v_own), channel_id=1, source_target_pairs={{0,2},{1,3},{2,0},{3,1},{4,6},{5,7},{6,4},{7,5},{8,10},{9,11},{10,... | collective-permute-start | bytes 196616 | tf_op jit(solution)/shard_map/ppermute | solution.py:452
  51.7 5.3 %prep.2 = (bf16[8,256,128]{2,1,0:T(8,128)(2,1)}, f32[8,256,128]{2,1,0:T(8,128)}, f32[8,256,128]{2,1,0:T(8,128)}, bf16[8,256,128]{2,1,0:T(8,128)(2,1)}) custom-call(f32[16,128]{1,0:T(8,128)} %bitcast.13, bf16[2176,128]{1,0:T(8,128)(2,1)} %collective-permute-done.14.refs_0_), custom_call_target="tpu_custom_call" | custom-call | flops 4294967296 | tf_op jit(solution)/shard_map/prep/pallas_call | solution.py:543
  58.2 2.9 %collective-permute-start.16 = (bf16[512,128]{1,0:T(8,128)(2,1)S(1)}, bf16[512,128]{1,0:T(8,128)(2,1)S(1)}, u32[]{:S(2)}, u32[]{:S(2)}) collective-permute-start(bf16[512,128]{1,0:T(8,128)(2,1)S(1)} %pad_maximum_fusion.1), channel_id=1, source_target_pairs={{0,8},{1,9},{2,10},{3,11},{4,12},{5,13},{6,14},{7,15},{8,0},{9,1},... | collective-permute-start | bytes 393224 | tf_op jit(solution)/shard_map/ppermute | solution.py:452
  62.9 8.1 %stats.1 = (bf16[8,256,128]{2,1,0:T(8,128)(2,1)S(1)}, bf16[8,128,256]{2,1,0:T(8,128)(2,1)S(1)}, f32[3,256]{1,0:T(4,128)S(1)}, f32[16,128]{1,0:T(8,128)S(1)}) custom-call(s32[8]{0:T(128)S(1)} %stack.35.place, s32[2]{0:T(128)S(1)} %copy-done.6, s32[1,256]{1,0:T(1,128)S(1)} %copy-done.5, s32[256,128]{1,0:T(8,128)S(1)} %copy-done.1, f32[16,128]{1,0:T(8,128)S(1)} %bitcast.14, ...), custom_call_target="tpu_custom_call" | custom-call | flops 17179869184 | tf_op jit(solution)/shard_map/stats/pallas_call | solution.py:567
  71.2 1.6 %stats_late.1.log_total_1 = f32[5,256]{1,0:T(8,128)S(1)} custom-call(s32[2]{0:T(128)S(1)} %copy-done.6, s32[1,256]{1,0:T(1,128)S(1)} %copy-done.5, bf16[8,128,256]{2,1,0:T(8,128)(2,1)S(1)} %get-tuple-element.60.q_t, bf16[8,256,128]{2,1,0:T(8,128)(2,1)S(1)} %copy-done.13, bf16[8,256,128]{2,1,0:T(8,128)(2,1)S(1)} %copy-done.9), custom_call_target="tpu_custom_call" | custom-call | flops 17179869184 | tf_op jit(solution)/shard_map/stats_late/pallas_call | solution.py:605
  73.8 7.3 %grad.1 = (bf16[256,1024]{1,0:T(8,128)(2,1)}, f32[16,128]{1,0:T(8,128)S(1)}) custom-call(s32[2]{0:T(128)S(1)} %copy-done.6, bf16[8,256,128]{2,1,0:T(8,128)(2,1)S(1)} %get-tuple-element.56.q_rot, bf16[8,128,256]{2,1,0:T(8,128)(2,1)S(1)} %get-tuple-element.60.q_t, f32[3,256]{1,0:T(4,128)S(1)} %get-tuple-element.58.log_total_0, ...), custom_call_target="tpu_custom_call" | custom-call | flops 8589934592 | bytes 8388608 | tf_op jit(solution)/shard_map/grad/pallas_call | solution.py:618
  82.3 4.6 %collective-permute-start.20 = (f32[16,128]{1,0:T(8,128)S(1)}, f32[16,128]{1,0:T(8,128)S(1)}, u32[]{:S(2)}, u32[]{:S(2)}) collective-permute-start(f32[16,128]{1,0:T(8,128)S(1)} %add.61), channel_id=1, source_target_pairs={{0,2},{1,3},{2,0},{3,1},{4,6},{5,7},{6,4},{7,5},{8,10},{9,11},{10,... | collective-permute-start | bytes 24584 | tf_op jit(solution)/shard_map/ppermute | solution.py:452
  88.5 9.1 %collective-permute-start.21 = (f32[16,128]{1,0:T(8,128)S(1)}, f32[16,128]{1,0:T(8,128)S(1)}, u32[]{:S(2)}, u32[]{:S(2)}) collective-permute-start(f32[16,128]{1,0:T(8,128)S(1)} %add.62), channel_id=1, source_target_pairs={{0,4},{1,5},{2,6},{3,7},{4,0},{5,1},{6,2},{7,3},{8,12},{9,13},{10,... | collective-permute-start | bytes 24584 | tf_op jit(solution)/shard_map/ppermute | solution.py:452
  97.6 1.6 %collective-permute-done.21 = f32[16,128]{1,0:T(8,128)S(1)} collective-permute-done((f32[16,128]{1,0:T(8,128)S(1)}, f32[16,128]{1,0:T(8,128)S(1)}, u32[]{:S(2)}, u32[]{:S(2)}) %collective-permute-start.21) | collective-permute-done | bytes 8224 | tf_op jit(solution)/shard_map/ppermute | solution.py:452
  99.2 20.8 %collective-permute-start.22 = (f32[16,128]{1,0:T(8,128)S(1)}, f32[16,128]{1,0:T(8,128)S(1)}, u32[]{:S(2)}, u32[]{:S(2)}) collective-permute-start(f32[16,128]{1,0:T(8,128)S(1)} %add.63), channel_id=1, source_target_pairs={{0,12},{1,13},{2,14},{3,15},{4,8},{5,9},{6,10},{7,11},{8,4},{9,5},... | collective-permute-start | bytes 24584 | tf_op jit(solution)/shard_map/ppermute | solution.py:452
  (86 shorter events, 15.5 us)
Async XLA Ops:
  0.6 24.4 %copy-start.2 = (bf16[256,1024]{1,0:T(8,128)(2,1)S(1)}, bf16[256,1024]{1,0:T(8,128)(2,1)}, u32[]{:S(2)}) copy-start(bf16[256,1024]{1,0:T(8,128)(2,1)} %refs_0_.1) | copy-start | bytes 1572868
  0.6 20.9 %collective-permute-start = (bf16[256,1024]{1,0:T(8,128)(2,1)}, bf16[256,1024]{1,0:T(8,128)(2,1)S(1)}, u32[]{:S(2)}, u32[]{:S(2)}) collective-permute-start(bf16[256,1024]{1,0:T(8,128)(2,1)} %refs_0_.1), channel_id=1, source_target_pairs={{0,32},{16,48},{32,64},{48,80},{64,96},{80,112},{96,0},{112,16},{1... | collective-permute-start | bytes 1572872 | tf_op jit(solution)/shard_map/ppermute | solution.py:469
  2.7 18.9 %collective-permute-start.1 = (bf16[256,1024]{1,0:T(8,128)(2,1)}, bf16[256,1024]{1,0:T(8,128)(2,1)S(1)}, u32[]{:S(2)}, u32[]{:S(2)}) collective-permute-start(bf16[256,1024]{1,0:T(8,128)(2,1)} %refs_0_.1), channel_id=1, source_target_pairs={{0,96},{16,112},{32,0},{48,16},{64,32},{80,48},{96,64},{112,80},{1... | collective-permute-start | bytes 1572872 | tf_op jit(solution)/shard_map/ppermute | solution.py:470
  4.9 16.7 %collective-permute-start.2 = (bf16[256,1024]{1,0:T(8,128)(2,1)}, bf16[256,1024]{1,0:T(8,128)(2,1)S(1)}, u32[]{:S(2)}, u32[]{:S(2)}) collective-permute-start(bf16[256,1024]{1,0:T(8,128)(2,1)} %refs_0_.1), channel_id=1, source_target_pairs={{0,16},{16,0},{32,48},{48,32},{64,80},{80,64},{96,112},{112,96},{1... | collective-permute-start | bytes 1572872 | tf_op jit(solution)/shard_map/ppermute | solution.py:471
  9.5 5.6 %collective-permute-start.3 = (bf16[272,128]{1,0:T(8,128)(2,1)}, bf16[272,128]{1,0:T(8,128)(2,1)S(1)}, u32[]{:S(2)}, u32[]{:S(2)}) collective-permute-start(bf16[272,128]{1,0:T(8,128)(2,1)} %get-tuple-element.37.refs_0_), channel_id=1, source_target_pairs={{0,4},{1,5},{2,6},{3,7},{4,0},{5,1},{6,2},{7,3},{8,12},{9,13},{10,... | collective-permute-start | bytes 208904 | tf_op jit(solution)/shard_map/ppermute | solution.py:452
  11.2 6.1 %collective-permute-start.4 = (bf16[272,128]{1,0:T(8,128)(2,1)}, bf16[272,128]{1,0:T(8,128)(2,1)S(1)}, u32[]{:S(2)}, u32[]{:S(2)}) collective-permute-start(bf16[272,128]{1,0:T(8,128)(2,1)} %get-tuple-element.37.refs_0_), channel_id=1, source_target_pairs={{0,8},{1,9},{2,10},{3,11},{4,12},{5,13},{6,14},{7,15},{8,0},{9,1},... | collective-permute-start | bytes 208904 | tf_op jit(solution)/shard_map/ppermute | solution.py:452
  15.1 5.8 %collective-permute-start.5 = (bf16[272,128]{1,0:T(8,128)(2,1)}, bf16[272,128]{1,0:T(8,128)(2,1)S(1)}, u32[]{:S(2)}, u32[]{:S(2)}) collective-permute-start(bf16[272,128]{1,0:T(8,128)(2,1)} %get-tuple-element.37.refs_0_), channel_id=1, source_target_pairs={{0,12},{1,13},{2,14},{3,15},{4,8},{5,9},{6,10},{7,11},{8,4},{9,5},... | collective-permute-start | bytes 208904 | tf_op jit(solution)/shard_map/ppermute | solution.py:452
  20.9 11.3 %collective-permute-start.8 = (bf16[1088,128]{1,0:T(8,128)(2,1)S(1)}, bf16[1088,128]{1,0:T(8,128)(2,1)S(1)}, u32[]{:S(2)}, u32[]{:S(2)}) collective-permute-start(bf16[1088,128]{1,0:T(8,128)(2,1)S(1)} %get-tuple-element.71), channel_id=1, source_target_pairs={{0,2},{1,3},{2,0},{3,1},{4,6},{5,7},{6,4},{7,5},{8,10},{9,11},{10,... | collective-permute-start | bytes 835592 | tf_op jit(solution)/shard_map/ppermute | solution.py:452
  21.6 10.6 %collective-permute-start.6 = (bf16[256,512]{1,0:T(8,128)(2,1)S(1)}, bf16[256,512]{1,0:T(8,128)(2,1)S(1)}, u32[]{:S(2)}, u32[]{:S(2)}) collective-permute-start(bf16[256,512]{1,0:T(8,128)(2,1)S(1)} %slice.6), channel_id=1, source_target_pairs={{0,32},{16,48},{32,64},{48,80},{64,96},{80,112},{96,0},{112,16},{1... | collective-permute-start | bytes 786440 | tf_op jit(solution)/shard_map/ppermute | solution.py:496
  21.7 10.5 %collective-permute-start.7 = (bf16[256,512]{1,0:T(8,128)(2,1)S(1)}, bf16[256,512]{1,0:T(8,128)(2,1)S(1)}, u32[]{:S(2)}, u32[]{:S(2)}) collective-permute-start(bf16[256,512]{1,0:T(8,128)(2,1)S(1)} %slice.7), channel_id=1, source_target_pairs={{0,96},{16,112},{32,0},{48,16},{64,32},{80,48},{96,64},{112,80},{1... | collective-permute-start | bytes 786440 | tf_op jit(solution)/shard_map/ppermute | solution.py:497
  32.3 14.9 %collective-permute-start.9 = (bf16[256,1024]{1,0:T(8,128)(2,1)S(1)}, bf16[256,1024]{1,0:T(8,128)(2,1)S(1)}, u32[]{:S(2)}, u32[]{:S(2)}) collective-permute-start(bf16[256,1024]{1,0:T(8,128)(2,1)S(1)} %collective-permute-done.2.refs_3_), channel_id=1, source_target_pairs={{0,32},{16,48},{32,64},{48,80},{64,96},{80,112},{96,0},{112,16},{1... | collective-permute-start | bytes 1572872 | tf_op jit(solution)/shard_map/ppermute | solution.py:515
  32.3 14.9 %collective-permute-start.10 = (bf16[256,1024]{1,0:T(8,128)(2,1)S(1)}, bf16[256,1024]{1,0:T(8,128)(2,1)S(1)}, u32[]{:S(2)}, u32[]{:S(2)}) collective-permute-start(bf16[256,1024]{1,0:T(8,128)(2,1)S(1)} %collective-permute-done.2.refs_3_), channel_id=1, source_target_pairs={{0,96},{16,112},{32,0},{48,16},{64,32},{80,48},{96,64},{112,80},{1... | collective-permute-start | bytes 1572872 | tf_op jit(solution)/shard_map/ppermute | solution.py:516
  35.6 9.8 %collective-permute-start.11 = (bf16[256,512]{1,0:T(8,128)(2,1)S(1)}, bf16[256,512]{1,0:T(8,128)(2,1)S(1)}, u32[]{:S(2)}, u32[]{:S(2)}) collective-permute-start(bf16[256,512]{1,0:T(8,128)(2,1)S(1)} %collective-permute-done.6.refs_0_), channel_id=1, source_target_pairs={{0,16},{16,0},{32,48},{48,32},{64,80},{80,64},{96,112},{112,96},{1... | collective-permute-start | bytes 786440 | tf_op jit(solution)/shard_map/ppermute | solution.py:517
  37.6 9.6 %collective-permute-start.12 = (bf16[256,512]{1,0:T(8,128)(2,1)S(1)}, bf16[256,512]{1,0:T(8,128)(2,1)S(1)}, u32[]{:S(2)}, u32[]{:S(2)}) collective-permute-start(bf16[256,512]{1,0:T(8,128)(2,1)S(1)} %collective-permute-done.7.refs_1_), channel_id=1, source_target_pairs={{0,16},{16,0},{32,48},{48,32},{64,80},{80,64},{96,112},{112,96},{1... | collective-permute-start | bytes 786440 | tf_op jit(solution)/shard_map/ppermute | solution.py:518
  39.1 12.5 %collective-permute-start.14 = (bf16[2176,128]{1,0:T(8,128)(2,1)S(1)}, bf16[2176,128]{1,0:T(8,128)(2,1)}, u32[]{:S(2)}, u32[]{:S(2)}) collective-permute-start(bf16[2176,128]{1,0:T(8,128)(2,1)S(1)} %constant_dynamic-update-slice_fusion.4), channel_id=1, source_target_pairs={{0,1},{1,0},{2,3},{3,2},{4,5},{5,4},{6,7},{7,6},{8,9},{9,8},{10,11... | collective-permute-start | bytes 1671176 | tf_op jit(solution)/shard_map/ppermute | solution.py:452
  50.0 7.0 %collective-permute-start.13 = (bf16[256,128]{1,0:T(8,128)(2,1)S(1)}, bf16[256,128]{1,0:T(8,128)(2,1)S(1)}, u32[]{:S(2)}, u32[]{:S(2)}) collective-permute-start(bf16[256,128]{1,0:T(8,128)(2,1)S(1)} %value.1.v_own), channel_id=1, source_target_pairs={{0,2},{1,3},{2,0},{3,1},{4,6},{5,7},{6,4},{7,5},{8,10},{9,11},{10,... | collective-permute-start | bytes 196616 | tf_op jit(solution)/shard_map/ppermute | solution.py:452
  57.0 13.9 %collective-permute-start.15 = (bf16[512,128]{1,0:T(8,128)(2,1)S(1)}, bf16[512,128]{1,0:T(8,128)(2,1)S(1)}, u32[]{:S(2)}, u32[]{:S(2)}) collective-permute-start(bf16[512,128]{1,0:T(8,128)(2,1)S(1)} %pad_maximum_fusion.1), channel_id=1, source_target_pairs={{0,4},{1,5},{2,6},{3,7},{4,0},{5,1},{6,2},{7,3},{8,12},{9,13},{10,... | collective-permute-start | bytes 393224 | tf_op jit(solution)/shard_map/ppermute | solution.py:452
  58.2 12.7 %collective-permute-start.16 = (bf16[512,128]{1,0:T(8,128)(2,1)S(1)}, bf16[512,128]{1,0:T(8,128)(2,1)S(1)}, u32[]{:S(2)}, u32[]{:S(2)}) collective-permute-start(bf16[512,128]{1,0:T(8,128)(2,1)S(1)} %pad_maximum_fusion.1), channel_id=1, source_target_pairs={{0,8},{1,9},{2,10},{3,11},{4,12},{5,13},{6,14},{7,15},{8,0},{9,1},... | collective-permute-start | bytes 393224 | tf_op jit(solution)/shard_map/ppermute | solution.py:452
  61.1 9.9 %collective-permute-start.17 = (bf16[512,128]{1,0:T(8,128)(2,1)S(1)}, bf16[512,128]{1,0:T(8,128)(2,1)S(1)}, u32[]{:S(2)}, u32[]{:S(2)}) collective-permute-start(bf16[512,128]{1,0:T(8,128)(2,1)S(1)} %pad_maximum_fusion.1), channel_id=1, source_target_pairs={{0,12},{1,13},{2,14},{3,15},{4,8},{5,9},{6,10},{7,11},{8,4},{9,5},... | collective-permute-start | bytes 393224 | tf_op jit(solution)/shard_map/ppermute | solution.py:452
  71.1 2.0 %collective-permute-start.18 = (bf16[2048,128]{1,0:T(8,128)(2,1)S(1)}, bf16[2048,128]{1,0:T(8,128)(2,1)S(1)}, u32[]{:S(2)}, u32[]{:S(2)}) collective-permute-start(bf16[2048,128]{1,0:T(8,128)(2,1)S(1)} %pad_maximum_fusion), channel_id=1, source_target_pairs={{0,1},{1,0},{2,3},{3,2},{4,5},{5,4},{6,7},{7,6},{8,9},{9,8},{10,11... | collective-permute-start | bytes 1572872 | tf_op jit(solution)/shard_map/ppermute | solution.py:452
  81.1 1.3 %collective-permute-start.19 = (f32[16,128]{1,0:T(8,128)S(1)}, f32[16,128]{1,0:T(8,128)S(1)}, u32[]{:S(2)}, u32[]{:S(2)}) collective-permute-start(f32[16,128]{1,0:T(8,128)S(1)} %get-tuple-element.69), channel_id=1, source_target_pairs={{0,1},{1,0},{2,3},{3,2},{4,5},{5,4},{6,7},{7,6},{8,9},{9,8},{10,11... | collective-permute-start | bytes 24584 | tf_op jit(solution)/shard_map/ppermute | solution.py:452
  82.3 6.2 %collective-permute-start.20 = (f32[16,128]{1,0:T(8,128)S(1)}, f32[16,128]{1,0:T(8,128)S(1)}, u32[]{:S(2)}, u32[]{:S(2)}) collective-permute-start(f32[16,128]{1,0:T(8,128)S(1)} %add.61), channel_id=1, source_target_pairs={{0,2},{1,3},{2,0},{3,1},{4,6},{5,7},{6,4},{7,5},{8,10},{9,11},{10,... | collective-permute-start | bytes 24584 | tf_op jit(solution)/shard_map/ppermute | solution.py:452
  88.5 10.7 %collective-permute-start.21 = (f32[16,128]{1,0:T(8,128)S(1)}, f32[16,128]{1,0:T(8,128)S(1)}, u32[]{:S(2)}, u32[]{:S(2)}) collective-permute-start(f32[16,128]{1,0:T(8,128)S(1)} %add.62), channel_id=1, source_target_pairs={{0,4},{1,5},{2,6},{3,7},{4,0},{5,1},{6,2},{7,3},{8,12},{9,13},{10,... | collective-permute-start | bytes 24584 | tf_op jit(solution)/shard_map/ppermute | solution.py:452
  99.2 22.4 %collective-permute-start.22 = (f32[16,128]{1,0:T(8,128)S(1)}, f32[16,128]{1,0:T(8,128)S(1)}, u32[]{:S(2)}, u32[]{:S(2)}) collective-permute-start(f32[16,128]{1,0:T(8,128)S(1)} %add.63), channel_id=1, source_target_pairs={{0,12},{1,13},{2,14},{3,15},{4,8},{5,9},{6,10},{7,11},{8,4},{9,5},... | collective-permute-start | bytes 24584 | tf_op jit(solution)/shard_map/ppermute | solution.py:452
  (20 other events, 129.6 us)

commit v12 on v11

--- a/solution.py
+++ b/solution.py
@@ -215,13 +215,22 @@
         copies.append(
             pltpu.make_async_copy(w.at[shard_rows(place, first + n, part), :], w_s.at[n], sems.at[len(copies)])
         )
-    for copy in copies:
+    loads, (first_sums, *weights) = copies[: len(pieces)], copies[len(pieces) :]
+    order, at = [[] for _ in range(count)], 0
+    for piece, copy in zip(pieces, loads):
+        order[at // part].append(copy)
+        at += piece.shape[1]
+    for n in range(count):
+        order[n].append(weights[n])
+    order[0].append(first_sums)
+    for copy in sum(order, []):
         copy.start()
-    for copy in copies:
-        copy.wait()
-    total = before_s[...]
+    total = None
     for n in range(count):
-        total += jnp.dot(x_s[:, n * part : (n + 1) * part], w_s[n], preferred_element_type=jnp.float32)
+        for copy in order[n]:
+            copy.wait()
+        term = jnp.dot(x_s[:, n * part : (n + 1) * part], w_s[n], preferred_element_type=jnp.float32)
+        total = before_s[...] + term if n == 0 else total + term
     value[...] = total.astype(jnp.bfloat16)
 
 

time: 123 us -> 123 us (level)
  no operation moved by 1% of the time
where the time goes in v12:
time: 123 us; the launch traced here: 121 us
  starting transfers between devices  64.8 us (53%)
  Pallas kernels  39 us (32%)
  waiting for transfers between devices  11.8 us (10%)
  local copies, waits for them, and re-layouts  3.9 us (3%)
    ppermute x14, starting transfers between devices, shards(): lax.ppermute(x, 'tokens', [(i, i ^ d) for i in range(ranks)])  47.3 us
    pallas_call x2, Pallas kernels, prep(): pl.pallas_call(functools.partial(prep_kernel, near, rows, few, levels), o...  11.5 us
    ppermute x14, waiting for transfers between devices, shards(): lax.ppermute(x, 'tokens', [(i, i ^ d) for i in range(ranks)])  10 us
    pallas_call x1, Pallas kernels, second(): pl.pallas_call(functools.partial(stats_kernel, count, heads, rows, levels...  8.06 us
    pallas_call x1, Pallas kernels, shards(): pl.pallas_call(functools.partial(grad_kernel, heads, rows, levels), out_s...  7.27 us
    pallas_call x1, Pallas kernels, shards(): pl.pallas_call(functools.partial(project_kernel, half, part), out_shape=(...  6.2 us
    unnamed x46, local copies, waits for them, and re-layouts  3.74 us
    ppermute x1, starting transfers between devices, shards(): far_b = send(high[:, n:], perm=down)  3.29 us
  transfers between devices with their start and end apart: 23, of which 8 were waited for; matrix products, arithmetic and copies ran while one was open for 1% of the time, Pallas kernels for 26%

profile of v12, /device:TPU:0, one launch (start us, length us, event | category | flops | bytes accessed | tf_op | source)
XLA Modules:
  0.0 121.3 jit_solution(17543269787253098761)
XLA Ops:
  0.6 2.1 %collective-permute-start = (bf16[256,1024]{1,0:T(8,128)(2,1)}, bf16[256,1024]{1,0:T(8,128)(2,1)S(1)}, u32[]{:S(2)}, u32[]{:S(2)}) collective-permute-start(bf16[256,1024]{1,0:T(8,128)(2,1)} %refs_0_.1), channel_id=1, source_target_pairs={{0,32},{16,48},{32,64},{48,80},{64,96},{80,112},{96,0},{112,16},{1... | collective-permute-start | bytes 1572872 | tf_op jit(solution)/shard_map/ppermute | solution.py:478
  2.7 2.2 %collective-permute-start.1 = (bf16[256,1024]{1,0:T(8,128)(2,1)}, bf16[256,1024]{1,0:T(8,128)(2,1)S(1)}, u32[]{:S(2)}, u32[]{:S(2)}) collective-permute-start(bf16[256,1024]{1,0:T(8,128)(2,1)} %refs_0_.1), channel_id=1, source_target_pairs={{0,96},{16,112},{32,0},{48,16},{64,32},{80,48},{96,64},{112,80},{1... | collective-permute-start | bytes 1572872 | tf_op jit(solution)/shard_map/ppermute | solution.py:479
  4.9 3.0 %collective-permute-start.2 = (bf16[256,1024]{1,0:T(8,128)(2,1)}, bf16[256,1024]{1,0:T(8,128)(2,1)S(1)}, u32[]{:S(2)}, u32[]{:S(2)}) collective-permute-start(bf16[256,1024]{1,0:T(8,128)(2,1)} %refs_0_.1), channel_id=1, source_target_pairs={{0,16},{16,0},{32,48},{48,32},{64,80},{80,64},{96,112},{112,96},{1... | collective-permute-start | bytes 1572872 | tf_op jit(solution)/shard_map/ppermute | solution.py:480
  9.5 1.7 %collective-permute-start.3 = (bf16[272,128]{1,0:T(8,128)(2,1)}, bf16[272,128]{1,0:T(8,128)(2,1)S(1)}, u32[]{:S(2)}, u32[]{:S(2)}) collective-permute-start(bf16[272,128]{1,0:T(8,128)(2,1)} %get-tuple-element.37.refs_0_), channel_id=1, source_target_pairs={{0,4},{1,5},{2,6},{3,7},{4,0},{5,1},{6,2},{7,3},{8,12},{9,13},{10,... | collective-permute-start | bytes 208904 | tf_op jit(solution)/shard_map/ppermute | solution.py:461
  11.2 2.9 %collective-permute-start.4 = (bf16[272,128]{1,0:T(8,128)(2,1)}, bf16[272,128]{1,0:T(8,128)(2,1)S(1)}, u32[]{:S(2)}, u32[]{:S(2)}) collective-permute-start(bf16[272,128]{1,0:T(8,128)(2,1)} %get-tuple-element.37.refs_0_), channel_id=1, source_target_pairs={{0,8},{1,9},{2,10},{3,11},{4,12},{5,13},{6,14},{7,15},{8,0},{9,1},... | collective-permute-start | bytes 208904 | tf_op jit(solution)/shard_map/ppermute | solution.py:461
  15.1 2.0 %collective-permute-start.5 = (bf16[272,128]{1,0:T(8,128)(2,1)}, bf16[272,128]{1,0:T(8,128)(2,1)S(1)}, u32[]{:S(2)}, u32[]{:S(2)}) collective-permute-start(bf16[272,128]{1,0:T(8,128)(2,1)} %get-tuple-element.37.refs_0_), channel_id=1, source_target_pairs={{0,12},{1,13},{2,14},{3,15},{4,8},{5,9},{6,10},{7,11},{8,4},{9,5},... | collective-permute-start | bytes 208904 | tf_op jit(solution)/shard_map/ppermute | solution.py:461
  17.3 3.6 %collective-permute-done.5.refs_3_ = bf16[272,128]{1,0:T(8,128)(2,1)S(1)} collective-permute-done((bf16[272,128]{1,0:T(8,128)(2,1)}, bf16[272,128]{1,0:T(8,128)(2,1)S(1)}, u32[]{:S(2)}, u32[]{:S(2)}) %collective-permute-start.5) | collective-permute-done | bytes 69664 | tf_op jit(solution)/shard_map/ppermute | solution.py:461
  21.7 3.3 %collective-permute-start.7 = (bf16[256,512]{1,0:T(8,128)(2,1)S(1)}, bf16[256,512]{1,0:T(8,128)(2,1)S(1)}, u32[]{:S(2)}, u32[]{:S(2)}) collective-permute-start(bf16[256,512]{1,0:T(8,128)(2,1)S(1)} %slice.7), channel_id=1, source_target_pairs={{0,96},{16,112},{32,0},{48,16},{64,32},{80,48},{96,64},{112,80},{1... | collective-permute-start | bytes 786440 | tf_op jit(solution)/shard_map/ppermute | solution.py:506
  25.0 6.2 %project.1 = (f32[256,1024]{1,0:T(8,128)S(1)}, f32[256,256]{1,0:T(8,128)S(1)}) custom-call(s32[8]{0:T(128)S(1)} %stack.35.place, bf16[8192,1024]{1,0:T(8,128)(2,1)} %wq.3, bf16[8192,128]{1,0:T(8,128)(2,1)} %wk.3, bf16[8192,128]{1,0:T(8,128)(2,1)} %w.1, bf16[256,1024]{1,0:T(8,128)(2,1)S(1)} %copy-done.2, bf16[256,1024]{1,0:T(8,128)(2,1)S(1)} %collective-permute-done.refs_1_, ...), custom_call_target="tpu_custom_call" | custom-call | flops 17179869184 | tf_op jit(solution)/shard_map/project/pallas_call | solution.py:508
  32.3 3.2 %collective-permute-start.10 = (bf16[256,1024]{1,0:T(8,128)(2,1)S(1)}, bf16[256,1024]{1,0:T(8,128)(2,1)S(1)}, u32[]{:S(2)}, u32[]{:S(2)}) collective-permute-start(bf16[256,1024]{1,0:T(8,128)(2,1)S(1)} %collective-permute-done.2.refs_3_), channel_id=1, source_target_pairs={{0,96},{16,112},{32,0},{48,16},{64,32},{80,48},{96,64},{112,80},{1... | collective-permute-start | bytes 1572872 | tf_op jit(solution)/shard_map/ppermute | solution.py:525
  35.6 2.0 %collective-permute-start.11 = (bf16[256,512]{1,0:T(8,128)(2,1)S(1)}, bf16[256,512]{1,0:T(8,128)(2,1)S(1)}, u32[]{:S(2)}, u32[]{:S(2)}) collective-permute-start(bf16[256,512]{1,0:T(8,128)(2,1)S(1)} %collective-permute-done.6.refs_0_), channel_id=1, source_target_pairs={{0,16},{16,0},{32,48},{48,32},{64,80},{80,64},{96,112},{112,96},{1... | collective-permute-start | bytes 786440 | tf_op jit(solution)/shard_map/ppermute | solution.py:526
  39.2 6.1 %prep.3 = (bf16[8,256,128]{2,1,0:T(8,128)(2,1)}, f32[8,256,128]{2,1,0:T(8,128)}, f32[8,256,128]{2,1,0:T(8,128)}, bf16[8,256,128]{2,1,0:T(8,128)(2,1)}, bf16[8,128,256]{2,1,0:T(8,128)(2,1)}) custom-call(f32[16,128]{1,0:T(8,128)} %bitcast.12, bf16[272,128]{1,0:T(8,128)(2,1)} %get-tuple-element.37.refs_0_, bf16[272,128]{1,0:T(8,128)(2,1)} %copy-done.18, ...), custom_call_target="tpu_custom_call" | custom-call | flops 17179869184 | tf_op jit(solution)/shard_map/prep/pallas_call | solution.py:552
  45.4 1.8 %collective-permute-done.12.refs_5_ = bf16[256,512]{1,0:T(8,128)(2,1)S(1)} collective-permute-done((bf16[256,512]{1,0:T(8,128)(2,1)S(1)}, bf16[256,512]{1,0:T(8,128)(2,1)S(1)}, u32[]{:S(2)}, u32[]{:S(2)}) %collective-permute-start.12) | collective-permute-done | bytes 262176 | tf_op jit(solution)/shard_map/ppermute | solution.py:527
  47.2 2.8 %value.1.v_own = bf16[256,128]{1,0:T(8,128)(2,1)S(1)} custom-call(s32[8]{0:T(128)S(1)} %stack.35.place, bf16[8192,128]{1,0:T(8,128)(2,1)} %w.1, f32[256,256]{1,0:T(8,128)S(1)} %get-tuple-element.41.before.kv_before, bf16[256,512]{1,0:T(8,128)(2,1)S(1)} %collective-permute-done.6.refs_0_, bf16[256,512]{1,0:T(8,128)(2,1)S(1)} %collective-permute-done.7.refs_1_, ...), custom_call_target="tpu_custom_call" | custom-call | tf_op jit(solution)/shard_map/value/pallas_call | solution.py:532
  50.1 1.7 %collective-permute-start.13 = (bf16[256,128]{1,0:T(8,128)(2,1)S(1)}, bf16[256,128]{1,0:T(8,128)(2,1)S(1)}, u32[]{:S(2)}, u32[]{:S(2)}) collective-permute-start(bf16[256,128]{1,0:T(8,128)(2,1)S(1)} %value.1.v_own), channel_id=1, source_target_pairs={{0,2},{1,3},{2,0},{3,1},{4,6},{5,7},{6,4},{7,5},{8,10},{9,11},{10,... | collective-permute-start | bytes 196616 | tf_op jit(solution)/shard_map/ppermute | solution.py:461
  51.8 5.3 %prep.2 = (bf16[8,256,128]{2,1,0:T(8,128)(2,1)}, f32[8,256,128]{2,1,0:T(8,128)}, f32[8,256,128]{2,1,0:T(8,128)}, bf16[8,256,128]{2,1,0:T(8,128)(2,1)}) custom-call(f32[16,128]{1,0:T(8,128)} %bitcast.13, bf16[2176,128]{1,0:T(8,128)(2,1)} %collective-permute-done.14.refs_0_), custom_call_target="tpu_custom_call" | custom-call | flops 4294967296 | tf_op jit(solution)/shard_map/prep/pallas_call | solution.py:552
  58.3 2.9 %collective-permute-start.16 = (bf16[512,128]{1,0:T(8,128)(2,1)S(1)}, bf16[512,128]{1,0:T(8,128)(2,1)S(1)}, u32[]{:S(2)}, u32[]{:S(2)}) collective-permute-start(bf16[512,128]{1,0:T(8,128)(2,1)S(1)} %pad_maximum_fusion.1), channel_id=1, source_target_pairs={{0,8},{1,9},{2,10},{3,11},{4,12},{5,13},{6,14},{7,15},{8,0},{9,1},... | collective-permute-start | bytes 393224 | tf_op jit(solution)/shard_map/ppermute | solution.py:461
  62.9 8.1 %stats.1 = (bf16[8,256,128]{2,1,0:T(8,128)(2,1)S(1)}, bf16[8,128,256]{2,1,0:T(8,128)(2,1)S(1)}, f32[3,256]{1,0:T(4,128)S(1)}, f32[16,128]{1,0:T(8,128)S(1)}) custom-call(s32[8]{0:T(128)S(1)} %stack.35.place, s32[2]{0:T(128)S(1)} %copy-done.6, s32[1,256]{1,0:T(1,128)S(1)} %copy-done.5, s32[256,128]{1,0:T(8,128)S(1)} %copy-done.1, f32[16,128]{1,0:T(8,128)S(1)} %bitcast.14, ...), custom_call_target="tpu_custom_call" | custom-call | flops 17179869184 | tf_op jit(solution)/shard_map/stats/pallas_call | solution.py:576
  71.3 1.6 %stats_late.1.log_total_1 = f32[5,256]{1,0:T(8,128)S(1)} custom-call(s32[2]{0:T(128)S(1)} %copy-done.6, s32[1,256]{1,0:T(1,128)S(1)} %copy-done.5, bf16[8,128,256]{2,1,0:T(8,128)(2,1)S(1)} %get-tuple-element.60.q_t, bf16[8,256,128]{2,1,0:T(8,128)(2,1)S(1)} %copy-done.13, bf16[8,256,128]{2,1,0:T(8,128)(2,1)S(1)} %copy-done.9), custom_call_target="tpu_custom_call" | custom-call | flops 17179869184 | tf_op jit(solution)/shard_map/stats_late/pallas_call | solution.py:614
  73.9 7.3 %grad.1 = (bf16[256,1024]{1,0:T(8,128)(2,1)}, f32[16,128]{1,0:T(8,128)S(1)}) custom-call(s32[2]{0:T(128)S(1)} %copy-done.6, bf16[8,256,128]{2,1,0:T(8,128)(2,1)S(1)} %get-tuple-element.56.q_rot, bf16[8,128,256]{2,1,0:T(8,128)(2,1)S(1)} %get-tuple-element.60.q_t, f32[3,256]{1,0:T(4,128)S(1)} %get-tuple-element.58.log_total_0, ...), custom_call_target="tpu_custom_call" | custom-call | flops 8589934592 | bytes 8388608 | tf_op jit(solution)/shard_map/grad/pallas_call | solution.py:627
  82.4 4.4 %collective-permute-start.20 = (f32[16,128]{1,0:T(8,128)S(1)}, f32[16,128]{1,0:T(8,128)S(1)}, u32[]{:S(2)}, u32[]{:S(2)}) collective-permute-start(f32[16,128]{1,0:T(8,128)S(1)} %add.61), channel_id=1, source_target_pairs={{0,2},{1,3},{2,0},{3,1},{4,6},{5,7},{6,4},{7,5},{8,10},{9,11},{10,... | collective-permute-start | bytes 24584 | tf_op jit(solution)/shard_map/ppermute | solution.py:461
  86.8 1.6 %collective-permute-done.20 = f32[16,128]{1,0:T(8,128)S(1)} collective-permute-done((f32[16,128]{1,0:T(8,128)S(1)}, f32[16,128]{1,0:T(8,128)S(1)}, u32[]{:S(2)}, u32[]{:S(2)}) %collective-permute-start.20) | collective-permute-done | bytes 8224 | tf_op jit(solution)/shard_map/ppermute | solution.py:461
  88.5 4.7 %collective-permute-start.21 = (f32[16,128]{1,0:T(8,128)S(1)}, f32[16,128]{1,0:T(8,128)S(1)}, u32[]{:S(2)}, u32[]{:S(2)}) collective-permute-start(f32[16,128]{1,0:T(8,128)S(1)} %add.62), channel_id=1, source_target_pairs={{0,4},{1,5},{2,6},{3,7},{4,0},{5,1},{6,2},{7,3},{8,12},{9,13},{10,... | collective-permute-start | bytes 24584 | tf_op jit(solution)/shard_map/ppermute | solution.py:461
  94.8 24.3 %collective-permute-start.22 = (f32[16,128]{1,0:T(8,128)S(1)}, f32[16,128]{1,0:T(8,128)S(1)}, u32[]{:S(2)}, u32[]{:S(2)}) collective-permute-start(f32[16,128]{1,0:T(8,128)S(1)} %add.63), channel_id=1, source_target_pairs={{0,12},{1,13},{2,14},{3,15},{4,8},{5,9},{6,10},{7,11},{8,4},{9,5},... | collective-permute-start | bytes 24584 | tf_op jit(solution)/shard_map/ppermute | solution.py:461
  (86 shorter events, 15.5 us)
Async XLA Ops:
  0.6 24.4 %copy-start.2 = (bf16[256,1024]{1,0:T(8,128)(2,1)S(1)}, bf16[256,1024]{1,0:T(8,128)(2,1)}, u32[]{:S(2)}) copy-start(bf16[256,1024]{1,0:T(8,128)(2,1)} %refs_0_.1) | copy-start | bytes 1572868
  0.6 20.9 %collective-permute-start = (bf16[256,1024]{1,0:T(8,128)(2,1)}, bf16[256,1024]{1,0:T(8,128)(2,1)S(1)}, u32[]{:S(2)}, u32[]{:S(2)}) collective-permute-start(bf16[256,1024]{1,0:T(8,128)(2,1)} %refs_0_.1), channel_id=1, source_target_pairs={{0,32},{16,48},{32,64},{48,80},{64,96},{80,112},{96,0},{112,16},{1... | collective-permute-start | bytes 1572872 | tf_op jit(solution)/shard_map/ppermute | solution.py:478
  2.7 18.9 %collective-permute-start.1 = (bf16[256,1024]{1,0:T(8,128)(2,1)}, bf16[256,1024]{1,0:T(8,128)(2,1)S(1)}, u32[]{:S(2)}, u32[]{:S(2)}) collective-permute-start(bf16[256,1024]{1,0:T(8,128)(2,1)} %refs_0_.1), channel_id=1, source_target_pairs={{0,96},{16,112},{32,0},{48,16},{64,32},{80,48},{96,64},{112,80},{1... | collective-permute-start | bytes 1572872 | tf_op jit(solution)/shard_map/ppermute | solution.py:479
  4.9 16.7 %collective-permute-start.2 = (bf16[256,1024]{1,0:T(8,128)(2,1)}, bf16[256,1024]{1,0:T(8,128)(2,1)S(1)}, u32[]{:S(2)}, u32[]{:S(2)}) collective-permute-start(bf16[256,1024]{1,0:T(8,128)(2,1)} %refs_0_.1), channel_id=1, source_target_pairs={{0,16},{16,0},{32,48},{48,32},{64,80},{80,64},{96,112},{112,96},{1... | collective-permute-start | bytes 1572872 | tf_op jit(solution)/shard_map/ppermute | solution.py:480
  9.5 5.6 %collective-permute-start.3 = (bf16[272,128]{1,0:T(8,128)(2,1)}, bf16[272,128]{1,0:T(8,128)(2,1)S(1)}, u32[]{:S(2)}, u32[]{:S(2)}) collective-permute-start(bf16[272,128]{1,0:T(8,128)(2,1)} %get-tuple-element.37.refs_0_), channel_id=1, source_target_pairs={{0,4},{1,5},{2,6},{3,7},{4,0},{5,1},{6,2},{7,3},{8,12},{9,13},{10,... | collective-permute-start | bytes 208904 | tf_op jit(solution)/shard_map/ppermute | solution.py:461
  11.2 6.1 %collective-permute-start.4 = (bf16[272,128]{1,0:T(8,128)(2,1)}, bf16[272,128]{1,0:T(8,128)(2,1)S(1)}, u32[]{:S(2)}, u32[]{:S(2)}) collective-permute-start(bf16[272,128]{1,0:T(8,128)(2,1)} %get-tuple-element.37.refs_0_), channel_id=1, source_target_pairs={{0,8},{1,9},{2,10},{3,11},{4,12},{5,13},{6,14},{7,15},{8,0},{9,1},... | collective-permute-start | bytes 208904 | tf_op jit(solution)/shard_map/ppermute | solution.py:461
  15.1 5.8 %collective-permute-start.5 = (bf16[272,128]{1,0:T(8,128)(2,1)}, bf16[272,128]{1,0:T(8,128)(2,1)S(1)}, u32[]{:S(2)}, u32[]{:S(2)}) collective-permute-start(bf16[272,128]{1,0:T(8,128)(2,1)} %get-tuple-element.37.refs_0_), channel_id=1, source_target_pairs={{0,12},{1,13},{2,14},{3,15},{4,8},{5,9},{6,10},{7,11},{8,4},{9,5},... | collective-permute-start | bytes 208904 | tf_op jit(solution)/shard_map/ppermute | solution.py:461
  20.9 11.3 %collective-permute-start.8 = (bf16[1088,128]{1,0:T(8,128)(2,1)S(1)}, bf16[1088,128]{1,0:T(8,128)(2,1)S(1)}, u32[]{:S(2)}, u32[]{:S(2)}) collective-permute-start(bf16[1088,128]{1,0:T(8,128)(2,1)S(1)} %get-tuple-element.71), channel_id=1, source_target_pairs={{0,2},{1,3},{2,0},{3,1},{4,6},{5,7},{6,4},{7,5},{8,10},{9,11},{10,... | collective-permute-start | bytes 835592 | tf_op jit(solution)/shard_map/ppermute | solution.py:461
  21.6 10.6 %collective-permute-start.6 = (bf16[256,512]{1,0:T(8,128)(2,1)S(1)}, bf16[256,512]{1,0:T(8,128)(2,1)S(1)}, u32[]{:S(2)}, u32[]{:S(2)}) collective-permute-start(bf16[256,512]{1,0:T(8,128)(2,1)S(1)} %slice.6), channel_id=1, source_target_pairs={{0,32},{16,48},{32,64},{48,80},{64,96},{80,112},{96,0},{112,16},{1... | collective-permute-start | bytes 786440 | tf_op jit(solution)/shard_map/ppermute | solution.py:505
  21.7 10.5 %collective-permute-start.7 = (bf16[256,512]{1,0:T(8,128)(2,1)S(1)}, bf16[256,512]{1,0:T(8,128)(2,1)S(1)}, u32[]{:S(2)}, u32[]{:S(2)}) collective-permute-start(bf16[256,512]{1,0:T(8,128)(2,1)S(1)} %slice.7), channel_id=1, source_target_pairs={{0,96},{16,112},{32,0},{48,16},{64,32},{80,48},{96,64},{112,80},{1... | collective-permute-start | bytes 786440 | tf_op jit(solution)/shard_map/ppermute | solution.py:506
  32.3 14.9 %collective-permute-start.9 = (bf16[256,1024]{1,0:T(8,128)(2,1)S(1)}, bf16[256,1024]{1,0:T(8,128)(2,1)S(1)}, u32[]{:S(2)}, u32[]{:S(2)}) collective-permute-start(bf16[256,1024]{1,0:T(8,128)(2,1)S(1)} %collective-permute-done.2.refs_3_), channel_id=1, source_target_pairs={{0,32},{16,48},{32,64},{48,80},{64,96},{80,112},{96,0},{112,16},{1... | collective-permute-start | bytes 1572872 | tf_op jit(solution)/shard_map/ppermute | solution.py:524
  32.3 14.9 %collective-permute-start.10 = (bf16[256,1024]{1,0:T(8,128)(2,1)S(1)}, bf16[256,1024]{1,0:T(8,128)(2,1)S(1)}, u32[]{:S(2)}, u32[]{:S(2)}) collective-permute-start(bf16[256,1024]{1,0:T(8,128)(2,1)S(1)} %collective-permute-done.2.refs_3_), channel_id=1, source_target_pairs={{0,96},{16,112},{32,0},{48,16},{64,32},{80,48},{96,64},{112,80},{1... | collective-permute-start | bytes 1572872 | tf_op jit(solution)/shard_map/ppermute | solution.py:525
  35.6 9.8 %collective-permute-start.11 = (bf16[256,512]{1,0:T(8,128)(2,1)S(1)}, bf16[256,512]{1,0:T(8,128)(2,1)S(1)}, u32[]{:S(2)}, u32[]{:S(2)}) collective-permute-start(bf16[256,512]{1,0:T(8,128)(2,1)S(1)} %collective-permute-done.6.refs_0_), channel_id=1, source_target_pairs={{0,16},{16,0},{32,48},{48,32},{64,80},{80,64},{96,112},{112,96},{1... | collective-permute-start | bytes 786440 | tf_op jit(solution)/shard_map/ppermute | solution.py:526
  37.6 9.6 %collective-permute-start.12 = (bf16[256,512]{1,0:T(8,128)(2,1)S(1)}, bf16[256,512]{1,0:T(8,128)(2,1)S(1)}, u32[]{:S(2)}, u32[]{:S(2)}) collective-permute-start(bf16[256,512]{1,0:T(8,128)(2,1)S(1)} %collective-permute-done.7.refs_1_), channel_id=1, source_target_pairs={{0,16},{16,0},{32,48},{48,32},{64,80},{80,64},{96,112},{112,96},{1... | collective-permute-start | bytes 786440 | tf_op jit(solution)/shard_map/ppermute | solution.py:527
  39.1 12.6 %collective-permute-start.14 = (bf16[2176,128]{1,0:T(8,128)(2,1)S(1)}, bf16[2176,128]{1,0:T(8,128)(2,1)}, u32[]{:S(2)}, u32[]{:S(2)}) collective-permute-start(bf16[2176,128]{1,0:T(8,128)(2,1)S(1)} %constant_dynamic-update-slice_fusion.4), channel_id=1, source_target_pairs={{0,1},{1,0},{2,3},{3,2},{4,5},{5,4},{6,7},{7,6},{8,9},{9,8},{10,11... | collective-permute-start | bytes 1671176 | tf_op jit(solution)/shard_map/ppermute | solution.py:461
  50.1 7.0 %collective-permute-start.13 = (bf16[256,128]{1,0:T(8,128)(2,1)S(1)}, bf16[256,128]{1,0:T(8,128)(2,1)S(1)}, u32[]{:S(2)}, u32[]{:S(2)}) collective-permute-start(bf16[256,128]{1,0:T(8,128)(2,1)S(1)} %value.1.v_own), channel_id=1, source_target_pairs={{0,2},{1,3},{2,0},{3,1},{4,6},{5,7},{6,4},{7,5},{8,10},{9,11},{10,... | collective-permute-start | bytes 196616 | tf_op jit(solution)/shard_map/ppermute | solution.py:461
  57.1 13.9 %collective-permute-start.15 = (bf16[512,128]{1,0:T(8,128)(2,1)S(1)}, bf16[512,128]{1,0:T(8,128)(2,1)S(1)}, u32[]{:S(2)}, u32[]{:S(2)}) collective-permute-start(bf16[512,128]{1,0:T(8,128)(2,1)S(1)} %pad_maximum_fusion.1), channel_id=1, source_target_pairs={{0,4},{1,5},{2,6},{3,7},{4,0},{5,1},{6,2},{7,3},{8,12},{9,13},{10,... | collective-permute-start | bytes 393224 | tf_op jit(solution)/shard_map/ppermute | solution.py:461
  58.3 12.7 %collective-permute-start.16 = (bf16[512,128]{1,0:T(8,128)(2,1)S(1)}, bf16[512,128]{1,0:T(8,128)(2,1)S(1)}, u32[]{:S(2)}, u32[]{:S(2)}) collective-permute-start(bf16[512,128]{1,0:T(8,128)(2,1)S(1)} %pad_maximum_fusion.1), channel_id=1, source_target_pairs={{0,8},{1,9},{2,10},{3,11},{4,12},{5,13},{6,14},{7,15},{8,0},{9,1},... | collective-permute-start | bytes 393224 | tf_op jit(solution)/shard_map/ppermute | solution.py:461
  61.2 9.9 %collective-permute-start.17 = (bf16[512,128]{1,0:T(8,128)(2,1)S(1)}, bf16[512,128]{1,0:T(8,128)(2,1)S(1)}, u32[]{:S(2)}, u32[]{:S(2)}) collective-permute-start(bf16[512,128]{1,0:T(8,128)(2,1)S(1)} %pad_maximum_fusion.1), channel_id=1, source_target_pairs={{0,12},{1,13},{2,14},{3,15},{4,8},{5,9},{6,10},{7,11},{8,4},{9,5},... | collective-permute-start | bytes 393224 | tf_op jit(solution)/shard_map/ppermute | solution.py:461
  71.2 2.0 %collective-permute-start.18 = (bf16[2048,128]{1,0:T(8,128)(2,1)S(1)}, bf16[2048,128]{1,0:T(8,128)(2,1)S(1)}, u32[]{:S(2)}, u32[]{:S(2)}) collective-permute-start(bf16[2048,128]{1,0:T(8,128)(2,1)S(1)} %pad_maximum_fusion), channel_id=1, source_target_pairs={{0,1},{1,0},{2,3},{3,2},{4,5},{5,4},{6,7},{7,6},{8,9},{9,8},{10,11... | collective-permute-start | bytes 1572872 | tf_op jit(solution)/shard_map/ppermute | solution.py:461
  81.2 1.3 %collective-permute-start.19 = (f32[16,128]{1,0:T(8,128)S(1)}, f32[16,128]{1,0:T(8,128)S(1)}, u32[]{:S(2)}, u32[]{:S(2)}) collective-permute-start(f32[16,128]{1,0:T(8,128)S(1)} %get-tuple-element.69), channel_id=1, source_target_pairs={{0,1},{1,0},{2,3},{3,2},{4,5},{5,4},{6,7},{7,6},{8,9},{9,8},{10,11... | collective-permute-start | bytes 24584 | tf_op jit(solution)/shard_map/ppermute | solution.py:461
  82.4 6.1 %collective-permute-start.20 = (f32[16,128]{1,0:T(8,128)S(1)}, f32[16,128]{1,0:T(8,128)S(1)}, u32[]{:S(2)}, u32[]{:S(2)}) collective-permute-start(f32[16,128]{1,0:T(8,128)S(1)} %add.61), channel_id=1, source_target_pairs={{0,2},{1,3},{2,0},{3,1},{4,6},{5,7},{6,4},{7,5},{8,10},{9,11},{10,... | collective-permute-start | bytes 24584 | tf_op jit(solution)/shard_map/ppermute | solution.py:461
  88.5 6.3 %collective-permute-start.21 = (f32[16,128]{1,0:T(8,128)S(1)}, f32[16,128]{1,0:T(8,128)S(1)}, u32[]{:S(2)}, u32[]{:S(2)}) collective-permute-start(f32[16,128]{1,0:T(8,128)S(1)} %add.62), channel_id=1, source_target_pairs={{0,4},{1,5},{2,6},{3,7},{4,0},{5,1},{6,2},{7,3},{8,12},{9,13},{10,... | collective-permute-start | bytes 24584 | tf_op jit(solution)/shard_map/ppermute | solution.py:461
  94.8 25.9 %collective-permute-start.22 = (f32[16,128]{1,0:T(8,128)S(1)}, f32[16,128]{1,0:T(8,128)S(1)}, u32[]{:S(2)}, u32[]{:S(2)}) collective-permute-start(f32[16,128]{1,0:T(8,128)S(1)} %add.63), channel_id=1, source_target_pairs={{0,12},{1,13},{2,14},{3,15},{4,8},{5,9},{6,10},{7,11},{8,4},{9,5},... | collective-permute-start | bytes 24584 | tf_op jit(solution)/shard_map/ppermute | solution.py:461
  (20 other events, 129.7 us)
